TPU v7x, 32 devices: a whole 2x2x4 slice. The times are simulated.
32 devices in a mesh: dom: 8 (over z, y), rep: 4 (over x, core).
Axes of the slice: x: 2, y: 2, z: 4, core: 2. Of those that a mesh axis runs over, the one named last changes fastest.
Arguments:
- features: bfloat16 [2048, 1024], P('dom', 'rep'), may hold values from -6 to 6
- w_self: bfloat16 [1024, 1024], P('rep'), may hold values from -0.1875 to 0.1875
- w_neigh: bfloat16 [1024, 1024], P('rep'), may hold values from -0.1875 to 0.1875
- grad_out: bfloat16 [2048, 1024], P('dom', 'rep'), may hold values from -6 to 6
- mirror_list: int32 [64, 64], P('dom'), may hold values from 0 to 255, as said below
- mirror_count: int32 [64], P('dom'), may hold values from 1 to 64, as said below
- tile_dst: int32 [64], P('dom'), may hold values from 0 to 1
- tile_src: int32 [64], P('dom'), may hold values from 0 to 5
- tiles: bfloat16 [64, 128, 128], P('dom'), may hold values from 0 to 4, as said below
Outputs:
- hidden_out: bfloat16 [2048, 1024], P('dom', 'rep')
- grad_features: bfloat16 [2048, 1024], P('dom', 'rep')
- grad_self: bfloat16 [1024, 1024], P('rep')
- grad_neigh: bfloat16 [1024, 1024], P('rep')
Inputs may be any that keep to these rules, and one draw needn't show every extreme that they name: `mirror_list`: the entries of one row are distinct. `mirror_count`: every partition has a peer whose count is exactly 64. Weights are zero in columns that fall on unused mirror slots; on each partition the slots after its live tiles hold zeros, and some partition has all 8 slots live.
All inputs are finite; a program needn't handle non-finite values.
Results may differ from a plain program's by a relative error of at most 0.0058.
Values may be sent and summed in bfloat16 or wider, within the bound.
No kernel may reach another device: no remote copies, remote signals or barrier semaphores. Data moves between devices by JAX's collectives and lax.ppermute only.
A program may use at most 64 MiB of HBM per device.

v0:
```python
import functools

import jax
import jax.numpy as jnp
from jax import lax
from jax.experimental import pallas as pl
from jax.experimental.pallas import tpu as pltpu
from jax.sharding import PartitionSpec as P

F32 = jnp.float32
BF16 = jnp.bfloat16
SPECS = {
    "v": pl.BlockSpec(memory_space=pltpu.VMEM),
    "s": pl.BlockSpec(memory_space=pltpu.SMEM),
    "h": pl.BlockSpec(memory_space=pltpu.HBM),
}
ROWS = (((0,), (0,)), ((), ()))
COLS = (((1,), (1,)), ((), ()))


def call(body, outs, ins, scratch=(), flops=0, moved=0, vmem=16, out="v"):
    return pl.pallas_call(
        body,
        out_shape=outs,
        in_specs=[SPECS[spec] for spec, _ in ins],
        out_specs=jax.tree.map(lambda _: SPECS[out], outs),
        scratch_shapes=list(scratch),
        compiler_params=pltpu.CompilerParams(vmem_limit_bytes=vmem * 1024 * 1024),
        cost_estimate=pl.CostEstimate(flops=flops, bytes_accessed=moved, transcendentals=0),
    )(*[array for _, array in ins])


def dot(left, right, dims=(((1,), (0,)), ((), ()))):
    return lax.dot_general(left, right, dims, preferred_element_type=F32)


def block_rows(place, offset, size):
    return pl.ds(pl.multiple_of(lax.bitwise_xor(place, offset) * size, size), size)


def row_onehot(count_ref, lists, rows):
    peers, slots = lists.shape
    peer = lax.broadcasted_iota(jnp.int32, (peers, slots), 0)
    slot = lax.broadcasted_iota(jnp.int32, (peers, slots), 1)

    def fill(at, used):
        return jnp.where(peer == at, count_ref[at], used)

    used = jnp.zeros((peers, slots), jnp.int32)
    if peers <= 16:
        for at in range(peers):
            used = fill(at, used)
    else:
        used = lax.fori_loop(0, peers, fill, used)
    index = jnp.where(slot < used, lists, -1).astype(F32).astype(BF16)
    flat = peers * slots
    spread = (
        lax.broadcasted_iota(jnp.int32, (slots, flat), 0)
        == lax.broadcasted_iota(jnp.int32, (slots, flat), 1) % slots
    )
    wide = dot(index, spread.astype(F32).astype(BF16))
    mine = (
        lax.broadcasted_iota(jnp.int32, (peers, flat), 0)
        == lax.broadcasted_iota(jnp.int32, (peers, flat), 1) // slots
    )
    line = jnp.sum(jnp.where(mine, wide, 0.0), axis=0, keepdims=True).astype(jnp.int32)
    hit = lax.broadcasted_iota(jnp.int32, (rows, flat), 0) == line
    return hit.astype(F32).astype(BF16)


def pick_body(
    count_hbm, list_hbm, feat_hbm, onehot_ref, out_ref, count_ref, list_ref, feat_ref, sems
):
    copies = [
        pltpu.make_async_copy(src, dst, sems.at[k])
        for k, (src, dst) in enumerate(
            ((count_hbm, count_ref), (list_hbm, list_ref), (feat_hbm, feat_ref))
        )
    ]
    for copy in copies:
        copy.start()
    for copy in copies:
        copy.wait()
    onehot = row_onehot(count_ref, list_ref[...], feat_ref.shape[0])
    onehot_ref[...] = onehot
    out_ref[...] = dot(onehot, feat_ref[...], ROWS).astype(BF16)


def prep_body(
    dst_ref, src_ref, tiles_ref, self_hbm, neigh_hbm,
    high_ref, low_ref, deg_ref, self_ref, neigh_ref, adj_ref, sems,
):
    copies = [
        pltpu.make_async_copy(src, dst, sems.at[k])
        for k, (src, dst) in enumerate(((self_hbm, self_ref), (neigh_hbm, neigh_ref)))
    ]
    for copy in copies:
        copy.start()
    slots, side, _ = tiles_ref.shape
    adj_ref[...] = jnp.zeros(adj_ref.shape, F32)
    for t in range(slots):
        dst = pl.ds(pl.multiple_of(dst_ref[t] * side, side), side)
        src = pl.ds(pl.multiple_of(src_ref[t] * side, side), side)
        adj_ref[dst, src] += tiles_ref[t].astype(F32)
    adj = adj_ref[...]
    high = adj.astype(BF16)
    high_ref[...] = high
    low_ref[...] = (adj - high.astype(F32)).astype(BF16)
    degree = jnp.maximum(jnp.sum(adj, axis=1, keepdims=True), 1.0)
    deg_ref[...] = jnp.broadcast_to(degree, deg_ref.shape)
    for copy in copies:
        copy.wait()


def column_block(split, rep, c, reps, cols):
    other = lax.bitwise_xor(rep, c) if split else c
    return pl.ds(pl.multiple_of(other * cols, cols), cols)


def wide_degree(deg_ref, cols):
    return jnp.concatenate([deg_ref[...]] * (cols // deg_ref.shape[1]), axis=1)


def aggregate_body(
    split, rep_ref, feat_ref, inc_ref, high_ref, low_ref, deg_ref, self_ref, neigh_ref,
    own_ref, agg_ref, *refs,
):
    part_refs, table_ref = refs[:-1], refs[-1]
    rows, cols = feat_ref.shape
    feat = feat_ref[...]
    table_ref[:rows] = feat
    table_ref[rows:] = inc_ref[...]
    table = table_ref[...]
    summed = dot(high_ref[...], table) + dot(low_ref[...], table)
    agg = (summed / wide_degree(deg_ref, cols)).astype(BF16)
    agg_ref[...] = agg
    reps = self_ref.shape[1] // cols
    for c in reversed(range(reps)):
        at = column_block(split, rep_ref[0], c, reps, cols)
        value = dot(feat, self_ref[:, at]) + dot(agg, neigh_ref[:, at])
        if not split:
            part_refs[0][c] = value.astype(BF16)

            @pl.when(rep_ref[0] == c)
            def _():
                own_ref[...] = value
        elif c == 0:
            own_ref[...] = value
        elif c == 2:
            part_refs[0][...] = value
        else:
            part_refs[1][c // 2] = value.astype(BF16)


def finish_gate(pre, gout_ref, hid_ref, gpre_ref):
    gate = jax.nn.sigmoid(pre)
    hid_ref[...] = (pre * gate).astype(BF16)
    gpre_ref[...] = (gout_ref[...].astype(F32) * (gate + pre * gate * (1.0 - gate))).astype(BF16)


def gate_body(rep_ref, recv_ref, own_ref, gout_ref, hid_ref, gpre_ref):
    pre = own_ref[...]
    for c in range(recv_ref.shape[0]):
        pre = pre + jnp.where(rep_ref[0] == c, 0.0, recv_ref[c].astype(F32))
    finish_gate(pre, gout_ref, hid_ref, gpre_ref)


def across_body(mine_ref, beside_ref, out_ref):
    out_ref[...] = (mine_ref[...] + beside_ref[1].astype(F32)).astype(BF16)


def gate_blocks_body(own_ref, gout_ref, beside_ref, across_ref, hid_ref, gpre_ref):
    pre = own_ref[...] + beside_ref[0].astype(F32) + across_ref[...].astype(F32)
    finish_gate(pre, gout_ref, hid_ref, gpre_ref)


def back_body(
    high_ref, low_ref, deg_ref, self_ref, neigh_ref, grad_ref, total_ref, mirror_ref
):
    rows, cols = total_ref.shape
    direct = jnp.zeros((rows, cols), F32)
    gagg = jnp.zeros((rows, cols), F32)
    for c in range(grad_ref.shape[0]):
        grad = grad_ref[c]
        at = slice(c * cols, (c + 1) * cols)
        gagg += dot(grad, neigh_ref[:, at], COLS)
        direct += dot(grad, self_ref[:, at], COLS)
    gagg = (gagg / wide_degree(deg_ref, cols)).astype(BF16)
    table = dot(high_ref[...], gagg, ROWS) + dot(low_ref[...], gagg, ROWS)
    total_ref[...] = direct + table[:rows]
    mirror_ref[...] = table[rows:].astype(BF16)


def weight_body(feat_ref, agg_ref, gfull_ref, out_ref):
    cols = feat_ref.shape[1]
    parts = out_ref.shape[0]
    piece = out_ref.shape[1] // 2
    for k, ref in enumerate((feat_ref, agg_ref)):
        left = ref[...]
        for c in range(gfull_ref.shape[0]):
            value = dot(left, gfull_ref[c], ROWS)
            out_ref[:, k * piece:(k + 1) * piece, c * cols:(c + 1) * cols] = value.reshape(
                parts, piece, cols
            ).astype(BF16)


def sum_body(scale, recv_ref, self_ref, neigh_ref):
    piece = self_ref.shape[0]
    for k, ref in enumerate((self_ref, neigh_ref)):
        total = jnp.zeros(ref.shape, F32)
        for d in range(recv_ref.shape[0]):
            total += recv_ref[d, k * piece:(k + 1) * piece].astype(F32)
        ref[...] = (total * scale).astype(BF16)


def group_weight_body(dom_ref, own_ref, other_ref, *refs):
    rows, mine_ref, send_refs, total_ref = refs[:4], refs[4], refs[5:-1], refs[-1]
    lanes = mine_ref.shape[2]
    layer, side = dom_ref[0] // 2, dom_ref[0] % 2
    count = other_ref.shape[0]
    for k in range(2):
        own, other = rows[2 * k][...], rows[2 * k + 1][...]
        for c in range(count):
            cols = own.shape[1]
            total_ref[:, c * cols:(c + 1) * cols] = dot(
                own, own_ref[side * count + c], ROWS
            ) + dot(other, other_ref[c], ROWS)
        mine_ref[k] = total_ref[:, block_rows(layer, 0, lanes)]
        for offset, ref in enumerate(send_refs):
            ref[k] = total_ref[:, block_rows(layer, offset + 1, lanes)].astype(BF16)


def join_body(scale, mine_ref, *refs):
    total = mine_ref[...]
    for ref in refs[:-1]:
        total = total + ref[...].astype(F32)
    refs[-1][...] = (total * scale).astype(BF16)


def place_body(dom_ref, *refs):
    blocks, outs, sems = refs[:-3], refs[-3:-1], refs[-1]
    copies = []
    lanes = blocks[0].shape[2]
    for offset, block in enumerate(blocks):
        place = lax.bitwise_xor(dom_ref[0], offset)
        at = (place % 2) * (len(blocks) // 2) + place // 2
        at = pl.ds(pl.multiple_of(at * lanes, lanes), lanes)
        for k, out_ref in enumerate(outs):
            copies.append(
                pltpu.make_async_copy(block.at[k], out_ref.at[:, at], sems.at[2 * offset + k])
            )
            copies[-1].start()
    for copy in copies:
        copy.wait()


def scatter_body(onehot_ref, total_ref, ret_ref, out_ref):
    out_ref[...] = (total_ref[...] + dot(onehot_ref[...], ret_ref[...])).astype(BF16)


def swap(array, axis, offset):
    return lax.ppermute(array, axis, [(i, i ^ offset) for i in range(lax.axis_size(axis))])


def gather_pieces(array, peers):
    out = {0: array, 4: swap(array, "dom", 4), 2: swap(array, "dom", 2)}
    out[1] = swap(array, "dom", 1)
    out[4], out[1] = lax.optimization_barrier((out[4], out[1]))
    out[6] = swap(out[4], "dom", 2)
    for offset in range(2, peers, 2):
        out[offset + 1] = swap(out[offset], "dom", 1)
    return [out[offset] for offset in range(peers)]


def local(
    features, w_self, w_neigh, grad_out, mirror_list, mirror_count, tile_dst, tile_src, tiles
):
    rows, cols = features.shape
    width = w_self.shape[1]
    peers, slots = mirror_list.shape
    mirrors = peers * slots
    table_rows = rows + mirrors
    reps = width // cols
    struct = jax.ShapeDtypeStruct
    block = struct((rows, cols), BF16)
    rep = lax.axis_index("rep").astype(jnp.int32).reshape(1)
    dom = lax.axis_index("dom").astype(jnp.int32).reshape(1)
    lanes = width // peers
    halves = peers // reps
    split = peers == 8 and reps == 4 and slots % 16 == 0 and lanes % 128 == 0
    mirror_out = struct((mirrors, cols), BF16)

    def exchange(array):
        return lax.all_to_all(
            array.reshape(peers, slots, cols), "dom", split_axis=0, concat_axis=0, tiled=True
        ).reshape(mirrors, cols)

    onehot, outgoing = call(
        pick_body, (struct((rows, mirrors), BF16), mirror_out),
        [("h", mirror_count), ("h", mirror_list), ("h", features)],
        scratch=[
            pltpu.SMEM(mirror_count.shape, jnp.int32), pltpu.VMEM(mirror_list.shape, jnp.int32),
            pltpu.VMEM((rows, cols), BF16), pltpu.SemaphoreType.DMA((3,)),
        ],
        vmem=58,
        flops=2 * mirrors * rows * cols, moved=600_000,
    )
    incoming = exchange(outgoing)
    tiles_late, feat_late, self_late, neigh_late, _ = lax.optimization_barrier(
        (tiles, features, w_self, w_neigh, outgoing)
    )
    high, low, degree, self_near, neigh_near = call(
        prep_body,
        (
            struct((rows, table_rows), BF16), struct((rows, table_rows), BF16),
            struct((rows, 128), F32), struct(w_self.shape, BF16), struct(w_neigh.shape, BF16),
        ),
        [
            ("s", tile_dst), ("s", tile_src), ("v", tiles_late), ("h", self_late),
            ("h", neigh_late),
        ],
        scratch=[pltpu.VMEM((rows, table_rows), F32), pltpu.SemaphoreType.DMA((2,))],
        flops=1_000_000, moved=3_000_000,
    )
    if split:
        feat_beside = swap(features, "dom", 1)
        incoming, feat_beside = lax.optimization_barrier((incoming, feat_beside))
    own, agg, *parts = call(
        functools.partial(aggregate_body, split),
        (struct((rows, cols), F32), block)
        + (
            (struct((rows, cols), F32), struct((2, rows, cols), BF16)) if split
            else (struct((reps, rows, cols), BF16),)
        ),
        [
            ("s", rep), ("v", feat_late), ("v", incoming), ("v", high), ("v", low),
            ("v", degree), ("v", self_near), ("v", neigh_near),
        ],
        scratch=[pltpu.VMEM((table_rows, cols), BF16)],
        flops=600_000_000, moved=3_000_000,
    )
    scale = float(rows * peers) ** (-0.5)
    if split:
        agg_beside = swap(agg, "dom", 1)
        grad_out, agg_beside = lax.optimization_barrier((grad_out, agg_beside))
        beside = swap(parts[1], "rep", 1)
        across = call(
            across_body, block, [("v", parts[0]), ("v", beside)], flops=100_000, moved=500_000
        )
        across = swap(across, "rep", 2)
        hidden, grad_pre = call(
            gate_blocks_body, (block, block),
            [("v", own), ("v", grad_out), ("v", beside), ("v", across)],
            flops=2_000_000, moved=1_300_000,
        )
    else:
        recv = lax.all_to_all(parts[0], "rep", split_axis=0, concat_axis=0, tiled=True)
        hidden, grad_pre = call(
            gate_body, (block, block),
            [("s", rep), ("v", recv), ("v", own), ("v", grad_out)],
            flops=2_000_000, moved=1_300_000,
        )
    grad_full = lax.all_gather(grad_pre, "rep", axis=0, tiled=False)
    total, mirror_grad = call(
        back_body, (struct((rows, cols), F32), mirror_out),
        [
            ("v", high), ("v", low), ("v", degree), ("v", self_near), ("v", neigh_near),
            ("v", grad_full),
        ],
        flops=600_000_000, moved=3_000_000,
    )
    if split:
        start = (1 - dom[0] % 2) * (reps // 2)
        half = swap(lax.dynamic_slice_in_dim(grad_full, start, reps // 2, 0), "dom", 1)
        half, mirror_grad = lax.optimization_barrier((half, mirror_grad))
        piece = struct((2, rows, lanes), BF16)
        mine, *sends = call(
            group_weight_body, (struct((2, rows, lanes), F32),) + (piece,) * (reps - 1),
            [
                ("s", dom), ("v", grad_full), ("v", half), ("v", features),
                ("v", feat_beside), ("v", agg), ("v", agg_beside),
            ],
            scratch=[pltpu.VMEM((rows, width // 2), F32)],
            flops=600_000_000, moved=3_000_000,
        )
        layers = [swap(send, "dom", 2 * k + 2) for k, send in enumerate(sends)]
        mine = call(
            functools.partial(join_body, scale), piece,
            [("v", mine)] + [("v", got) for got in layers], flops=200_000, moved=500_000,
        )
        pieces = gather_pieces(mine, peers)
    returned = exchange(mirror_grad)
    grad_features = call(
        scatter_body, block, [("v", onehot), ("v", total), ("v", returned)],
        flops=2 * mirrors * rows * cols, moved=700_000,
    )
    if split:
        out_self, out_neigh = call(
            place_body, (struct((rows, width), BF16), struct((rows, width), BF16)),
            [("s", dom)] + [("v", part) for part in pieces],
            scratch=[pltpu.SemaphoreType.DMA((2 * peers,))], moved=2_000_000, out="h",
        )
    else:
        piece = cols // peers
        partial = call(
            weight_body, struct((peers, 2 * piece, width), BF16),
            [("v", features), ("v", agg), ("v", grad_full)],
            flops=600_000_000, moved=2_000_000,
        )
        gathered = lax.all_to_all(partial, "dom", split_axis=0, concat_axis=0, tiled=True)
        mine_self, mine_neigh = call(
            functools.partial(sum_body, scale),
            (struct((piece, width), BF16), struct((piece, width), BF16)),
            [("v", gathered)], flops=1_000_000, moved=1_200_000,
        )
        out_self = lax.all_gather(mine_self, "dom", axis=0, tiled=True)
        out_neigh = lax.all_gather(mine_neigh, "dom", axis=0, tiled=True)
    return hidden, grad_features, out_self, out_neigh


def solution(mesh):
    in_specs = (
        P("dom", "rep"),
        P("rep", None),
        P("rep", None),
        P("dom", "rep"),
        P("dom", None),
        P("dom"),
        P("dom"),
        P("dom"),
        P("dom", None, None),
    )
    out_specs = (P("dom", "rep"), P("dom", "rep"), P("rep", None), P("rep", None))
    return jax.shard_map(local, mesh=mesh, in_specs=in_specs, out_specs=out_specs, check_vma=False)
```

profile of v0, /device:TPU:0, one launch (start us, length us, event | category | flops | bytes accessed | tf_op | source)
XLA Modules:
  0.0 81.9 jit_solution(7219177401797277223)
XLA Ops:
  0.6 2.1 %shard_map.120 = (bf16[256,512]{1,0:T(8,128)(2,1)}, bf16[512,256]{1,0:T(8,128)(2,1)}) custom-call(s32[8]{0:T(128)} %count_hbm.1, s32[8,64]{1,0:T(8,128)} %list_hbm.1, bf16[256,256]{1,0:T(8,128)(2,1)} %refs_0_.1), custom_call_target="tpu_custom_call" | custom-call | flops 67108864 | bytes 600000 | tf_op jit(solution)/shard_map/pallas_call | solution.py:22
  2.8 7.4 %all-to-all-start = ((bf16[8,64,256]{2,1,0:T(8,128)(2,1)}), bf16[8,64,256]{2,1,0:T(8,128)(2,1)S(1)}, u32[]{:S(2)}, u32[]{:S(2)}) async-start(bf16[8,64,256]{2,1,0:T(8,128)(2,1)} %bitcast.12), calls=%async_computation | async-start | bytes 524288 | tf_op jit(solution)/shard_map/all_to_all | solution.py:294
  10.2 2.0 %collective-permute-start = (bf16[256,256]{1,0:T(8,128)(2,1)S(1)}, bf16[256,256]{1,0:T(8,128)(2,1)S(1)}, u32[]{:S(2)}, u32[]{:S(2)}) collective-permute-start(bf16[256,256]{1,0:T(8,128)(2,1)S(1)} %copy-done.4), channel_id=1, source_target_pairs={{0,4},{4,0},{8,12},{12,8},{16,20},{20,16},{24,28},{28,24},{1,5},{5... | collective-permute-start | bytes 393224 | tf_op jit(solution)/shard_map/ppermute | solution.py:262
  12.9 1.0 %copy-done.1 = bf16[256,1024]{1,0:T(8,128)(2,1)S(1)} copy-done((bf16[256,1024]{1,0:T(8,128)(2,1)S(1)}, bf16[256,1024]{1,0:T(8,128)(2,1)}, u32[]{:S(2)}) %copy-start.1) | copy-done | bytes 524312
  14.0 0.9 %copy-done.3 = bf16[8,128,128]{2,1,0:T(8,128)(2,1)S(1)} copy-done((bf16[8,128,128]{2,1,0:T(8,128)(2,1)S(1)}, bf16[8,128,128]{2,1,0:T(8,128)(2,1)}, u32[]{:S(2)}) %copy-start.3) | copy-done | bytes 262168
  14.9 0.9 %shard_map.121 = (bf16[256,768]{1,0:T(8,128)(2,1)S(1)}, bf16[256,768]{1,0:T(8,128)(2,1)S(1)}, f32[256,128]{1,0:T(8,128)S(1)}, bf16[256,1024]{1,0:T(8,128)(2,1)S(1)}, bf16[256,1024]{1,0:T(8,128)(2,1)S(1)}) custom-call(s32[8]{0:T(128)S(1)} %copy-done.6, s32[8]{0:T(128)S(1)} %copy-done.7, bf16[8,128,128]{2,1,0:T(8,128)(2,1)S(1)} %copy-done.3, ...), custom_call_target="tpu_custom_call" | custom-call | flops 1000000 | bytes 3000000 | tf_op jit(solution)/shard_map/pallas_call | solution.py:22
  15.9 2.0 %collective-permute-done.refs_1_ = bf16[256,256]{1,0:T(8,128)(2,1)S(1)} collective-permute-done((bf16[256,256]{1,0:T(8,128)(2,1)S(1)}, bf16[256,256]{1,0:T(8,128)(2,1)S(1)}, u32[]{:S(2)}, u32[]{:S(2)}) %collective-permute-start) | collective-permute-done | bytes 131104 | tf_op jit(solution)/shard_map/ppermute | solution.py:262
  17.8 1.3 %all-to-all-done = bf16[8,64,256]{2,1,0:T(8,128)(2,1)S(1)} async-done(((bf16[8,64,256]{2,1,0:T(8,128)(2,1)}), bf16[8,64,256]{2,1,0:T(8,128)(2,1)S(1)}, u32[]{:S(2)}, u32[]{:S(2)}) %all-to-all-start) | async-done | bytes 262176 | tf_op jit(solution)/shard_map/all_to_all | solution.py:294
  19.1 1.0 %shard_map.122 = (f32[256,256]{1,0:T(8,128)S(1)}, bf16[256,256]{1,0:T(8,128)(2,1)S(1)}, f32[256,256]{1,0:T(8,128)S(1)}, bf16[2,256,256]{2,1,0:T(8,128)(2,1)S(1)}) custom-call(s32[1]{0:T(128)} %bitcast.rep_ref, bf16[256,256]{1,0:T(8,128)(2,1)S(1)} %copy-done.4, bf16[512,256]{1,0:T(8,128)(2,1)S(1)} %bitcast.11, ...), custom_call_target="tpu_custom_call" | custom-call | flops 600000000 | bytes 3000000 | tf_op jit(solution)/shard_map/pallas_call | solution.py:22
  20.2 1.5 %collective-permute-start.1 = (bf16[256,256]{1,0:T(8,128)(2,1)S(1)}, bf16[256,256]{1,0:T(8,128)(2,1)S(1)}, u32[]{:S(2)}, u32[]{:S(2)}) collective-permute-start(bf16[256,256]{1,0:T(8,128)(2,1)S(1)} %get-tuple-element.49.refs_2_), channel_id=1, source_target_pairs={{0,4},{4,0},{8,12},{12,8},{16,20},{20,16},{24,28},{28,24},{1,5},{5... | collective-permute-start | bytes 393224 | tf_op jit(solution)/shard_map/ppermute | solution.py:262
  21.7 1.6 %collective-permute-start.3 = (bf16[256,256]{1,0:T(8,128)(2,1)S(1)}, bf16[256,256]{1,0:T(8,128)(2,1)S(1)}, u32[]{:S(2)}, u32[]{:S(2)}) collective-permute-start(bf16[256,256]{1,0:T(8,128)(2,1)S(1)} %shard_map.123), channel_id=1, source_target_pairs={{0,2},{1,3},{2,0},{3,1},{4,6},{5,7},{6,4},{7,5},{8,10},{9,11},{10,... | collective-permute-start | bytes 393224 | tf_op jit(solution)/shard_map/ppermute | solution.py:262
  23.3 2.8 %collective-permute-done.1.refs_3_ = bf16[256,256]{1,0:T(8,128)(2,1)S(1)} collective-permute-done((bf16[256,256]{1,0:T(8,128)(2,1)S(1)}, bf16[256,256]{1,0:T(8,128)(2,1)S(1)}, u32[]{:S(2)}, u32[]{:S(2)}) %collective-permute-start.1) | collective-permute-done | bytes 131104 | tf_op jit(solution)/shard_map/ppermute | solution.py:262
  26.1 1.2 %collective-permute-done.3.across_ref = bf16[256,256]{1,0:T(8,128)(2,1)S(1)} collective-permute-done((bf16[256,256]{1,0:T(8,128)(2,1)S(1)}, bf16[256,256]{1,0:T(8,128)(2,1)S(1)}, u32[]{:S(2)}, u32[]{:S(2)}) %collective-permute-start.3) | collective-permute-done | bytes 131104 | tf_op jit(solution)/shard_map/ppermute | solution.py:262
  28.1 7.2 %all-gather = bf16[1024,256]{1,0:T(8,128)(2,1)S(1)} all-gather(bf16[256,256]{1,0:T(8,128)(2,1)S(1)} %get-tuple-element.55), channel_id=2, replica_groups=mesh['dom'=8,'rep'=4] {'rep'}, dimensions={0}, use_global_device_ids=true | all-gather | bytes 655360 | tf_op jit(solution)/shard_map/all_gather | solution.py:363
  35.3 1.5 %collective-permute-start.4 = (bf16[2,256,256]{2,1,0:T(8,128)(2,1)S(1)}, bf16[2,256,256]{2,1,0:T(8,128)(2,1)S(1)}, u32[]{:S(2)}, u32[]{:S(2)}) collective-permute-start(bf16[2,256,256]{2,1,0:T(8,128)(2,1)S(1)} %constant_dynamic-slice_fusion), channel_id=1, source_target_pairs={{0,4},{4,0},{8,12},{12,8},{16,20},{20,16},{24,28},{28,24},{1,5},{5... | collective-permute-start | bytes 786440 | tf_op jit(solution)/shard_map/ppermute | solution.py:262
  36.7 1.5 %shard_map.125 = (f32[256,256]{1,0:T(8,128)S(1)}, bf16[512,256]{1,0:T(8,128)(2,1)}) custom-call(bf16[256,768]{1,0:T(8,128)(2,1)S(1)} %get-tuple-element.43.high_ref, bf16[256,768]{1,0:T(8,128)(2,1)S(1)} %get-tuple-element.44.low_ref, f32[256,128]{1,0:T(8,128)S(1)} %get-tuple-element.45.deg_ref, bf16[256,1024]{1,0:T(8,128)(2,1)S(1)} %get-tuple-element.46.self_ref, ...), custom_call_target="tpu_custom_call" | custom-call | flops 600000000 | bytes 3000000 | tf_op jit(solution)/shard_map/pallas_call | solution.py:22
  38.3 5.6 %collective-permute-done.4.other_ref = bf16[2,256,256]{2,1,0:T(8,128)(2,1)S(1)} collective-permute-done((bf16[2,256,256]{2,1,0:T(8,128)(2,1)S(1)}, bf16[2,256,256]{2,1,0:T(8,128)(2,1)S(1)}, u32[]{:S(2)}, u32[]{:S(2)}) %collective-permute-start.4) | collective-permute-done | bytes 262176 | tf_op jit(solution)/shard_map/ppermute | solution.py:262
  44.4 1.1 %collective-permute-start.5 = (bf16[2,256,128]{2,1,0:T(8,128)(2,1)S(1)}, bf16[2,256,128]{2,1,0:T(8,128)(2,1)S(1)}, u32[]{:S(2)}, u32[]{:S(2)}) collective-permute-start(bf16[2,256,128]{2,1,0:T(8,128)(2,1)S(1)} %get-tuple-element.63), channel_id=1, source_target_pairs={{0,8},{4,12},{8,0},{12,4},{16,24},{20,28},{24,16},{28,20},{1,9},{5... | collective-permute-start | bytes 393224 | tf_op jit(solution)/shard_map/ppermute | solution.py:262
  45.6 1.8 %collective-permute-start.6 = (bf16[2,256,128]{2,1,0:T(8,128)(2,1)S(1)}, bf16[2,256,128]{2,1,0:T(8,128)(2,1)S(1)}, u32[]{:S(2)}, u32[]{:S(2)}) collective-permute-start(bf16[2,256,128]{2,1,0:T(8,128)(2,1)S(1)} %get-tuple-element.64), channel_id=1, source_target_pairs={{0,16},{4,20},{8,24},{12,28},{16,0},{20,4},{24,8},{28,12},{1,17},{... | collective-permute-start | bytes 393224 | tf_op jit(solution)/shard_map/ppermute | solution.py:262
  47.4 1.5 %collective-permute-start.7 = (bf16[2,256,128]{2,1,0:T(8,128)(2,1)S(1)}, bf16[2,256,128]{2,1,0:T(8,128)(2,1)S(1)}, u32[]{:S(2)}, u32[]{:S(2)}) collective-permute-start(bf16[2,256,128]{2,1,0:T(8,128)(2,1)S(1)} %get-tuple-element.65), channel_id=1, source_target_pairs={{0,24},{4,28},{8,16},{12,20},{16,8},{20,12},{24,0},{28,4},{1,25},{... | collective-permute-start | bytes 393224 | tf_op jit(solution)/shard_map/ppermute | solution.py:262
  48.9 3.6 %all-to-all-start.1 = ((bf16[8,64,256]{2,1,0:T(8,128)(2,1)}), bf16[8,64,256]{2,1,0:T(8,128)(2,1)S(1)}, u32[]{:S(2)}, u32[]{:S(2)}) async-start(bf16[8,64,256]{2,1,0:T(8,128)(2,1)} %bitcast.4), calls=%async_computation.1 | async-start | bytes 524288 | tf_op jit(solution)/shard_map/all_to_all | solution.py:294
  52.5 8.2 %collective-permute-done.6.refs_1_ = bf16[2,256,128]{2,1,0:T(8,128)(2,1)S(1)} collective-permute-done((bf16[2,256,128]{2,1,0:T(8,128)(2,1)S(1)}, bf16[2,256,128]{2,1,0:T(8,128)(2,1)S(1)}, u32[]{:S(2)}, u32[]{:S(2)}) %collective-permute-start.6) | collective-permute-done | bytes 131104 | tf_op jit(solution)/shard_map/ppermute | solution.py:262
  60.8 4.0 %collective-permute-start.8 = (bf16[2,256,128]{2,1,0:T(8,128)(2,1)S(1)}, bf16[2,256,128]{2,1,0:T(8,128)(2,1)S(1)}, u32[]{:S(2)}, u32[]{:S(2)}) collective-permute-start(bf16[2,256,128]{2,1,0:T(8,128)(2,1)S(1)} %shard_map.128.refs_0_), channel_id=1, source_target_pairs={{0,16},{4,20},{8,24},{12,28},{16,0},{20,4},{24,8},{28,12},{1,17},{... | collective-permute-start | bytes 393224 | tf_op jit(solution)/shard_map/ppermute | solution.py:262
  65.5 5.4 %collective-permute-done.8.refs_4_ = bf16[2,256,128]{2,1,0:T(8,128)(2,1)S(1)} collective-permute-done((bf16[2,256,128]{2,1,0:T(8,128)(2,1)S(1)}, bf16[2,256,128]{2,1,0:T(8,128)(2,1)S(1)}, u32[]{:S(2)}, u32[]{:S(2)}) %collective-permute-start.8) | collective-permute-done | bytes 131104 | tf_op jit(solution)/shard_map/ppermute | solution.py:262
  70.9 0.8 collective-permute-start.12
  72.2 1.8 %collective-permute-start.11 = (bf16[2,256,128]{2,1,0:T(8,128)(2,1)S(1)}, bf16[2,256,128]{2,1,0:T(8,128)(2,1)S(1)}, u32[]{:S(2)}, u32[]{:S(2)}) collective-permute-start(bf16[2,256,128]{2,1,0:T(8,128)(2,1)S(1)} %collective-permute-done.10.refs_2_), channel_id=1, source_target_pairs={{0,4},{4,0},{8,12},{12,8},{16,20},{20,16},{24,28},{28,24},{1,5},{5... | collective-permute-start | bytes 393224 | tf_op jit(solution)/shard_map/ppermute | solution.py:262
  74.0 1.9 %collective-permute-done.13.refs_6_ = bf16[2,256,128]{2,1,0:T(8,128)(2,1)S(1)} collective-permute-done((bf16[2,256,128]{2,1,0:T(8,128)(2,1)S(1)}, bf16[2,256,128]{2,1,0:T(8,128)(2,1)S(1)}, u32[]{:S(2)}, u32[]{:S(2)}) %collective-permute-start.13) | collective-permute-done | bytes 131104 | tf_op jit(solution)/shard_map/ppermute | solution.py:262
  75.9 0.8 collective-permute-start.14
  76.7 0.9 %shard_map.126 = bf16[256,256]{1,0:T(8,128)(2,1)} custom-call(bf16[256,512]{1,0:T(8,128)(2,1)S(1)} %copy-done.2, f32[256,256]{1,0:T(8,128)S(1)} %get-tuple-element.56.total_ref, bf16[512,256]{1,0:T(8,128)(2,1)S(1)} %bitcast.10), custom_call_target="tpu_custom_call" | custom-call | flops 67108864 | bytes 700000 | tf_op jit(solution)/shard_map/pallas_call | solution.py:22
  77.6 1.1 %collective-permute-done.11.refs_3_ = bf16[2,256,128]{2,1,0:T(8,128)(2,1)S(1)} collective-permute-done((bf16[2,256,128]{2,1,0:T(8,128)(2,1)S(1)}, bf16[2,256,128]{2,1,0:T(8,128)(2,1)S(1)}, u32[]{:S(2)}, u32[]{:S(2)}) %collective-permute-start.11) | collective-permute-done | bytes 131104 | tf_op jit(solution)/shard_map/ppermute | solution.py:262
  78.7 2.2 %collective-permute-done.14.refs_7_ = bf16[2,256,128]{2,1,0:T(8,128)(2,1)S(1)} collective-permute-done((bf16[2,256,128]{2,1,0:T(8,128)(2,1)S(1)}, bf16[2,256,128]{2,1,0:T(8,128)(2,1)S(1)}, u32[]{:S(2)}, u32[]{:S(2)}) %collective-permute-start.14) | collective-permute-done | bytes 131104 | tf_op jit(solution)/shard_map/ppermute | solution.py:262
  80.8 1.1 %shard_map.129 = (bf16[256,1024]{1,0:T(8,128)(2,1)}, bf16[256,1024]{1,0:T(8,128)(2,1)}) custom-call(s32[1]{0:T(128)} %bitcast.6.dom_ref, bf16[2,256,128]{2,1,0:T(8,128)(2,1)S(1)} %shard_map.128.refs_0_, bf16[2,256,128]{2,1,0:T(8,128)(2,1)S(1)} %collective-permute-done.9.refs_1_, bf16[2,256,128]{2,1,0:T(8,128)(2,1)S(1)} %collective-permute-done.10.refs_2_, ...), custom_call_target="tpu_custom_call" | custom-call | bytes 2000000 | tf_op jit(solution)/shard_map/pallas_call | solution.py:22
  (30 shorter events, 3.4 us)
Async XLA Ops:
  0.6 11.6 %copy-start = (bf16[256,1024]{1,0:T(8,128)(2,1)S(1)}, bf16[256,1024]{1,0:T(8,128)(2,1)}, u32[]{:S(2)}) copy-start(bf16[256,1024]{1,0:T(8,128)(2,1)} %self_hbm) | copy-start | bytes 1572868
  2.8 7.4 %copy-start.4 = (bf16[256,256]{1,0:T(8,128)(2,1)S(1)}, bf16[256,256]{1,0:T(8,128)(2,1)}, u32[]{:S(2)}) copy-start(bf16[256,256]{1,0:T(8,128)(2,1)} %refs_0_.1) | copy-start | bytes 393220
  2.8 16.3 %all-to-all-start = ((bf16[8,64,256]{2,1,0:T(8,128)(2,1)}), bf16[8,64,256]{2,1,0:T(8,128)(2,1)S(1)}, u32[]{:S(2)}, u32[]{:S(2)}) async-start(bf16[8,64,256]{2,1,0:T(8,128)(2,1)} %bitcast.12), calls=%async_computation | async-start | bytes 524288 | tf_op jit(solution)/shard_map/all_to_all | solution.py:294
  10.2 7.6 %collective-permute-start = (bf16[256,256]{1,0:T(8,128)(2,1)S(1)}, bf16[256,256]{1,0:T(8,128)(2,1)S(1)}, u32[]{:S(2)}, u32[]{:S(2)}) collective-permute-start(bf16[256,256]{1,0:T(8,128)(2,1)S(1)} %copy-done.4), channel_id=1, source_target_pairs={{0,4},{4,0},{8,12},{12,8},{16,20},{20,16},{24,28},{28,24},{1,5},{5... | collective-permute-start | bytes 393224 | tf_op jit(solution)/shard_map/ppermute | solution.py:262
  12.2 0.7 copy-start.6
  12.2 0.7 copy-start.7
  12.9 1.0 %copy-start.1 = (bf16[256,1024]{1,0:T(8,128)(2,1)S(1)}, bf16[256,1024]{1,0:T(8,128)(2,1)}, u32[]{:S(2)}) copy-start(bf16[256,1024]{1,0:T(8,128)(2,1)} %neigh_hbm) | copy-start | bytes 1572868
  14.0 0.9 %copy-start.3 = (bf16[8,128,128]{2,1,0:T(8,128)(2,1)S(1)}, bf16[8,128,128]{2,1,0:T(8,128)(2,1)}, u32[]{:S(2)}) copy-start(bf16[8,128,128]{2,1,0:T(8,128)(2,1)} %tiles_ref) | copy-start | bytes 786436
  20.1 1.6 %collective-permute-start.2 = (bf16[2,256,256]{2,1,0:T(8,128)(2,1)S(1)}, bf16[2,256,256]{2,1,0:T(8,128)(2,1)S(1)}, u32[]{:S(2)}, u32[]{:S(2)}) collective-permute-start(bf16[2,256,256]{2,1,0:T(8,128)(2,1)S(1)} %get-tuple-element.51), channel_id=1, source_target_pairs={{0,1},{1,0},{2,3},{3,2},{4,5},{5,4},{6,7},{7,6},{8,9},{9,8},{10,11... | collective-permute-start | bytes 786440 | tf_op jit(solution)/shard_map/ppermute | solution.py:262
  20.2 5.9 %collective-permute-start.1 = (bf16[256,256]{1,0:T(8,128)(2,1)S(1)}, bf16[256,256]{1,0:T(8,128)(2,1)S(1)}, u32[]{:S(2)}, u32[]{:S(2)}) collective-permute-start(bf16[256,256]{1,0:T(8,128)(2,1)S(1)} %get-tuple-element.49.refs_2_), channel_id=1, source_target_pairs={{0,4},{4,0},{8,12},{12,8},{16,20},{20,16},{24,28},{28,24},{1,5},{5... | collective-permute-start | bytes 393224 | tf_op jit(solution)/shard_map/ppermute | solution.py:262
  21.7 5.6 %copy-start.5 = (bf16[256,256]{1,0:T(8,128)(2,1)S(1)}, bf16[256,256]{1,0:T(8,128)(2,1)}, u32[]{:S(2)}) copy-start(bf16[256,256]{1,0:T(8,128)(2,1)} %gout_ref) | copy-start | bytes 393220
  21.7 5.6 %collective-permute-start.3 = (bf16[256,256]{1,0:T(8,128)(2,1)S(1)}, bf16[256,256]{1,0:T(8,128)(2,1)S(1)}, u32[]{:S(2)}, u32[]{:S(2)}) collective-permute-start(bf16[256,256]{1,0:T(8,128)(2,1)S(1)} %shard_map.123), channel_id=1, source_target_pairs={{0,2},{1,3},{2,0},{3,1},{4,6},{5,7},{6,4},{7,5},{8,10},{9,11},{10,... | collective-permute-start | bytes 393224 | tf_op jit(solution)/shard_map/ppermute | solution.py:262
  35.3 8.6 %collective-permute-start.4 = (bf16[2,256,256]{2,1,0:T(8,128)(2,1)S(1)}, bf16[2,256,256]{2,1,0:T(8,128)(2,1)S(1)}, u32[]{:S(2)}, u32[]{:S(2)}) collective-permute-start(bf16[2,256,256]{2,1,0:T(8,128)(2,1)S(1)} %constant_dynamic-slice_fusion), channel_id=1, source_target_pairs={{0,4},{4,0},{8,12},{12,8},{16,20},{20,16},{24,28},{28,24},{1,5},{5... | collective-permute-start | bytes 786440 | tf_op jit(solution)/shard_map/ppermute | solution.py:262
  44.4 8.1 %collective-permute-start.5 = (bf16[2,256,128]{2,1,0:T(8,128)(2,1)S(1)}, bf16[2,256,128]{2,1,0:T(8,128)(2,1)S(1)}, u32[]{:S(2)}, u32[]{:S(2)}) collective-permute-start(bf16[2,256,128]{2,1,0:T(8,128)(2,1)S(1)} %get-tuple-element.63), channel_id=1, source_target_pairs={{0,8},{4,12},{8,0},{12,4},{16,24},{20,28},{24,16},{28,20},{1,9},{5... | collective-permute-start | bytes 393224 | tf_op jit(solution)/shard_map/ppermute | solution.py:262
  45.6 15.2 %collective-permute-start.6 = (bf16[2,256,128]{2,1,0:T(8,128)(2,1)S(1)}, bf16[2,256,128]{2,1,0:T(8,128)(2,1)S(1)}, u32[]{:S(2)}, u32[]{:S(2)}) collective-permute-start(bf16[2,256,128]{2,1,0:T(8,128)(2,1)S(1)} %get-tuple-element.64), channel_id=1, source_target_pairs={{0,16},{4,20},{8,24},{12,28},{16,0},{20,4},{24,8},{28,12},{1,17},{... | collective-permute-start | bytes 393224 | tf_op jit(solution)/shard_map/ppermute | solution.py:262
  47.4 13.3 %collective-permute-start.7 = (bf16[2,256,128]{2,1,0:T(8,128)(2,1)S(1)}, bf16[2,256,128]{2,1,0:T(8,128)(2,1)S(1)}, u32[]{:S(2)}, u32[]{:S(2)}) collective-permute-start(bf16[2,256,128]{2,1,0:T(8,128)(2,1)S(1)} %get-tuple-element.65), channel_id=1, source_target_pairs={{0,24},{4,28},{8,16},{12,20},{16,8},{20,12},{24,0},{28,4},{1,25},{... | collective-permute-start | bytes 393224 | tf_op jit(solution)/shard_map/ppermute | solution.py:262
  48.9 27.8 %all-to-all-start.1 = ((bf16[8,64,256]{2,1,0:T(8,128)(2,1)}), bf16[8,64,256]{2,1,0:T(8,128)(2,1)S(1)}, u32[]{:S(2)}, u32[]{:S(2)}) async-start(bf16[8,64,256]{2,1,0:T(8,128)(2,1)} %bitcast.4), calls=%async_computation.1 | async-start | bytes 524288 | tf_op jit(solution)/shard_map/all_to_all | solution.py:294
  60.7 16.0 %copy-start.2 = (bf16[256,512]{1,0:T(8,128)(2,1)S(1)}, bf16[256,512]{1,0:T(8,128)(2,1)}, u32[]{:S(2)}) copy-start(bf16[256,512]{1,0:T(8,128)(2,1)} %get-tuple-element.54.onehot_ref) | copy-start | bytes 786436
  60.8 10.1 %collective-permute-start.8 = (bf16[2,256,128]{2,1,0:T(8,128)(2,1)S(1)}, bf16[2,256,128]{2,1,0:T(8,128)(2,1)S(1)}, u32[]{:S(2)}, u32[]{:S(2)}) collective-permute-start(bf16[2,256,128]{2,1,0:T(8,128)(2,1)S(1)} %shard_map.128.refs_0_), channel_id=1, source_target_pairs={{0,16},{4,20},{8,24},{12,28},{16,0},{20,4},{24,8},{28,12},{1,17},{... | collective-permute-start | bytes 393224 | tf_op jit(solution)/shard_map/ppermute | solution.py:262
  64.8 6.1 %collective-permute-start.9 = (bf16[2,256,128]{2,1,0:T(8,128)(2,1)S(1)}, bf16[2,256,128]{2,1,0:T(8,128)(2,1)S(1)}, u32[]{:S(2)}, u32[]{:S(2)}) collective-permute-start(bf16[2,256,128]{2,1,0:T(8,128)(2,1)S(1)} %shard_map.128.refs_0_), channel_id=1, source_target_pairs={{0,4},{4,0},{8,12},{12,8},{16,20},{20,16},{24,28},{28,24},{1,5},{5... | collective-permute-start | bytes 393224 | tf_op jit(solution)/shard_map/ppermute | solution.py:262
  65.5 6.7 %collective-permute-start.10 = (bf16[2,256,128]{2,1,0:T(8,128)(2,1)S(1)}, bf16[2,256,128]{2,1,0:T(8,128)(2,1)S(1)}, u32[]{:S(2)}, u32[]{:S(2)}) collective-permute-start(bf16[2,256,128]{2,1,0:T(8,128)(2,1)S(1)} %shard_map.128.refs_0_), channel_id=1, source_target_pairs={{0,8},{4,12},{8,0},{12,4},{16,24},{20,28},{24,16},{28,20},{1,9},{5... | collective-permute-start | bytes 393224 | tf_op jit(solution)/shard_map/ppermute | solution.py:262
  70.9 5.0 %collective-permute-start.13 = (bf16[2,256,128]{2,1,0:T(8,128)(2,1)S(1)}, bf16[2,256,128]{2,1,0:T(8,128)(2,1)S(1)}, u32[]{:S(2)}, u32[]{:S(2)}) collective-permute-start(bf16[2,256,128]{2,1,0:T(8,128)(2,1)S(1)} %collective-permute-done.8.refs_4_), channel_id=1, source_target_pairs={{0,8},{4,12},{8,0},{12,4},{16,24},{20,28},{24,16},{28,20},{1,9},{5... | collective-permute-start | bytes 393224 | tf_op jit(solution)/shard_map/ppermute | solution.py:262
  70.9 7.8 %collective-permute-start.12 = (bf16[2,256,128]{2,1,0:T(8,128)(2,1)S(1)}, bf16[2,256,128]{2,1,0:T(8,128)(2,1)S(1)}, u32[]{:S(2)}, u32[]{:S(2)}) collective-permute-start(bf16[2,256,128]{2,1,0:T(8,128)(2,1)S(1)} %collective-permute-done.8.refs_4_), channel_id=1, source_target_pairs={{0,4},{4,0},{8,12},{12,8},{16,20},{20,16},{24,28},{28,24},{1,5},{5... | collective-permute-start | bytes 393224 | tf_op jit(solution)/shard_map/ppermute | solution.py:262
  72.2 6.5 %collective-permute-start.11 = (bf16[2,256,128]{2,1,0:T(8,128)(2,1)S(1)}, bf16[2,256,128]{2,1,0:T(8,128)(2,1)S(1)}, u32[]{:S(2)}, u32[]{:S(2)}) collective-permute-start(bf16[2,256,128]{2,1,0:T(8,128)(2,1)S(1)} %collective-permute-done.10.refs_2_), channel_id=1, source_target_pairs={{0,4},{4,0},{8,12},{12,8},{16,20},{20,16},{24,28},{28,24},{1,5},{5... | collective-permute-start | bytes 393224 | tf_op jit(solution)/shard_map/ppermute | solution.py:262
  75.9 5.0 %collective-permute-start.14 = (bf16[2,256,128]{2,1,0:T(8,128)(2,1)S(1)}, bf16[2,256,128]{2,1,0:T(8,128)(2,1)S(1)}, u32[]{:S(2)}, u32[]{:S(2)}) collective-permute-start(bf16[2,256,128]{2,1,0:T(8,128)(2,1)S(1)} %collective-permute-done.13.refs_6_), channel_id=1, source_target_pairs={{0,4},{4,0},{8,12},{12,8},{16,20},{20,16},{24,28},{28,24},{1,5},{5... | collective-permute-start | bytes 393224 | tf_op jit(solution)/shard_map/ppermute | solution.py:262
where the time goes:
time: 82.4 us; the launch traced here: 81.9 us
  waiting for transfers between devices  32.3 us (39%)
  starting transfers between devices  30.2 us (37%)
  Pallas kernels  8.93 us (11%)
  blocking collectives  7.15 us (9%)
  local copies, waits for them, and re-layouts  2.69 us (3%)
    ppermute x15, waiting for transfers between devices, swap(): lax.ppermute(array, axis, [(i, i ^ offset) for i in range(lax.axis_size(a...  31 us
    ppermute x15, starting transfers between devices, swap(): lax.ppermute(array, axis, [(i, i ^ offset) for i in range(lax.axis_size(a...  19.1 us
    all_to_all x2, starting transfers between devices, exchange(): lax.all_to_all(array.reshape(peers, slots, cols), 'dom', split_axis=0, co...  11.1 us
    pallas_call x10, Pallas kernels, call(): pl.pallas_call(body, out_shape=outs, in_specs=[SPECS[spec] for spec, _ in...  8.93 us
    all_gather x1, blocking collectives, local(): grad_full = lax.all_gather(grad_pre, 'rep', axis=0, tiled=False)  7.15 us
    unnamed x16, local copies, waits for them, and re-layouts  2.68 us
  transfers between devices with their start and end apart: 17, of which 11 were waited for; matrix products, arithmetic and copies ran while one was open for 0% of the time, Pallas kernels for 4%

commit v1 on v0

--- a/solution.py
+++ b/solution.py
@@ -169,20 +169,23 @@
     out_ref[...] = (mine_ref[...] + beside_ref[1].astype(F32)).astype(BF16)
 
 
-def gate_blocks_body(own_ref, gout_ref, beside_ref, across_ref, hid_ref, gpre_ref):
+def gate_blocks_body(dom_ref, own_ref, gout_ref, beside_ref, across_ref, hid_ref, gpre_ref, send_ref):
     pre = own_ref[...] + beside_ref[0].astype(F32) + across_ref[...].astype(F32)
     finish_gate(pre, gout_ref, hid_ref, gpre_ref)
+    send_ref[...] = gpre_ref[:, block_rows(dom_ref[0] % 2, 1, send_ref.shape[1])]
 
 
 def back_body(
-    high_ref, low_ref, deg_ref, self_ref, neigh_ref, grad_ref, total_ref, mirror_ref
+    split, rep_ref, high_ref, low_ref, deg_ref, self_ref, neigh_ref, *refs,
 ):
+    grads, (total_ref, mirror_ref) = refs[:-2], refs[-2:]
     rows, cols = total_ref.shape
+    reps = self_ref.shape[1] // cols
     direct = jnp.zeros((rows, cols), F32)
     gagg = jnp.zeros((rows, cols), F32)
-    for c in range(grad_ref.shape[0]):
-        grad = grad_ref[c]
-        at = slice(c * cols, (c + 1) * cols)
+    for c in range(reps):
+        grad = grads[c][...] if split else grads[0][c]
+        at = column_block(split, rep_ref[0], c, reps, cols)
         gagg += dot(grad, neigh_ref[:, at], COLS)
         direct += dot(grad, self_ref[:, at], COLS)
     gagg = (gagg / wide_degree(deg_ref, cols)).astype(BF16)
@@ -213,28 +216,32 @@
         ref[...] = (total * scale).astype(BF16)
 
 
-def group_weight_body(dom_ref, own_ref, other_ref, *refs):
-    rows, mine_ref, send_refs, total_ref = refs[:4], refs[4], refs[5:-1], refs[-1]
+def group_weight_body(dom_ref, rep_ref, *refs):
+    rows, (mine_ref, far_ref, send_ref, hold_ref) = refs[:4], refs[-4:]
+    grads = refs[4:-4]
+    count = len(grads) // 2
     lanes = mine_ref.shape[2]
     layer, side = dom_ref[0] // 2, dom_ref[0] % 2
-    count = other_ref.shape[0]
+    for c in range(count):
+        at = lax.bitwise_xor(rep_ref[0], c)
+        hold_ref[0, at] = grads[c][:, block_rows(side, 0, lanes)]
+        hold_ref[1, at] = grads[count + c][...]
     for k in range(2):
         own, other = rows[2 * k][...], rows[2 * k + 1][...]
-        for c in range(count):
-            cols = own.shape[1]
-            total_ref[:, c * cols:(c + 1) * cols] = dot(
-                own, own_ref[side * count + c], ROWS
-            ) + dot(other, other_ref[c], ROWS)
-        mine_ref[k] = total_ref[:, block_rows(layer, 0, lanes)]
-        for offset, ref in enumerate(send_refs):
-            ref[k] = total_ref[:, block_rows(layer, offset + 1, lanes)].astype(BF16)
-
-
-def join_body(scale, mine_ref, *refs):
-    total = mine_ref[...]
-    for ref in refs[:-1]:
-        total = total + ref[...].astype(F32)
-    refs[-1][...] = (total * scale).astype(BF16)
+        for offset in range(count):
+            at = lax.bitwise_xor(layer, offset)
+            value = dot(own, hold_ref[0, at], ROWS) + dot(other, hold_ref[1, at], ROWS)
+            if offset == 0:
+                mine_ref[k] = value
+            elif offset == 2:
+                far_ref[k] = value
+            else:
+                send_ref[offset // 2, k] = value.astype(BF16)
+
+
+def join_body(scale, mine_ref, next_ref, far_ref, out_ref):
+    total = mine_ref[...] + next_ref[0].astype(F32) + far_ref[...].astype(F32)
+    out_ref[...] = (total * scale).astype(BF16)
 
 
 def place_body(dom_ref, *refs):
@@ -242,9 +249,7 @@
     copies = []
     lanes = blocks[0].shape[2]
     for offset, block in enumerate(blocks):
-        place = lax.bitwise_xor(dom_ref[0], offset)
-        at = (place % 2) * (len(blocks) // 2) + place // 2
-        at = pl.ds(pl.multiple_of(at * lanes, lanes), lanes)
+        at = block_rows(dom_ref[0], offset, lanes)
         for k, out_ref in enumerate(outs):
             copies.append(
                 pltpu.make_async_copy(block.at[k], out_ref.at[:, at], sems.at[2 * offset + k])
@@ -260,6 +265,11 @@
 
 def swap(array, axis, offset):
     return lax.ppermute(array, axis, [(i, i ^ offset) for i in range(lax.axis_size(axis))])
+
+
+def gather_columns(array):
+    across = swap(array, "rep", 2)
+    return [array, swap(array, "rep", 1), across, swap(across, "rep", 1)]
 
 
 def gather_pieces(array, peers):
@@ -286,7 +296,6 @@
     rep = lax.axis_index("rep").astype(jnp.int32).reshape(1)
     dom = lax.axis_index("dom").astype(jnp.int32).reshape(1)
     lanes = width // peers
-    halves = peers // reps
     split = peers == 8 and reps == 4 and slots % 16 == 0 and lanes % 128 == 0
     mirror_out = struct((mirrors, cols), BF16)
 
@@ -348,11 +357,13 @@
             across_body, block, [("v", parts[0]), ("v", beside)], flops=100_000, moved=500_000
         )
         across = swap(across, "rep", 2)
-        hidden, grad_pre = call(
-            gate_blocks_body, (block, block),
-            [("v", own), ("v", grad_out), ("v", beside), ("v", across)],
+        hidden, grad_pre, half = call(
+            gate_blocks_body, (block, block, struct((rows, lanes), BF16)),
+            [("s", dom), ("v", own), ("v", grad_out), ("v", beside), ("v", across)],
             flops=2_000_000, moved=1_300_000,
         )
+        grad_full = gather_columns(grad_pre)
+        halves = gather_columns(swap(half, "dom", 1))
     else:
         recv = lax.all_to_all(parts[0], "rep", split_axis=0, concat_axis=0, tiled=True)
         hidden, grad_pre = call(
@@ -360,33 +371,33 @@
             [("s", rep), ("v", recv), ("v", own), ("v", grad_out)],
             flops=2_000_000, moved=1_300_000,
         )
-    grad_full = lax.all_gather(grad_pre, "rep", axis=0, tiled=False)
+        grad_full = [lax.all_gather(grad_pre, "rep", axis=0, tiled=False)]
     total, mirror_grad = call(
-        back_body, (struct((rows, cols), F32), mirror_out),
+        functools.partial(back_body, split), (struct((rows, cols), F32), mirror_out),
         [
-            ("v", high), ("v", low), ("v", degree), ("v", self_near), ("v", neigh_near),
-            ("v", grad_full),
-        ],
+            ("s", rep), ("v", high), ("v", low), ("v", degree), ("v", self_near),
+            ("v", neigh_near),
+        ] + [("v", got) for got in grad_full],
         flops=600_000_000, moved=3_000_000,
     )
     if split:
-        start = (1 - dom[0] % 2) * (reps // 2)
-        half = swap(lax.dynamic_slice_in_dim(grad_full, start, reps // 2, 0), "dom", 1)
-        half, mirror_grad = lax.optimization_barrier((half, mirror_grad))
+        piece = struct((2, rows, lanes), F32)
+        mine, far, send = call(
+            group_weight_body, (piece, piece, struct((2, 2, rows, lanes), BF16)),
+            [
+                ("s", dom), ("s", rep), ("v", features), ("v", feat_beside), ("v", agg),
+                ("v", agg_beside),
+            ] + [("v", got) for got in grad_full + halves],
+            scratch=[pltpu.VMEM((2, reps, rows, lanes), BF16)],
+            flops=600_000_000, moved=3_000_000,
+        )
         piece = struct((2, rows, lanes), BF16)
-        mine, *sends = call(
-            group_weight_body, (struct((2, rows, lanes), F32),) + (piece,) * (reps - 1),
-            [
-                ("s", dom), ("v", grad_full), ("v", half), ("v", features),
-                ("v", feat_beside), ("v", agg), ("v", agg_beside),
-            ],
-            scratch=[pltpu.VMEM((rows, width // 2), F32)],
-            flops=600_000_000, moved=3_000_000,
-        )
-        layers = [swap(send, "dom", 2 * k + 2) for k, send in enumerate(sends)]
+        beside = swap(send, "dom", 2)
+        far = call(across_body, piece, [("v", far), ("v", beside)], flops=100_000, moved=500_000)
         mine = call(
             functools.partial(join_body, scale), piece,
-            [("v", mine)] + [("v", got) for got in layers], flops=200_000, moved=500_000,
+            [("v", mine), ("v", beside), ("v", swap(far, "dom", 4))],
+            flops=200_000, moved=500_000,
         )
         pieces = gather_pieces(mine, peers)
     returned = exchange(mirror_grad)
@@ -404,7 +415,7 @@
         piece = cols // peers
         partial = call(
             weight_body, struct((peers, 2 * piece, width), BF16),
-            [("v", features), ("v", agg), ("v", grad_full)],
+            [("v", features), ("v", agg), ("v", grad_full[0])],
             flops=600_000_000, moved=2_000_000,
         )
         gathered = lax.all_to_all(partial, "dom", split_axis=0, concat_axis=0, tiled=True)

time: 82.4 us -> 80.6 us (0.978)
  blocking collectives: 7.15 us -> 0 us
  waiting for transfers between devices: 32.3 us -> 36.5 us
  starting transfers between devices: 30.2 us -> 31.1 us
    all_gather x1 -> x0, blocking collectives: 7.15 us -> none  [local(): grad_full = lax.all_gather(grad_pre, 'rep', axis=0, tiled=False)]
    ppermute x15 -> x20, waiting for transfers between devices: 31 us -> 35.2 us  [swap(): lax.ppermute(array, axis, [(i, i ^ offset) for i in range(lax.axis_size(a...]
    ppermute x15 -> x20, starting transfers between devices: 19.1 us -> 20 us  [swap(): lax.ppermute(array, axis, [(i, i ^ offset) for i in range(lax.axis_size(a...]
    pallas_call x10 -> x11, Pallas kernels: 8.93 us -> 9.18 us  [call(): pl.pallas_call(body, out_shape=outs, in_specs=[SPECS[spec] for spec, _ in...]
  transfers between devices with their start and end apart: 17 -> 22, of which waited for: 11 -> 13; matrix products, arithmetic and copies ran while one was open for 0% -> 0% of each run, Pallas kernels for 4% -> 4%
where the time goes in v1:
time: 80.6 us; the launch traced here: 80.2 us
  waiting for transfers between devices  36.5 us (45%)
  starting transfers between devices  31.1 us (39%)
  Pallas kernels  9.18 us (11%)
  local copies, waits for them, and re-layouts  2.68 us (3%)
    ppermute x20, waiting for transfers between devices, swap(): lax.ppermute(array, axis, [(i, i ^ offset) for i in range(lax.axis_size(a...  35.2 us
    ppermute x20, starting transfers between devices, swap(): lax.ppermute(array, axis, [(i, i ^ offset) for i in range(lax.axis_size(a...  20 us
    all_to_all x2, starting transfers between devices, exchange(): lax.all_to_all(array.reshape(peers, slots, cols), 'dom', split_axis=0, co...  11.1 us
    pallas_call x11, Pallas kernels, call(): pl.pallas_call(body, out_shape=outs, in_specs=[SPECS[spec] for spec, _ in...  9.18 us
    unnamed x16, local copies, waits for them, and re-layouts  2.68 us
  transfers between devices with their start and end apart: 22, of which 13 were waited for; matrix products, arithmetic and copies ran while one was open for 0% of the time, Pallas kernels for 4%

profile of v1, /device:TPU:0, one launch (start us, length us, event | category | flops | bytes accessed | tf_op | source)
XLA Modules:
  0.0 80.2 jit_solution(11276476208044599730)
XLA Ops:
  0.6 2.1 %shard_map.120 = (bf16[256,512]{1,0:T(8,128)(2,1)}, bf16[512,256]{1,0:T(8,128)(2,1)}) custom-call(s32[8]{0:T(128)} %count_hbm.1, s32[8,64]{1,0:T(8,128)} %list_hbm.1, bf16[256,256]{1,0:T(8,128)(2,1)} %refs_0_.1), custom_call_target="tpu_custom_call" | custom-call | flops 67108864 | bytes 600000 | tf_op jit(solution)/shard_map/pallas_call | solution.py:22
  2.8 7.4 %all-to-all-start = ((bf16[8,64,256]{2,1,0:T(8,128)(2,1)}), bf16[8,64,256]{2,1,0:T(8,128)(2,1)S(1)}, u32[]{:S(2)}, u32[]{:S(2)}) async-start(bf16[8,64,256]{2,1,0:T(8,128)(2,1)} %bitcast.8), calls=%async_computation | async-start | bytes 524288 | tf_op jit(solution)/shard_map/all_to_all | solution.py:303
  10.2 2.0 %collective-permute-start = (bf16[256,256]{1,0:T(8,128)(2,1)S(1)}, bf16[256,256]{1,0:T(8,128)(2,1)S(1)}, u32[]{:S(2)}, u32[]{:S(2)}) collective-permute-start(bf16[256,256]{1,0:T(8,128)(2,1)S(1)} %copy-done.4), channel_id=1, source_target_pairs={{0,4},{4,0},{8,12},{12,8},{16,20},{20,16},{24,28},{28,24},{1,5},{5... | collective-permute-start | bytes 393224 | tf_op jit(solution)/shard_map/ppermute | solution.py:267
  12.9 1.0 %copy-done.1 = bf16[256,1024]{1,0:T(8,128)(2,1)S(1)} copy-done((bf16[256,1024]{1,0:T(8,128)(2,1)S(1)}, bf16[256,1024]{1,0:T(8,128)(2,1)}, u32[]{:S(2)}) %copy-start.1) | copy-done | bytes 524312
  15.9 2.0 %collective-permute-done.refs_1_ = bf16[256,256]{1,0:T(8,128)(2,1)S(1)} collective-permute-done((bf16[256,256]{1,0:T(8,128)(2,1)S(1)}, bf16[256,256]{1,0:T(8,128)(2,1)S(1)}, u32[]{:S(2)}, u32[]{:S(2)}) %collective-permute-start) | collective-permute-done | bytes 131104 | tf_op jit(solution)/shard_map/ppermute | solution.py:267
  17.8 1.3 %all-to-all-done = bf16[8,64,256]{2,1,0:T(8,128)(2,1)S(1)} async-done(((bf16[8,64,256]{2,1,0:T(8,128)(2,1)}), bf16[8,64,256]{2,1,0:T(8,128)(2,1)S(1)}, u32[]{:S(2)}, u32[]{:S(2)}) %all-to-all-start) | async-done | bytes 262176 | tf_op jit(solution)/shard_map/all_to_all | solution.py:303
  19.1 1.0 %shard_map.122 = (f32[256,256]{1,0:T(8,128)S(1)}, bf16[256,256]{1,0:T(8,128)(2,1)S(1)}, f32[256,256]{1,0:T(8,128)S(1)}, bf16[2,256,256]{2,1,0:T(8,128)(2,1)S(1)}) custom-call(s32[1]{0:T(128)} %bitcast.1.rep_ref, bf16[256,256]{1,0:T(8,128)(2,1)S(1)} %copy-done.4, bf16[512,256]{1,0:T(8,128)(2,1)S(1)} %bitcast.7, ...), custom_call_target="tpu_custom_call" | custom-call | flops 600000000 | bytes 3000000 | tf_op jit(solution)/shard_map/pallas_call | solution.py:22
  20.2 1.5 %collective-permute-start.1 = (bf16[256,256]{1,0:T(8,128)(2,1)S(1)}, bf16[256,256]{1,0:T(8,128)(2,1)S(1)}, u32[]{:S(2)}, u32[]{:S(2)}) collective-permute-start(bf16[256,256]{1,0:T(8,128)(2,1)S(1)} %get-tuple-element.47.refs_2_), channel_id=1, source_target_pairs={{0,4},{4,0},{8,12},{12,8},{16,20},{20,16},{24,28},{28,24},{1,5},{5... | collective-permute-start | bytes 393224 | tf_op jit(solution)/shard_map/ppermute | solution.py:267
  21.7 1.6 %collective-permute-start.3 = (bf16[256,256]{1,0:T(8,128)(2,1)S(1)}, bf16[256,256]{1,0:T(8,128)(2,1)S(1)}, u32[]{:S(2)}, u32[]{:S(2)}) collective-permute-start(bf16[256,256]{1,0:T(8,128)(2,1)S(1)} %shard_map.123), channel_id=1, source_target_pairs={{0,2},{1,3},{2,0},{3,1},{4,6},{5,7},{6,4},{7,5},{8,10},{9,11},{10,... | collective-permute-start | bytes 393224 | tf_op jit(solution)/shard_map/ppermute | solution.py:267
  23.3 2.8 %collective-permute-done.1.refs_3_ = bf16[256,256]{1,0:T(8,128)(2,1)S(1)} collective-permute-done((bf16[256,256]{1,0:T(8,128)(2,1)S(1)}, bf16[256,256]{1,0:T(8,128)(2,1)S(1)}, u32[]{:S(2)}, u32[]{:S(2)}) %collective-permute-start.1) | collective-permute-done | bytes 131104 | tf_op jit(solution)/shard_map/ppermute | solution.py:267
  26.1 1.2 %collective-permute-done.3.across_ref = bf16[256,256]{1,0:T(8,128)(2,1)S(1)} collective-permute-done((bf16[256,256]{1,0:T(8,128)(2,1)S(1)}, bf16[256,256]{1,0:T(8,128)(2,1)S(1)}, u32[]{:S(2)}, u32[]{:S(2)}) %collective-permute-start.3) | collective-permute-done | bytes 131104 | tf_op jit(solution)/shard_map/ppermute | solution.py:267
  28.1 1.5 %collective-permute-start.5 = (bf16[256,256]{1,0:T(8,128)(2,1)S(1)}, bf16[256,256]{1,0:T(8,128)(2,1)S(1)}, u32[]{:S(2)}, u32[]{:S(2)}) collective-permute-start(bf16[256,256]{1,0:T(8,128)(2,1)S(1)} %get-tuple-element.53.refs_0_.refs_4_), channel_id=1, source_target_pairs={{0,2},{1,3},{2,0},{3,1},{4,6},{5,7},{6,4},{7,5},{8,10},{9,11},{10,... | collective-permute-start | bytes 393224 | tf_op jit(solution)/shard_map/ppermute | solution.py:267
  29.6 1.4 %collective-permute-start.7 = (bf16[256,128]{1,0:T(8,128)(2,1)S(1)}, bf16[256,128]{1,0:T(8,128)(2,1)S(1)}, u32[]{:S(2)}, u32[]{:S(2)}) collective-permute-start(bf16[256,128]{1,0:T(8,128)(2,1)S(1)} %get-tuple-element.58), channel_id=1, source_target_pairs={{0,4},{4,0},{8,12},{12,8},{16,20},{20,16},{24,28},{28,24},{1,5},{5... | collective-permute-start | bytes 196616 | tf_op jit(solution)/shard_map/ppermute | solution.py:267
  31.0 2.9 %collective-permute-done.7.refs_8_ = bf16[256,128]{1,0:T(8,128)(2,1)S(1)} collective-permute-done((bf16[256,128]{1,0:T(8,128)(2,1)S(1)}, bf16[256,128]{1,0:T(8,128)(2,1)S(1)}, u32[]{:S(2)}, u32[]{:S(2)}) %collective-permute-start.7) | collective-permute-done | bytes 65568 | tf_op jit(solution)/shard_map/ppermute | solution.py:267
  34.9 3.2 %collective-permute-done.9.refs_10_ = bf16[256,128]{1,0:T(8,128)(2,1)S(1)} collective-permute-done((bf16[256,128]{1,0:T(8,128)(2,1)S(1)}, bf16[256,128]{1,0:T(8,128)(2,1)S(1)}, u32[]{:S(2)}, u32[]{:S(2)}) %collective-permute-start.9) | collective-permute-done | bytes 65568 | tf_op jit(solution)/shard_map/ppermute | solution.py:267
  38.1 1.2 %collective-permute-done.10.refs_11_ = bf16[256,128]{1,0:T(8,128)(2,1)S(1)} collective-permute-done((bf16[256,128]{1,0:T(8,128)(2,1)S(1)}, bf16[256,128]{1,0:T(8,128)(2,1)S(1)}, u32[]{:S(2)}, u32[]{:S(2)}) %collective-permute-start.10) | collective-permute-done | bytes 65568 | tf_op jit(solution)/shard_map/ppermute | solution.py:267
  40.2 1.1 %collective-permute-start.11 = (bf16[2,2,256,128]{3,2,1,0:T(8,128)(2,1)S(1)}, bf16[2,2,256,128]{3,2,1,0:T(8,128)(2,1)S(1)}, u32[]{:S(2)}, u32[]{:S(2)}) collective-permute-start(bf16[2,2,256,128]{3,2,1,0:T(8,128)(2,1)S(1)} %get-tuple-element.60), channel_id=1, source_target_pairs={{0,8},{4,12},{8,0},{12,4},{16,24},{20,28},{24,16},{28,20},{1,9},{5... | collective-permute-start | bytes 786440 | tf_op jit(solution)/shard_map/ppermute | solution.py:267
  41.3 7.3 %collective-permute-done.11.beside_ref.next_ref = bf16[2,2,256,128]{3,2,1,0:T(8,128)(2,1)S(1)} collective-permute-done((bf16[2,2,256,128]{3,2,1,0:T(8,128)(2,1)S(1)}, bf16[2,2,256,128]{3,2,1,0:T(8,128)(2,1)S(1)}, u32[]{:S(2)}, u32[]{:S(2)}) %collective-permute-start.11) | collective-permute-done | bytes 262176 | tf_op jit(solution)/shard_map/ppermute | solution.py:267
  48.6 1.5 %collective-permute-start.12 = (bf16[2,256,128]{2,1,0:T(8,128)(2,1)S(1)}, bf16[2,256,128]{2,1,0:T(8,128)(2,1)S(1)}, u32[]{:S(2)}, u32[]{:S(2)}) collective-permute-start(bf16[2,256,128]{2,1,0:T(8,128)(2,1)S(1)} %shard_map.128), channel_id=1, source_target_pairs={{0,16},{4,20},{8,24},{12,28},{16,0},{20,4},{24,8},{28,12},{1,17},{... | collective-permute-start | bytes 393224 | tf_op jit(solution)/shard_map/ppermute | solution.py:267
  50.1 1.5 %shard_map.125 = (f32[256,256]{1,0:T(8,128)S(1)}, bf16[512,256]{1,0:T(8,128)(2,1)}) custom-call(s32[1]{0:T(128)} %bitcast.1.rep_ref, bf16[256,768]{1,0:T(8,128)(2,1)S(1)} %get-tuple-element.41.high_ref, bf16[256,768]{1,0:T(8,128)(2,1)S(1)} %get-tuple-element.42.low_ref, f32[256,128]{1,0:T(8,128)S(1)} %get-tuple-element.43.deg_ref, ...), custom_call_target="tpu_custom_call" | custom-call | flops 600000000 | bytes 3000000 | tf_op jit(solution)/shard_map/pallas_call | solution.py:22
  51.6 3.6 %all-to-all-start.1 = ((bf16[8,64,256]{2,1,0:T(8,128)(2,1)}), bf16[8,64,256]{2,1,0:T(8,128)(2,1)S(1)}, u32[]{:S(2)}, u32[]{:S(2)}) async-start(bf16[8,64,256]{2,1,0:T(8,128)(2,1)} %bitcast.4), calls=%async_computation.1 | async-start | bytes 524288 | tf_op jit(solution)/shard_map/all_to_all | solution.py:303
  55.3 1.9 %collective-permute-done.12.far_ref = bf16[2,256,128]{2,1,0:T(8,128)(2,1)S(1)} collective-permute-done((bf16[2,256,128]{2,1,0:T(8,128)(2,1)S(1)}, bf16[2,256,128]{2,1,0:T(8,128)(2,1)S(1)}, u32[]{:S(2)}, u32[]{:S(2)}) %collective-permute-start.12) | collective-permute-done | bytes 131104 | tf_op jit(solution)/shard_map/ppermute | solution.py:267
  57.2 1.1 %collective-permute-start.13 = (bf16[2,256,128]{2,1,0:T(8,128)(2,1)S(1)}, bf16[2,256,128]{2,1,0:T(8,128)(2,1)S(1)}, u32[]{:S(2)}, u32[]{:S(2)}) collective-permute-start(bf16[2,256,128]{2,1,0:T(8,128)(2,1)S(1)} %shard_map.129.refs_0_), channel_id=1, source_target_pairs={{0,16},{4,20},{8,24},{12,28},{16,0},{20,4},{24,8},{28,12},{1,17},{... | collective-permute-start | bytes 393224 | tf_op jit(solution)/shard_map/ppermute | solution.py:267
  58.3 1.5 %collective-permute-start.14 = (bf16[2,256,128]{2,1,0:T(8,128)(2,1)S(1)}, bf16[2,256,128]{2,1,0:T(8,128)(2,1)S(1)}, u32[]{:S(2)}, u32[]{:S(2)}) collective-permute-start(bf16[2,256,128]{2,1,0:T(8,128)(2,1)S(1)} %shard_map.129.refs_0_), channel_id=1, source_target_pairs={{0,4},{4,0},{8,12},{12,8},{16,20},{20,16},{24,28},{28,24},{1,5},{5... | collective-permute-start | bytes 393224 | tf_op jit(solution)/shard_map/ppermute | solution.py:267
  59.8 2.4 %collective-permute-start.15 = (bf16[2,256,128]{2,1,0:T(8,128)(2,1)S(1)}, bf16[2,256,128]{2,1,0:T(8,128)(2,1)S(1)}, u32[]{:S(2)}, u32[]{:S(2)}) collective-permute-start(bf16[2,256,128]{2,1,0:T(8,128)(2,1)S(1)} %shard_map.129.refs_0_), channel_id=1, source_target_pairs={{0,8},{4,12},{8,0},{12,4},{16,24},{20,28},{24,16},{28,20},{1,9},{5... | collective-permute-start | bytes 393224 | tf_op jit(solution)/shard_map/ppermute | solution.py:267
  62.2 7.0 %collective-permute-done.13.refs_4_ = bf16[2,256,128]{2,1,0:T(8,128)(2,1)S(1)} collective-permute-done((bf16[2,256,128]{2,1,0:T(8,128)(2,1)S(1)}, bf16[2,256,128]{2,1,0:T(8,128)(2,1)S(1)}, u32[]{:S(2)}, u32[]{:S(2)}) %collective-permute-start.13) | collective-permute-done | bytes 131104 | tf_op jit(solution)/shard_map/ppermute | solution.py:267
  69.2 1.4 %collective-permute-start.17 = (bf16[2,256,128]{2,1,0:T(8,128)(2,1)S(1)}, bf16[2,256,128]{2,1,0:T(8,128)(2,1)S(1)}, u32[]{:S(2)}, u32[]{:S(2)}) collective-permute-start(bf16[2,256,128]{2,1,0:T(8,128)(2,1)S(1)} %collective-permute-done.13.refs_4_), channel_id=1, source_target_pairs={{0,4},{4,0},{8,12},{12,8},{16,20},{20,16},{24,28},{28,24},{1,5},{5... | collective-permute-start | bytes 393224 | tf_op jit(solution)/shard_map/ppermute | solution.py:267
  71.2 2.9 %collective-permute-done.18.refs_6_ = bf16[2,256,128]{2,1,0:T(8,128)(2,1)S(1)} collective-permute-done((bf16[2,256,128]{2,1,0:T(8,128)(2,1)S(1)}, bf16[2,256,128]{2,1,0:T(8,128)(2,1)S(1)}, u32[]{:S(2)}, u32[]{:S(2)}) %collective-permute-start.18) | collective-permute-done | bytes 131104 | tf_op jit(solution)/shard_map/ppermute | solution.py:267
  74.1 1.4 %collective-permute-start.19 = (bf16[2,256,128]{2,1,0:T(8,128)(2,1)S(1)}, bf16[2,256,128]{2,1,0:T(8,128)(2,1)S(1)}, u32[]{:S(2)}, u32[]{:S(2)}) collective-permute-start(bf16[2,256,128]{2,1,0:T(8,128)(2,1)S(1)} %collective-permute-done.18.refs_6_), channel_id=1, source_target_pairs={{0,4},{4,0},{8,12},{12,8},{16,20},{20,16},{24,28},{28,24},{1,5},{5... | collective-permute-start | bytes 393224 | tf_op jit(solution)/shard_map/ppermute | solution.py:267
  76.4 1.1 %collective-permute-done.16.refs_3_ = bf16[2,256,128]{2,1,0:T(8,128)(2,1)S(1)} collective-permute-done((bf16[2,256,128]{2,1,0:T(8,128)(2,1)S(1)}, bf16[2,256,128]{2,1,0:T(8,128)(2,1)S(1)}, u32[]{:S(2)}, u32[]{:S(2)}) %collective-permute-start.16) | collective-permute-done | bytes 131104 | tf_op jit(solution)/shard_map/ppermute | solution.py:267
  77.5 1.6 %collective-permute-done.19.refs_7_ = bf16[2,256,128]{2,1,0:T(8,128)(2,1)S(1)} collective-permute-done((bf16[2,256,128]{2,1,0:T(8,128)(2,1)S(1)}, bf16[2,256,128]{2,1,0:T(8,128)(2,1)S(1)}, u32[]{:S(2)}, u32[]{:S(2)}) %collective-permute-start.19) | collective-permute-done | bytes 131104 | tf_op jit(solution)/shard_map/ppermute | solution.py:267
  79.1 1.1 %shard_map.130 = (bf16[256,1024]{1,0:T(8,128)(2,1)}, bf16[256,1024]{1,0:T(8,128)(2,1)}) custom-call(s32[1]{0:T(128)} %bitcast.dom_ref, bf16[2,256,128]{2,1,0:T(8,128)(2,1)S(1)} %shard_map.129.refs_0_, bf16[2,256,128]{2,1,0:T(8,128)(2,1)S(1)} %collective-permute-done.14.refs_1_, bf16[2,256,128]{2,1,0:T(8,128)(2,1)S(1)} %collective-permute-done.15.refs_2_, ...), custom_call_target="tpu_custom_call" | custom-call | bytes 2000000 | tf_op jit(solution)/shard_map/pallas_call | solution.py:22
  (39 shorter events, 7.0 us)
Async XLA Ops:
  0.6 11.6 %copy-start = (bf16[256,1024]{1,0:T(8,128)(2,1)S(1)}, bf16[256,1024]{1,0:T(8,128)(2,1)}, u32[]{:S(2)}) copy-start(bf16[256,1024]{1,0:T(8,128)(2,1)} %self_hbm) | copy-start | bytes 1572868
  2.8 7.4 %copy-start.4 = (bf16[256,256]{1,0:T(8,128)(2,1)S(1)}, bf16[256,256]{1,0:T(8,128)(2,1)}, u32[]{:S(2)}) copy-start(bf16[256,256]{1,0:T(8,128)(2,1)} %refs_0_.1) | copy-start | bytes 393220
  2.8 16.3 %all-to-all-start = ((bf16[8,64,256]{2,1,0:T(8,128)(2,1)}), bf16[8,64,256]{2,1,0:T(8,128)(2,1)S(1)}, u32[]{:S(2)}, u32[]{:S(2)}) async-start(bf16[8,64,256]{2,1,0:T(8,128)(2,1)} %bitcast.8), calls=%async_computation | async-start | bytes 524288 | tf_op jit(solution)/shard_map/all_to_all | solution.py:303
  10.2 7.6 %collective-permute-start = (bf16[256,256]{1,0:T(8,128)(2,1)S(1)}, bf16[256,256]{1,0:T(8,128)(2,1)S(1)}, u32[]{:S(2)}, u32[]{:S(2)}) collective-permute-start(bf16[256,256]{1,0:T(8,128)(2,1)S(1)} %copy-done.4), channel_id=1, source_target_pairs={{0,4},{4,0},{8,12},{12,8},{16,20},{20,16},{24,28},{28,24},{1,5},{5... | collective-permute-start | bytes 393224 | tf_op jit(solution)/shard_map/ppermute | solution.py:267
  12.2 0.7 copy-start.6
  12.2 0.7 copy-start.7
  12.9 1.0 %copy-start.1 = (bf16[256,1024]{1,0:T(8,128)(2,1)S(1)}, bf16[256,1024]{1,0:T(8,128)(2,1)}, u32[]{:S(2)}) copy-start(bf16[256,1024]{1,0:T(8,128)(2,1)} %neigh_hbm) | copy-start | bytes 1572868
  14.0 0.9 %copy-start.3 = (bf16[8,128,128]{2,1,0:T(8,128)(2,1)S(1)}, bf16[8,128,128]{2,1,0:T(8,128)(2,1)}, u32[]{:S(2)}) copy-start(bf16[8,128,128]{2,1,0:T(8,128)(2,1)} %tiles_ref) | copy-start | bytes 786436
  20.1 1.6 %collective-permute-start.2 = (bf16[2,256,256]{2,1,0:T(8,128)(2,1)S(1)}, bf16[2,256,256]{2,1,0:T(8,128)(2,1)S(1)}, u32[]{:S(2)}, u32[]{:S(2)}) collective-permute-start(bf16[2,256,256]{2,1,0:T(8,128)(2,1)S(1)} %get-tuple-element.49), channel_id=1, source_target_pairs={{0,1},{1,0},{2,3},{3,2},{4,5},{5,4},{6,7},{7,6},{8,9},{9,8},{10,11... | collective-permute-start | bytes 786440 | tf_op jit(solution)/shard_map/ppermute | solution.py:267
  20.2 5.9 %collective-permute-start.1 = (bf16[256,256]{1,0:T(8,128)(2,1)S(1)}, bf16[256,256]{1,0:T(8,128)(2,1)S(1)}, u32[]{:S(2)}, u32[]{:S(2)}) collective-permute-start(bf16[256,256]{1,0:T(8,128)(2,1)S(1)} %get-tuple-element.47.refs_2_), channel_id=1, source_target_pairs={{0,4},{4,0},{8,12},{12,8},{16,20},{20,16},{24,28},{28,24},{1,5},{5... | collective-permute-start | bytes 393224 | tf_op jit(solution)/shard_map/ppermute | solution.py:267
  21.7 5.6 %copy-start.5 = (bf16[256,256]{1,0:T(8,128)(2,1)S(1)}, bf16[256,256]{1,0:T(8,128)(2,1)}, u32[]{:S(2)}) copy-start(bf16[256,256]{1,0:T(8,128)(2,1)} %gout_ref) | copy-start | bytes 393220
  21.7 5.6 %collective-permute-start.3 = (bf16[256,256]{1,0:T(8,128)(2,1)S(1)}, bf16[256,256]{1,0:T(8,128)(2,1)S(1)}, u32[]{:S(2)}, u32[]{:S(2)}) collective-permute-start(bf16[256,256]{1,0:T(8,128)(2,1)S(1)} %shard_map.123), channel_id=1, source_target_pairs={{0,2},{1,3},{2,0},{3,1},{4,6},{5,7},{6,4},{7,5},{8,10},{9,11},{10,... | collective-permute-start | bytes 393224 | tf_op jit(solution)/shard_map/ppermute | solution.py:267
  28.1 6.3 %collective-permute-start.5 = (bf16[256,256]{1,0:T(8,128)(2,1)S(1)}, bf16[256,256]{1,0:T(8,128)(2,1)S(1)}, u32[]{:S(2)}, u32[]{:S(2)}) collective-permute-start(bf16[256,256]{1,0:T(8,128)(2,1)S(1)} %get-tuple-element.53.refs_0_.refs_4_), channel_id=1, source_target_pairs={{0,2},{1,3},{2,0},{3,1},{4,6},{5,7},{6,4},{7,5},{8,10},{9,11},{10,... | collective-permute-start | bytes 393224 | tf_op jit(solution)/shard_map/ppermute | solution.py:267
  29.6 4.3 %collective-permute-start.7 = (bf16[256,128]{1,0:T(8,128)(2,1)S(1)}, bf16[256,128]{1,0:T(8,128)(2,1)S(1)}, u32[]{:S(2)}, u32[]{:S(2)}) collective-permute-start(bf16[256,128]{1,0:T(8,128)(2,1)S(1)} %get-tuple-element.58), channel_id=1, source_target_pairs={{0,4},{4,0},{8,12},{12,8},{16,20},{20,16},{24,28},{28,24},{1,5},{5... | collective-permute-start | bytes 196616 | tf_op jit(solution)/shard_map/ppermute | solution.py:267
  31.0 7.1 %collective-permute-start.4 = (bf16[256,256]{1,0:T(8,128)(2,1)S(1)}, bf16[256,256]{1,0:T(8,128)(2,1)S(1)}, u32[]{:S(2)}, u32[]{:S(2)}) collective-permute-start(bf16[256,256]{1,0:T(8,128)(2,1)S(1)} %get-tuple-element.53.refs_0_.refs_4_), channel_id=1, source_target_pairs={{0,1},{1,0},{2,3},{3,2},{4,5},{5,4},{6,7},{7,6},{8,9},{9,8},{10,11... | collective-permute-start | bytes 393224 | tf_op jit(solution)/shard_map/ppermute | solution.py:267
  33.9 4.3 %collective-permute-start.9 = (bf16[256,128]{1,0:T(8,128)(2,1)S(1)}, bf16[256,128]{1,0:T(8,128)(2,1)S(1)}, u32[]{:S(2)}, u32[]{:S(2)}) collective-permute-start(bf16[256,128]{1,0:T(8,128)(2,1)S(1)} %collective-permute-done.7.refs_8_), channel_id=1, source_target_pairs={{0,2},{1,3},{2,0},{3,1},{4,6},{5,7},{6,4},{7,5},{8,10},{9,11},{10,... | collective-permute-start | bytes 196616 | tf_op jit(solution)/shard_map/ppermute | solution.py:267
  34.4 5.0 %collective-permute-start.6 = (bf16[256,256]{1,0:T(8,128)(2,1)S(1)}, bf16[256,256]{1,0:T(8,128)(2,1)S(1)}, u32[]{:S(2)}, u32[]{:S(2)}) collective-permute-start(bf16[256,256]{1,0:T(8,128)(2,1)S(1)} %collective-permute-done.5.refs_2_.refs_6_), channel_id=1, source_target_pairs={{0,1},{1,0},{2,3},{3,2},{4,5},{5,4},{6,7},{7,6},{8,9},{9,8},{10,11... | collective-permute-start | bytes 393224 | tf_op jit(solution)/shard_map/ppermute | solution.py:267
  34.4 3.7 %collective-permute-start.8 = (bf16[256,128]{1,0:T(8,128)(2,1)S(1)}, bf16[256,128]{1,0:T(8,128)(2,1)S(1)}, u32[]{:S(2)}, u32[]{:S(2)}) collective-permute-start(bf16[256,128]{1,0:T(8,128)(2,1)S(1)} %collective-permute-done.7.refs_8_), channel_id=1, source_target_pairs={{0,1},{1,0},{2,3},{3,2},{4,5},{5,4},{6,7},{7,6},{8,9},{9,8},{10,11... | collective-permute-start | bytes 196616 | tf_op jit(solution)/shard_map/ppermute | solution.py:267
  38.1 1.3 %collective-permute-start.10 = (bf16[256,128]{1,0:T(8,128)(2,1)S(1)}, bf16[256,128]{1,0:T(8,128)(2,1)S(1)}, u32[]{:S(2)}, u32[]{:S(2)}) collective-permute-start(bf16[256,128]{1,0:T(8,128)(2,1)S(1)} %collective-permute-done.9.refs_10_), channel_id=1, source_target_pairs={{0,1},{1,0},{2,3},{3,2},{4,5},{5,4},{6,7},{7,6},{8,9},{9,8},{10,11... | collective-permute-start | bytes 196616 | tf_op jit(solution)/shard_map/ppermute | solution.py:267
  40.2 8.4 %collective-permute-start.11 = (bf16[2,2,256,128]{3,2,1,0:T(8,128)(2,1)S(1)}, bf16[2,2,256,128]{3,2,1,0:T(8,128)(2,1)S(1)}, u32[]{:S(2)}, u32[]{:S(2)}) collective-permute-start(bf16[2,2,256,128]{3,2,1,0:T(8,128)(2,1)S(1)} %get-tuple-element.60), channel_id=1, source_target_pairs={{0,8},{4,12},{8,0},{12,4},{16,24},{20,28},{24,16},{28,20},{1,9},{5... | collective-permute-start | bytes 786440 | tf_op jit(solution)/shard_map/ppermute | solution.py:267
  48.6 8.5 %collective-permute-start.12 = (bf16[2,256,128]{2,1,0:T(8,128)(2,1)S(1)}, bf16[2,256,128]{2,1,0:T(8,128)(2,1)S(1)}, u32[]{:S(2)}, u32[]{:S(2)}) collective-permute-start(bf16[2,256,128]{2,1,0:T(8,128)(2,1)S(1)} %shard_map.128), channel_id=1, source_target_pairs={{0,16},{4,20},{8,24},{12,28},{16,0},{20,4},{24,8},{28,12},{1,17},{... | collective-permute-start | bytes 393224 | tf_op jit(solution)/shard_map/ppermute | solution.py:267
  51.6 23.9 %all-to-all-start.1 = ((bf16[8,64,256]{2,1,0:T(8,128)(2,1)}), bf16[8,64,256]{2,1,0:T(8,128)(2,1)S(1)}, u32[]{:S(2)}, u32[]{:S(2)}) async-start(bf16[8,64,256]{2,1,0:T(8,128)(2,1)} %bitcast.4), calls=%async_computation.1 | async-start | bytes 524288 | tf_op jit(solution)/shard_map/all_to_all | solution.py:303
  57.2 18.4 %copy-start.2 = (bf16[256,512]{1,0:T(8,128)(2,1)S(1)}, bf16[256,512]{1,0:T(8,128)(2,1)}, u32[]{:S(2)}) copy-start(bf16[256,512]{1,0:T(8,128)(2,1)} %get-tuple-element.52.onehot_ref) | copy-start | bytes 786436
  57.2 12.0 %collective-permute-start.13 = (bf16[2,256,128]{2,1,0:T(8,128)(2,1)S(1)}, bf16[2,256,128]{2,1,0:T(8,128)(2,1)S(1)}, u32[]{:S(2)}, u32[]{:S(2)}) collective-permute-start(bf16[2,256,128]{2,1,0:T(8,128)(2,1)S(1)} %shard_map.129.refs_0_), channel_id=1, source_target_pairs={{0,16},{4,20},{8,24},{12,28},{16,0},{20,4},{24,8},{28,12},{1,17},{... | collective-permute-start | bytes 393224 | tf_op jit(solution)/shard_map/ppermute | solution.py:267
  58.3 10.8 %collective-permute-start.14 = (bf16[2,256,128]{2,1,0:T(8,128)(2,1)S(1)}, bf16[2,256,128]{2,1,0:T(8,128)(2,1)S(1)}, u32[]{:S(2)}, u32[]{:S(2)}) collective-permute-start(bf16[2,256,128]{2,1,0:T(8,128)(2,1)S(1)} %shard_map.129.refs_0_), channel_id=1, source_target_pairs={{0,4},{4,0},{8,12},{12,8},{16,20},{20,16},{24,28},{28,24},{1,5},{5... | collective-permute-start | bytes 393224 | tf_op jit(solution)/shard_map/ppermute | solution.py:267
  59.8 10.8 %collective-permute-start.15 = (bf16[2,256,128]{2,1,0:T(8,128)(2,1)S(1)}, bf16[2,256,128]{2,1,0:T(8,128)(2,1)S(1)}, u32[]{:S(2)}, u32[]{:S(2)}) collective-permute-start(bf16[2,256,128]{2,1,0:T(8,128)(2,1)S(1)} %shard_map.129.refs_0_), channel_id=1, source_target_pairs={{0,8},{4,12},{8,0},{12,4},{16,24},{20,28},{24,16},{28,20},{1,9},{5... | collective-permute-start | bytes 393224 | tf_op jit(solution)/shard_map/ppermute | solution.py:267
  69.2 5.0 %collective-permute-start.18 = (bf16[2,256,128]{2,1,0:T(8,128)(2,1)S(1)}, bf16[2,256,128]{2,1,0:T(8,128)(2,1)S(1)}, u32[]{:S(2)}, u32[]{:S(2)}) collective-permute-start(bf16[2,256,128]{2,1,0:T(8,128)(2,1)S(1)} %collective-permute-done.13.refs_4_), channel_id=1, source_target_pairs={{0,8},{4,12},{8,0},{12,4},{16,24},{20,28},{24,16},{28,20},{1,9},{5... | collective-permute-start | bytes 393224 | tf_op jit(solution)/shard_map/ppermute | solution.py:267
  69.2 8.3 %collective-permute-start.17 = (bf16[2,256,128]{2,1,0:T(8,128)(2,1)S(1)}, bf16[2,256,128]{2,1,0:T(8,128)(2,1)S(1)}, u32[]{:S(2)}, u32[]{:S(2)}) collective-permute-start(bf16[2,256,128]{2,1,0:T(8,128)(2,1)S(1)} %collective-permute-done.13.refs_4_), channel_id=1, source_target_pairs={{0,4},{4,0},{8,12},{12,8},{16,20},{20,16},{24,28},{28,24},{1,5},{5... | collective-permute-start | bytes 393224 | tf_op jit(solution)/shard_map/ppermute | solution.py:267
  70.5 7.0 %collective-permute-start.16 = (bf16[2,256,128]{2,1,0:T(8,128)(2,1)S(1)}, bf16[2,256,128]{2,1,0:T(8,128)(2,1)S(1)}, u32[]{:S(2)}, u32[]{:S(2)}) collective-permute-start(bf16[2,256,128]{2,1,0:T(8,128)(2,1)S(1)} %collective-permute-done.15.refs_2_), channel_id=1, source_target_pairs={{0,4},{4,0},{8,12},{12,8},{16,20},{20,16},{24,28},{28,24},{1,5},{5... | collective-permute-start | bytes 393224 | tf_op jit(solution)/shard_map/ppermute | solution.py:267
  74.1 5.0 %collective-permute-start.19 = (bf16[2,256,128]{2,1,0:T(8,128)(2,1)S(1)}, bf16[2,256,128]{2,1,0:T(8,128)(2,1)S(1)}, u32[]{:S(2)}, u32[]{:S(2)}) collective-permute-start(bf16[2,256,128]{2,1,0:T(8,128)(2,1)S(1)} %collective-permute-done.18.refs_6_), channel_id=1, source_target_pairs={{0,4},{4,0},{8,12},{12,8},{16,20},{20,16},{24,28},{28,24},{1,5},{5... | collective-permute-start | bytes 393224 | tf_op jit(solution)/shard_map/ppermute | solution.py:267

commit v2 on v1

--- a/solution.py
+++ b/solution.py
@@ -275,9 +275,10 @@
 def gather_pieces(array, peers):
     out = {0: array, 4: swap(array, "dom", 4), 2: swap(array, "dom", 2)}
     out[1] = swap(array, "dom", 1)
-    out[4], out[1] = lax.optimization_barrier((out[4], out[1]))
+    out[3] = swap(out[2], "dom", 1)
+    out[4], out[1], out[3] = lax.optimization_barrier((out[4], out[1], out[3]))
     out[6] = swap(out[4], "dom", 2)
-    for offset in range(2, peers, 2):
+    for offset in range(4, peers, 2):
         out[offset + 1] = swap(out[offset], "dom", 1)
     return [out[offset] for offset in range(peers)]
 
@@ -393,14 +394,18 @@
         )
         piece = struct((2, rows, lanes), BF16)
         beside = swap(send, "dom", 2)
+        beside, mirror_grad = lax.optimization_barrier((beside, mirror_grad))
+        returned = exchange(mirror_grad)
         far = call(across_body, piece, [("v", far), ("v", beside)], flops=100_000, moved=500_000)
+        far, returned = lax.optimization_barrier((swap(far, "dom", 4), returned))
         mine = call(
             functools.partial(join_body, scale), piece,
-            [("v", mine), ("v", beside), ("v", swap(far, "dom", 4))],
+            [("v", mine), ("v", beside), ("v", far)],
             flops=200_000, moved=500_000,
         )
         pieces = gather_pieces(mine, peers)
-    returned = exchange(mirror_grad)
+    else:
+        returned = exchange(mirror_grad)
     grad_features = call(
         scatter_body, block, [("v", onehot), ("v", total), ("v", returned)],
         flops=2 * mirrors * rows * cols, moved=700_000,

time: 80.6 us -> 88.5 us (1.098)
  waiting for transfers between devices: 36.5 us -> 41.5 us
  starting transfers between devices: 31.1 us -> 34 us
    ppermute x20, waiting for transfers between devices: 35.2 us -> 40.2 us  [swap(): lax.ppermute(array, axis, [(i, i ^ offset) for i in range(lax.axis_size(a...]
    ppermute x20, starting transfers between devices: 20 us -> 22.9 us  [swap(): lax.ppermute(array, axis, [(i, i ^ offset) for i in range(lax.axis_size(a...]
  transfers between devices with their start and end apart: 22 -> 22, of which waited for: 13 -> 14; matrix products, arithmetic and copies ran while one was open for 0% -> 0% of each run, Pallas kernels for 4% -> 4%
where the time goes in v2:
time: 88.5 us; the launch traced here: 88.1 us
  waiting for transfers between devices  41.5 us (47%)
  starting transfers between devices  34 us (38%)
  Pallas kernels  9.18 us (10%)
  local copies, waits for them, and re-layouts  2.68 us (3%)
    ppermute x20, waiting for transfers between devices, swap(): lax.ppermute(array, axis, [(i, i ^ offset) for i in range(lax.axis_size(a...  40.2 us
    ppermute x20, starting transfers between devices, swap(): lax.ppermute(array, axis, [(i, i ^ offset) for i in range(lax.axis_size(a...  22.9 us
    all_to_all x2, starting transfers between devices, exchange(): lax.all_to_all(array.reshape(peers, slots, cols), 'dom', split_axis=0, co...  11.1 us
    pallas_call x11, Pallas kernels, call(): pl.pallas_call(body, out_shape=outs, in_specs=[SPECS[spec] for spec, _ in...  9.18 us
    unnamed x16, local copies, waits for them, and re-layouts  2.68 us
  transfers between devices with their start and end apart: 22, of which 14 were waited for; matrix products, arithmetic and copies ran while one was open for 0% of the time, Pallas kernels for 4%

profile of v2, /device:TPU:0, one launch (start us, length us, event | category | flops | bytes accessed | tf_op | source)
XLA Modules:
  0.0 88.1 jit_solution(7710782890133909077)
XLA Ops:
  0.6 2.1 %shard_map.120 = (bf16[256,512]{1,0:T(8,128)(2,1)}, bf16[512,256]{1,0:T(8,128)(2,1)}) custom-call(s32[8]{0:T(128)} %count_hbm.1, s32[8,64]{1,0:T(8,128)} %list_hbm.1, bf16[256,256]{1,0:T(8,128)(2,1)} %refs_0_.1), custom_call_target="tpu_custom_call" | custom-call | flops 67108864 | bytes 600000 | tf_op jit(solution)/shard_map/pallas_call | solution.py:22
  2.8 7.4 %all-to-all-start = ((bf16[8,64,256]{2,1,0:T(8,128)(2,1)}), bf16[8,64,256]{2,1,0:T(8,128)(2,1)S(1)}, u32[]{:S(2)}, u32[]{:S(2)}) async-start(bf16[8,64,256]{2,1,0:T(8,128)(2,1)} %bitcast.8), calls=%async_computation | async-start | bytes 524288 | tf_op jit(solution)/shard_map/all_to_all | solution.py:304
  10.2 2.0 %collective-permute-start = (bf16[256,256]{1,0:T(8,128)(2,1)S(1)}, bf16[256,256]{1,0:T(8,128)(2,1)S(1)}, u32[]{:S(2)}, u32[]{:S(2)}) collective-permute-start(bf16[256,256]{1,0:T(8,128)(2,1)S(1)} %copy-done.4), channel_id=1, source_target_pairs={{0,4},{4,0},{8,12},{12,8},{16,20},{20,16},{24,28},{28,24},{1,5},{5... | collective-permute-start | bytes 393224 | tf_op jit(solution)/shard_map/ppermute | solution.py:267
  12.9 1.0 %copy-done.1 = bf16[256,1024]{1,0:T(8,128)(2,1)S(1)} copy-done((bf16[256,1024]{1,0:T(8,128)(2,1)S(1)}, bf16[256,1024]{1,0:T(8,128)(2,1)}, u32[]{:S(2)}) %copy-start.1) | copy-done | bytes 524312
  15.9 2.0 %collective-permute-done.refs_1_ = bf16[256,256]{1,0:T(8,128)(2,1)S(1)} collective-permute-done((bf16[256,256]{1,0:T(8,128)(2,1)S(1)}, bf16[256,256]{1,0:T(8,128)(2,1)S(1)}, u32[]{:S(2)}, u32[]{:S(2)}) %collective-permute-start) | collective-permute-done | bytes 131104 | tf_op jit(solution)/shard_map/ppermute | solution.py:267
  17.8 1.3 %all-to-all-done = bf16[8,64,256]{2,1,0:T(8,128)(2,1)S(1)} async-done(((bf16[8,64,256]{2,1,0:T(8,128)(2,1)}), bf16[8,64,256]{2,1,0:T(8,128)(2,1)S(1)}, u32[]{:S(2)}, u32[]{:S(2)}) %all-to-all-start) | async-done | bytes 262176 | tf_op jit(solution)/shard_map/all_to_all | solution.py:304
  19.1 1.0 %shard_map.122 = (f32[256,256]{1,0:T(8,128)S(1)}, bf16[256,256]{1,0:T(8,128)(2,1)S(1)}, f32[256,256]{1,0:T(8,128)S(1)}, bf16[2,256,256]{2,1,0:T(8,128)(2,1)S(1)}) custom-call(s32[1]{0:T(128)} %bitcast.1.rep_ref, bf16[256,256]{1,0:T(8,128)(2,1)S(1)} %copy-done.4, bf16[512,256]{1,0:T(8,128)(2,1)S(1)} %bitcast.7, ...), custom_call_target="tpu_custom_call" | custom-call | flops 600000000 | bytes 3000000 | tf_op jit(solution)/shard_map/pallas_call | solution.py:22
  20.2 1.5 %collective-permute-start.1 = (bf16[256,256]{1,0:T(8,128)(2,1)S(1)}, bf16[256,256]{1,0:T(8,128)(2,1)S(1)}, u32[]{:S(2)}, u32[]{:S(2)}) collective-permute-start(bf16[256,256]{1,0:T(8,128)(2,1)S(1)} %get-tuple-element.52.refs_2_), channel_id=1, source_target_pairs={{0,4},{4,0},{8,12},{12,8},{16,20},{20,16},{24,28},{28,24},{1,5},{5... | collective-permute-start | bytes 393224 | tf_op jit(solution)/shard_map/ppermute | solution.py:267
  21.7 1.6 %collective-permute-start.3 = (bf16[256,256]{1,0:T(8,128)(2,1)S(1)}, bf16[256,256]{1,0:T(8,128)(2,1)S(1)}, u32[]{:S(2)}, u32[]{:S(2)}) collective-permute-start(bf16[256,256]{1,0:T(8,128)(2,1)S(1)} %shard_map.123), channel_id=1, source_target_pairs={{0,2},{1,3},{2,0},{3,1},{4,6},{5,7},{6,4},{7,5},{8,10},{9,11},{10,... | collective-permute-start | bytes 393224 | tf_op jit(solution)/shard_map/ppermute | solution.py:267
  23.3 2.8 %collective-permute-done.1.refs_3_ = bf16[256,256]{1,0:T(8,128)(2,1)S(1)} collective-permute-done((bf16[256,256]{1,0:T(8,128)(2,1)S(1)}, bf16[256,256]{1,0:T(8,128)(2,1)S(1)}, u32[]{:S(2)}, u32[]{:S(2)}) %collective-permute-start.1) | collective-permute-done | bytes 131104 | tf_op jit(solution)/shard_map/ppermute | solution.py:267
  26.1 1.2 %collective-permute-done.3.across_ref = bf16[256,256]{1,0:T(8,128)(2,1)S(1)} collective-permute-done((bf16[256,256]{1,0:T(8,128)(2,1)S(1)}, bf16[256,256]{1,0:T(8,128)(2,1)S(1)}, u32[]{:S(2)}, u32[]{:S(2)}) %collective-permute-start.3) | collective-permute-done | bytes 131104 | tf_op jit(solution)/shard_map/ppermute | solution.py:267
  28.1 1.5 %collective-permute-start.5 = (bf16[256,256]{1,0:T(8,128)(2,1)S(1)}, bf16[256,256]{1,0:T(8,128)(2,1)S(1)}, u32[]{:S(2)}, u32[]{:S(2)}) collective-permute-start(bf16[256,256]{1,0:T(8,128)(2,1)S(1)} %get-tuple-element.58.refs_0_.refs_4_), channel_id=1, source_target_pairs={{0,2},{1,3},{2,0},{3,1},{4,6},{5,7},{6,4},{7,5},{8,10},{9,11},{10,... | collective-permute-start | bytes 393224 | tf_op jit(solution)/shard_map/ppermute | solution.py:267
  29.6 1.4 %collective-permute-start.7 = (bf16[256,128]{1,0:T(8,128)(2,1)S(1)}, bf16[256,128]{1,0:T(8,128)(2,1)S(1)}, u32[]{:S(2)}, u32[]{:S(2)}) collective-permute-start(bf16[256,128]{1,0:T(8,128)(2,1)S(1)} %get-tuple-element.62), channel_id=1, source_target_pairs={{0,4},{4,0},{8,12},{12,8},{16,20},{20,16},{24,28},{28,24},{1,5},{5... | collective-permute-start | bytes 196616 | tf_op jit(solution)/shard_map/ppermute | solution.py:267
  31.0 2.9 %collective-permute-done.7.refs_8_ = bf16[256,128]{1,0:T(8,128)(2,1)S(1)} collective-permute-done((bf16[256,128]{1,0:T(8,128)(2,1)S(1)}, bf16[256,128]{1,0:T(8,128)(2,1)S(1)}, u32[]{:S(2)}, u32[]{:S(2)}) %collective-permute-start.7) | collective-permute-done | bytes 65568 | tf_op jit(solution)/shard_map/ppermute | solution.py:267
  34.9 3.2 %collective-permute-done.9.refs_10_ = bf16[256,128]{1,0:T(8,128)(2,1)S(1)} collective-permute-done((bf16[256,128]{1,0:T(8,128)(2,1)S(1)}, bf16[256,128]{1,0:T(8,128)(2,1)S(1)}, u32[]{:S(2)}, u32[]{:S(2)}) %collective-permute-start.9) | collective-permute-done | bytes 65568 | tf_op jit(solution)/shard_map/ppermute | solution.py:267
  38.1 1.2 %collective-permute-done.10.refs_11_ = bf16[256,128]{1,0:T(8,128)(2,1)S(1)} collective-permute-done((bf16[256,128]{1,0:T(8,128)(2,1)S(1)}, bf16[256,128]{1,0:T(8,128)(2,1)S(1)}, u32[]{:S(2)}, u32[]{:S(2)}) %collective-permute-start.10) | collective-permute-done | bytes 65568 | tf_op jit(solution)/shard_map/ppermute | solution.py:267
  40.2 1.1 %collective-permute-start.11 = (bf16[2,2,256,128]{3,2,1,0:T(8,128)(2,1)S(1)}, bf16[2,2,256,128]{3,2,1,0:T(8,128)(2,1)S(1)}, u32[]{:S(2)}, u32[]{:S(2)}) collective-permute-start(bf16[2,2,256,128]{3,2,1,0:T(8,128)(2,1)S(1)} %get-tuple-element.64), channel_id=1, source_target_pairs={{0,8},{4,12},{8,0},{12,4},{16,24},{20,28},{24,16},{28,20},{1,9},{5... | collective-permute-start | bytes 786440 | tf_op jit(solution)/shard_map/ppermute | solution.py:267
  41.3 1.5 %shard_map.125 = (f32[256,256]{1,0:T(8,128)S(1)}, bf16[512,256]{1,0:T(8,128)(2,1)}) custom-call(s32[1]{0:T(128)} %bitcast.1.rep_ref, bf16[256,768]{1,0:T(8,128)(2,1)S(1)} %get-tuple-element.46.high_ref, bf16[256,768]{1,0:T(8,128)(2,1)S(1)} %get-tuple-element.47.low_ref, f32[256,128]{1,0:T(8,128)S(1)} %get-tuple-element.48.deg_ref, ...), custom_call_target="tpu_custom_call" | custom-call | flops 600000000 | bytes 3000000 | tf_op jit(solution)/shard_map/pallas_call | solution.py:22
  42.8 5.8 %collective-permute-done.11.beside_ref.next_ref = bf16[2,2,256,128]{3,2,1,0:T(8,128)(2,1)S(1)} collective-permute-done((bf16[2,2,256,128]{3,2,1,0:T(8,128)(2,1)S(1)}, bf16[2,2,256,128]{3,2,1,0:T(8,128)(2,1)S(1)}, u32[]{:S(2)}, u32[]{:S(2)}) %collective-permute-start.11) | collective-permute-done | bytes 262176 | tf_op jit(solution)/shard_map/ppermute | solution.py:267
  48.6 3.6 %all-to-all-start.1 = ((bf16[8,64,256]{2,1,0:T(8,128)(2,1)}), bf16[8,64,256]{2,1,0:T(8,128)(2,1)S(1)}, u32[]{:S(2)}, u32[]{:S(2)}) async-start(bf16[8,64,256]{2,1,0:T(8,128)(2,1)} %bitcast.4), calls=%async_computation.1 | async-start | bytes 524288 | tf_op jit(solution)/shard_map/all_to_all | solution.py:304
  52.3 3.0 %collective-permute-start.12 = (bf16[2,256,128]{2,1,0:T(8,128)(2,1)S(1)}, bf16[2,256,128]{2,1,0:T(8,128)(2,1)S(1)}, u32[]{:S(2)}, u32[]{:S(2)}) collective-permute-start(bf16[2,256,128]{2,1,0:T(8,128)(2,1)S(1)} %shard_map.127), channel_id=1, source_target_pairs={{0,16},{4,20},{8,24},{12,28},{16,0},{20,4},{24,8},{28,12},{1,17},{... | collective-permute-start | bytes 393224 | tf_op jit(solution)/shard_map/ppermute | solution.py:267
  55.2 11.0 %collective-permute-done.12.far_ref = bf16[2,256,128]{2,1,0:T(8,128)(2,1)S(1)} collective-permute-done((bf16[2,256,128]{2,1,0:T(8,128)(2,1)S(1)}, bf16[2,256,128]{2,1,0:T(8,128)(2,1)S(1)}, u32[]{:S(2)}, u32[]{:S(2)}) %collective-permute-start.12) | collective-permute-done | bytes 131104 | tf_op jit(solution)/shard_map/ppermute | solution.py:267
  66.4 1.7 %collective-permute-start.13 = (bf16[2,256,128]{2,1,0:T(8,128)(2,1)S(1)}, bf16[2,256,128]{2,1,0:T(8,128)(2,1)S(1)}, u32[]{:S(2)}, u32[]{:S(2)}) collective-permute-start(bf16[2,256,128]{2,1,0:T(8,128)(2,1)S(1)} %shard_map.129.refs_0_), channel_id=1, source_target_pairs={{0,16},{4,20},{8,24},{12,28},{16,0},{20,4},{24,8},{28,12},{1,17},{... | collective-permute-start | bytes 393224 | tf_op jit(solution)/shard_map/ppermute | solution.py:267
  68.1 1.7 %collective-permute-start.14 = (bf16[2,256,128]{2,1,0:T(8,128)(2,1)S(1)}, bf16[2,256,128]{2,1,0:T(8,128)(2,1)S(1)}, u32[]{:S(2)}, u32[]{:S(2)}) collective-permute-start(bf16[2,256,128]{2,1,0:T(8,128)(2,1)S(1)} %shard_map.129.refs_0_), channel_id=1, source_target_pairs={{0,4},{4,0},{8,12},{12,8},{16,20},{20,16},{24,28},{28,24},{1,5},{5... | collective-permute-start | bytes 393224 | tf_op jit(solution)/shard_map/ppermute | solution.py:267
  69.8 2.2 %collective-permute-done.15.refs_2_ = bf16[2,256,128]{2,1,0:T(8,128)(2,1)S(1)} collective-permute-done((bf16[2,256,128]{2,1,0:T(8,128)(2,1)S(1)}, bf16[2,256,128]{2,1,0:T(8,128)(2,1)S(1)}, u32[]{:S(2)}, u32[]{:S(2)}) %collective-permute-start.15) | collective-permute-done | bytes 131104 | tf_op jit(solution)/shard_map/ppermute | solution.py:267
  72.0 2.0 %collective-permute-start.16 = (bf16[2,256,128]{2,1,0:T(8,128)(2,1)S(1)}, bf16[2,256,128]{2,1,0:T(8,128)(2,1)S(1)}, u32[]{:S(2)}, u32[]{:S(2)}) collective-permute-start(bf16[2,256,128]{2,1,0:T(8,128)(2,1)S(1)} %collective-permute-done.15.refs_2_), channel_id=1, source_target_pairs={{0,4},{4,0},{8,12},{12,8},{16,20},{20,16},{24,28},{28,24},{1,5},{5... | collective-permute-start | bytes 393224 | tf_op jit(solution)/shard_map/ppermute | solution.py:267
  74.4 2.6 %collective-permute-done.16.refs_3_ = bf16[2,256,128]{2,1,0:T(8,128)(2,1)S(1)} collective-permute-done((bf16[2,256,128]{2,1,0:T(8,128)(2,1)S(1)}, bf16[2,256,128]{2,1,0:T(8,128)(2,1)S(1)}, u32[]{:S(2)}, u32[]{:S(2)}) %collective-permute-start.16) | collective-permute-done | bytes 131104 | tf_op jit(solution)/shard_map/ppermute | solution.py:267
  77.5 1.6 %collective-permute-start.17 = (bf16[2,256,128]{2,1,0:T(8,128)(2,1)S(1)}, bf16[2,256,128]{2,1,0:T(8,128)(2,1)S(1)}, u32[]{:S(2)}, u32[]{:S(2)}) collective-permute-start(bf16[2,256,128]{2,1,0:T(8,128)(2,1)S(1)} %collective-permute-done.13.refs_4_), channel_id=1, source_target_pairs={{0,4},{4,0},{8,12},{12,8},{16,20},{20,16},{24,28},{28,24},{1,5},{5... | collective-permute-start | bytes 393224 | tf_op jit(solution)/shard_map/ppermute | solution.py:267
  79.1 2.8 %collective-permute-done.18.refs_6_ = bf16[2,256,128]{2,1,0:T(8,128)(2,1)S(1)} collective-permute-done((bf16[2,256,128]{2,1,0:T(8,128)(2,1)S(1)}, bf16[2,256,128]{2,1,0:T(8,128)(2,1)S(1)}, u32[]{:S(2)}, u32[]{:S(2)}) %collective-permute-start.18) | collective-permute-done | bytes 131104 | tf_op jit(solution)/shard_map/ppermute | solution.py:267
  82.0 2.1 %collective-permute-start.19 = (bf16[2,256,128]{2,1,0:T(8,128)(2,1)S(1)}, bf16[2,256,128]{2,1,0:T(8,128)(2,1)S(1)}, u32[]{:S(2)}, u32[]{:S(2)}) collective-permute-start(bf16[2,256,128]{2,1,0:T(8,128)(2,1)S(1)} %collective-permute-done.18.refs_6_), channel_id=1, source_target_pairs={{0,4},{4,0},{8,12},{12,8},{16,20},{20,16},{24,28},{28,24},{1,5},{5... | collective-permute-start | bytes 393224 | tf_op jit(solution)/shard_map/ppermute | solution.py:267
  84.9 2.0 %collective-permute-done.19.refs_7_ = bf16[2,256,128]{2,1,0:T(8,128)(2,1)S(1)} collective-permute-done((bf16[2,256,128]{2,1,0:T(8,128)(2,1)S(1)}, bf16[2,256,128]{2,1,0:T(8,128)(2,1)S(1)}, u32[]{:S(2)}, u32[]{:S(2)}) %collective-permute-start.19) | collective-permute-done | bytes 131104 | tf_op jit(solution)/shard_map/ppermute | solution.py:267
  87.0 1.1 %shard_map.130 = (bf16[256,1024]{1,0:T(8,128)(2,1)}, bf16[256,1024]{1,0:T(8,128)(2,1)}) custom-call(s32[1]{0:T(128)} %bitcast.dom_ref, bf16[2,256,128]{2,1,0:T(8,128)(2,1)S(1)} %shard_map.129.refs_0_, bf16[2,256,128]{2,1,0:T(8,128)(2,1)S(1)} %collective-permute-done.14.refs_1_, bf16[2,256,128]{2,1,0:T(8,128)(2,1)S(1)} %collective-permute-done.15.refs_2_, ...), custom_call_target="tpu_custom_call" | custom-call | bytes 2000000 | tf_op jit(solution)/shard_map/pallas_call | solution.py:22
  (39 shorter events, 7.2 us)
Async XLA Ops:
  0.6 11.6 %copy-start = (bf16[256,1024]{1,0:T(8,128)(2,1)S(1)}, bf16[256,1024]{1,0:T(8,128)(2,1)}, u32[]{:S(2)}) copy-start(bf16[256,1024]{1,0:T(8,128)(2,1)} %self_hbm) | copy-start | bytes 1572868
  2.8 7.4 %copy-start.4 = (bf16[256,256]{1,0:T(8,128)(2,1)S(1)}, bf16[256,256]{1,0:T(8,128)(2,1)}, u32[]{:S(2)}) copy-start(bf16[256,256]{1,0:T(8,128)(2,1)} %refs_0_.1) | copy-start | bytes 393220
  2.8 16.3 %all-to-all-start = ((bf16[8,64,256]{2,1,0:T(8,128)(2,1)}), bf16[8,64,256]{2,1,0:T(8,128)(2,1)S(1)}, u32[]{:S(2)}, u32[]{:S(2)}) async-start(bf16[8,64,256]{2,1,0:T(8,128)(2,1)} %bitcast.8), calls=%async_computation | async-start | bytes 524288 | tf_op jit(solution)/shard_map/all_to_all | solution.py:304
  10.2 7.6 %collective-permute-start = (bf16[256,256]{1,0:T(8,128)(2,1)S(1)}, bf16[256,256]{1,0:T(8,128)(2,1)S(1)}, u32[]{:S(2)}, u32[]{:S(2)}) collective-permute-start(bf16[256,256]{1,0:T(8,128)(2,1)S(1)} %copy-done.4), channel_id=1, source_target_pairs={{0,4},{4,0},{8,12},{12,8},{16,20},{20,16},{24,28},{28,24},{1,5},{5... | collective-permute-start | bytes 393224 | tf_op jit(solution)/shard_map/ppermute | solution.py:267
  12.2 0.7 copy-start.6
  12.2 0.7 copy-start.7
  12.9 1.0 %copy-start.1 = (bf16[256,1024]{1,0:T(8,128)(2,1)S(1)}, bf16[256,1024]{1,0:T(8,128)(2,1)}, u32[]{:S(2)}) copy-start(bf16[256,1024]{1,0:T(8,128)(2,1)} %neigh_hbm) | copy-start | bytes 1572868
  14.0 0.9 %copy-start.3 = (bf16[8,128,128]{2,1,0:T(8,128)(2,1)S(1)}, bf16[8,128,128]{2,1,0:T(8,128)(2,1)}, u32[]{:S(2)}) copy-start(bf16[8,128,128]{2,1,0:T(8,128)(2,1)} %tiles_ref) | copy-start | bytes 786436
  20.1 1.6 %collective-permute-start.2 = (bf16[2,256,256]{2,1,0:T(8,128)(2,1)S(1)}, bf16[2,256,256]{2,1,0:T(8,128)(2,1)S(1)}, u32[]{:S(2)}, u32[]{:S(2)}) collective-permute-start(bf16[2,256,256]{2,1,0:T(8,128)(2,1)S(1)} %get-tuple-element.54), channel_id=1, source_target_pairs={{0,1},{1,0},{2,3},{3,2},{4,5},{5,4},{6,7},{7,6},{8,9},{9,8},{10,11... | collective-permute-start | bytes 786440 | tf_op jit(solution)/shard_map/ppermute | solution.py:267
  20.2 5.9 %collective-permute-start.1 = (bf16[256,256]{1,0:T(8,128)(2,1)S(1)}, bf16[256,256]{1,0:T(8,128)(2,1)S(1)}, u32[]{:S(2)}, u32[]{:S(2)}) collective-permute-start(bf16[256,256]{1,0:T(8,128)(2,1)S(1)} %get-tuple-element.52.refs_2_), channel_id=1, source_target_pairs={{0,4},{4,0},{8,12},{12,8},{16,20},{20,16},{24,28},{28,24},{1,5},{5... | collective-permute-start | bytes 393224 | tf_op jit(solution)/shard_map/ppermute | solution.py:267
  21.7 5.6 %copy-start.5 = (bf16[256,256]{1,0:T(8,128)(2,1)S(1)}, bf16[256,256]{1,0:T(8,128)(2,1)}, u32[]{:S(2)}) copy-start(bf16[256,256]{1,0:T(8,128)(2,1)} %gout_ref) | copy-start | bytes 393220
  21.7 5.6 %collective-permute-start.3 = (bf16[256,256]{1,0:T(8,128)(2,1)S(1)}, bf16[256,256]{1,0:T(8,128)(2,1)S(1)}, u32[]{:S(2)}, u32[]{:S(2)}) collective-permute-start(bf16[256,256]{1,0:T(8,128)(2,1)S(1)} %shard_map.123), channel_id=1, source_target_pairs={{0,2},{1,3},{2,0},{3,1},{4,6},{5,7},{6,4},{7,5},{8,10},{9,11},{10,... | collective-permute-start | bytes 393224 | tf_op jit(solution)/shard_map/ppermute | solution.py:267
  28.1 6.3 %collective-permute-start.5 = (bf16[256,256]{1,0:T(8,128)(2,1)S(1)}, bf16[256,256]{1,0:T(8,128)(2,1)S(1)}, u32[]{:S(2)}, u32[]{:S(2)}) collective-permute-start(bf16[256,256]{1,0:T(8,128)(2,1)S(1)} %get-tuple-element.58.refs_0_.refs_4_), channel_id=1, source_target_pairs={{0,2},{1,3},{2,0},{3,1},{4,6},{5,7},{6,4},{7,5},{8,10},{9,11},{10,... | collective-permute-start | bytes 393224 | tf_op jit(solution)/shard_map/ppermute | solution.py:267
  29.6 4.3 %collective-permute-start.7 = (bf16[256,128]{1,0:T(8,128)(2,1)S(1)}, bf16[256,128]{1,0:T(8,128)(2,1)S(1)}, u32[]{:S(2)}, u32[]{:S(2)}) collective-permute-start(bf16[256,128]{1,0:T(8,128)(2,1)S(1)} %get-tuple-element.62), channel_id=1, source_target_pairs={{0,4},{4,0},{8,12},{12,8},{16,20},{20,16},{24,28},{28,24},{1,5},{5... | collective-permute-start | bytes 196616 | tf_op jit(solution)/shard_map/ppermute | solution.py:267
  31.0 7.1 %collective-permute-start.4 = (bf16[256,256]{1,0:T(8,128)(2,1)S(1)}, bf16[256,256]{1,0:T(8,128)(2,1)S(1)}, u32[]{:S(2)}, u32[]{:S(2)}) collective-permute-start(bf16[256,256]{1,0:T(8,128)(2,1)S(1)} %get-tuple-element.58.refs_0_.refs_4_), channel_id=1, source_target_pairs={{0,1},{1,0},{2,3},{3,2},{4,5},{5,4},{6,7},{7,6},{8,9},{9,8},{10,11... | collective-permute-start | bytes 393224 | tf_op jit(solution)/shard_map/ppermute | solution.py:267
  33.9 4.3 %collective-permute-start.9 = (bf16[256,128]{1,0:T(8,128)(2,1)S(1)}, bf16[256,128]{1,0:T(8,128)(2,1)S(1)}, u32[]{:S(2)}, u32[]{:S(2)}) collective-permute-start(bf16[256,128]{1,0:T(8,128)(2,1)S(1)} %collective-permute-done.7.refs_8_), channel_id=1, source_target_pairs={{0,2},{1,3},{2,0},{3,1},{4,6},{5,7},{6,4},{7,5},{8,10},{9,11},{10,... | collective-permute-start | bytes 196616 | tf_op jit(solution)/shard_map/ppermute | solution.py:267
  34.4 5.0 %collective-permute-start.6 = (bf16[256,256]{1,0:T(8,128)(2,1)S(1)}, bf16[256,256]{1,0:T(8,128)(2,1)S(1)}, u32[]{:S(2)}, u32[]{:S(2)}) collective-permute-start(bf16[256,256]{1,0:T(8,128)(2,1)S(1)} %collective-permute-done.5.refs_2_.refs_6_), channel_id=1, source_target_pairs={{0,1},{1,0},{2,3},{3,2},{4,5},{5,4},{6,7},{7,6},{8,9},{9,8},{10,11... | collective-permute-start | bytes 393224 | tf_op jit(solution)/shard_map/ppermute | solution.py:267
  34.4 3.7 %collective-permute-start.8 = (bf16[256,128]{1,0:T(8,128)(2,1)S(1)}, bf16[256,128]{1,0:T(8,128)(2,1)S(1)}, u32[]{:S(2)}, u32[]{:S(2)}) collective-permute-start(bf16[256,128]{1,0:T(8,128)(2,1)S(1)} %collective-permute-done.7.refs_8_), channel_id=1, source_target_pairs={{0,1},{1,0},{2,3},{3,2},{4,5},{5,4},{6,7},{7,6},{8,9},{9,8},{10,11... | collective-permute-start | bytes 196616 | tf_op jit(solution)/shard_map/ppermute | solution.py:267
  38.1 1.3 %collective-permute-start.10 = (bf16[256,128]{1,0:T(8,128)(2,1)S(1)}, bf16[256,128]{1,0:T(8,128)(2,1)S(1)}, u32[]{:S(2)}, u32[]{:S(2)}) collective-permute-start(bf16[256,128]{1,0:T(8,128)(2,1)S(1)} %collective-permute-done.9.refs_10_), channel_id=1, source_target_pairs={{0,1},{1,0},{2,3},{3,2},{4,5},{5,4},{6,7},{7,6},{8,9},{9,8},{10,11... | collective-permute-start | bytes 196616 | tf_op jit(solution)/shard_map/ppermute | solution.py:267
  40.2 8.4 %collective-permute-start.11 = (bf16[2,2,256,128]{3,2,1,0:T(8,128)(2,1)S(1)}, bf16[2,2,256,128]{3,2,1,0:T(8,128)(2,1)S(1)}, u32[]{:S(2)}, u32[]{:S(2)}) collective-permute-start(bf16[2,2,256,128]{3,2,1,0:T(8,128)(2,1)S(1)} %get-tuple-element.64), channel_id=1, source_target_pairs={{0,8},{4,12},{8,0},{12,4},{16,24},{20,28},{24,16},{28,20},{1,9},{5... | collective-permute-start | bytes 786440 | tf_op jit(solution)/shard_map/ppermute | solution.py:267
  48.6 17.6 %all-to-all-start.1 = ((bf16[8,64,256]{2,1,0:T(8,128)(2,1)}), bf16[8,64,256]{2,1,0:T(8,128)(2,1)S(1)}, u32[]{:S(2)}, u32[]{:S(2)}) async-start(bf16[8,64,256]{2,1,0:T(8,128)(2,1)} %bitcast.4), calls=%async_computation.1 | async-start | bytes 524288 | tf_op jit(solution)/shard_map/all_to_all | solution.py:304
  52.3 13.9 %collective-permute-start.12 = (bf16[2,256,128]{2,1,0:T(8,128)(2,1)S(1)}, bf16[2,256,128]{2,1,0:T(8,128)(2,1)S(1)}, u32[]{:S(2)}, u32[]{:S(2)}) collective-permute-start(bf16[2,256,128]{2,1,0:T(8,128)(2,1)S(1)} %shard_map.127), channel_id=1, source_target_pairs={{0,16},{4,20},{8,24},{12,28},{16,0},{20,4},{24,8},{28,12},{1,17},{... | collective-permute-start | bytes 393224 | tf_op jit(solution)/shard_map/ppermute | solution.py:267
  66.2 17.8 %copy-start.2 = (bf16[256,512]{1,0:T(8,128)(2,1)S(1)}, bf16[256,512]{1,0:T(8,128)(2,1)}, u32[]{:S(2)}) copy-start(bf16[256,512]{1,0:T(8,128)(2,1)} %get-tuple-element.57.onehot_ref) | copy-start | bytes 786436
  66.3 5.8 %collective-permute-start.15 = (bf16[2,256,128]{2,1,0:T(8,128)(2,1)S(1)}, bf16[2,256,128]{2,1,0:T(8,128)(2,1)S(1)}, u32[]{:S(2)}, u32[]{:S(2)}) collective-permute-start(bf16[2,256,128]{2,1,0:T(8,128)(2,1)S(1)} %shard_map.129.refs_0_), channel_id=1, source_target_pairs={{0,8},{4,12},{8,0},{12,4},{16,24},{20,28},{24,16},{28,20},{1,9},{5... | collective-permute-start | bytes 393224 | tf_op jit(solution)/shard_map/ppermute | solution.py:267
  66.4 8.0 %collective-permute-start.13 = (bf16[2,256,128]{2,1,0:T(8,128)(2,1)S(1)}, bf16[2,256,128]{2,1,0:T(8,128)(2,1)S(1)}, u32[]{:S(2)}, u32[]{:S(2)}) collective-permute-start(bf16[2,256,128]{2,1,0:T(8,128)(2,1)S(1)} %shard_map.129.refs_0_), channel_id=1, source_target_pairs={{0,16},{4,20},{8,24},{12,28},{16,0},{20,4},{24,8},{28,12},{1,17},{... | collective-permute-start | bytes 393224 | tf_op jit(solution)/shard_map/ppermute | solution.py:267
  68.1 6.3 %collective-permute-start.14 = (bf16[2,256,128]{2,1,0:T(8,128)(2,1)S(1)}, bf16[2,256,128]{2,1,0:T(8,128)(2,1)S(1)}, u32[]{:S(2)}, u32[]{:S(2)}) collective-permute-start(bf16[2,256,128]{2,1,0:T(8,128)(2,1)S(1)} %shard_map.129.refs_0_), channel_id=1, source_target_pairs={{0,4},{4,0},{8,12},{12,8},{16,20},{20,16},{24,28},{28,24},{1,5},{5... | collective-permute-start | bytes 393224 | tf_op jit(solution)/shard_map/ppermute | solution.py:267
  72.0 5.0 %collective-permute-start.16 = (bf16[2,256,128]{2,1,0:T(8,128)(2,1)S(1)}, bf16[2,256,128]{2,1,0:T(8,128)(2,1)S(1)}, u32[]{:S(2)}, u32[]{:S(2)}) collective-permute-start(bf16[2,256,128]{2,1,0:T(8,128)(2,1)S(1)} %collective-permute-done.15.refs_2_), channel_id=1, source_target_pairs={{0,4},{4,0},{8,12},{12,8},{16,20},{20,16},{24,28},{28,24},{1,5},{5... | collective-permute-start | bytes 393224 | tf_op jit(solution)/shard_map/ppermute | solution.py:267
  77.0 5.0 %collective-permute-start.18 = (bf16[2,256,128]{2,1,0:T(8,128)(2,1)S(1)}, bf16[2,256,128]{2,1,0:T(8,128)(2,1)S(1)}, u32[]{:S(2)}, u32[]{:S(2)}) collective-permute-start(bf16[2,256,128]{2,1,0:T(8,128)(2,1)S(1)} %collective-permute-done.13.refs_4_), channel_id=1, source_target_pairs={{0,8},{4,12},{8,0},{12,4},{16,24},{20,28},{24,16},{28,20},{1,9},{5... | collective-permute-start | bytes 393224 | tf_op jit(solution)/shard_map/ppermute | solution.py:267
  77.5 7.4 %collective-permute-start.17 = (bf16[2,256,128]{2,1,0:T(8,128)(2,1)S(1)}, bf16[2,256,128]{2,1,0:T(8,128)(2,1)S(1)}, u32[]{:S(2)}, u32[]{:S(2)}) collective-permute-start(bf16[2,256,128]{2,1,0:T(8,128)(2,1)S(1)} %collective-permute-done.13.refs_4_), channel_id=1, source_target_pairs={{0,4},{4,0},{8,12},{12,8},{16,20},{20,16},{24,28},{28,24},{1,5},{5... | collective-permute-start | bytes 393224 | tf_op jit(solution)/shard_map/ppermute | solution.py:267
  82.0 5.0 %collective-permute-start.19 = (bf16[2,256,128]{2,1,0:T(8,128)(2,1)S(1)}, bf16[2,256,128]{2,1,0:T(8,128)(2,1)S(1)}, u32[]{:S(2)}, u32[]{:S(2)}) collective-permute-start(bf16[2,256,128]{2,1,0:T(8,128)(2,1)S(1)} %collective-permute-done.18.refs_6_), channel_id=1, source_target_pairs={{0,4},{4,0},{8,12},{12,8},{16,20},{20,16},{24,28},{28,24},{1,5},{5... | collective-permute-start | bytes 393224 | tf_op jit(solution)/shard_map/ppermute | solution.py:267

commit v3 on v2

--- a/solution.py
+++ b/solution.py
@@ -275,10 +275,9 @@
 def gather_pieces(array, peers):
     out = {0: array, 4: swap(array, "dom", 4), 2: swap(array, "dom", 2)}
     out[1] = swap(array, "dom", 1)
-    out[3] = swap(out[2], "dom", 1)
-    out[4], out[1], out[3] = lax.optimization_barrier((out[4], out[1], out[3]))
+    out[4], out[1] = lax.optimization_barrier((out[4], out[1]))
     out[6] = swap(out[4], "dom", 2)
-    for offset in range(4, peers, 2):
+    for offset in range(2, peers, 2):
         out[offset + 1] = swap(out[offset], "dom", 1)
     return [out[offset] for offset in range(peers)]
 
@@ -394,7 +393,6 @@
         )
         piece = struct((2, rows, lanes), BF16)
         beside = swap(send, "dom", 2)
-        beside, mirror_grad = lax.optimization_barrier((beside, mirror_grad))
         returned = exchange(mirror_grad)
         far = call(across_body, piece, [("v", far), ("v", beside)], flops=100_000, moved=500_000)
         far, returned = lax.optimization_barrier((swap(far, "dom", 4), returned))

time: 88.5 us -> 85.7 us (0.968)
  waiting for transfers between devices: 41.5 us -> 39.2 us
    ppermute x20, waiting for transfers between devices: 40.2 us -> 37.9 us  [swap(): lax.ppermute(array, axis, [(i, i ^ offset) for i in range(lax.axis_size(a...]
  transfers between devices with their start and end apart: 22 -> 22, of which waited for: 14 -> 13; matrix products, arithmetic and copies ran while one was open for 0% -> 0% of each run, Pallas kernels for 4% -> 5%
where the time goes in v3:
time: 85.7 us; the launch traced here: 85.3 us
  waiting for transfers between devices  39.2 us (46%)
  starting transfers between devices  33.5 us (39%)
  Pallas kernels  9.2 us (11%)
  local copies, waits for them, and re-layouts  2.68 us (3%)
    ppermute x20, waiting for transfers between devices, swap(): lax.ppermute(array, axis, [(i, i ^ offset) for i in range(lax.axis_size(a...  37.9 us
    ppermute x20, starting transfers between devices, swap(): lax.ppermute(array, axis, [(i, i ^ offset) for i in range(lax.axis_size(a...  22.5 us
    all_to_all x2, starting transfers between devices, exchange(): lax.all_to_all(array.reshape(peers, slots, cols), 'dom', split_axis=0, co...  11.1 us
    pallas_call x11, Pallas kernels, call(): pl.pallas_call(body, out_shape=outs, in_specs=[SPECS[spec] for spec, _ in...  9.2 us
    unnamed x16, local copies, waits for them, and re-layouts  2.68 us
  transfers between devices with their start and end apart: 22, of which 13 were waited for; matrix products, arithmetic and copies ran while one was open for 0% of the time, Pallas kernels for 5%

profile of v3, /device:TPU:0, one launch (start us, length us, event | category | flops | bytes accessed | tf_op | source)
XLA Modules:
  0.0 85.3 jit_solution(17877152866034971172)
XLA Ops:
  0.6 2.1 %shard_map.120 = (bf16[256,512]{1,0:T(8,128)(2,1)}, bf16[512,256]{1,0:T(8,128)(2,1)}) custom-call(s32[8]{0:T(128)} %count_hbm.1, s32[8,64]{1,0:T(8,128)} %list_hbm.1, bf16[256,256]{1,0:T(8,128)(2,1)} %refs_0_.1), custom_call_target="tpu_custom_call" | custom-call | flops 67108864 | bytes 600000 | tf_op jit(solution)/shard_map/pallas_call | solution.py:22
  2.8 7.4 %all-to-all-start = ((bf16[8,64,256]{2,1,0:T(8,128)(2,1)}), bf16[8,64,256]{2,1,0:T(8,128)(2,1)S(1)}, u32[]{:S(2)}, u32[]{:S(2)}) async-start(bf16[8,64,256]{2,1,0:T(8,128)(2,1)} %bitcast.8), calls=%async_computation | async-start | bytes 524288 | tf_op jit(solution)/shard_map/all_to_all | solution.py:303
  10.2 2.0 %collective-permute-start = (bf16[256,256]{1,0:T(8,128)(2,1)S(1)}, bf16[256,256]{1,0:T(8,128)(2,1)S(1)}, u32[]{:S(2)}, u32[]{:S(2)}) collective-permute-start(bf16[256,256]{1,0:T(8,128)(2,1)S(1)} %copy-done.4), channel_id=1, source_target_pairs={{0,4},{4,0},{8,12},{12,8},{16,20},{20,16},{24,28},{28,24},{1,5},{5... | collective-permute-start | bytes 393224 | tf_op jit(solution)/shard_map/ppermute | solution.py:267
  12.9 1.0 %copy-done.1 = bf16[256,1024]{1,0:T(8,128)(2,1)S(1)} copy-done((bf16[256,1024]{1,0:T(8,128)(2,1)S(1)}, bf16[256,1024]{1,0:T(8,128)(2,1)}, u32[]{:S(2)}) %copy-start.1) | copy-done | bytes 524312
  14.0 0.9 %copy-done.3 = bf16[8,128,128]{2,1,0:T(8,128)(2,1)S(1)} copy-done((bf16[8,128,128]{2,1,0:T(8,128)(2,1)S(1)}, bf16[8,128,128]{2,1,0:T(8,128)(2,1)}, u32[]{:S(2)}) %copy-start.3) | copy-done | bytes 262168
  14.9 0.9 %shard_map.121 = (bf16[256,768]{1,0:T(8,128)(2,1)S(1)}, bf16[256,768]{1,0:T(8,128)(2,1)S(1)}, f32[256,128]{1,0:T(8,128)S(1)}, bf16[256,1024]{1,0:T(8,128)(2,1)S(1)}, bf16[256,1024]{1,0:T(8,128)(2,1)S(1)}) custom-call(s32[8]{0:T(128)S(1)} %copy-done.6, s32[8]{0:T(128)S(1)} %copy-done.7, bf16[8,128,128]{2,1,0:T(8,128)(2,1)S(1)} %copy-done.3, ...), custom_call_target="tpu_custom_call" | custom-call | flops 1000000 | bytes 3000000 | tf_op jit(solution)/shard_map/pallas_call | solution.py:22
  15.9 2.0 %collective-permute-done.refs_1_ = bf16[256,256]{1,0:T(8,128)(2,1)S(1)} collective-permute-done((bf16[256,256]{1,0:T(8,128)(2,1)S(1)}, bf16[256,256]{1,0:T(8,128)(2,1)S(1)}, u32[]{:S(2)}, u32[]{:S(2)}) %collective-permute-start) | collective-permute-done | bytes 131104 | tf_op jit(solution)/shard_map/ppermute | solution.py:267
  17.8 1.3 %all-to-all-done = bf16[8,64,256]{2,1,0:T(8,128)(2,1)S(1)} async-done(((bf16[8,64,256]{2,1,0:T(8,128)(2,1)}), bf16[8,64,256]{2,1,0:T(8,128)(2,1)S(1)}, u32[]{:S(2)}, u32[]{:S(2)}) %all-to-all-start) | async-done | bytes 262176 | tf_op jit(solution)/shard_map/all_to_all | solution.py:303
  19.1 1.0 %shard_map.122 = (f32[256,256]{1,0:T(8,128)S(1)}, bf16[256,256]{1,0:T(8,128)(2,1)S(1)}, f32[256,256]{1,0:T(8,128)S(1)}, bf16[2,256,256]{2,1,0:T(8,128)(2,1)S(1)}) custom-call(s32[1]{0:T(128)} %bitcast.1.rep_ref, bf16[256,256]{1,0:T(8,128)(2,1)S(1)} %copy-done.4, bf16[512,256]{1,0:T(8,128)(2,1)S(1)} %bitcast.7, ...), custom_call_target="tpu_custom_call" | custom-call | flops 600000000 | bytes 3000000 | tf_op jit(solution)/shard_map/pallas_call | solution.py:22
  20.2 1.5 %collective-permute-start.1 = (bf16[256,256]{1,0:T(8,128)(2,1)S(1)}, bf16[256,256]{1,0:T(8,128)(2,1)S(1)}, u32[]{:S(2)}, u32[]{:S(2)}) collective-permute-start(bf16[256,256]{1,0:T(8,128)(2,1)S(1)} %get-tuple-element.49.refs_2_), channel_id=1, source_target_pairs={{0,4},{4,0},{8,12},{12,8},{16,20},{20,16},{24,28},{28,24},{1,5},{5... | collective-permute-start | bytes 393224 | tf_op jit(solution)/shard_map/ppermute | solution.py:267
  21.7 1.6 %collective-permute-start.3 = (bf16[256,256]{1,0:T(8,128)(2,1)S(1)}, bf16[256,256]{1,0:T(8,128)(2,1)S(1)}, u32[]{:S(2)}, u32[]{:S(2)}) collective-permute-start(bf16[256,256]{1,0:T(8,128)(2,1)S(1)} %shard_map.123), channel_id=1, source_target_pairs={{0,2},{1,3},{2,0},{3,1},{4,6},{5,7},{6,4},{7,5},{8,10},{9,11},{10,... | collective-permute-start | bytes 393224 | tf_op jit(solution)/shard_map/ppermute | solution.py:267
  23.3 2.8 %collective-permute-done.1.refs_3_ = bf16[256,256]{1,0:T(8,128)(2,1)S(1)} collective-permute-done((bf16[256,256]{1,0:T(8,128)(2,1)S(1)}, bf16[256,256]{1,0:T(8,128)(2,1)S(1)}, u32[]{:S(2)}, u32[]{:S(2)}) %collective-permute-start.1) | collective-permute-done | bytes 131104 | tf_op jit(solution)/shard_map/ppermute | solution.py:267
  26.1 1.2 %collective-permute-done.3.across_ref = bf16[256,256]{1,0:T(8,128)(2,1)S(1)} collective-permute-done((bf16[256,256]{1,0:T(8,128)(2,1)S(1)}, bf16[256,256]{1,0:T(8,128)(2,1)S(1)}, u32[]{:S(2)}, u32[]{:S(2)}) %collective-permute-start.3) | collective-permute-done | bytes 131104 | tf_op jit(solution)/shard_map/ppermute | solution.py:267
  28.1 1.5 %collective-permute-start.5 = (bf16[256,256]{1,0:T(8,128)(2,1)S(1)}, bf16[256,256]{1,0:T(8,128)(2,1)S(1)}, u32[]{:S(2)}, u32[]{:S(2)}) collective-permute-start(bf16[256,256]{1,0:T(8,128)(2,1)S(1)} %get-tuple-element.55.refs_0_.refs_4_), channel_id=1, source_target_pairs={{0,2},{1,3},{2,0},{3,1},{4,6},{5,7},{6,4},{7,5},{8,10},{9,11},{10,... | collective-permute-start | bytes 393224 | tf_op jit(solution)/shard_map/ppermute | solution.py:267
  29.6 1.4 %collective-permute-start.7 = (bf16[256,128]{1,0:T(8,128)(2,1)S(1)}, bf16[256,128]{1,0:T(8,128)(2,1)S(1)}, u32[]{:S(2)}, u32[]{:S(2)}) collective-permute-start(bf16[256,128]{1,0:T(8,128)(2,1)S(1)} %get-tuple-element.59), channel_id=1, source_target_pairs={{0,4},{4,0},{8,12},{12,8},{16,20},{20,16},{24,28},{28,24},{1,5},{5... | collective-permute-start | bytes 196616 | tf_op jit(solution)/shard_map/ppermute | solution.py:267
  31.0 2.1 %collective-permute-done.5.refs_2_.refs_6_ = bf16[256,256]{1,0:T(8,128)(2,1)S(1)} collective-permute-done((bf16[256,256]{1,0:T(8,128)(2,1)S(1)}, bf16[256,256]{1,0:T(8,128)(2,1)S(1)}, u32[]{:S(2)}, u32[]{:S(2)}) %collective-permute-start.5) | collective-permute-done | bytes 131104 | tf_op jit(solution)/shard_map/ppermute | solution.py:267
  34.8 3.3 %collective-permute-done.9.refs_10_ = bf16[256,128]{1,0:T(8,128)(2,1)S(1)} collective-permute-done((bf16[256,128]{1,0:T(8,128)(2,1)S(1)}, bf16[256,128]{1,0:T(8,128)(2,1)S(1)}, u32[]{:S(2)}, u32[]{:S(2)}) %collective-permute-start.9) | collective-permute-done | bytes 65568 | tf_op jit(solution)/shard_map/ppermute | solution.py:267
  38.1 1.5 %shard_map.125 = (f32[256,256]{1,0:T(8,128)S(1)}, bf16[512,256]{1,0:T(8,128)(2,1)}) custom-call(s32[1]{0:T(128)} %bitcast.1.rep_ref, bf16[256,768]{1,0:T(8,128)(2,1)S(1)} %get-tuple-element.43.high_ref, bf16[256,768]{1,0:T(8,128)(2,1)S(1)} %get-tuple-element.44.low_ref, f32[256,128]{1,0:T(8,128)S(1)} %get-tuple-element.45.deg_ref, ...), custom_call_target="tpu_custom_call" | custom-call | flops 600000000 | bytes 3000000 | tf_op jit(solution)/shard_map/pallas_call | solution.py:22
  39.7 3.6 %all-to-all-start.1 = ((bf16[8,64,256]{2,1,0:T(8,128)(2,1)}), bf16[8,64,256]{2,1,0:T(8,128)(2,1)S(1)}, u32[]{:S(2)}, u32[]{:S(2)}) async-start(bf16[8,64,256]{2,1,0:T(8,128)(2,1)} %bitcast.4), calls=%async_computation.1 | async-start | bytes 524288 | tf_op jit(solution)/shard_map/all_to_all | solution.py:303
  44.1 2.1 %collective-permute-start.11 = (bf16[2,2,256,128]{3,2,1,0:T(8,128)(2,1)S(1)}, bf16[2,2,256,128]{3,2,1,0:T(8,128)(2,1)S(1)}, u32[]{:S(2)}, u32[]{:S(2)}) collective-permute-start(bf16[2,2,256,128]{3,2,1,0:T(8,128)(2,1)S(1)} %get-tuple-element.61), channel_id=1, source_target_pairs={{0,8},{4,12},{8,0},{12,4},{16,24},{20,28},{24,16},{28,20},{1,9},{5... | collective-permute-start | bytes 786440 | tf_op jit(solution)/shard_map/ppermute | solution.py:267
  46.2 10.0 %collective-permute-done.11.beside_ref.next_ref = bf16[2,2,256,128]{3,2,1,0:T(8,128)(2,1)S(1)} collective-permute-done((bf16[2,2,256,128]{3,2,1,0:T(8,128)(2,1)S(1)}, bf16[2,2,256,128]{3,2,1,0:T(8,128)(2,1)S(1)}, u32[]{:S(2)}, u32[]{:S(2)}) %collective-permute-start.11) | collective-permute-done | bytes 262176 | tf_op jit(solution)/shard_map/ppermute | solution.py:267
  56.2 2.4 %collective-permute-start.12 = (bf16[2,256,128]{2,1,0:T(8,128)(2,1)S(1)}, bf16[2,256,128]{2,1,0:T(8,128)(2,1)S(1)}, u32[]{:S(2)}, u32[]{:S(2)}) collective-permute-start(bf16[2,256,128]{2,1,0:T(8,128)(2,1)S(1)} %shard_map.127), channel_id=1, source_target_pairs={{0,16},{4,20},{8,24},{12,28},{16,0},{20,4},{24,8},{28,12},{1,17},{... | collective-permute-start | bytes 393224 | tf_op jit(solution)/shard_map/ppermute | solution.py:267
  58.6 6.2 %collective-permute-done.12.far_ref = bf16[2,256,128]{2,1,0:T(8,128)(2,1)S(1)} collective-permute-done((bf16[2,256,128]{2,1,0:T(8,128)(2,1)S(1)}, bf16[2,256,128]{2,1,0:T(8,128)(2,1)S(1)}, u32[]{:S(2)}, u32[]{:S(2)}) %collective-permute-start.12) | collective-permute-done | bytes 131104 | tf_op jit(solution)/shard_map/ppermute | solution.py:267
  64.9 1.5 %collective-permute-start.14 = (bf16[2,256,128]{2,1,0:T(8,128)(2,1)S(1)}, bf16[2,256,128]{2,1,0:T(8,128)(2,1)S(1)}, u32[]{:S(2)}, u32[]{:S(2)}) collective-permute-start(bf16[2,256,128]{2,1,0:T(8,128)(2,1)S(1)} %shard_map.129.refs_0_), channel_id=1, source_target_pairs={{0,4},{4,0},{8,12},{12,8},{16,20},{20,16},{24,28},{28,24},{1,5},{5... | collective-permute-start | bytes 393224 | tf_op jit(solution)/shard_map/ppermute | solution.py:267
  66.5 3.1 %collective-permute-start.15 = (bf16[2,256,128]{2,1,0:T(8,128)(2,1)S(1)}, bf16[2,256,128]{2,1,0:T(8,128)(2,1)S(1)}, u32[]{:S(2)}, u32[]{:S(2)}) collective-permute-start(bf16[2,256,128]{2,1,0:T(8,128)(2,1)S(1)} %shard_map.129.refs_0_), channel_id=1, source_target_pairs={{0,8},{4,12},{8,0},{12,4},{16,24},{20,28},{24,16},{28,20},{1,9},{5... | collective-permute-start | bytes 393224 | tf_op jit(solution)/shard_map/ppermute | solution.py:267
  69.6 3.5 %collective-permute-done.13.refs_4_ = bf16[2,256,128]{2,1,0:T(8,128)(2,1)S(1)} collective-permute-done((bf16[2,256,128]{2,1,0:T(8,128)(2,1)S(1)}, bf16[2,256,128]{2,1,0:T(8,128)(2,1)S(1)}, u32[]{:S(2)}, u32[]{:S(2)}) %collective-permute-start.13) | collective-permute-done | bytes 131104 | tf_op jit(solution)/shard_map/ppermute | solution.py:267
  73.1 1.8 %collective-permute-start.17 = (bf16[2,256,128]{2,1,0:T(8,128)(2,1)S(1)}, bf16[2,256,128]{2,1,0:T(8,128)(2,1)S(1)}, u32[]{:S(2)}, u32[]{:S(2)}) collective-permute-start(bf16[2,256,128]{2,1,0:T(8,128)(2,1)S(1)} %collective-permute-done.13.refs_4_), channel_id=1, source_target_pairs={{0,4},{4,0},{8,12},{12,8},{16,20},{20,16},{24,28},{28,24},{1,5},{5... | collective-permute-start | bytes 393224 | tf_op jit(solution)/shard_map/ppermute | solution.py:267
  75.6 2.9 %collective-permute-done.18.refs_6_ = bf16[2,256,128]{2,1,0:T(8,128)(2,1)S(1)} collective-permute-done((bf16[2,256,128]{2,1,0:T(8,128)(2,1)S(1)}, bf16[2,256,128]{2,1,0:T(8,128)(2,1)S(1)}, u32[]{:S(2)}, u32[]{:S(2)}) %collective-permute-start.18) | collective-permute-done | bytes 131104 | tf_op jit(solution)/shard_map/ppermute | solution.py:267
  78.5 1.8 %collective-permute-start.19 = (bf16[2,256,128]{2,1,0:T(8,128)(2,1)S(1)}, bf16[2,256,128]{2,1,0:T(8,128)(2,1)S(1)}, u32[]{:S(2)}, u32[]{:S(2)}) collective-permute-start(bf16[2,256,128]{2,1,0:T(8,128)(2,1)S(1)} %collective-permute-done.18.refs_6_), channel_id=1, source_target_pairs={{0,4},{4,0},{8,12},{12,8},{16,20},{20,16},{24,28},{28,24},{1,5},{5... | collective-permute-start | bytes 393224 | tf_op jit(solution)/shard_map/ppermute | solution.py:267
  81.2 1.1 %collective-permute-done.16.refs_3_ = bf16[2,256,128]{2,1,0:T(8,128)(2,1)S(1)} collective-permute-done((bf16[2,256,128]{2,1,0:T(8,128)(2,1)S(1)}, bf16[2,256,128]{2,1,0:T(8,128)(2,1)S(1)}, u32[]{:S(2)}, u32[]{:S(2)}) %collective-permute-start.16) | collective-permute-done | bytes 131104 | tf_op jit(solution)/shard_map/ppermute | solution.py:267
  82.3 1.9 %collective-permute-done.19.refs_7_ = bf16[2,256,128]{2,1,0:T(8,128)(2,1)S(1)} collective-permute-done((bf16[2,256,128]{2,1,0:T(8,128)(2,1)S(1)}, bf16[2,256,128]{2,1,0:T(8,128)(2,1)S(1)}, u32[]{:S(2)}, u32[]{:S(2)}) %collective-permute-start.19) | collective-permute-done | bytes 131104 | tf_op jit(solution)/shard_map/ppermute | solution.py:267
  84.2 1.1 %shard_map.130 = (bf16[256,1024]{1,0:T(8,128)(2,1)}, bf16[256,1024]{1,0:T(8,128)(2,1)}) custom-call(s32[1]{0:T(128)} %bitcast.dom_ref, bf16[2,256,128]{2,1,0:T(8,128)(2,1)S(1)} %shard_map.129.refs_0_, bf16[2,256,128]{2,1,0:T(8,128)(2,1)S(1)} %collective-permute-done.14.refs_1_, bf16[2,256,128]{2,1,0:T(8,128)(2,1)S(1)} %collective-permute-done.15.refs_2_, ...), custom_call_target="tpu_custom_call" | custom-call | bytes 2000000 | tf_op jit(solution)/shard_map/pallas_call | solution.py:22
  (39 shorter events, 5.8 us)
Async XLA Ops:
  0.6 11.6 %copy-start = (bf16[256,1024]{1,0:T(8,128)(2,1)S(1)}, bf16[256,1024]{1,0:T(8,128)(2,1)}, u32[]{:S(2)}) copy-start(bf16[256,1024]{1,0:T(8,128)(2,1)} %self_hbm) | copy-start | bytes 1572868
  2.8 7.4 %copy-start.4 = (bf16[256,256]{1,0:T(8,128)(2,1)S(1)}, bf16[256,256]{1,0:T(8,128)(2,1)}, u32[]{:S(2)}) copy-start(bf16[256,256]{1,0:T(8,128)(2,1)} %refs_0_.1) | copy-start | bytes 393220
  2.8 16.3 %all-to-all-start = ((bf16[8,64,256]{2,1,0:T(8,128)(2,1)}), bf16[8,64,256]{2,1,0:T(8,128)(2,1)S(1)}, u32[]{:S(2)}, u32[]{:S(2)}) async-start(bf16[8,64,256]{2,1,0:T(8,128)(2,1)} %bitcast.8), calls=%async_computation | async-start | bytes 524288 | tf_op jit(solution)/shard_map/all_to_all | solution.py:303
  10.2 7.6 %collective-permute-start = (bf16[256,256]{1,0:T(8,128)(2,1)S(1)}, bf16[256,256]{1,0:T(8,128)(2,1)S(1)}, u32[]{:S(2)}, u32[]{:S(2)}) collective-permute-start(bf16[256,256]{1,0:T(8,128)(2,1)S(1)} %copy-done.4), channel_id=1, source_target_pairs={{0,4},{4,0},{8,12},{12,8},{16,20},{20,16},{24,28},{28,24},{1,5},{5... | collective-permute-start | bytes 393224 | tf_op jit(solution)/shard_map/ppermute | solution.py:267
  12.2 0.7 copy-start.6
  12.2 0.7 copy-start.7
  12.9 1.0 %copy-start.1 = (bf16[256,1024]{1,0:T(8,128)(2,1)S(1)}, bf16[256,1024]{1,0:T(8,128)(2,1)}, u32[]{:S(2)}) copy-start(bf16[256,1024]{1,0:T(8,128)(2,1)} %neigh_hbm) | copy-start | bytes 1572868
  14.0 0.9 %copy-start.3 = (bf16[8,128,128]{2,1,0:T(8,128)(2,1)S(1)}, bf16[8,128,128]{2,1,0:T(8,128)(2,1)}, u32[]{:S(2)}) copy-start(bf16[8,128,128]{2,1,0:T(8,128)(2,1)} %tiles_ref) | copy-start | bytes 786436
  20.1 1.6 %collective-permute-start.2 = (bf16[2,256,256]{2,1,0:T(8,128)(2,1)S(1)}, bf16[2,256,256]{2,1,0:T(8,128)(2,1)S(1)}, u32[]{:S(2)}, u32[]{:S(2)}) collective-permute-start(bf16[2,256,256]{2,1,0:T(8,128)(2,1)S(1)} %get-tuple-element.51), channel_id=1, source_target_pairs={{0,1},{1,0},{2,3},{3,2},{4,5},{5,4},{6,7},{7,6},{8,9},{9,8},{10,11... | collective-permute-start | bytes 786440 | tf_op jit(solution)/shard_map/ppermute | solution.py:267
  20.2 5.9 %collective-permute-start.1 = (bf16[256,256]{1,0:T(8,128)(2,1)S(1)}, bf16[256,256]{1,0:T(8,128)(2,1)S(1)}, u32[]{:S(2)}, u32[]{:S(2)}) collective-permute-start(bf16[256,256]{1,0:T(8,128)(2,1)S(1)} %get-tuple-element.49.refs_2_), channel_id=1, source_target_pairs={{0,4},{4,0},{8,12},{12,8},{16,20},{20,16},{24,28},{28,24},{1,5},{5... | collective-permute-start | bytes 393224 | tf_op jit(solution)/shard_map/ppermute | solution.py:267
  21.7 5.6 %copy-start.5 = (bf16[256,256]{1,0:T(8,128)(2,1)S(1)}, bf16[256,256]{1,0:T(8,128)(2,1)}, u32[]{:S(2)}) copy-start(bf16[256,256]{1,0:T(8,128)(2,1)} %gout_ref) | copy-start | bytes 393220
  21.7 5.6 %collective-permute-start.3 = (bf16[256,256]{1,0:T(8,128)(2,1)S(1)}, bf16[256,256]{1,0:T(8,128)(2,1)S(1)}, u32[]{:S(2)}, u32[]{:S(2)}) collective-permute-start(bf16[256,256]{1,0:T(8,128)(2,1)S(1)} %shard_map.123), channel_id=1, source_target_pairs={{0,2},{1,3},{2,0},{3,1},{4,6},{5,7},{6,4},{7,5},{8,10},{9,11},{10,... | collective-permute-start | bytes 393224 | tf_op jit(solution)/shard_map/ppermute | solution.py:267
  28.1 5.0 %collective-permute-start.5 = (bf16[256,256]{1,0:T(8,128)(2,1)S(1)}, bf16[256,256]{1,0:T(8,128)(2,1)S(1)}, u32[]{:S(2)}, u32[]{:S(2)}) collective-permute-start(bf16[256,256]{1,0:T(8,128)(2,1)S(1)} %get-tuple-element.55.refs_0_.refs_4_), channel_id=1, source_target_pairs={{0,2},{1,3},{2,0},{3,1},{4,6},{5,7},{6,4},{7,5},{8,10},{9,11},{10,... | collective-permute-start | bytes 393224 | tf_op jit(solution)/shard_map/ppermute | solution.py:267
  29.6 4.3 %collective-permute-start.7 = (bf16[256,128]{1,0:T(8,128)(2,1)S(1)}, bf16[256,128]{1,0:T(8,128)(2,1)S(1)}, u32[]{:S(2)}, u32[]{:S(2)}) collective-permute-start(bf16[256,128]{1,0:T(8,128)(2,1)S(1)} %get-tuple-element.59), channel_id=1, source_target_pairs={{0,4},{4,0},{8,12},{12,8},{16,20},{20,16},{24,28},{28,24},{1,5},{5... | collective-permute-start | bytes 196616 | tf_op jit(solution)/shard_map/ppermute | solution.py:267
  31.0 7.1 %collective-permute-start.4 = (bf16[256,256]{1,0:T(8,128)(2,1)S(1)}, bf16[256,256]{1,0:T(8,128)(2,1)S(1)}, u32[]{:S(2)}, u32[]{:S(2)}) collective-permute-start(bf16[256,256]{1,0:T(8,128)(2,1)S(1)} %get-tuple-element.55.refs_0_.refs_4_), channel_id=1, source_target_pairs={{0,1},{1,0},{2,3},{3,2},{4,5},{5,4},{6,7},{7,6},{8,9},{9,8},{10,11... | collective-permute-start | bytes 393224 | tf_op jit(solution)/shard_map/ppermute | solution.py:267
  33.1 5.1 %collective-permute-start.6 = (bf16[256,256]{1,0:T(8,128)(2,1)S(1)}, bf16[256,256]{1,0:T(8,128)(2,1)S(1)}, u32[]{:S(2)}, u32[]{:S(2)}) collective-permute-start(bf16[256,256]{1,0:T(8,128)(2,1)S(1)} %collective-permute-done.5.refs_2_.refs_6_), channel_id=1, source_target_pairs={{0,1},{1,0},{2,3},{3,2},{4,5},{5,4},{6,7},{7,6},{8,9},{9,8},{10,11... | collective-permute-start | bytes 393224 | tf_op jit(solution)/shard_map/ppermute | solution.py:267
  33.9 4.3 %collective-permute-start.9 = (bf16[256,128]{1,0:T(8,128)(2,1)S(1)}, bf16[256,128]{1,0:T(8,128)(2,1)S(1)}, u32[]{:S(2)}, u32[]{:S(2)}) collective-permute-start(bf16[256,128]{1,0:T(8,128)(2,1)S(1)} %collective-permute-done.7.refs_8_), channel_id=1, source_target_pairs={{0,2},{1,3},{2,0},{3,1},{4,6},{5,7},{6,4},{7,5},{8,10},{9,11},{10,... | collective-permute-start | bytes 196616 | tf_op jit(solution)/shard_map/ppermute | solution.py:267
  34.6 8.7 %collective-permute-start.8 = (bf16[256,128]{1,0:T(8,128)(2,1)S(1)}, bf16[256,128]{1,0:T(8,128)(2,1)S(1)}, u32[]{:S(2)}, u32[]{:S(2)}) collective-permute-start(bf16[256,128]{1,0:T(8,128)(2,1)S(1)} %collective-permute-done.7.refs_8_), channel_id=1, source_target_pairs={{0,1},{1,0},{2,3},{3,2},{4,5},{5,4},{6,7},{7,6},{8,9},{9,8},{10,11... | collective-permute-start | bytes 196616 | tf_op jit(solution)/shard_map/ppermute | solution.py:267
  38.1 5.2 %collective-permute-start.10 = (bf16[256,128]{1,0:T(8,128)(2,1)S(1)}, bf16[256,128]{1,0:T(8,128)(2,1)S(1)}, u32[]{:S(2)}, u32[]{:S(2)}) collective-permute-start(bf16[256,128]{1,0:T(8,128)(2,1)S(1)} %collective-permute-done.9.refs_10_), channel_id=1, source_target_pairs={{0,1},{1,0},{2,3},{3,2},{4,5},{5,4},{6,7},{7,6},{8,9},{9,8},{10,11... | collective-permute-start | bytes 196616 | tf_op jit(solution)/shard_map/ppermute | solution.py:267
  39.7 25.1 %all-to-all-start.1 = ((bf16[8,64,256]{2,1,0:T(8,128)(2,1)}), bf16[8,64,256]{2,1,0:T(8,128)(2,1)S(1)}, u32[]{:S(2)}, u32[]{:S(2)}) async-start(bf16[8,64,256]{2,1,0:T(8,128)(2,1)} %bitcast.4), calls=%async_computation.1 | async-start | bytes 524288 | tf_op jit(solution)/shard_map/all_to_all | solution.py:303
  44.1 12.1 %collective-permute-start.11 = (bf16[2,2,256,128]{3,2,1,0:T(8,128)(2,1)S(1)}, bf16[2,2,256,128]{3,2,1,0:T(8,128)(2,1)S(1)}, u32[]{:S(2)}, u32[]{:S(2)}) collective-permute-start(bf16[2,2,256,128]{3,2,1,0:T(8,128)(2,1)S(1)} %get-tuple-element.61), channel_id=1, source_target_pairs={{0,8},{4,12},{8,0},{12,4},{16,24},{20,28},{24,16},{28,20},{1,9},{5... | collective-permute-start | bytes 786440 | tf_op jit(solution)/shard_map/ppermute | solution.py:267
  56.2 8.6 %collective-permute-start.12 = (bf16[2,256,128]{2,1,0:T(8,128)(2,1)S(1)}, bf16[2,256,128]{2,1,0:T(8,128)(2,1)S(1)}, u32[]{:S(2)}, u32[]{:S(2)}) collective-permute-start(bf16[2,256,128]{2,1,0:T(8,128)(2,1)S(1)} %shard_map.127), channel_id=1, source_target_pairs={{0,16},{4,20},{8,24},{12,28},{16,0},{20,4},{24,8},{28,12},{1,17},{... | collective-permute-start | bytes 393224 | tf_op jit(solution)/shard_map/ppermute | solution.py:267
  64.8 15.5 %copy-start.2 = (bf16[256,512]{1,0:T(8,128)(2,1)S(1)}, bf16[256,512]{1,0:T(8,128)(2,1)}, u32[]{:S(2)}) copy-start(bf16[256,512]{1,0:T(8,128)(2,1)} %get-tuple-element.54.onehot_ref) | copy-start | bytes 786436
  64.9 8.3 %collective-permute-start.13 = (bf16[2,256,128]{2,1,0:T(8,128)(2,1)S(1)}, bf16[2,256,128]{2,1,0:T(8,128)(2,1)S(1)}, u32[]{:S(2)}, u32[]{:S(2)}) collective-permute-start(bf16[2,256,128]{2,1,0:T(8,128)(2,1)S(1)} %shard_map.129.refs_0_), channel_id=1, source_target_pairs={{0,16},{4,20},{8,24},{12,28},{16,0},{20,4},{24,8},{28,12},{1,17},{... | collective-permute-start | bytes 393224 | tf_op jit(solution)/shard_map/ppermute | solution.py:267
  64.9 8.2 %collective-permute-start.14 = (bf16[2,256,128]{2,1,0:T(8,128)(2,1)S(1)}, bf16[2,256,128]{2,1,0:T(8,128)(2,1)S(1)}, u32[]{:S(2)}, u32[]{:S(2)}) collective-permute-start(bf16[2,256,128]{2,1,0:T(8,128)(2,1)S(1)} %shard_map.129.refs_0_), channel_id=1, source_target_pairs={{0,4},{4,0},{8,12},{12,8},{16,20},{20,16},{24,28},{28,24},{1,5},{5... | collective-permute-start | bytes 393224 | tf_op jit(solution)/shard_map/ppermute | solution.py:267
  66.5 8.5 %collective-permute-start.15 = (bf16[2,256,128]{2,1,0:T(8,128)(2,1)S(1)}, bf16[2,256,128]{2,1,0:T(8,128)(2,1)S(1)}, u32[]{:S(2)}, u32[]{:S(2)}) collective-permute-start(bf16[2,256,128]{2,1,0:T(8,128)(2,1)S(1)} %shard_map.129.refs_0_), channel_id=1, source_target_pairs={{0,8},{4,12},{8,0},{12,4},{16,24},{20,28},{24,16},{28,20},{1,9},{5... | collective-permute-start | bytes 393224 | tf_op jit(solution)/shard_map/ppermute | solution.py:267
  73.1 5.4 %collective-permute-start.18 = (bf16[2,256,128]{2,1,0:T(8,128)(2,1)S(1)}, bf16[2,256,128]{2,1,0:T(8,128)(2,1)S(1)}, u32[]{:S(2)}, u32[]{:S(2)}) collective-permute-start(bf16[2,256,128]{2,1,0:T(8,128)(2,1)S(1)} %collective-permute-done.13.refs_4_), channel_id=1, source_target_pairs={{0,8},{4,12},{8,0},{12,4},{16,24},{20,28},{24,16},{28,20},{1,9},{5... | collective-permute-start | bytes 393224 | tf_op jit(solution)/shard_map/ppermute | solution.py:267
  73.1 9.2 %collective-permute-start.17 = (bf16[2,256,128]{2,1,0:T(8,128)(2,1)S(1)}, bf16[2,256,128]{2,1,0:T(8,128)(2,1)S(1)}, u32[]{:S(2)}, u32[]{:S(2)}) collective-permute-start(bf16[2,256,128]{2,1,0:T(8,128)(2,1)S(1)} %collective-permute-done.13.refs_4_), channel_id=1, source_target_pairs={{0,4},{4,0},{8,12},{12,8},{16,20},{20,16},{24,28},{28,24},{1,5},{5... | collective-permute-start | bytes 393224 | tf_op jit(solution)/shard_map/ppermute | solution.py:267
  75.0 7.3 %collective-permute-start.16 = (bf16[2,256,128]{2,1,0:T(8,128)(2,1)S(1)}, bf16[2,256,128]{2,1,0:T(8,128)(2,1)S(1)}, u32[]{:S(2)}, u32[]{:S(2)}) collective-permute-start(bf16[2,256,128]{2,1,0:T(8,128)(2,1)S(1)} %collective-permute-done.15.refs_2_), channel_id=1, source_target_pairs={{0,4},{4,0},{8,12},{12,8},{16,20},{20,16},{24,28},{28,24},{1,5},{5... | collective-permute-start | bytes 393224 | tf_op jit(solution)/shard_map/ppermute | solution.py:267
  78.5 5.7 %collective-permute-start.19 = (bf16[2,256,128]{2,1,0:T(8,128)(2,1)S(1)}, bf16[2,256,128]{2,1,0:T(8,128)(2,1)S(1)}, u32[]{:S(2)}, u32[]{:S(2)}) collective-permute-start(bf16[2,256,128]{2,1,0:T(8,128)(2,1)S(1)} %collective-permute-done.18.refs_6_), channel_id=1, source_target_pairs={{0,4},{4,0},{8,12},{12,8},{16,20},{20,16},{24,28},{28,24},{1,5},{5... | collective-permute-start | bytes 393224 | tf_op jit(solution)/shard_map/ppermute | solution.py:267

commit v4 on v1

--- a/solution.py
+++ b/solution.py
@@ -275,10 +275,12 @@
 def gather_pieces(array, peers):
     out = {0: array, 4: swap(array, "dom", 4), 2: swap(array, "dom", 2)}
     out[1] = swap(array, "dom", 1)
+    out[3] = swap(out[2], "dom", 1)
     out[4], out[1] = lax.optimization_barrier((out[4], out[1]))
     out[6] = swap(out[4], "dom", 2)
-    for offset in range(2, peers, 2):
-        out[offset + 1] = swap(out[offset], "dom", 1)
+    late, out[3] = lax.optimization_barrier((out[4], out[3]))
+    out[5] = swap(late, "dom", 1)
+    out[7] = swap(out[6], "dom", 1)
     return [out[offset] for offset in range(peers)]
 
 
@@ -363,7 +365,8 @@
             flops=2_000_000, moved=1_300_000,
         )
         grad_full = gather_columns(grad_pre)
-        halves = gather_columns(swap(half, "dom", 1))
+        half = swap(half, "dom", 1)
+        halves = [half] + [swap(half, "rep", offset) for offset in (1, 2, 3)]
     else:
         recv = lax.all_to_all(parts[0], "rep", split_axis=0, concat_axis=0, tiled=True)
         hidden, grad_pre = call(

time: 80.6 us -> 80.7 us (level)
  starting transfers between devices: 31.1 us -> 34.9 us
  waiting for transfers between devices: 36.5 us -> 32.8 us
    ppermute x20, starting transfers between devices: 20 us -> 23.8 us  [swap(): lax.ppermute(array, axis, [(i, i ^ offset) for i in range(lax.axis_size(a...]
    ppermute x20, waiting for transfers between devices: 35.2 us -> 31.5 us  [swap(): lax.ppermute(array, axis, [(i, i ^ offset) for i in range(lax.axis_size(a...]
  transfers between devices with their start and end apart: 22 -> 22, of which waited for: 13 -> 16; matrix products, arithmetic and copies ran while one was open for 0% -> 0% of each run, Pallas kernels for 4% -> 4%
where the time goes in v4:
time: 80.7 us; the launch traced here: 80.3 us
  starting transfers between devices  34.9 us (43%)
  waiting for transfers between devices  32.8 us (41%)
  Pallas kernels  9.18 us (11%)
  local copies, waits for them, and re-layouts  2.68 us (3%)
    ppermute x20, waiting for transfers between devices, swap(): lax.ppermute(array, axis, [(i, i ^ offset) for i in range(lax.axis_size(a...  31.5 us
    ppermute x20, starting transfers between devices, swap(): lax.ppermute(array, axis, [(i, i ^ offset) for i in range(lax.axis_size(a...  23.8 us
    all_to_all x2, starting transfers between devices, exchange(): lax.all_to_all(array.reshape(peers, slots, cols), 'dom', split_axis=0, co...  11.1 us
    pallas_call x11, Pallas kernels, call(): pl.pallas_call(body, out_shape=outs, in_specs=[SPECS[spec] for spec, _ in...  9.18 us
    unnamed x16, local copies, waits for them, and re-layouts  2.68 us
  transfers between devices with their start and end apart: 22, of which 16 were waited for; matrix products, arithmetic and copies ran while one was open for 0% of the time, Pallas kernels for 4%

profile of v4, /device:TPU:0, one launch (start us, length us, event | category | flops | bytes accessed | tf_op | source)
XLA Modules:
  0.0 80.3 jit_solution(4317028910547828527)
XLA Ops:
  0.6 2.1 %shard_map.120 = (bf16[256,512]{1,0:T(8,128)(2,1)}, bf16[512,256]{1,0:T(8,128)(2,1)}) custom-call(s32[8]{0:T(128)} %count_hbm.1, s32[8,64]{1,0:T(8,128)} %list_hbm.1, bf16[256,256]{1,0:T(8,128)(2,1)} %refs_0_.1), custom_call_target="tpu_custom_call" | custom-call | flops 67108864 | bytes 600000 | tf_op jit(solution)/shard_map/pallas_call | solution.py:22
  2.8 7.4 %all-to-all-start = ((bf16[8,64,256]{2,1,0:T(8,128)(2,1)}), bf16[8,64,256]{2,1,0:T(8,128)(2,1)S(1)}, u32[]{:S(2)}, u32[]{:S(2)}) async-start(bf16[8,64,256]{2,1,0:T(8,128)(2,1)} %bitcast.8), calls=%async_computation | async-start | bytes 524288 | tf_op jit(solution)/shard_map/all_to_all | solution.py:305
  10.2 2.0 %collective-permute-start = (bf16[256,256]{1,0:T(8,128)(2,1)S(1)}, bf16[256,256]{1,0:T(8,128)(2,1)S(1)}, u32[]{:S(2)}, u32[]{:S(2)}) collective-permute-start(bf16[256,256]{1,0:T(8,128)(2,1)S(1)} %copy-done.4), channel_id=1, source_target_pairs={{0,4},{4,0},{8,12},{12,8},{16,20},{20,16},{24,28},{28,24},{1,5},{5... | collective-permute-start | bytes 393224 | tf_op jit(solution)/shard_map/ppermute | solution.py:267
  12.9 1.0 %copy-done.1 = bf16[256,1024]{1,0:T(8,128)(2,1)S(1)} copy-done((bf16[256,1024]{1,0:T(8,128)(2,1)S(1)}, bf16[256,1024]{1,0:T(8,128)(2,1)}, u32[]{:S(2)}) %copy-start.1) | copy-done | bytes 524312
  14.0 0.9 %copy-done.3 = bf16[8,128,128]{2,1,0:T(8,128)(2,1)S(1)} copy-done((bf16[8,128,128]{2,1,0:T(8,128)(2,1)S(1)}, bf16[8,128,128]{2,1,0:T(8,128)(2,1)}, u32[]{:S(2)}) %copy-start.3) | copy-done | bytes 262168
  14.9 0.9 %shard_map.121 = (bf16[256,768]{1,0:T(8,128)(2,1)S(1)}, bf16[256,768]{1,0:T(8,128)(2,1)S(1)}, f32[256,128]{1,0:T(8,128)S(1)}, bf16[256,1024]{1,0:T(8,128)(2,1)S(1)}, bf16[256,1024]{1,0:T(8,128)(2,1)S(1)}) custom-call(s32[8]{0:T(128)S(1)} %copy-done.6, s32[8]{0:T(128)S(1)} %copy-done.7, bf16[8,128,128]{2,1,0:T(8,128)(2,1)S(1)} %copy-done.3, ...), custom_call_target="tpu_custom_call" | custom-call | flops 1000000 | bytes 3000000 | tf_op jit(solution)/shard_map/pallas_call | solution.py:22
  15.9 2.0 %collective-permute-done.refs_1_ = bf16[256,256]{1,0:T(8,128)(2,1)S(1)} collective-permute-done((bf16[256,256]{1,0:T(8,128)(2,1)S(1)}, bf16[256,256]{1,0:T(8,128)(2,1)S(1)}, u32[]{:S(2)}, u32[]{:S(2)}) %collective-permute-start) | collective-permute-done | bytes 131104 | tf_op jit(solution)/shard_map/ppermute | solution.py:267
  17.8 1.3 %all-to-all-done = bf16[8,64,256]{2,1,0:T(8,128)(2,1)S(1)} async-done(((bf16[8,64,256]{2,1,0:T(8,128)(2,1)}), bf16[8,64,256]{2,1,0:T(8,128)(2,1)S(1)}, u32[]{:S(2)}, u32[]{:S(2)}) %all-to-all-start) | async-done | bytes 262176 | tf_op jit(solution)/shard_map/all_to_all | solution.py:305
  19.1 1.0 %shard_map.122 = (f32[256,256]{1,0:T(8,128)S(1)}, bf16[256,256]{1,0:T(8,128)(2,1)S(1)}, f32[256,256]{1,0:T(8,128)S(1)}, bf16[2,256,256]{2,1,0:T(8,128)(2,1)S(1)}) custom-call(s32[1]{0:T(128)} %bitcast.1.rep_ref, bf16[256,256]{1,0:T(8,128)(2,1)S(1)} %copy-done.4, bf16[512,256]{1,0:T(8,128)(2,1)S(1)} %bitcast.7, ...), custom_call_target="tpu_custom_call" | custom-call | flops 600000000 | bytes 3000000 | tf_op jit(solution)/shard_map/pallas_call | solution.py:22
  20.2 1.5 %collective-permute-start.1 = (bf16[256,256]{1,0:T(8,128)(2,1)S(1)}, bf16[256,256]{1,0:T(8,128)(2,1)S(1)}, u32[]{:S(2)}, u32[]{:S(2)}) collective-permute-start(bf16[256,256]{1,0:T(8,128)(2,1)S(1)} %get-tuple-element.49.refs_2_), channel_id=1, source_target_pairs={{0,4},{4,0},{8,12},{12,8},{16,20},{20,16},{24,28},{28,24},{1,5},{5... | collective-permute-start | bytes 393224 | tf_op jit(solution)/shard_map/ppermute | solution.py:267
  21.7 1.6 %collective-permute-start.3 = (bf16[256,256]{1,0:T(8,128)(2,1)S(1)}, bf16[256,256]{1,0:T(8,128)(2,1)S(1)}, u32[]{:S(2)}, u32[]{:S(2)}) collective-permute-start(bf16[256,256]{1,0:T(8,128)(2,1)S(1)} %shard_map.123), channel_id=1, source_target_pairs={{0,2},{1,3},{2,0},{3,1},{4,6},{5,7},{6,4},{7,5},{8,10},{9,11},{10,... | collective-permute-start | bytes 393224 | tf_op jit(solution)/shard_map/ppermute | solution.py:267
  23.3 2.8 %collective-permute-done.1.refs_3_ = bf16[256,256]{1,0:T(8,128)(2,1)S(1)} collective-permute-done((bf16[256,256]{1,0:T(8,128)(2,1)S(1)}, bf16[256,256]{1,0:T(8,128)(2,1)S(1)}, u32[]{:S(2)}, u32[]{:S(2)}) %collective-permute-start.1) | collective-permute-done | bytes 131104 | tf_op jit(solution)/shard_map/ppermute | solution.py:267
  26.1 1.2 %collective-permute-done.3.across_ref = bf16[256,256]{1,0:T(8,128)(2,1)S(1)} collective-permute-done((bf16[256,256]{1,0:T(8,128)(2,1)S(1)}, bf16[256,256]{1,0:T(8,128)(2,1)S(1)}, u32[]{:S(2)}, u32[]{:S(2)}) %collective-permute-start.3) | collective-permute-done | bytes 131104 | tf_op jit(solution)/shard_map/ppermute | solution.py:267
  28.1 1.5 %collective-permute-start.5 = (bf16[256,256]{1,0:T(8,128)(2,1)S(1)}, bf16[256,256]{1,0:T(8,128)(2,1)S(1)}, u32[]{:S(2)}, u32[]{:S(2)}) collective-permute-start(bf16[256,256]{1,0:T(8,128)(2,1)S(1)} %get-tuple-element.55.refs_0_.refs_4_), channel_id=1, source_target_pairs={{0,2},{1,3},{2,0},{3,1},{4,6},{5,7},{6,4},{7,5},{8,10},{9,11},{10,... | collective-permute-start | bytes 393224 | tf_op jit(solution)/shard_map/ppermute | solution.py:267
  29.6 1.4 %collective-permute-start.7 = (bf16[256,128]{1,0:T(8,128)(2,1)S(1)}, bf16[256,128]{1,0:T(8,128)(2,1)S(1)}, u32[]{:S(2)}, u32[]{:S(2)}) collective-permute-start(bf16[256,128]{1,0:T(8,128)(2,1)S(1)} %get-tuple-element.60), channel_id=1, source_target_pairs={{0,4},{4,0},{8,12},{12,8},{16,20},{20,16},{24,28},{28,24},{1,5},{5... | collective-permute-start | bytes 196616 | tf_op jit(solution)/shard_map/ppermute | solution.py:267
  31.0 2.1 %collective-permute-done.5.refs_2_.refs_6_ = bf16[256,256]{1,0:T(8,128)(2,1)S(1)} collective-permute-done((bf16[256,256]{1,0:T(8,128)(2,1)S(1)}, bf16[256,256]{1,0:T(8,128)(2,1)S(1)}, u32[]{:S(2)}, u32[]{:S(2)}) %collective-permute-start.5) | collective-permute-done | bytes 131104 | tf_op jit(solution)/shard_map/ppermute | solution.py:267
  33.9 1.2 %collective-permute-start.9 = (bf16[256,128]{1,0:T(8,128)(2,1)S(1)}, bf16[256,128]{1,0:T(8,128)(2,1)S(1)}, u32[]{:S(2)}, u32[]{:S(2)}) collective-permute-start(bf16[256,128]{1,0:T(8,128)(2,1)S(1)} %collective-permute-done.7.refs_8_), channel_id=1, source_target_pairs={{0,2},{1,3},{2,0},{3,1},{4,6},{5,7},{6,4},{7,5},{8,10},{9,11},{10,... | collective-permute-start | bytes 196616 | tf_op jit(solution)/shard_map/ppermute | solution.py:267
  35.7 3.0 %collective-permute-done.9.refs_10_ = bf16[256,128]{1,0:T(8,128)(2,1)S(1)} collective-permute-done((bf16[256,128]{1,0:T(8,128)(2,1)S(1)}, bf16[256,128]{1,0:T(8,128)(2,1)S(1)}, u32[]{:S(2)}, u32[]{:S(2)}) %collective-permute-start.9) | collective-permute-done | bytes 65568 | tf_op jit(solution)/shard_map/ppermute | solution.py:267
  40.2 1.1 %collective-permute-start.11 = (bf16[2,2,256,128]{3,2,1,0:T(8,128)(2,1)S(1)}, bf16[2,2,256,128]{3,2,1,0:T(8,128)(2,1)S(1)}, u32[]{:S(2)}, u32[]{:S(2)}) collective-permute-start(bf16[2,2,256,128]{3,2,1,0:T(8,128)(2,1)S(1)} %get-tuple-element.62), channel_id=1, source_target_pairs={{0,8},{4,12},{8,0},{12,4},{16,24},{20,28},{24,16},{28,20},{1,9},{5... | collective-permute-start | bytes 786440 | tf_op jit(solution)/shard_map/ppermute | solution.py:267
  41.3 7.3 %collective-permute-done.11.beside_ref.next_ref = bf16[2,2,256,128]{3,2,1,0:T(8,128)(2,1)S(1)} collective-permute-done((bf16[2,2,256,128]{3,2,1,0:T(8,128)(2,1)S(1)}, bf16[2,2,256,128]{3,2,1,0:T(8,128)(2,1)S(1)}, u32[]{:S(2)}, u32[]{:S(2)}) %collective-permute-start.11) | collective-permute-done | bytes 262176 | tf_op jit(solution)/shard_map/ppermute | solution.py:267
  48.7 1.5 %collective-permute-start.12 = (bf16[2,256,128]{2,1,0:T(8,128)(2,1)S(1)}, bf16[2,256,128]{2,1,0:T(8,128)(2,1)S(1)}, u32[]{:S(2)}, u32[]{:S(2)}) collective-permute-start(bf16[2,256,128]{2,1,0:T(8,128)(2,1)S(1)} %shard_map.128), channel_id=1, source_target_pairs={{0,16},{4,20},{8,24},{12,28},{16,0},{20,4},{24,8},{28,12},{1,17},{... | collective-permute-start | bytes 393224 | tf_op jit(solution)/shard_map/ppermute | solution.py:267
  50.2 1.5 %shard_map.125 = (f32[256,256]{1,0:T(8,128)S(1)}, bf16[512,256]{1,0:T(8,128)(2,1)}) custom-call(s32[1]{0:T(128)} %bitcast.1.rep_ref, bf16[256,768]{1,0:T(8,128)(2,1)S(1)} %get-tuple-element.43.high_ref, bf16[256,768]{1,0:T(8,128)(2,1)S(1)} %get-tuple-element.44.low_ref, f32[256,128]{1,0:T(8,128)S(1)} %get-tuple-element.45.deg_ref, ...), custom_call_target="tpu_custom_call" | custom-call | flops 600000000 | bytes 3000000 | tf_op jit(solution)/shard_map/pallas_call | solution.py:22
  51.7 3.6 %all-to-all-start.1 = ((bf16[8,64,256]{2,1,0:T(8,128)(2,1)}), bf16[8,64,256]{2,1,0:T(8,128)(2,1)S(1)}, u32[]{:S(2)}, u32[]{:S(2)}) async-start(bf16[8,64,256]{2,1,0:T(8,128)(2,1)} %bitcast.4), calls=%async_computation.1 | async-start | bytes 524288 | tf_op jit(solution)/shard_map/all_to_all | solution.py:305
  55.3 1.9 %collective-permute-done.12.far_ref = bf16[2,256,128]{2,1,0:T(8,128)(2,1)S(1)} collective-permute-done((bf16[2,256,128]{2,1,0:T(8,128)(2,1)S(1)}, bf16[2,256,128]{2,1,0:T(8,128)(2,1)S(1)}, u32[]{:S(2)}, u32[]{:S(2)}) %collective-permute-start.12) | collective-permute-done | bytes 131104 | tf_op jit(solution)/shard_map/ppermute | solution.py:267
  57.6 4.6 %collective-permute-start.13 = (bf16[2,256,128]{2,1,0:T(8,128)(2,1)S(1)}, bf16[2,256,128]{2,1,0:T(8,128)(2,1)S(1)}, u32[]{:S(2)}, u32[]{:S(2)}) collective-permute-start(bf16[2,256,128]{2,1,0:T(8,128)(2,1)S(1)} %shard_map.129.refs_0_), channel_id=1, source_target_pairs={{0,16},{4,20},{8,24},{12,28},{16,0},{20,4},{24,8},{28,12},{1,17},{... | collective-permute-start | bytes 393224 | tf_op jit(solution)/shard_map/ppermute | solution.py:267
  62.2 3.8 %collective-permute-done.15.refs_2_ = bf16[2,256,128]{2,1,0:T(8,128)(2,1)S(1)} collective-permute-done((bf16[2,256,128]{2,1,0:T(8,128)(2,1)S(1)}, bf16[2,256,128]{2,1,0:T(8,128)(2,1)S(1)}, u32[]{:S(2)}, u32[]{:S(2)}) %collective-permute-start.15) | collective-permute-done | bytes 131104 | tf_op jit(solution)/shard_map/ppermute | solution.py:267
  66.0 3.0 %collective-permute-start.16 = (bf16[2,256,128]{2,1,0:T(8,128)(2,1)S(1)}, bf16[2,256,128]{2,1,0:T(8,128)(2,1)S(1)}, u32[]{:S(2)}, u32[]{:S(2)}) collective-permute-start(bf16[2,256,128]{2,1,0:T(8,128)(2,1)S(1)} %collective-permute-done.15.refs_2_), channel_id=1, source_target_pairs={{0,4},{4,0},{8,12},{12,8},{16,20},{20,16},{24,28},{28,24},{1,5},{5... | collective-permute-start | bytes 393224 | tf_op jit(solution)/shard_map/ppermute | solution.py:267
  69.3 2.6 %collective-permute-done.16.refs_3_ = bf16[2,256,128]{2,1,0:T(8,128)(2,1)S(1)} collective-permute-done((bf16[2,256,128]{2,1,0:T(8,128)(2,1)S(1)}, bf16[2,256,128]{2,1,0:T(8,128)(2,1)S(1)}, u32[]{:S(2)}, u32[]{:S(2)}) %collective-permute-start.16) | collective-permute-done | bytes 131104 | tf_op jit(solution)/shard_map/ppermute | solution.py:267
  71.9 2.1 %collective-permute-start.17 = (bf16[2,256,128]{2,1,0:T(8,128)(2,1)S(1)}, bf16[2,256,128]{2,1,0:T(8,128)(2,1)S(1)}, u32[]{:S(2)}, u32[]{:S(2)}) collective-permute-start(bf16[2,256,128]{2,1,0:T(8,128)(2,1)S(1)} %collective-permute-done.13.refs_4_), channel_id=1, source_target_pairs={{0,4},{4,0},{8,12},{12,8},{16,20},{20,16},{24,28},{28,24},{1,5},{5... | collective-permute-start | bytes 393224 | tf_op jit(solution)/shard_map/ppermute | solution.py:267
  74.2 1.3 %collective-permute-start.19 = (bf16[2,256,128]{2,1,0:T(8,128)(2,1)S(1)}, bf16[2,256,128]{2,1,0:T(8,128)(2,1)S(1)}, u32[]{:S(2)}, u32[]{:S(2)}) collective-permute-start(bf16[2,256,128]{2,1,0:T(8,128)(2,1)S(1)} %collective-permute-done.18.refs_6_), channel_id=1, source_target_pairs={{0,4},{4,0},{8,12},{12,8},{16,20},{20,16},{24,28},{28,24},{1,5},{5... | collective-permute-start | bytes 393224 | tf_op jit(solution)/shard_map/ppermute | solution.py:267
  77.0 2.2 %collective-permute-done.19.refs_7_ = bf16[2,256,128]{2,1,0:T(8,128)(2,1)S(1)} collective-permute-done((bf16[2,256,128]{2,1,0:T(8,128)(2,1)S(1)}, bf16[2,256,128]{2,1,0:T(8,128)(2,1)S(1)}, u32[]{:S(2)}, u32[]{:S(2)}) %collective-permute-start.19) | collective-permute-done | bytes 131104 | tf_op jit(solution)/shard_map/ppermute | solution.py:267
  79.2 1.1 %shard_map.130 = (bf16[256,1024]{1,0:T(8,128)(2,1)}, bf16[256,1024]{1,0:T(8,128)(2,1)}) custom-call(s32[1]{0:T(128)} %bitcast.dom_ref, bf16[2,256,128]{2,1,0:T(8,128)(2,1)S(1)} %shard_map.129.refs_0_, bf16[2,256,128]{2,1,0:T(8,128)(2,1)S(1)} %collective-permute-done.14.refs_1_, bf16[2,256,128]{2,1,0:T(8,128)(2,1)S(1)} %collective-permute-done.15.refs_2_, ...), custom_call_target="tpu_custom_call" | custom-call | bytes 2000000 | tf_op jit(solution)/shard_map/pallas_call | solution.py:22
  (39 shorter events, 6.8 us)
Async XLA Ops:
  0.6 11.6 %copy-start = (bf16[256,1024]{1,0:T(8,128)(2,1)S(1)}, bf16[256,1024]{1,0:T(8,128)(2,1)}, u32[]{:S(2)}) copy-start(bf16[256,1024]{1,0:T(8,128)(2,1)} %self_hbm) | copy-start | bytes 1572868
  2.8 7.4 %copy-start.4 = (bf16[256,256]{1,0:T(8,128)(2,1)S(1)}, bf16[256,256]{1,0:T(8,128)(2,1)}, u32[]{:S(2)}) copy-start(bf16[256,256]{1,0:T(8,128)(2,1)} %refs_0_.1) | copy-start | bytes 393220
  2.8 16.3 %all-to-all-start = ((bf16[8,64,256]{2,1,0:T(8,128)(2,1)}), bf16[8,64,256]{2,1,0:T(8,128)(2,1)S(1)}, u32[]{:S(2)}, u32[]{:S(2)}) async-start(bf16[8,64,256]{2,1,0:T(8,128)(2,1)} %bitcast.8), calls=%async_computation | async-start | bytes 524288 | tf_op jit(solution)/shard_map/all_to_all | solution.py:305
  10.2 7.6 %collective-permute-start = (bf16[256,256]{1,0:T(8,128)(2,1)S(1)}, bf16[256,256]{1,0:T(8,128)(2,1)S(1)}, u32[]{:S(2)}, u32[]{:S(2)}) collective-permute-start(bf16[256,256]{1,0:T(8,128)(2,1)S(1)} %copy-done.4), channel_id=1, source_target_pairs={{0,4},{4,0},{8,12},{12,8},{16,20},{20,16},{24,28},{28,24},{1,5},{5... | collective-permute-start | bytes 393224 | tf_op jit(solution)/shard_map/ppermute | solution.py:267
  12.2 0.7 copy-start.6
  12.2 0.7 copy-start.7
  12.9 1.0 %copy-start.1 = (bf16[256,1024]{1,0:T(8,128)(2,1)S(1)}, bf16[256,1024]{1,0:T(8,128)(2,1)}, u32[]{:S(2)}) copy-start(bf16[256,1024]{1,0:T(8,128)(2,1)} %neigh_hbm) | copy-start | bytes 1572868
  14.0 0.9 %copy-start.3 = (bf16[8,128,128]{2,1,0:T(8,128)(2,1)S(1)}, bf16[8,128,128]{2,1,0:T(8,128)(2,1)}, u32[]{:S(2)}) copy-start(bf16[8,128,128]{2,1,0:T(8,128)(2,1)} %tiles_ref) | copy-start | bytes 786436
  20.1 1.6 %collective-permute-start.2 = (bf16[2,256,256]{2,1,0:T(8,128)(2,1)S(1)}, bf16[2,256,256]{2,1,0:T(8,128)(2,1)S(1)}, u32[]{:S(2)}, u32[]{:S(2)}) collective-permute-start(bf16[2,256,256]{2,1,0:T(8,128)(2,1)S(1)} %get-tuple-element.51), channel_id=1, source_target_pairs={{0,1},{1,0},{2,3},{3,2},{4,5},{5,4},{6,7},{7,6},{8,9},{9,8},{10,11... | collective-permute-start | bytes 786440 | tf_op jit(solution)/shard_map/ppermute | solution.py:267
  20.2 5.9 %collective-permute-start.1 = (bf16[256,256]{1,0:T(8,128)(2,1)S(1)}, bf16[256,256]{1,0:T(8,128)(2,1)S(1)}, u32[]{:S(2)}, u32[]{:S(2)}) collective-permute-start(bf16[256,256]{1,0:T(8,128)(2,1)S(1)} %get-tuple-element.49.refs_2_), channel_id=1, source_target_pairs={{0,4},{4,0},{8,12},{12,8},{16,20},{20,16},{24,28},{28,24},{1,5},{5... | collective-permute-start | bytes 393224 | tf_op jit(solution)/shard_map/ppermute | solution.py:267
  21.7 5.6 %copy-start.5 = (bf16[256,256]{1,0:T(8,128)(2,1)S(1)}, bf16[256,256]{1,0:T(8,128)(2,1)}, u32[]{:S(2)}) copy-start(bf16[256,256]{1,0:T(8,128)(2,1)} %gout_ref) | copy-start | bytes 393220
  21.7 5.6 %collective-permute-start.3 = (bf16[256,256]{1,0:T(8,128)(2,1)S(1)}, bf16[256,256]{1,0:T(8,128)(2,1)S(1)}, u32[]{:S(2)}, u32[]{:S(2)}) collective-permute-start(bf16[256,256]{1,0:T(8,128)(2,1)S(1)} %shard_map.123), channel_id=1, source_target_pairs={{0,2},{1,3},{2,0},{3,1},{4,6},{5,7},{6,4},{7,5},{8,10},{9,11},{10,... | collective-permute-start | bytes 393224 | tf_op jit(solution)/shard_map/ppermute | solution.py:267
  28.1 5.0 %collective-permute-start.5 = (bf16[256,256]{1,0:T(8,128)(2,1)S(1)}, bf16[256,256]{1,0:T(8,128)(2,1)S(1)}, u32[]{:S(2)}, u32[]{:S(2)}) collective-permute-start(bf16[256,256]{1,0:T(8,128)(2,1)S(1)} %get-tuple-element.55.refs_0_.refs_4_), channel_id=1, source_target_pairs={{0,2},{1,3},{2,0},{3,1},{4,6},{5,7},{6,4},{7,5},{8,10},{9,11},{10,... | collective-permute-start | bytes 393224 | tf_op jit(solution)/shard_map/ppermute | solution.py:267
  29.6 4.3 %collective-permute-start.7 = (bf16[256,128]{1,0:T(8,128)(2,1)S(1)}, bf16[256,128]{1,0:T(8,128)(2,1)S(1)}, u32[]{:S(2)}, u32[]{:S(2)}) collective-permute-start(bf16[256,128]{1,0:T(8,128)(2,1)S(1)} %get-tuple-element.60), channel_id=1, source_target_pairs={{0,4},{4,0},{8,12},{12,8},{16,20},{20,16},{24,28},{28,24},{1,5},{5... | collective-permute-start | bytes 196616 | tf_op jit(solution)/shard_map/ppermute | solution.py:267
  31.0 4.7 %collective-permute-start.4 = (bf16[256,256]{1,0:T(8,128)(2,1)S(1)}, bf16[256,256]{1,0:T(8,128)(2,1)S(1)}, u32[]{:S(2)}, u32[]{:S(2)}) collective-permute-start(bf16[256,256]{1,0:T(8,128)(2,1)S(1)} %get-tuple-element.55.refs_0_.refs_4_), channel_id=1, source_target_pairs={{0,1},{1,0},{2,3},{3,2},{4,5},{5,4},{6,7},{7,6},{8,9},{9,8},{10,11... | collective-permute-start | bytes 393224 | tf_op jit(solution)/shard_map/ppermute | solution.py:267
  33.1 6.3 %collective-permute-start.6 = (bf16[256,256]{1,0:T(8,128)(2,1)S(1)}, bf16[256,256]{1,0:T(8,128)(2,1)S(1)}, u32[]{:S(2)}, u32[]{:S(2)}) collective-permute-start(bf16[256,256]{1,0:T(8,128)(2,1)S(1)} %collective-permute-done.5.refs_2_.refs_6_), channel_id=1, source_target_pairs={{0,1},{1,0},{2,3},{3,2},{4,5},{5,4},{6,7},{7,6},{8,9},{9,8},{10,11... | collective-permute-start | bytes 393224 | tf_op jit(solution)/shard_map/ppermute | solution.py:267
  33.9 1.9 %collective-permute-start.8 = (bf16[256,128]{1,0:T(8,128)(2,1)S(1)}, bf16[256,128]{1,0:T(8,128)(2,1)S(1)}, u32[]{:S(2)}, u32[]{:S(2)}) collective-permute-start(bf16[256,128]{1,0:T(8,128)(2,1)S(1)} %collective-permute-done.7.refs_8_), channel_id=1, source_target_pairs={{0,1},{1,0},{2,3},{3,2},{4,5},{5,4},{6,7},{7,6},{8,9},{9,8},{10,11... | collective-permute-start | bytes 196616 | tf_op jit(solution)/shard_map/ppermute | solution.py:267
  33.9 4.9 %collective-permute-start.9 = (bf16[256,128]{1,0:T(8,128)(2,1)S(1)}, bf16[256,128]{1,0:T(8,128)(2,1)S(1)}, u32[]{:S(2)}, u32[]{:S(2)}) collective-permute-start(bf16[256,128]{1,0:T(8,128)(2,1)S(1)} %collective-permute-done.7.refs_8_), channel_id=1, source_target_pairs={{0,2},{1,3},{2,0},{3,1},{4,6},{5,7},{6,4},{7,5},{8,10},{9,11},{10,... | collective-permute-start | bytes 196616 | tf_op jit(solution)/shard_map/ppermute | solution.py:267
  35.1 4.3 %collective-permute-start.10 = (bf16[256,128]{1,0:T(8,128)(2,1)S(1)}, bf16[256,128]{1,0:T(8,128)(2,1)S(1)}, u32[]{:S(2)}, u32[]{:S(2)}) collective-permute-start(bf16[256,128]{1,0:T(8,128)(2,1)S(1)} %collective-permute-done.7.refs_8_), channel_id=1, source_target_pairs={{0,3},{1,2},{2,1},{3,0},{4,7},{5,6},{6,5},{7,4},{8,11},{9,10},{10,... | collective-permute-start | bytes 196616 | tf_op jit(solution)/shard_map/ppermute | solution.py:267
  40.2 8.5 %collective-permute-start.11 = (bf16[2,2,256,128]{3,2,1,0:T(8,128)(2,1)S(1)}, bf16[2,2,256,128]{3,2,1,0:T(8,128)(2,1)S(1)}, u32[]{:S(2)}, u32[]{:S(2)}) collective-permute-start(bf16[2,2,256,128]{3,2,1,0:T(8,128)(2,1)S(1)} %get-tuple-element.62), channel_id=1, source_target_pairs={{0,8},{4,12},{8,0},{12,4},{16,24},{20,28},{24,16},{28,20},{1,9},{5... | collective-permute-start | bytes 786440 | tf_op jit(solution)/shard_map/ppermute | solution.py:267
  48.7 8.6 %collective-permute-start.12 = (bf16[2,256,128]{2,1,0:T(8,128)(2,1)S(1)}, bf16[2,256,128]{2,1,0:T(8,128)(2,1)S(1)}, u32[]{:S(2)}, u32[]{:S(2)}) collective-permute-start(bf16[2,256,128]{2,1,0:T(8,128)(2,1)S(1)} %shard_map.128), channel_id=1, source_target_pairs={{0,16},{4,20},{8,24},{12,28},{16,0},{20,4},{24,8},{28,12},{1,17},{... | collective-permute-start | bytes 393224 | tf_op jit(solution)/shard_map/ppermute | solution.py:267
  51.7 23.9 %all-to-all-start.1 = ((bf16[8,64,256]{2,1,0:T(8,128)(2,1)}), bf16[8,64,256]{2,1,0:T(8,128)(2,1)S(1)}, u32[]{:S(2)}, u32[]{:S(2)}) async-start(bf16[8,64,256]{2,1,0:T(8,128)(2,1)} %bitcast.4), calls=%async_computation.1 | async-start | bytes 524288 | tf_op jit(solution)/shard_map/all_to_all | solution.py:305
  57.2 18.3 %copy-start.2 = (bf16[256,512]{1,0:T(8,128)(2,1)S(1)}, bf16[256,512]{1,0:T(8,128)(2,1)}, u32[]{:S(2)}) copy-start(bf16[256,512]{1,0:T(8,128)(2,1)} %get-tuple-element.54.onehot_ref) | copy-start | bytes 786436
  57.3 8.7 %collective-permute-start.15 = (bf16[2,256,128]{2,1,0:T(8,128)(2,1)S(1)}, bf16[2,256,128]{2,1,0:T(8,128)(2,1)S(1)}, u32[]{:S(2)}, u32[]{:S(2)}) collective-permute-start(bf16[2,256,128]{2,1,0:T(8,128)(2,1)S(1)} %shard_map.129.refs_0_), channel_id=1, source_target_pairs={{0,8},{4,12},{8,0},{12,4},{16,24},{20,28},{24,16},{28,20},{1,9},{5... | collective-permute-start | bytes 393224 | tf_op jit(solution)/shard_map/ppermute | solution.py:267
  57.6 11.7 %collective-permute-start.13 = (bf16[2,256,128]{2,1,0:T(8,128)(2,1)S(1)}, bf16[2,256,128]{2,1,0:T(8,128)(2,1)S(1)}, u32[]{:S(2)}, u32[]{:S(2)}) collective-permute-start(bf16[2,256,128]{2,1,0:T(8,128)(2,1)S(1)} %shard_map.129.refs_0_), channel_id=1, source_target_pairs={{0,16},{4,20},{8,24},{12,28},{16,0},{20,4},{24,8},{28,12},{1,17},{... | collective-permute-start | bytes 393224 | tf_op jit(solution)/shard_map/ppermute | solution.py:267
  62.2 7.1 %collective-permute-start.14 = (bf16[2,256,128]{2,1,0:T(8,128)(2,1)S(1)}, bf16[2,256,128]{2,1,0:T(8,128)(2,1)S(1)}, u32[]{:S(2)}, u32[]{:S(2)}) collective-permute-start(bf16[2,256,128]{2,1,0:T(8,128)(2,1)S(1)} %shard_map.129.refs_0_), channel_id=1, source_target_pairs={{0,4},{4,0},{8,12},{12,8},{16,20},{20,16},{24,28},{28,24},{1,5},{5... | collective-permute-start | bytes 393224 | tf_op jit(solution)/shard_map/ppermute | solution.py:267
  66.0 5.9 %collective-permute-start.16 = (bf16[2,256,128]{2,1,0:T(8,128)(2,1)S(1)}, bf16[2,256,128]{2,1,0:T(8,128)(2,1)S(1)}, u32[]{:S(2)}, u32[]{:S(2)}) collective-permute-start(bf16[2,256,128]{2,1,0:T(8,128)(2,1)S(1)} %collective-permute-done.15.refs_2_), channel_id=1, source_target_pairs={{0,4},{4,0},{8,12},{12,8},{16,20},{20,16},{24,28},{28,24},{1,5},{5... | collective-permute-start | bytes 393224 | tf_op jit(solution)/shard_map/ppermute | solution.py:267
  69.3 5.0 %collective-permute-start.18 = (bf16[2,256,128]{2,1,0:T(8,128)(2,1)S(1)}, bf16[2,256,128]{2,1,0:T(8,128)(2,1)S(1)}, u32[]{:S(2)}, u32[]{:S(2)}) collective-permute-start(bf16[2,256,128]{2,1,0:T(8,128)(2,1)S(1)} %collective-permute-done.13.refs_4_), channel_id=1, source_target_pairs={{0,8},{4,12},{8,0},{12,4},{16,24},{20,28},{24,16},{28,20},{1,9},{5... | collective-permute-start | bytes 393224 | tf_op jit(solution)/shard_map/ppermute | solution.py:267
  71.9 5.1 %collective-permute-start.17 = (bf16[2,256,128]{2,1,0:T(8,128)(2,1)S(1)}, bf16[2,256,128]{2,1,0:T(8,128)(2,1)S(1)}, u32[]{:S(2)}, u32[]{:S(2)}) collective-permute-start(bf16[2,256,128]{2,1,0:T(8,128)(2,1)S(1)} %collective-permute-done.13.refs_4_), channel_id=1, source_target_pairs={{0,4},{4,0},{8,12},{12,8},{16,20},{20,16},{24,28},{28,24},{1,5},{5... | collective-permute-start | bytes 393224 | tf_op jit(solution)/shard_map/ppermute | solution.py:267
  74.2 5.0 %collective-permute-start.19 = (bf16[2,256,128]{2,1,0:T(8,128)(2,1)S(1)}, bf16[2,256,128]{2,1,0:T(8,128)(2,1)S(1)}, u32[]{:S(2)}, u32[]{:S(2)}) collective-permute-start(bf16[2,256,128]{2,1,0:T(8,128)(2,1)S(1)} %collective-permute-done.18.refs_6_), channel_id=1, source_target_pairs={{0,4},{4,0},{8,12},{12,8},{16,20},{20,16},{24,28},{28,24},{1,5},{5... | collective-permute-start | bytes 393224 | tf_op jit(solution)/shard_map/ppermute | solution.py:267

commit v5 on v4

--- a/solution.py
+++ b/solution.py
@@ -69,7 +69,7 @@
 
 
 def pick_body(
-    count_hbm, list_hbm, feat_hbm, onehot_ref, out_ref, count_ref, list_ref, feat_ref, sems
+    count_hbm, list_hbm, feat_hbm, out_ref, count_ref, list_ref, feat_ref, sems
 ):
     copies = [
         pltpu.make_async_copy(src, dst, sems.at[k])
@@ -82,13 +82,12 @@
     for copy in copies:
         copy.wait()
     onehot = row_onehot(count_ref, list_ref[...], feat_ref.shape[0])
-    onehot_ref[...] = onehot
     out_ref[...] = dot(onehot, feat_ref[...], ROWS).astype(BF16)
 
 
 def prep_body(
-    dst_ref, src_ref, tiles_ref, self_hbm, neigh_hbm,
-    high_ref, low_ref, deg_ref, self_ref, neigh_ref, adj_ref, sems,
+    dst_ref, src_ref, count_ref, list_ref, tiles_ref, self_hbm, neigh_hbm,
+    onehot_ref, high_ref, low_ref, deg_ref, self_ref, neigh_ref, adj_ref, sems,
 ):
     copies = [
         pltpu.make_async_copy(src, dst, sems.at[k])
@@ -96,6 +95,7 @@
     ]
     for copy in copies:
         copy.start()
+    onehot_ref[...] = row_onehot(count_ref, list_ref[...], onehot_ref.shape[0])
     slots, side, _ = tiles_ref.shape
     adj_ref[...] = jnp.zeros(adj_ref.shape, F32)
     for t in range(slots):
@@ -268,8 +268,7 @@
 
 
 def gather_columns(array):
-    across = swap(array, "rep", 2)
-    return [array, swap(array, "rep", 1), across, swap(across, "rep", 1)]
+    return [array] + [swap(array, "rep", offset) for offset in (1, 2, 3)]
 
 
 def gather_pieces(array, peers):
@@ -306,8 +305,8 @@
             array.reshape(peers, slots, cols), "dom", split_axis=0, concat_axis=0, tiled=True
         ).reshape(mirrors, cols)
 
-    onehot, outgoing = call(
-        pick_body, (struct((rows, mirrors), BF16), mirror_out),
+    outgoing = call(
+        pick_body, mirror_out,
         [("h", mirror_count), ("h", mirror_list), ("h", features)],
         scratch=[
             pltpu.SMEM(mirror_count.shape, jnp.int32), pltpu.VMEM(mirror_list.shape, jnp.int32),
@@ -320,14 +319,16 @@
     tiles_late, feat_late, self_late, neigh_late, _ = lax.optimization_barrier(
         (tiles, features, w_self, w_neigh, outgoing)
     )
-    high, low, degree, self_near, neigh_near = call(
+    onehot, high, low, degree, self_near, neigh_near = call(
         prep_body,
         (
+            struct((rows, mirrors), BF16),
             struct((rows, table_rows), BF16), struct((rows, table_rows), BF16),
             struct((rows, 128), F32), struct(w_self.shape, BF16), struct(w_neigh.shape, BF16),
         ),
         [
-            ("s", tile_dst), ("s", tile_src), ("v", tiles_late), ("h", self_late),
+            ("s", tile_dst), ("s", tile_src), ("s", mirror_count), ("v", mirror_list),
+            ("v", tiles_late), ("h", self_late),
             ("h", neigh_late),
         ],
         scratch=[pltpu.VMEM((rows, table_rows), F32), pltpu.SemaphoreType.DMA((2,))],
@@ -365,8 +366,7 @@
             flops=2_000_000, moved=1_300_000,
         )
         grad_full = gather_columns(grad_pre)
-        half = swap(half, "dom", 1)
-        halves = [half] + [swap(half, "rep", offset) for offset in (1, 2, 3)]
+        halves = gather_columns(swap(half, "dom", 1))
     else:
         recv = lax.all_to_all(parts[0], "rep", split_axis=0, concat_axis=0, tiled=True)
         hidden, grad_pre = call(

time: 80.7 us -> 82.5 us (1.022)
  waiting for transfers between devices: 32.8 us -> 39.3 us
  starting transfers between devices: 34.9 us -> 30.2 us
  local copies, waits for them, and re-layouts: 2.68 us -> 1.73 us
  Pallas kernels: 9.18 us -> 10.1 us
    ppermute x20, waiting for transfers between devices: 31.5 us -> 38 us  [swap(): lax.ppermute(array, axis, [(i, i ^ offset) for i in range(lax.axis_size(a...]
    ppermute x20, starting transfers between devices: 23.8 us -> 18.8 us  [swap(): lax.ppermute(array, axis, [(i, i ^ offset) for i in range(lax.axis_size(a...]
    unnamed x16 -> x18, local copies, waits for them, and re-layouts: 2.68 us -> 1.73 us
    pallas_call x11, Pallas kernels: 9.18 us -> 10.1 us  [call(): pl.pallas_call(body, out_shape=outs, in_specs=[SPECS[spec] for spec, _ in...]
where the time goes in v5:
time: 82.5 us; the launch traced here: 82.1 us
  waiting for transfers between devices  39.3 us (48%)
  starting transfers between devices  30.2 us (37%)
  Pallas kernels  10.1 us (12%)
  local copies, waits for them, and re-layouts  1.73 us (2%)
    ppermute x20, waiting for transfers between devices, swap(): lax.ppermute(array, axis, [(i, i ^ offset) for i in range(lax.axis_size(a...  38 us
    ppermute x20, starting transfers between devices, swap(): lax.ppermute(array, axis, [(i, i ^ offset) for i in range(lax.axis_size(a...  18.8 us
    all_to_all x2, starting transfers between devices, exchange(): lax.all_to_all(array.reshape(peers, slots, cols), 'dom', split_axis=0, co...  11.4 us
    pallas_call x11, Pallas kernels, call(): pl.pallas_call(body, out_shape=outs, in_specs=[SPECS[spec] for spec, _ in...  10.1 us
    unnamed x18, local copies, waits for them, and re-layouts  1.73 us
  transfers between devices with their start and end apart: 22, of which 16 were waited for; matrix products, arithmetic and copies ran while one was open for 0% of the time, Pallas kernels for 4%

profile of v5, /device:TPU:0, one launch (start us, length us, event | category | flops | bytes accessed | tf_op | source)
XLA Modules:
  0.0 82.1 jit_solution(974067972991065209)
XLA Ops:
  0.6 2.1 %shard_map.120 = bf16[512,256]{1,0:T(8,128)(2,1)} custom-call(s32[8]{0:T(128)} %count_ref.1, s32[8,64]{1,0:T(8,128)} %list_ref.1, bf16[256,256]{1,0:T(8,128)(2,1)} %refs_0_.1), custom_call_target="tpu_custom_call" | custom-call | flops 67108864 | bytes 600000 | tf_op jit(solution)/shard_map/pallas_call | solution.py:22
  2.8 7.4 %all-to-all-start = ((bf16[8,64,256]{2,1,0:T(8,128)(2,1)}), bf16[8,64,256]{2,1,0:T(8,128)(2,1)S(1)}, u32[]{:S(2)}, u32[]{:S(2)}) async-start(bf16[8,64,256]{2,1,0:T(8,128)(2,1)} %bitcast.8), calls=%async_computation | async-start | bytes 524288 | tf_op jit(solution)/shard_map/all_to_all | solution.py:304
  10.2 2.1 %collective-permute-start = (bf16[256,256]{1,0:T(8,128)(2,1)S(1)}, bf16[256,256]{1,0:T(8,128)(2,1)S(1)}, u32[]{:S(2)}, u32[]{:S(2)}) collective-permute-start(bf16[256,256]{1,0:T(8,128)(2,1)S(1)} %copy-done), channel_id=1, source_target_pairs={{0,4},{4,0},{8,12},{12,8},{16,20},{20,16},{24,28},{28,24},{1,5},{5... | collective-permute-start | bytes 393224 | tf_op jit(solution)/shard_map/ppermute | solution.py:267
  15.0 2.8 %collective-permute-done.refs_1_ = bf16[256,256]{1,0:T(8,128)(2,1)S(1)} collective-permute-done((bf16[256,256]{1,0:T(8,128)(2,1)S(1)}, bf16[256,256]{1,0:T(8,128)(2,1)S(1)}, u32[]{:S(2)}, u32[]{:S(2)}) %collective-permute-start) | collective-permute-done | bytes 131104 | tf_op jit(solution)/shard_map/ppermute | solution.py:267
  17.8 1.3 %all-to-all-done = bf16[8,64,256]{2,1,0:T(8,128)(2,1)S(1)} async-done(((bf16[8,64,256]{2,1,0:T(8,128)(2,1)}), bf16[8,64,256]{2,1,0:T(8,128)(2,1)S(1)}, u32[]{:S(2)}, u32[]{:S(2)}) %all-to-all-start) | async-done | bytes 262176 | tf_op jit(solution)/shard_map/all_to_all | solution.py:304
  20.2 1.5 %collective-permute-start.1 = (bf16[256,256]{1,0:T(8,128)(2,1)S(1)}, bf16[256,256]{1,0:T(8,128)(2,1)}, u32[]{:S(2)}, u32[]{:S(2)}) collective-permute-start(bf16[256,256]{1,0:T(8,128)(2,1)S(1)} %get-tuple-element.47.refs_2_), channel_id=1, source_target_pairs={{0,4},{4,0},{8,12},{12,8},{16,20},{20,16},{24,28},{28,24},{1,5},{5... | collective-permute-start | bytes 393224 | tf_op jit(solution)/shard_map/ppermute | solution.py:267
  21.8 1.6 %collective-permute-start.3 = (bf16[256,256]{1,0:T(8,128)(2,1)S(1)}, bf16[256,256]{1,0:T(8,128)(2,1)S(1)}, u32[]{:S(2)}, u32[]{:S(2)}) collective-permute-start(bf16[256,256]{1,0:T(8,128)(2,1)S(1)} %shard_map.123), channel_id=1, source_target_pairs={{0,2},{1,3},{2,0},{3,1},{4,6},{5,7},{6,4},{7,5},{8,10},{9,11},{10,... | collective-permute-start | bytes 393224 | tf_op jit(solution)/shard_map/ppermute | solution.py:267
  23.3 2.9 %collective-permute-done.1.refs_3_ = bf16[256,256]{1,0:T(8,128)(2,1)} collective-permute-done((bf16[256,256]{1,0:T(8,128)(2,1)S(1)}, bf16[256,256]{1,0:T(8,128)(2,1)}, u32[]{:S(2)}, u32[]{:S(2)}) %collective-permute-start.1) | collective-permute-done | bytes 131104 | tf_op jit(solution)/shard_map/ppermute | solution.py:267
  26.2 1.1 %collective-permute-done.3.across_ref = bf16[256,256]{1,0:T(8,128)(2,1)S(1)} collective-permute-done((bf16[256,256]{1,0:T(8,128)(2,1)S(1)}, bf16[256,256]{1,0:T(8,128)(2,1)S(1)}, u32[]{:S(2)}, u32[]{:S(2)}) %collective-permute-start.3) | collective-permute-done | bytes 131104 | tf_op jit(solution)/shard_map/ppermute | solution.py:267
  28.1 1.4 %collective-permute-start.7 = (bf16[256,128]{1,0:T(8,128)(2,1)S(1)}, bf16[256,128]{1,0:T(8,128)(2,1)S(1)}, u32[]{:S(2)}, u32[]{:S(2)}) collective-permute-start(bf16[256,128]{1,0:T(8,128)(2,1)S(1)} %get-tuple-element.58), channel_id=1, source_target_pairs={{0,4},{4,0},{8,12},{12,8},{16,20},{20,16},{24,28},{28,24},{1,5},{5... | collective-permute-start | bytes 196616 | tf_op jit(solution)/shard_map/ppermute | solution.py:267
  29.5 1.5 %collective-permute-start.5 = (bf16[256,256]{1,0:T(8,128)(2,1)S(1)}, bf16[256,256]{1,0:T(8,128)(2,1)S(1)}, u32[]{:S(2)}, u32[]{:S(2)}) collective-permute-start(bf16[256,256]{1,0:T(8,128)(2,1)S(1)} %get-tuple-element.53.refs_0_.refs_4_), channel_id=1, source_target_pairs={{0,2},{1,3},{2,0},{3,1},{4,6},{5,7},{6,4},{7,5},{8,10},{9,11},{10,... | collective-permute-start | bytes 393224 | tf_op jit(solution)/shard_map/ppermute | solution.py:267
  31.1 1.5 %collective-permute-done.7.refs_8_ = bf16[256,128]{1,0:T(8,128)(2,1)S(1)} collective-permute-done((bf16[256,128]{1,0:T(8,128)(2,1)S(1)}, bf16[256,128]{1,0:T(8,128)(2,1)S(1)}, u32[]{:S(2)}, u32[]{:S(2)}) %collective-permute-start.7) | collective-permute-done | bytes 65568 | tf_op jit(solution)/shard_map/ppermute | solution.py:267
  32.6 1.5 %collective-permute-start.9 = (bf16[256,128]{1,0:T(8,128)(2,1)S(1)}, bf16[256,128]{1,0:T(8,128)(2,1)S(1)}, u32[]{:S(2)}, u32[]{:S(2)}) collective-permute-start(bf16[256,128]{1,0:T(8,128)(2,1)S(1)} %collective-permute-done.7.refs_8_), channel_id=1, source_target_pairs={{0,2},{1,3},{2,0},{3,1},{4,6},{5,7},{6,4},{7,5},{8,10},{9,11},{10,... | collective-permute-start | bytes 196616 | tf_op jit(solution)/shard_map/ppermute | solution.py:267
  34.5 1.4 %collective-permute-done.5.refs_2_.refs_6_ = bf16[256,256]{1,0:T(8,128)(2,1)S(1)} collective-permute-done((bf16[256,256]{1,0:T(8,128)(2,1)S(1)}, bf16[256,256]{1,0:T(8,128)(2,1)S(1)}, u32[]{:S(2)}, u32[]{:S(2)}) %collective-permute-start.5) | collective-permute-done | bytes 131104 | tf_op jit(solution)/shard_map/ppermute | solution.py:267
  35.9 1.8 %collective-permute-done.6.refs_3_.refs_7_ = bf16[256,256]{1,0:T(8,128)(2,1)S(1)} collective-permute-done((bf16[256,256]{1,0:T(8,128)(2,1)S(1)}, bf16[256,256]{1,0:T(8,128)(2,1)S(1)}, u32[]{:S(2)}, u32[]{:S(2)}) %collective-permute-start.6) | collective-permute-done | bytes 131104 | tf_op jit(solution)/shard_map/ppermute | solution.py:267
  37.7 2.4 %collective-permute-done.9.refs_10_ = bf16[256,128]{1,0:T(8,128)(2,1)S(1)} collective-permute-done((bf16[256,128]{1,0:T(8,128)(2,1)S(1)}, bf16[256,128]{1,0:T(8,128)(2,1)S(1)}, u32[]{:S(2)}, u32[]{:S(2)}) %collective-permute-start.9) | collective-permute-done | bytes 65568 | tf_op jit(solution)/shard_map/ppermute | solution.py:267
  40.1 1.7 %shard_map.127 = (f32[2,256,128]{2,1,0:T(8,128)S(1)}, f32[2,256,128]{2,1,0:T(8,128)S(1)}, bf16[2,2,256,128]{3,2,1,0:T(8,128)(2,1)S(1)}) custom-call(s32[1]{0:T(128)} %bitcast.dom_ref, s32[1]{0:T(128)} %bitcast.1.rep_ref, bf16[256,256]{1,0:T(8,128)(2,1)S(1)} %copy-done, bf16[256,256]{1,0:T(8,128)(2,1)S(1)} %collective-permute-done.refs_1_, ...), custom_call_target="tpu_custom_call" | custom-call | flops 600000000 | bytes 3000000 | tf_op jit(solution)/shard_map/pallas_call | solution.py:22
  42.1 8.5 %collective-permute-done.11.beside_ref.next_ref = bf16[2,2,256,128]{3,2,1,0:T(8,128)(2,1)S(1)} collective-permute-done((bf16[2,2,256,128]{3,2,1,0:T(8,128)(2,1)S(1)}, bf16[2,2,256,128]{3,2,1,0:T(8,128)(2,1)S(1)}, u32[]{:S(2)}, u32[]{:S(2)}) %collective-permute-start.11) | collective-permute-done | bytes 262176 | tf_op jit(solution)/shard_map/ppermute | solution.py:267
  51.4 1.5 %shard_map.125 = (f32[256,256]{1,0:T(8,128)S(1)}, bf16[512,256]{1,0:T(8,128)(2,1)}) custom-call(s32[1]{0:T(128)} %bitcast.1.rep_ref, bf16[256,768]{1,0:T(8,128)(2,1)S(1)} %get-tuple-element.41.high_ref, bf16[256,768]{1,0:T(8,128)(2,1)S(1)} %get-tuple-element.42.low_ref, f32[256,128]{1,0:T(8,128)S(1)} %get-tuple-element.43.deg_ref, ...), custom_call_target="tpu_custom_call" | custom-call | flops 600000000 | bytes 3000000 | tf_op jit(solution)/shard_map/pallas_call | solution.py:22
  53.0 4.0 %all-to-all-start.1 = ((bf16[8,64,256]{2,1,0:T(8,128)(2,1)}), bf16[8,64,256]{2,1,0:T(8,128)(2,1)S(1)}, u32[]{:S(2)}, u32[]{:S(2)}) async-start(bf16[8,64,256]{2,1,0:T(8,128)(2,1)} %bitcast.4), calls=%async_computation.1 | async-start | bytes 524288 | tf_op jit(solution)/shard_map/all_to_all | solution.py:304
  56.9 2.4 %collective-permute-done.12.far_ref = bf16[2,256,128]{2,1,0:T(8,128)(2,1)S(1)} collective-permute-done((bf16[2,256,128]{2,1,0:T(8,128)(2,1)S(1)}, bf16[2,256,128]{2,1,0:T(8,128)(2,1)S(1)}, u32[]{:S(2)}, u32[]{:S(2)}) %collective-permute-start.12) | collective-permute-done | bytes 131104 | tf_op jit(solution)/shard_map/ppermute | solution.py:267
  59.5 2.2 %collective-permute-start.13 = (bf16[2,256,128]{2,1,0:T(8,128)(2,1)S(1)}, bf16[2,256,128]{2,1,0:T(8,128)(2,1)S(1)}, u32[]{:S(2)}, u32[]{:S(2)}) collective-permute-start(bf16[2,256,128]{2,1,0:T(8,128)(2,1)S(1)} %shard_map.129.refs_0_), channel_id=1, source_target_pairs={{0,16},{4,20},{8,24},{12,28},{16,0},{20,4},{24,8},{28,12},{1,17},{... | collective-permute-start | bytes 393224 | tf_op jit(solution)/shard_map/ppermute | solution.py:267
  61.7 1.4 %collective-permute-start.14 = (bf16[2,256,128]{2,1,0:T(8,128)(2,1)S(1)}, bf16[2,256,128]{2,1,0:T(8,128)(2,1)S(1)}, u32[]{:S(2)}, u32[]{:S(2)}) collective-permute-start(bf16[2,256,128]{2,1,0:T(8,128)(2,1)S(1)} %shard_map.129.refs_0_), channel_id=1, source_target_pairs={{0,4},{4,0},{8,12},{12,8},{16,20},{20,16},{24,28},{28,24},{1,5},{5... | collective-permute-start | bytes 393224 | tf_op jit(solution)/shard_map/ppermute | solution.py:267
  63.1 5.5 %collective-permute-done.15.refs_2_ = bf16[2,256,128]{2,1,0:T(8,128)(2,1)S(1)} collective-permute-done((bf16[2,256,128]{2,1,0:T(8,128)(2,1)S(1)}, bf16[2,256,128]{2,1,0:T(8,128)(2,1)S(1)}, u32[]{:S(2)}, u32[]{:S(2)}) %collective-permute-start.15) | collective-permute-done | bytes 131104 | tf_op jit(solution)/shard_map/ppermute | solution.py:267
  68.6 1.1 %collective-permute-start.16 = (bf16[2,256,128]{2,1,0:T(8,128)(2,1)S(1)}, bf16[2,256,128]{2,1,0:T(8,128)(2,1)S(1)}, u32[]{:S(2)}, u32[]{:S(2)}) collective-permute-start(bf16[2,256,128]{2,1,0:T(8,128)(2,1)S(1)} %collective-permute-done.15.refs_2_), channel_id=1, source_target_pairs={{0,4},{4,0},{8,12},{12,8},{16,20},{20,16},{24,28},{28,24},{1,5},{5... | collective-permute-start | bytes 393224 | tf_op jit(solution)/shard_map/ppermute | solution.py:267
  69.7 1.3 %collective-permute-done.13.refs_4_ = bf16[2,256,128]{2,1,0:T(8,128)(2,1)S(1)} collective-permute-done((bf16[2,256,128]{2,1,0:T(8,128)(2,1)S(1)}, bf16[2,256,128]{2,1,0:T(8,128)(2,1)S(1)}, u32[]{:S(2)}, u32[]{:S(2)}) %collective-permute-start.13) | collective-permute-done | bytes 131104 | tf_op jit(solution)/shard_map/ppermute | solution.py:267
  71.2 2.4 %collective-permute-done.16.refs_3_ = bf16[2,256,128]{2,1,0:T(8,128)(2,1)S(1)} collective-permute-done((bf16[2,256,128]{2,1,0:T(8,128)(2,1)S(1)}, bf16[2,256,128]{2,1,0:T(8,128)(2,1)S(1)}, u32[]{:S(2)}, u32[]{:S(2)}) %collective-permute-start.16) | collective-permute-done | bytes 131104 | tf_op jit(solution)/shard_map/ppermute | solution.py:267
  73.6 1.1 %collective-permute-start.17 = (bf16[2,256,128]{2,1,0:T(8,128)(2,1)S(1)}, bf16[2,256,128]{2,1,0:T(8,128)(2,1)S(1)}, u32[]{:S(2)}, u32[]{:S(2)}) collective-permute-start(bf16[2,256,128]{2,1,0:T(8,128)(2,1)S(1)} %collective-permute-done.13.refs_4_), channel_id=1, source_target_pairs={{0,4},{4,0},{8,12},{12,8},{16,20},{20,16},{24,28},{28,24},{1,5},{5... | collective-permute-start | bytes 393224 | tf_op jit(solution)/shard_map/ppermute | solution.py:267
  74.7 1.4 %collective-permute-done.18.refs_6_ = bf16[2,256,128]{2,1,0:T(8,128)(2,1)S(1)} collective-permute-done((bf16[2,256,128]{2,1,0:T(8,128)(2,1)S(1)}, bf16[2,256,128]{2,1,0:T(8,128)(2,1)S(1)}, u32[]{:S(2)}, u32[]{:S(2)}) %collective-permute-start.18) | collective-permute-done | bytes 131104 | tf_op jit(solution)/shard_map/ppermute | solution.py:267
  76.1 1.5 %collective-permute-start.19 = (bf16[2,256,128]{2,1,0:T(8,128)(2,1)S(1)}, bf16[2,256,128]{2,1,0:T(8,128)(2,1)S(1)}, u32[]{:S(2)}, u32[]{:S(2)}) collective-permute-start(bf16[2,256,128]{2,1,0:T(8,128)(2,1)S(1)} %collective-permute-done.18.refs_6_), channel_id=1, source_target_pairs={{0,4},{4,0},{8,12},{12,8},{16,20},{20,16},{24,28},{28,24},{1,5},{5... | collective-permute-start | bytes 393224 | tf_op jit(solution)/shard_map/ppermute | solution.py:267
  78.6 2.5 %collective-permute-done.19.refs_7_ = bf16[2,256,128]{2,1,0:T(8,128)(2,1)S(1)} collective-permute-done((bf16[2,256,128]{2,1,0:T(8,128)(2,1)S(1)}, bf16[2,256,128]{2,1,0:T(8,128)(2,1)S(1)}, u32[]{:S(2)}, u32[]{:S(2)}) %collective-permute-start.19) | collective-permute-done | bytes 131104 | tf_op jit(solution)/shard_map/ppermute | solution.py:267
  81.0 1.1 %shard_map.130 = (bf16[256,1024]{1,0:T(8,128)(2,1)}, bf16[256,1024]{1,0:T(8,128)(2,1)}) custom-call(s32[1]{0:T(128)} %bitcast.dom_ref, bf16[2,256,128]{2,1,0:T(8,128)(2,1)S(1)} %shard_map.129.refs_0_, bf16[2,256,128]{2,1,0:T(8,128)(2,1)S(1)} %collective-permute-done.14.refs_1_, bf16[2,256,128]{2,1,0:T(8,128)(2,1)S(1)} %collective-permute-done.15.refs_2_, ...), custom_call_target="tpu_custom_call" | custom-call | bytes 2000000 | tf_op jit(solution)/shard_map/pallas_call | solution.py:22
  (41 shorter events, 7.5 us)
Async XLA Ops:
  0.6 11.7 %copy-start.1 = (bf16[256,1024]{1,0:T(8,128)(2,1)S(1)}, bf16[256,1024]{1,0:T(8,128)(2,1)}, u32[]{:S(2)}) copy-start(bf16[256,1024]{1,0:T(8,128)(2,1)} %self_hbm) | copy-start | bytes 1572868
  2.8 7.5 %copy-start = (bf16[256,256]{1,0:T(8,128)(2,1)S(1)}, bf16[256,256]{1,0:T(8,128)(2,1)}, u32[]{:S(2)}) copy-start(bf16[256,256]{1,0:T(8,128)(2,1)} %refs_0_.1) | copy-start | bytes 393220
  2.8 9.5 %copy-start.3 = (bf16[8,128,128]{2,1,0:T(8,128)(2,1)S(1)}, bf16[8,128,128]{2,1,0:T(8,128)(2,1)}, u32[]{:S(2)}) copy-start(bf16[8,128,128]{2,1,0:T(8,128)(2,1)} %tiles_ref) | copy-start | bytes 786436
  2.8 16.3 %all-to-all-start = ((bf16[8,64,256]{2,1,0:T(8,128)(2,1)}), bf16[8,64,256]{2,1,0:T(8,128)(2,1)S(1)}, u32[]{:S(2)}, u32[]{:S(2)}) async-start(bf16[8,64,256]{2,1,0:T(8,128)(2,1)} %bitcast.8), calls=%async_computation | async-start | bytes 524288 | tf_op jit(solution)/shard_map/all_to_all | solution.py:304
  10.2 2.1 %copy-start.5 = (s32[8,64]{1,0:T(8,128)S(1)}, s32[8,64]{1,0:T(8,128)}, u32[]{:S(2)}) copy-start(s32[8,64]{1,0:T(8,128)} %list_ref.1) | copy-start | bytes 6148
  10.2 7.6 %collective-permute-start = (bf16[256,256]{1,0:T(8,128)(2,1)S(1)}, bf16[256,256]{1,0:T(8,128)(2,1)S(1)}, u32[]{:S(2)}, u32[]{:S(2)}) collective-permute-start(bf16[256,256]{1,0:T(8,128)(2,1)S(1)} %copy-done), channel_id=1, source_target_pairs={{0,4},{4,0},{8,12},{12,8},{16,20},{20,16},{24,28},{28,24},{1,5},{5... | collective-permute-start | bytes 393224 | tf_op jit(solution)/shard_map/ppermute | solution.py:267
  12.3 0.7 copy-start.6
  12.3 0.7 copy-start.7
  12.3 0.7 copy-start.8
  13.0 1.0 %copy-start.2 = (bf16[256,1024]{1,0:T(8,128)(2,1)S(1)}, bf16[256,1024]{1,0:T(8,128)(2,1)}, u32[]{:S(2)}) copy-start(bf16[256,1024]{1,0:T(8,128)(2,1)} %neigh_hbm) | copy-start | bytes 1572868
  20.1 1.6 %collective-permute-start.2 = (bf16[2,256,256]{2,1,0:T(8,128)(2,1)S(1)}, bf16[2,256,256]{2,1,0:T(8,128)(2,1)S(1)}, u32[]{:S(2)}, u32[]{:S(2)}) collective-permute-start(bf16[2,256,256]{2,1,0:T(8,128)(2,1)S(1)} %get-tuple-element.49), channel_id=1, source_target_pairs={{0,1},{1,0},{2,3},{3,2},{4,5},{5,4},{6,7},{7,6},{8,9},{9,8},{10,11... | collective-permute-start | bytes 786440 | tf_op jit(solution)/shard_map/ppermute | solution.py:267
  20.2 6.0 %collective-permute-start.1 = (bf16[256,256]{1,0:T(8,128)(2,1)S(1)}, bf16[256,256]{1,0:T(8,128)(2,1)}, u32[]{:S(2)}, u32[]{:S(2)}) collective-permute-start(bf16[256,256]{1,0:T(8,128)(2,1)S(1)} %get-tuple-element.47.refs_2_), channel_id=1, source_target_pairs={{0,4},{4,0},{8,12},{12,8},{16,20},{20,16},{24,28},{28,24},{1,5},{5... | collective-permute-start | bytes 393224 | tf_op jit(solution)/shard_map/ppermute | solution.py:267
  21.7 5.6 %copy-start.4 = (bf16[256,256]{1,0:T(8,128)(2,1)S(1)}, bf16[256,256]{1,0:T(8,128)(2,1)}, u32[]{:S(2)}) copy-start(bf16[256,256]{1,0:T(8,128)(2,1)} %gout_ref) | copy-start | bytes 393220
  21.8 5.6 %collective-permute-start.3 = (bf16[256,256]{1,0:T(8,128)(2,1)S(1)}, bf16[256,256]{1,0:T(8,128)(2,1)S(1)}, u32[]{:S(2)}, u32[]{:S(2)}) collective-permute-start(bf16[256,256]{1,0:T(8,128)(2,1)S(1)} %shard_map.123), channel_id=1, source_target_pairs={{0,2},{1,3},{2,0},{3,1},{4,6},{5,7},{6,4},{7,5},{8,10},{9,11},{10,... | collective-permute-start | bytes 393224 | tf_op jit(solution)/shard_map/ppermute | solution.py:267
  28.1 6.0 %collective-permute-start.4 = (bf16[256,256]{1,0:T(8,128)(2,1)S(1)}, bf16[256,256]{1,0:T(8,128)(2,1)S(1)}, u32[]{:S(2)}, u32[]{:S(2)}) collective-permute-start(bf16[256,256]{1,0:T(8,128)(2,1)S(1)} %get-tuple-element.53.refs_0_.refs_4_), channel_id=1, source_target_pairs={{0,1},{1,0},{2,3},{3,2},{4,5},{5,4},{6,7},{7,6},{8,9},{9,8},{10,11... | collective-permute-start | bytes 393224 | tf_op jit(solution)/shard_map/ppermute | solution.py:267
  28.1 4.5 %collective-permute-start.7 = (bf16[256,128]{1,0:T(8,128)(2,1)S(1)}, bf16[256,128]{1,0:T(8,128)(2,1)S(1)}, u32[]{:S(2)}, u32[]{:S(2)}) collective-permute-start(bf16[256,128]{1,0:T(8,128)(2,1)S(1)} %get-tuple-element.58), channel_id=1, source_target_pairs={{0,4},{4,0},{8,12},{12,8},{16,20},{20,16},{24,28},{28,24},{1,5},{5... | collective-permute-start | bytes 196616 | tf_op jit(solution)/shard_map/ppermute | solution.py:267
  29.5 6.3 %collective-permute-start.5 = (bf16[256,256]{1,0:T(8,128)(2,1)S(1)}, bf16[256,256]{1,0:T(8,128)(2,1)S(1)}, u32[]{:S(2)}, u32[]{:S(2)}) collective-permute-start(bf16[256,256]{1,0:T(8,128)(2,1)S(1)} %get-tuple-element.53.refs_0_.refs_4_), channel_id=1, source_target_pairs={{0,2},{1,3},{2,0},{3,1},{4,6},{5,7},{6,4},{7,5},{8,10},{9,11},{10,... | collective-permute-start | bytes 393224 | tf_op jit(solution)/shard_map/ppermute | solution.py:267
  31.0 6.7 %collective-permute-start.6 = (bf16[256,256]{1,0:T(8,128)(2,1)S(1)}, bf16[256,256]{1,0:T(8,128)(2,1)S(1)}, u32[]{:S(2)}, u32[]{:S(2)}) collective-permute-start(bf16[256,256]{1,0:T(8,128)(2,1)S(1)} %get-tuple-element.53.refs_0_.refs_4_), channel_id=1, source_target_pairs={{0,3},{1,2},{2,1},{3,0},{4,7},{5,6},{6,5},{7,4},{8,11},{9,10},{10,... | collective-permute-start | bytes 393224 | tf_op jit(solution)/shard_map/ppermute | solution.py:267
  32.6 5.1 %collective-permute-start.8 = (bf16[256,128]{1,0:T(8,128)(2,1)S(1)}, bf16[256,128]{1,0:T(8,128)(2,1)S(1)}, u32[]{:S(2)}, u32[]{:S(2)}) collective-permute-start(bf16[256,128]{1,0:T(8,128)(2,1)S(1)} %collective-permute-done.7.refs_8_), channel_id=1, source_target_pairs={{0,1},{1,0},{2,3},{3,2},{4,5},{5,4},{6,7},{7,6},{8,9},{9,8},{10,11... | collective-permute-start | bytes 196616 | tf_op jit(solution)/shard_map/ppermute | solution.py:267
  32.6 7.5 %collective-permute-start.9 = (bf16[256,128]{1,0:T(8,128)(2,1)S(1)}, bf16[256,128]{1,0:T(8,128)(2,1)S(1)}, u32[]{:S(2)}, u32[]{:S(2)}) collective-permute-start(bf16[256,128]{1,0:T(8,128)(2,1)S(1)} %collective-permute-done.7.refs_8_), channel_id=1, source_target_pairs={{0,2},{1,3},{2,0},{3,1},{4,6},{5,7},{6,4},{7,5},{8,10},{9,11},{10,... | collective-permute-start | bytes 196616 | tf_op jit(solution)/shard_map/ppermute | solution.py:267
  34.1 6.0 %collective-permute-start.10 = (bf16[256,128]{1,0:T(8,128)(2,1)S(1)}, bf16[256,128]{1,0:T(8,128)(2,1)S(1)}, u32[]{:S(2)}, u32[]{:S(2)}) collective-permute-start(bf16[256,128]{1,0:T(8,128)(2,1)S(1)} %collective-permute-done.7.refs_8_), channel_id=1, source_target_pairs={{0,3},{1,2},{2,1},{3,0},{4,7},{5,6},{6,5},{7,4},{8,11},{9,10},{10,... | collective-permute-start | bytes 196616 | tf_op jit(solution)/shard_map/ppermute | solution.py:267
  41.8 8.8 %collective-permute-start.11 = (bf16[2,2,256,128]{3,2,1,0:T(8,128)(2,1)S(1)}, bf16[2,2,256,128]{3,2,1,0:T(8,128)(2,1)S(1)}, u32[]{:S(2)}, u32[]{:S(2)}) collective-permute-start(bf16[2,2,256,128]{3,2,1,0:T(8,128)(2,1)S(1)} %get-tuple-element.60), channel_id=1, source_target_pairs={{0,8},{4,12},{8,0},{12,4},{16,24},{20,28},{24,16},{28,20},{1,9},{5... | collective-permute-start | bytes 786440 | tf_op jit(solution)/shard_map/ppermute | solution.py:267
  50.6 8.7 %collective-permute-start.12 = (bf16[2,256,128]{2,1,0:T(8,128)(2,1)S(1)}, bf16[2,256,128]{2,1,0:T(8,128)(2,1)S(1)}, u32[]{:S(2)}, u32[]{:S(2)}) collective-permute-start(bf16[2,256,128]{2,1,0:T(8,128)(2,1)S(1)} %shard_map.128), channel_id=1, source_target_pairs={{0,16},{4,20},{8,24},{12,28},{16,0},{20,4},{24,8},{28,12},{1,17},{... | collective-permute-start | bytes 393224 | tf_op jit(solution)/shard_map/ppermute | solution.py:267
  53.0 24.6 %all-to-all-start.1 = ((bf16[8,64,256]{2,1,0:T(8,128)(2,1)}), bf16[8,64,256]{2,1,0:T(8,128)(2,1)S(1)}, u32[]{:S(2)}, u32[]{:S(2)}) async-start(bf16[8,64,256]{2,1,0:T(8,128)(2,1)} %bitcast.4), calls=%async_computation.1 | async-start | bytes 524288 | tf_op jit(solution)/shard_map/all_to_all | solution.py:304
  59.4 9.2 %collective-permute-start.15 = (bf16[2,256,128]{2,1,0:T(8,128)(2,1)S(1)}, bf16[2,256,128]{2,1,0:T(8,128)(2,1)S(1)}, u32[]{:S(2)}, u32[]{:S(2)}) collective-permute-start(bf16[2,256,128]{2,1,0:T(8,128)(2,1)S(1)} %shard_map.129.refs_0_), channel_id=1, source_target_pairs={{0,8},{4,12},{8,0},{12,4},{16,24},{20,28},{24,16},{28,20},{1,9},{5... | collective-permute-start | bytes 393224 | tf_op jit(solution)/shard_map/ppermute | solution.py:267
  59.5 11.6 %collective-permute-start.13 = (bf16[2,256,128]{2,1,0:T(8,128)(2,1)S(1)}, bf16[2,256,128]{2,1,0:T(8,128)(2,1)S(1)}, u32[]{:S(2)}, u32[]{:S(2)}) collective-permute-start(bf16[2,256,128]{2,1,0:T(8,128)(2,1)S(1)} %shard_map.129.refs_0_), channel_id=1, source_target_pairs={{0,16},{4,20},{8,24},{12,28},{16,0},{20,4},{24,8},{28,12},{1,17},{... | collective-permute-start | bytes 393224 | tf_op jit(solution)/shard_map/ppermute | solution.py:267
  61.7 9.4 %collective-permute-start.14 = (bf16[2,256,128]{2,1,0:T(8,128)(2,1)S(1)}, bf16[2,256,128]{2,1,0:T(8,128)(2,1)S(1)}, u32[]{:S(2)}, u32[]{:S(2)}) collective-permute-start(bf16[2,256,128]{2,1,0:T(8,128)(2,1)S(1)} %shard_map.129.refs_0_), channel_id=1, source_target_pairs={{0,4},{4,0},{8,12},{12,8},{16,20},{20,16},{24,28},{28,24},{1,5},{5... | collective-permute-start | bytes 393224 | tf_op jit(solution)/shard_map/ppermute | solution.py:267
  68.6 5.0 %collective-permute-start.16 = (bf16[2,256,128]{2,1,0:T(8,128)(2,1)S(1)}, bf16[2,256,128]{2,1,0:T(8,128)(2,1)S(1)}, u32[]{:S(2)}, u32[]{:S(2)}) collective-permute-start(bf16[2,256,128]{2,1,0:T(8,128)(2,1)S(1)} %collective-permute-done.15.refs_2_), channel_id=1, source_target_pairs={{0,4},{4,0},{8,12},{12,8},{16,20},{20,16},{24,28},{28,24},{1,5},{5... | collective-permute-start | bytes 393224 | tf_op jit(solution)/shard_map/ppermute | solution.py:267
  71.1 5.0 %collective-permute-start.18 = (bf16[2,256,128]{2,1,0:T(8,128)(2,1)S(1)}, bf16[2,256,128]{2,1,0:T(8,128)(2,1)S(1)}, u32[]{:S(2)}, u32[]{:S(2)}) collective-permute-start(bf16[2,256,128]{2,1,0:T(8,128)(2,1)S(1)} %collective-permute-done.13.refs_4_), channel_id=1, source_target_pairs={{0,8},{4,12},{8,0},{12,4},{16,24},{20,28},{24,16},{28,20},{1,9},{5... | collective-permute-start | bytes 393224 | tf_op jit(solution)/shard_map/ppermute | solution.py:267
  73.6 5.0 %collective-permute-start.17 = (bf16[2,256,128]{2,1,0:T(8,128)(2,1)S(1)}, bf16[2,256,128]{2,1,0:T(8,128)(2,1)S(1)}, u32[]{:S(2)}, u32[]{:S(2)}) collective-permute-start(bf16[2,256,128]{2,1,0:T(8,128)(2,1)S(1)} %collective-permute-done.13.refs_4_), channel_id=1, source_target_pairs={{0,4},{4,0},{8,12},{12,8},{16,20},{20,16},{24,28},{28,24},{1,5},{5... | collective-permute-start | bytes 393224 | tf_op jit(solution)/shard_map/ppermute | solution.py:267
  76.1 5.0 %collective-permute-start.19 = (bf16[2,256,128]{2,1,0:T(8,128)(2,1)S(1)}, bf16[2,256,128]{2,1,0:T(8,128)(2,1)S(1)}, u32[]{:S(2)}, u32[]{:S(2)}) collective-permute-start(bf16[2,256,128]{2,1,0:T(8,128)(2,1)S(1)} %collective-permute-done.18.refs_6_), channel_id=1, source_target_pairs={{0,4},{4,0},{8,12},{12,8},{16,20},{20,16},{24,28},{28,24},{1,5},{5... | collective-permute-start | bytes 393224 | tf_op jit(solution)/shard_map/ppermute | solution.py:267

commit v6 on v1

--- a/solution.py
+++ b/solution.py
@@ -273,11 +273,9 @@
 
 
 def gather_pieces(array, peers):
-    out = {0: array, 4: swap(array, "dom", 4), 2: swap(array, "dom", 2)}
-    out[1] = swap(array, "dom", 1)
-    out[4], out[1] = lax.optimization_barrier((out[4], out[1]))
-    out[6] = swap(out[4], "dom", 2)
-    for offset in range(2, peers, 2):
+    out = {offset: swap(array, "dom", offset) for offset in range(peers - 2, 0, -2)}
+    out[0] = array
+    for offset in range(0, peers, 2):
         out[offset + 1] = swap(out[offset], "dom", 1)
     return [out[offset] for offset in range(peers)]
 

time: 80.6 us -> 82.6 us (1.025)
  starting transfers between devices: 31.1 us -> 32.2 us
  local copies, waits for them, and re-layouts: 2.68 us -> 3.59 us
    ppermute x20, starting transfers between devices: 20 us -> 21.3 us  [swap(): lax.ppermute(array, axis, [(i, i ^ offset) for i in range(lax.axis_size(a...]
    unnamed x16 -> x24, local copies, waits for them, and re-layouts: 2.68 us -> 3.59 us
where the time goes in v6:
time: 82.6 us; the launch traced here: 82.1 us
  waiting for transfers between devices  36.4 us (44%)
  starting transfers between devices  32.2 us (39%)
  Pallas kernels  9.18 us (11%)
  local copies, waits for them, and re-layouts  3.59 us (4%)
    ppermute x20, waiting for transfers between devices, swap(): lax.ppermute(array, axis, [(i, i ^ offset) for i in range(lax.axis_size(a...  35.1 us
    ppermute x20, starting transfers between devices, swap(): lax.ppermute(array, axis, [(i, i ^ offset) for i in range(lax.axis_size(a...  21.3 us
    all_to_all x2, starting transfers between devices, exchange(): lax.all_to_all(array.reshape(peers, slots, cols), 'dom', split_axis=0, co...  10.8 us
    pallas_call x11, Pallas kernels, call(): pl.pallas_call(body, out_shape=outs, in_specs=[SPECS[spec] for spec, _ in...  9.18 us
    unnamed x24, local copies, waits for them, and re-layouts  3.59 us
  transfers between devices with their start and end apart: 22, of which 13 were waited for; matrix products, arithmetic and copies ran while one was open for 0% of the time, Pallas kernels for 4%

profile of v6, /device:TPU:0, one launch (start us, length us, event | category | flops | bytes accessed | tf_op | source)
XLA Modules:
  0.0 82.1 jit_solution(5307009770128425974)
XLA Ops:
  0.6 2.1 %shard_map.120 = (bf16[256,512]{1,0:T(8,128)(2,1)}, bf16[512,256]{1,0:T(8,128)(2,1)}) custom-call(s32[8]{0:T(128)} %count_hbm.1, s32[8,64]{1,0:T(8,128)} %list_hbm.1, bf16[256,256]{1,0:T(8,128)(2,1)} %refs_0_.1), custom_call_target="tpu_custom_call" | custom-call | flops 67108864 | bytes 600000 | tf_op jit(solution)/shard_map/pallas_call | solution.py:22
  2.8 7.4 %all-to-all-start = ((bf16[8,64,256]{2,1,0:T(8,128)(2,1)}), bf16[8,64,256]{2,1,0:T(8,128)(2,1)S(1)}, u32[]{:S(2)}, u32[]{:S(2)}) async-start(bf16[8,64,256]{2,1,0:T(8,128)(2,1)} %bitcast.8), calls=%async_computation | async-start | bytes 524288 | tf_op jit(solution)/shard_map/all_to_all | solution.py:301
  10.2 2.0 %collective-permute-start = (bf16[256,256]{1,0:T(8,128)(2,1)S(1)}, bf16[256,256]{1,0:T(8,128)(2,1)S(1)}, u32[]{:S(2)}, u32[]{:S(2)}) collective-permute-start(bf16[256,256]{1,0:T(8,128)(2,1)S(1)} %copy-done.4), channel_id=1, source_target_pairs={{0,4},{4,0},{8,12},{12,8},{16,20},{20,16},{24,28},{28,24},{1,5},{5... | collective-permute-start | bytes 393224 | tf_op jit(solution)/shard_map/ppermute | solution.py:267
  12.9 1.0 %copy-done.1 = bf16[256,1024]{1,0:T(8,128)(2,1)S(1)} copy-done((bf16[256,1024]{1,0:T(8,128)(2,1)S(1)}, bf16[256,1024]{1,0:T(8,128)(2,1)}, u32[]{:S(2)}) %copy-start.1) | copy-done | bytes 524312
  14.0 0.9 %copy-done.3 = bf16[8,128,128]{2,1,0:T(8,128)(2,1)S(1)} copy-done((bf16[8,128,128]{2,1,0:T(8,128)(2,1)S(1)}, bf16[8,128,128]{2,1,0:T(8,128)(2,1)}, u32[]{:S(2)}) %copy-start.3) | copy-done | bytes 262168
  15.9 2.0 %collective-permute-done.refs_1_ = bf16[256,256]{1,0:T(8,128)(2,1)S(1)} collective-permute-done((bf16[256,256]{1,0:T(8,128)(2,1)S(1)}, bf16[256,256]{1,0:T(8,128)(2,1)S(1)}, u32[]{:S(2)}, u32[]{:S(2)}) %collective-permute-start) | collective-permute-done | bytes 131104 | tf_op jit(solution)/shard_map/ppermute | solution.py:267
  17.8 1.3 %all-to-all-done = bf16[8,64,256]{2,1,0:T(8,128)(2,1)S(1)} async-done(((bf16[8,64,256]{2,1,0:T(8,128)(2,1)}), bf16[8,64,256]{2,1,0:T(8,128)(2,1)S(1)}, u32[]{:S(2)}, u32[]{:S(2)}) %all-to-all-start) | async-done | bytes 262176 | tf_op jit(solution)/shard_map/all_to_all | solution.py:301
  19.1 1.0 %shard_map.122 = (f32[256,256]{1,0:T(8,128)S(1)}, bf16[256,256]{1,0:T(8,128)(2,1)S(1)}, f32[256,256]{1,0:T(8,128)S(1)}, bf16[2,256,256]{2,1,0:T(8,128)(2,1)S(1)}) custom-call(s32[1]{0:T(128)} %bitcast.1.rep_ref, bf16[256,256]{1,0:T(8,128)(2,1)S(1)} %copy-done.4, bf16[512,256]{1,0:T(8,128)(2,1)S(1)} %bitcast.7, ...), custom_call_target="tpu_custom_call" | custom-call | flops 600000000 | bytes 3000000 | tf_op jit(solution)/shard_map/pallas_call | solution.py:22
  20.2 1.5 %collective-permute-start.1 = (bf16[256,256]{1,0:T(8,128)(2,1)S(1)}, bf16[256,256]{1,0:T(8,128)(2,1)S(1)}, u32[]{:S(2)}, u32[]{:S(2)}) collective-permute-start(bf16[256,256]{1,0:T(8,128)(2,1)S(1)} %get-tuple-element.45.refs_2_), channel_id=1, source_target_pairs={{0,4},{4,0},{8,12},{12,8},{16,20},{20,16},{24,28},{28,24},{1,5},{5... | collective-permute-start | bytes 393224 | tf_op jit(solution)/shard_map/ppermute | solution.py:267
  21.8 1.6 %collective-permute-start.3 = (bf16[256,256]{1,0:T(8,128)(2,1)S(1)}, bf16[256,256]{1,0:T(8,128)(2,1)S(1)}, u32[]{:S(2)}, u32[]{:S(2)}) collective-permute-start(bf16[256,256]{1,0:T(8,128)(2,1)S(1)} %shard_map.123), channel_id=1, source_target_pairs={{0,2},{1,3},{2,0},{3,1},{4,6},{5,7},{6,4},{7,5},{8,10},{9,11},{10,... | collective-permute-start | bytes 393224 | tf_op jit(solution)/shard_map/ppermute | solution.py:267
  23.3 2.8 %collective-permute-done.1.refs_3_ = bf16[256,256]{1,0:T(8,128)(2,1)S(1)} collective-permute-done((bf16[256,256]{1,0:T(8,128)(2,1)S(1)}, bf16[256,256]{1,0:T(8,128)(2,1)S(1)}, u32[]{:S(2)}, u32[]{:S(2)}) %collective-permute-start.1) | collective-permute-done | bytes 131104 | tf_op jit(solution)/shard_map/ppermute | solution.py:267
  26.1 1.3 %collective-permute-done.3.across_ref = bf16[256,256]{1,0:T(8,128)(2,1)S(1)} collective-permute-done((bf16[256,256]{1,0:T(8,128)(2,1)S(1)}, bf16[256,256]{1,0:T(8,128)(2,1)S(1)}, u32[]{:S(2)}, u32[]{:S(2)}) %collective-permute-start.3) | collective-permute-done | bytes 131104 | tf_op jit(solution)/shard_map/ppermute | solution.py:267
  28.1 1.5 %collective-permute-start.5 = (bf16[256,256]{1,0:T(8,128)(2,1)S(1)}, bf16[256,256]{1,0:T(8,128)(2,1)S(1)}, u32[]{:S(2)}, u32[]{:S(2)}) collective-permute-start(bf16[256,256]{1,0:T(8,128)(2,1)S(1)} %get-tuple-element.51.refs_0_.refs_4_), channel_id=1, source_target_pairs={{0,2},{1,3},{2,0},{3,1},{4,6},{5,7},{6,4},{7,5},{8,10},{9,11},{10,... | collective-permute-start | bytes 393224 | tf_op jit(solution)/shard_map/ppermute | solution.py:267
  29.6 1.4 %collective-permute-start.7 = (bf16[256,128]{1,0:T(8,128)(2,1)S(1)}, bf16[256,128]{1,0:T(8,128)(2,1)S(1)}, u32[]{:S(2)}, u32[]{:S(2)}) collective-permute-start(bf16[256,128]{1,0:T(8,128)(2,1)S(1)} %get-tuple-element.56), channel_id=1, source_target_pairs={{0,4},{4,0},{8,12},{12,8},{16,20},{20,16},{24,28},{28,24},{1,5},{5... | collective-permute-start | bytes 196616 | tf_op jit(solution)/shard_map/ppermute | solution.py:267
  31.0 2.9 %collective-permute-done.7.refs_8_ = bf16[256,128]{1,0:T(8,128)(2,1)S(1)} collective-permute-done((bf16[256,128]{1,0:T(8,128)(2,1)S(1)}, bf16[256,128]{1,0:T(8,128)(2,1)S(1)}, u32[]{:S(2)}, u32[]{:S(2)}) %collective-permute-start.7) | collective-permute-done | bytes 65568 | tf_op jit(solution)/shard_map/ppermute | solution.py:267
  34.9 3.2 %collective-permute-done.9.refs_10_ = bf16[256,128]{1,0:T(8,128)(2,1)S(1)} collective-permute-done((bf16[256,128]{1,0:T(8,128)(2,1)S(1)}, bf16[256,128]{1,0:T(8,128)(2,1)S(1)}, u32[]{:S(2)}, u32[]{:S(2)}) %collective-permute-start.9) | collective-permute-done | bytes 65568 | tf_op jit(solution)/shard_map/ppermute | solution.py:267
  38.2 1.2 %collective-permute-done.10.refs_11_ = bf16[256,128]{1,0:T(8,128)(2,1)S(1)} collective-permute-done((bf16[256,128]{1,0:T(8,128)(2,1)S(1)}, bf16[256,128]{1,0:T(8,128)(2,1)S(1)}, u32[]{:S(2)}, u32[]{:S(2)}) %collective-permute-start.10) | collective-permute-done | bytes 65568 | tf_op jit(solution)/shard_map/ppermute | solution.py:267
  41.1 1.1 %collective-permute-start.11 = (bf16[2,2,256,128]{3,2,1,0:T(8,128)(2,1)S(1)}, bf16[2,2,256,128]{3,2,1,0:T(8,128)(2,1)S(1)}, u32[]{:S(2)}, u32[]{:S(2)}) collective-permute-start(bf16[2,2,256,128]{3,2,1,0:T(8,128)(2,1)S(1)} %get-tuple-element.58), channel_id=1, source_target_pairs={{0,8},{4,12},{8,0},{12,4},{16,24},{20,28},{24,16},{28,20},{1,9},{5... | collective-permute-start | bytes 786440 | tf_op jit(solution)/shard_map/ppermute | solution.py:267
  42.2 1.5 %shard_map.125 = (f32[256,256]{1,0:T(8,128)S(1)}, bf16[512,256]{1,0:T(8,128)(2,1)}) custom-call(s32[1]{0:T(128)} %bitcast.1.rep_ref, bf16[256,768]{1,0:T(8,128)(2,1)S(1)} %get-tuple-element.39.high_ref, bf16[256,768]{1,0:T(8,128)(2,1)S(1)} %get-tuple-element.40.low_ref, f32[256,128]{1,0:T(8,128)S(1)} %get-tuple-element.41.deg_ref, ...), custom_call_target="tpu_custom_call" | custom-call | flops 600000000 | bytes 3000000 | tf_op jit(solution)/shard_map/pallas_call | solution.py:22
  43.8 3.4 %all-to-all-start.1 = ((bf16[8,64,256]{2,1,0:T(8,128)(2,1)}), bf16[8,64,256]{2,1,0:T(8,128)(2,1)S(1)}, u32[]{:S(2)}, u32[]{:S(2)}) async-start(bf16[8,64,256]{2,1,0:T(8,128)(2,1)} %bitcast.4), calls=%async_computation.1 | async-start | bytes 524288 | tf_op jit(solution)/shard_map/all_to_all | solution.py:301
  47.2 2.4 %collective-permute-done.11.beside_ref.next_ref = bf16[2,2,256,128]{3,2,1,0:T(8,128)(2,1)S(1)} collective-permute-done((bf16[2,2,256,128]{3,2,1,0:T(8,128)(2,1)S(1)}, bf16[2,2,256,128]{3,2,1,0:T(8,128)(2,1)S(1)}, u32[]{:S(2)}, u32[]{:S(2)}) %collective-permute-start.11) | collective-permute-done | bytes 262176 | tf_op jit(solution)/shard_map/ppermute | solution.py:267
  49.6 1.5 %collective-permute-start.12 = (bf16[2,256,128]{2,1,0:T(8,128)(2,1)S(1)}, bf16[2,256,128]{2,1,0:T(8,128)(2,1)S(1)}, u32[]{:S(2)}, u32[]{:S(2)}) collective-permute-start(bf16[2,256,128]{2,1,0:T(8,128)(2,1)S(1)} %shard_map.128), channel_id=1, source_target_pairs={{0,16},{4,20},{8,24},{12,28},{16,0},{20,4},{24,8},{28,12},{1,17},{... | collective-permute-start | bytes 393224 | tf_op jit(solution)/shard_map/ppermute | solution.py:267
  51.0 10.9 %collective-permute-done.12.far_ref = bf16[2,256,128]{2,1,0:T(8,128)(2,1)S(1)} collective-permute-done((bf16[2,256,128]{2,1,0:T(8,128)(2,1)S(1)}, bf16[2,256,128]{2,1,0:T(8,128)(2,1)S(1)}, u32[]{:S(2)}, u32[]{:S(2)}) %collective-permute-start.12) | collective-permute-done | bytes 131104 | tf_op jit(solution)/shard_map/ppermute | solution.py:267
  62.0 1.9 %collective-permute-start.16 = (bf16[2,256,128]{2,1,0:T(8,128)(2,1)S(1)}, bf16[2,256,128]{2,1,0:T(8,128)(2,1)S(1)}, u32[]{:S(2)}, u32[]{:S(2)}) collective-permute-start(bf16[2,256,128]{2,1,0:T(8,128)(2,1)S(1)} %shard_map.129.refs_0_), channel_id=1, source_target_pairs={{0,16},{4,20},{8,24},{12,28},{16,0},{20,4},{24,8},{28,12},{1,17},{... | collective-permute-start | bytes 393224 | tf_op jit(solution)/shard_map/ppermute | solution.py:267
  64.0 2.5 %collective-permute-start.18 = (bf16[2,256,128]{2,1,0:T(8,128)(2,1)S(1)}, bf16[2,256,128]{2,1,0:T(8,128)(2,1)S(1)}, u32[]{:S(2)}, u32[]{:S(2)}) collective-permute-start(bf16[2,256,128]{2,1,0:T(8,128)(2,1)S(1)} %shard_map.129.refs_0_), channel_id=1, source_target_pairs={{0,24},{4,28},{8,16},{12,20},{16,8},{20,12},{24,0},{28,4},{1,25},{... | collective-permute-start | bytes 393224 | tf_op jit(solution)/shard_map/ppermute | solution.py:267
  66.4 1.5 %collective-permute-start.13 = (bf16[2,256,128]{2,1,0:T(8,128)(2,1)S(1)}, bf16[2,256,128]{2,1,0:T(8,128)(2,1)S(1)}, u32[]{:S(2)}, u32[]{:S(2)}) collective-permute-start(bf16[2,256,128]{2,1,0:T(8,128)(2,1)S(1)} %shard_map.129.refs_0_), channel_id=1, source_target_pairs={{0,4},{4,0},{8,12},{12,8},{16,20},{20,16},{24,28},{28,24},{1,5},{5... | collective-permute-start | bytes 393224 | tf_op jit(solution)/shard_map/ppermute | solution.py:267
  68.0 1.7 %collective-permute-start.15 = (bf16[2,256,128]{2,1,0:T(8,128)(2,1)S(1)}, bf16[2,256,128]{2,1,0:T(8,128)(2,1)S(1)}, u32[]{:S(2)}, u32[]{:S(2)}) collective-permute-start(bf16[2,256,128]{2,1,0:T(8,128)(2,1)S(1)} %collective-permute-done.14.refs_2_), channel_id=1, source_target_pairs={{0,4},{4,0},{8,12},{12,8},{16,20},{20,16},{24,28},{28,24},{1,5},{5... | collective-permute-start | bytes 393224 | tf_op jit(solution)/shard_map/ppermute | solution.py:267
  69.7 4.8 %collective-permute-done.16.refs_4_ = bf16[2,256,128]{2,1,0:T(8,128)(2,1)S(1)} collective-permute-done((bf16[2,256,128]{2,1,0:T(8,128)(2,1)S(1)}, bf16[2,256,128]{2,1,0:T(8,128)(2,1)S(1)}, u32[]{:S(2)}, u32[]{:S(2)}) %collective-permute-start.16) | collective-permute-done | bytes 131104 | tf_op jit(solution)/shard_map/ppermute | solution.py:267
  74.5 1.5 %collective-permute-start.17 = (bf16[2,256,128]{2,1,0:T(8,128)(2,1)S(1)}, bf16[2,256,128]{2,1,0:T(8,128)(2,1)S(1)}, u32[]{:S(2)}, u32[]{:S(2)}) collective-permute-start(bf16[2,256,128]{2,1,0:T(8,128)(2,1)S(1)} %collective-permute-done.16.refs_4_), channel_id=1, source_target_pairs={{0,4},{4,0},{8,12},{12,8},{16,20},{20,16},{24,28},{28,24},{1,5},{5... | collective-permute-start | bytes 393224 | tf_op jit(solution)/shard_map/ppermute | solution.py:267
  77.4 2.0 %collective-permute-done.17.refs_5_ = bf16[2,256,128]{2,1,0:T(8,128)(2,1)S(1)} collective-permute-done((bf16[2,256,128]{2,1,0:T(8,128)(2,1)S(1)}, bf16[2,256,128]{2,1,0:T(8,128)(2,1)S(1)}, u32[]{:S(2)}, u32[]{:S(2)}) %collective-permute-start.17) | collective-permute-done | bytes 131104 | tf_op jit(solution)/shard_map/ppermute | solution.py:267
  79.5 1.6 %collective-permute-done.19.refs_7_ = bf16[2,256,128]{2,1,0:T(8,128)(2,1)S(1)} collective-permute-done((bf16[2,256,128]{2,1,0:T(8,128)(2,1)S(1)}, bf16[2,256,128]{2,1,0:T(8,128)(2,1)S(1)}, u32[]{:S(2)}, u32[]{:S(2)}) %collective-permute-start.19) | collective-permute-done | bytes 131104 | tf_op jit(solution)/shard_map/ppermute | solution.py:267
  81.0 1.1 %shard_map.130 = (bf16[256,1024]{1,0:T(8,128)(2,1)}, bf16[256,1024]{1,0:T(8,128)(2,1)}) custom-call(s32[1]{0:T(128)} %bitcast.dom_ref, bf16[2,256,128]{2,1,0:T(8,128)(2,1)S(1)} %shard_map.129.refs_0_, bf16[2,256,128]{2,1,0:T(8,128)(2,1)S(1)} %collective-permute-done.13.refs_1_, bf16[2,256,128]{2,1,0:T(8,128)(2,1)S(1)} %collective-permute-done.14.refs_2_, ...), custom_call_target="tpu_custom_call" | custom-call | bytes 2000000 | tf_op jit(solution)/shard_map/pallas_call | solution.py:22
  (47 shorter events, 6.9 us)
Async XLA Ops:
  0.6 11.6 %copy-start = (bf16[256,1024]{1,0:T(8,128)(2,1)S(1)}, bf16[256,1024]{1,0:T(8,128)(2,1)}, u32[]{:S(2)}) copy-start(bf16[256,1024]{1,0:T(8,128)(2,1)} %self_hbm) | copy-start | bytes 1572868
  2.8 7.4 %copy-start.4 = (bf16[256,256]{1,0:T(8,128)(2,1)S(1)}, bf16[256,256]{1,0:T(8,128)(2,1)}, u32[]{:S(2)}) copy-start(bf16[256,256]{1,0:T(8,128)(2,1)} %refs_0_.1) | copy-start | bytes 393220
  2.8 16.3 %all-to-all-start = ((bf16[8,64,256]{2,1,0:T(8,128)(2,1)}), bf16[8,64,256]{2,1,0:T(8,128)(2,1)S(1)}, u32[]{:S(2)}, u32[]{:S(2)}) async-start(bf16[8,64,256]{2,1,0:T(8,128)(2,1)} %bitcast.8), calls=%async_computation | async-start | bytes 524288 | tf_op jit(solution)/shard_map/all_to_all | solution.py:301
  10.2 7.6 %collective-permute-start = (bf16[256,256]{1,0:T(8,128)(2,1)S(1)}, bf16[256,256]{1,0:T(8,128)(2,1)S(1)}, u32[]{:S(2)}, u32[]{:S(2)}) collective-permute-start(bf16[256,256]{1,0:T(8,128)(2,1)S(1)} %copy-done.4), channel_id=1, source_target_pairs={{0,4},{4,0},{8,12},{12,8},{16,20},{20,16},{24,28},{28,24},{1,5},{5... | collective-permute-start | bytes 393224 | tf_op jit(solution)/shard_map/ppermute | solution.py:267
  12.9 1.0 %copy-start.1 = (bf16[256,1024]{1,0:T(8,128)(2,1)S(1)}, bf16[256,1024]{1,0:T(8,128)(2,1)}, u32[]{:S(2)}) copy-start(bf16[256,1024]{1,0:T(8,128)(2,1)} %neigh_hbm) | copy-start | bytes 1572868
  14.0 0.9 %copy-start.3 = (bf16[8,128,128]{2,1,0:T(8,128)(2,1)S(1)}, bf16[8,128,128]{2,1,0:T(8,128)(2,1)}, u32[]{:S(2)}) copy-start(bf16[8,128,128]{2,1,0:T(8,128)(2,1)} %tiles_ref) | copy-start | bytes 786436
  20.1 1.6 %copy-start.8 = (bf16[256,256]{1,0:T(8,128)(2,1)}, bf16[256,256]{1,0:T(8,128)(2,1)S(1)}, u32[]{:S(2)}) copy-start(bf16[256,256]{1,0:T(8,128)(2,1)S(1)} %get-tuple-element.45.refs_2_) | copy-start | bytes 393220
  20.1 1.6 %collective-permute-start.2 = (bf16[2,256,256]{2,1,0:T(8,128)(2,1)S(1)}, bf16[2,256,256]{2,1,0:T(8,128)(2,1)S(1)}, u32[]{:S(2)}, u32[]{:S(2)}) collective-permute-start(bf16[2,256,256]{2,1,0:T(8,128)(2,1)S(1)} %get-tuple-element.47), channel_id=1, source_target_pairs={{0,1},{1,0},{2,3},{3,2},{4,5},{5,4},{6,7},{7,6},{8,9},{9,8},{10,11... | collective-permute-start | bytes 786440 | tf_op jit(solution)/shard_map/ppermute | solution.py:267
  20.2 5.9 %collective-permute-start.1 = (bf16[256,256]{1,0:T(8,128)(2,1)S(1)}, bf16[256,256]{1,0:T(8,128)(2,1)S(1)}, u32[]{:S(2)}, u32[]{:S(2)}) collective-permute-start(bf16[256,256]{1,0:T(8,128)(2,1)S(1)} %get-tuple-element.45.refs_2_), channel_id=1, source_target_pairs={{0,4},{4,0},{8,12},{12,8},{16,20},{20,16},{24,28},{28,24},{1,5},{5... | collective-permute-start | bytes 393224 | tf_op jit(solution)/shard_map/ppermute | solution.py:267
  21.7 5.6 %copy-start.5 = (bf16[256,256]{1,0:T(8,128)(2,1)S(1)}, bf16[256,256]{1,0:T(8,128)(2,1)}, u32[]{:S(2)}) copy-start(bf16[256,256]{1,0:T(8,128)(2,1)} %gout_ref) | copy-start | bytes 393220
  21.8 5.6 %collective-permute-start.3 = (bf16[256,256]{1,0:T(8,128)(2,1)S(1)}, bf16[256,256]{1,0:T(8,128)(2,1)S(1)}, u32[]{:S(2)}, u32[]{:S(2)}) collective-permute-start(bf16[256,256]{1,0:T(8,128)(2,1)S(1)} %shard_map.123), channel_id=1, source_target_pairs={{0,2},{1,3},{2,0},{3,1},{4,6},{5,7},{6,4},{7,5},{8,10},{9,11},{10,... | collective-permute-start | bytes 393224 | tf_op jit(solution)/shard_map/ppermute | solution.py:267
  26.1 2.0 %copy-start.10 = (bf16[256,256]{1,0:T(8,128)(2,1)}, bf16[256,256]{1,0:T(8,128)(2,1)S(1)}, u32[]{:S(2)}) copy-start(bf16[256,256]{1,0:T(8,128)(2,1)S(1)} %collective-permute-done.1.refs_3_) | copy-start | bytes 393220
  27.4 12.0 %copy-start.9 = (bf16[256,256]{1,0:T(8,128)(2,1)S(1)}, bf16[256,256]{1,0:T(8,128)(2,1)}, u32[]{:S(2)}) copy-start(bf16[256,256]{1,0:T(8,128)(2,1)} %copy-done.8) | copy-start | bytes 393220
  28.1 6.3 %collective-permute-start.5 = (bf16[256,256]{1,0:T(8,128)(2,1)S(1)}, bf16[256,256]{1,0:T(8,128)(2,1)S(1)}, u32[]{:S(2)}, u32[]{:S(2)}) collective-permute-start(bf16[256,256]{1,0:T(8,128)(2,1)S(1)} %get-tuple-element.51.refs_0_.refs_4_), channel_id=1, source_target_pairs={{0,2},{1,3},{2,0},{3,1},{4,6},{5,7},{6,4},{7,5},{8,10},{9,11},{10,... | collective-permute-start | bytes 393224 | tf_op jit(solution)/shard_map/ppermute | solution.py:267
  29.6 4.3 %collective-permute-start.7 = (bf16[256,128]{1,0:T(8,128)(2,1)S(1)}, bf16[256,128]{1,0:T(8,128)(2,1)S(1)}, u32[]{:S(2)}, u32[]{:S(2)}) collective-permute-start(bf16[256,128]{1,0:T(8,128)(2,1)S(1)} %get-tuple-element.56), channel_id=1, source_target_pairs={{0,4},{4,0},{8,12},{12,8},{16,20},{20,16},{24,28},{28,24},{1,5},{5... | collective-permute-start | bytes 196616 | tf_op jit(solution)/shard_map/ppermute | solution.py:267
  31.0 7.1 %collective-permute-start.4 = (bf16[256,256]{1,0:T(8,128)(2,1)S(1)}, bf16[256,256]{1,0:T(8,128)(2,1)S(1)}, u32[]{:S(2)}, u32[]{:S(2)}) collective-permute-start(bf16[256,256]{1,0:T(8,128)(2,1)S(1)} %get-tuple-element.51.refs_0_.refs_4_), channel_id=1, source_target_pairs={{0,1},{1,0},{2,3},{3,2},{4,5},{5,4},{6,7},{7,6},{8,9},{9,8},{10,11... | collective-permute-start | bytes 393224 | tf_op jit(solution)/shard_map/ppermute | solution.py:267
  33.9 4.3 %collective-permute-start.9 = (bf16[256,128]{1,0:T(8,128)(2,1)S(1)}, bf16[256,128]{1,0:T(8,128)(2,1)S(1)}, u32[]{:S(2)}, u32[]{:S(2)}) collective-permute-start(bf16[256,128]{1,0:T(8,128)(2,1)S(1)} %collective-permute-done.7.refs_8_), channel_id=1, source_target_pairs={{0,2},{1,3},{2,0},{3,1},{4,6},{5,7},{6,4},{7,5},{8,10},{9,11},{10,... | collective-permute-start | bytes 196616 | tf_op jit(solution)/shard_map/ppermute | solution.py:267
  34.4 5.0 %collective-permute-start.6 = (bf16[256,256]{1,0:T(8,128)(2,1)S(1)}, bf16[256,256]{1,0:T(8,128)(2,1)S(1)}, u32[]{:S(2)}, u32[]{:S(2)}) collective-permute-start(bf16[256,256]{1,0:T(8,128)(2,1)S(1)} %collective-permute-done.5.refs_2_.refs_6_), channel_id=1, source_target_pairs={{0,1},{1,0},{2,3},{3,2},{4,5},{5,4},{6,7},{7,6},{8,9},{9,8},{10,11... | collective-permute-start | bytes 393224 | tf_op jit(solution)/shard_map/ppermute | solution.py:267
  34.4 3.7 %collective-permute-start.8 = (bf16[256,128]{1,0:T(8,128)(2,1)S(1)}, bf16[256,128]{1,0:T(8,128)(2,1)S(1)}, u32[]{:S(2)}, u32[]{:S(2)}) collective-permute-start(bf16[256,128]{1,0:T(8,128)(2,1)S(1)} %collective-permute-done.7.refs_8_), channel_id=1, source_target_pairs={{0,1},{1,0},{2,3},{3,2},{4,5},{5,4},{6,7},{7,6},{8,9},{9,8},{10,11... | collective-permute-start | bytes 196616 | tf_op jit(solution)/shard_map/ppermute | solution.py:267
  38.2 1.3 %collective-permute-start.10 = (bf16[256,128]{1,0:T(8,128)(2,1)S(1)}, bf16[256,128]{1,0:T(8,128)(2,1)S(1)}, u32[]{:S(2)}, u32[]{:S(2)}) collective-permute-start(bf16[256,128]{1,0:T(8,128)(2,1)S(1)} %collective-permute-done.9.refs_10_), channel_id=1, source_target_pairs={{0,1},{1,0},{2,3},{3,2},{4,5},{5,4},{6,7},{7,6},{8,9},{9,8},{10,11... | collective-permute-start | bytes 196616 | tf_op jit(solution)/shard_map/ppermute | solution.py:267
  39.4 0.9 %copy-start.11 = (bf16[256,256]{1,0:T(8,128)(2,1)S(1)}, bf16[256,256]{1,0:T(8,128)(2,1)}, u32[]{:S(2)}) copy-start(bf16[256,256]{1,0:T(8,128)(2,1)} %copy-done.10) | copy-start | bytes 393220
  41.1 8.4 %collective-permute-start.11 = (bf16[2,2,256,128]{3,2,1,0:T(8,128)(2,1)S(1)}, bf16[2,2,256,128]{3,2,1,0:T(8,128)(2,1)S(1)}, u32[]{:S(2)}, u32[]{:S(2)}) collective-permute-start(bf16[2,2,256,128]{3,2,1,0:T(8,128)(2,1)S(1)} %get-tuple-element.58), channel_id=1, source_target_pairs={{0,8},{4,12},{8,0},{12,4},{16,24},{20,28},{24,16},{28,20},{1,9},{5... | collective-permute-start | bytes 786440 | tf_op jit(solution)/shard_map/ppermute | solution.py:267
  43.8 32.8 %all-to-all-start.1 = ((bf16[8,64,256]{2,1,0:T(8,128)(2,1)}), bf16[8,64,256]{2,1,0:T(8,128)(2,1)S(1)}, u32[]{:S(2)}, u32[]{:S(2)}) async-start(bf16[8,64,256]{2,1,0:T(8,128)(2,1)} %bitcast.4), calls=%async_computation.1 | async-start | bytes 524288 | tf_op jit(solution)/shard_map/all_to_all | solution.py:301
  49.6 12.3 %collective-permute-start.12 = (bf16[2,256,128]{2,1,0:T(8,128)(2,1)S(1)}, bf16[2,256,128]{2,1,0:T(8,128)(2,1)S(1)}, u32[]{:S(2)}, u32[]{:S(2)}) collective-permute-start(bf16[2,256,128]{2,1,0:T(8,128)(2,1)S(1)} %shard_map.128), channel_id=1, source_target_pairs={{0,16},{4,20},{8,24},{12,28},{16,0},{20,4},{24,8},{28,12},{1,17},{... | collective-permute-start | bytes 393224 | tf_op jit(solution)/shard_map/ppermute | solution.py:267
  61.9 14.6 %copy-start.2 = (bf16[256,512]{1,0:T(8,128)(2,1)S(1)}, bf16[256,512]{1,0:T(8,128)(2,1)}, u32[]{:S(2)}) copy-start(bf16[256,512]{1,0:T(8,128)(2,1)} %get-tuple-element.50.onehot_ref) | copy-start | bytes 786436
  62.0 6.1 %collective-permute-start.14 = (bf16[2,256,128]{2,1,0:T(8,128)(2,1)S(1)}, bf16[2,256,128]{2,1,0:T(8,128)(2,1)S(1)}, u32[]{:S(2)}, u32[]{:S(2)}) collective-permute-start(bf16[2,256,128]{2,1,0:T(8,128)(2,1)S(1)} %shard_map.129.refs_0_), channel_id=1, source_target_pairs={{0,8},{4,12},{8,0},{12,4},{16,24},{20,28},{24,16},{28,20},{1,9},{5... | collective-permute-start | bytes 393224 | tf_op jit(solution)/shard_map/ppermute | solution.py:267
  62.0 12.4 %collective-permute-start.16 = (bf16[2,256,128]{2,1,0:T(8,128)(2,1)S(1)}, bf16[2,256,128]{2,1,0:T(8,128)(2,1)S(1)}, u32[]{:S(2)}, u32[]{:S(2)}) collective-permute-start(bf16[2,256,128]{2,1,0:T(8,128)(2,1)S(1)} %shard_map.129.refs_0_), channel_id=1, source_target_pairs={{0,16},{4,20},{8,24},{12,28},{16,0},{20,4},{24,8},{28,12},{1,17},{... | collective-permute-start | bytes 393224 | tf_op jit(solution)/shard_map/ppermute | solution.py:267
  64.0 12.1 %collective-permute-start.18 = (bf16[2,256,128]{2,1,0:T(8,128)(2,1)S(1)}, bf16[2,256,128]{2,1,0:T(8,128)(2,1)S(1)}, u32[]{:S(2)}, u32[]{:S(2)}) collective-permute-start(bf16[2,256,128]{2,1,0:T(8,128)(2,1)S(1)} %shard_map.129.refs_0_), channel_id=1, source_target_pairs={{0,24},{4,28},{8,16},{12,20},{16,8},{20,12},{24,0},{28,4},{1,25},{... | collective-permute-start | bytes 393224 | tf_op jit(solution)/shard_map/ppermute | solution.py:267
  66.4 11.0 %collective-permute-start.13 = (bf16[2,256,128]{2,1,0:T(8,128)(2,1)S(1)}, bf16[2,256,128]{2,1,0:T(8,128)(2,1)S(1)}, u32[]{:S(2)}, u32[]{:S(2)}) collective-permute-start(bf16[2,256,128]{2,1,0:T(8,128)(2,1)S(1)} %shard_map.129.refs_0_), channel_id=1, source_target_pairs={{0,4},{4,0},{8,12},{12,8},{16,20},{20,16},{24,28},{28,24},{1,5},{5... | collective-permute-start | bytes 393224 | tf_op jit(solution)/shard_map/ppermute | solution.py:267
  68.0 9.4 %collective-permute-start.15 = (bf16[2,256,128]{2,1,0:T(8,128)(2,1)S(1)}, bf16[2,256,128]{2,1,0:T(8,128)(2,1)S(1)}, u32[]{:S(2)}, u32[]{:S(2)}) collective-permute-start(bf16[2,256,128]{2,1,0:T(8,128)(2,1)S(1)} %collective-permute-done.14.refs_2_), channel_id=1, source_target_pairs={{0,4},{4,0},{8,12},{12,8},{16,20},{20,16},{24,28},{28,24},{1,5},{5... | collective-permute-start | bytes 393224 | tf_op jit(solution)/shard_map/ppermute | solution.py:267
  74.5 5.0 %collective-permute-start.17 = (bf16[2,256,128]{2,1,0:T(8,128)(2,1)S(1)}, bf16[2,256,128]{2,1,0:T(8,128)(2,1)S(1)}, u32[]{:S(2)}, u32[]{:S(2)}) collective-permute-start(bf16[2,256,128]{2,1,0:T(8,128)(2,1)S(1)} %collective-permute-done.16.refs_4_), channel_id=1, source_target_pairs={{0,4},{4,0},{8,12},{12,8},{16,20},{20,16},{24,28},{28,24},{1,5},{5... | collective-permute-start | bytes 393224 | tf_op jit(solution)/shard_map/ppermute | solution.py:267
  76.0 5.0 %collective-permute-start.19 = (bf16[2,256,128]{2,1,0:T(8,128)(2,1)S(1)}, bf16[2,256,128]{2,1,0:T(8,128)(2,1)S(1)}, u32[]{:S(2)}, u32[]{:S(2)}) collective-permute-start(bf16[2,256,128]{2,1,0:T(8,128)(2,1)S(1)} %collective-permute-done.18.refs_6_), channel_id=1, source_target_pairs={{0,4},{4,0},{8,12},{12,8},{16,20},{20,16},{24,28},{28,24},{1,5},{5... | collective-permute-start | bytes 393224 | tf_op jit(solution)/shard_map/ppermute | solution.py:267
  (2 other events, 1.3 us)

commit v7 on v1

--- a/solution.py
+++ b/solution.py
@@ -18,13 +18,14 @@
 COLS = (((1,), (1,)), ((), ()))
 
 
-def call(body, outs, ins, scratch=(), flops=0, moved=0, vmem=16, out="v"):
+def call(body, outs, ins, scratch=(), flops=0, moved=0, vmem=16, out="v", aliases=None):
     return pl.pallas_call(
         body,
         out_shape=outs,
         in_specs=[SPECS[spec] for spec, _ in ins],
         out_specs=jax.tree.map(lambda _: SPECS[out], outs),
         scratch_shapes=list(scratch),
+        input_output_aliases=aliases or {},
         compiler_params=pltpu.CompilerParams(vmem_limit_bytes=vmem * 1024 * 1024),
         cost_estimate=pl.CostEstimate(flops=flops, bytes_accessed=moved, transcendentals=0),
     )(*[array for _, array in ins])
@@ -244,15 +245,15 @@
     out_ref[...] = (total * scale).astype(BF16)
 
 
-def place_body(dom_ref, *refs):
-    blocks, outs, sems = refs[:-3], refs[-3:-1], refs[-1]
+def place_body(offsets, dom_ref, *refs):
+    blocks, outs, sems = refs[:len(offsets)], refs[-3:-1], refs[-1]
+    lanes = blocks[0].shape[2]
     copies = []
-    lanes = blocks[0].shape[2]
-    for offset, block in enumerate(blocks):
+    for offset, block in zip(offsets, blocks):
         at = block_rows(dom_ref[0], offset, lanes)
         for k, out_ref in enumerate(outs):
             copies.append(
-                pltpu.make_async_copy(block.at[k], out_ref.at[:, at], sems.at[2 * offset + k])
+                pltpu.make_async_copy(block.at[k], out_ref.at[:, at], sems.at[len(copies)])
             )
             copies[-1].start()
     for copy in copies:
@@ -406,11 +407,15 @@
         flops=2 * mirrors * rows * cols, moved=700_000,
     )
     if split:
-        out_self, out_neigh = call(
-            place_body, (struct((rows, width), BF16), struct((rows, width), BF16)),
-            [("s", dom)] + [("v", part) for part in pieces],
-            scratch=[pltpu.SemaphoreType.DMA((2 * peers,))], moved=2_000_000, out="h",
-        )
+        outs = ()
+        for offsets in ((0, 1, 2, 4), (3, 5, 6, 7)):
+            outs = call(
+                functools.partial(place_body, offsets), (struct((rows, width), BF16),) * 2,
+                [("s", dom)] + [("v", pieces[k]) for k in offsets] + [("h", out) for out in outs],
+                scratch=[pltpu.SemaphoreType.DMA((2 * len(offsets),))], moved=1_000_000, out="h",
+                aliases={len(offsets) + 1 + k: k for k in range(len(outs))},
+            )
+        out_self, out_neigh = outs
     else:
         piece = cols // peers
         partial = call(

time: 80.6 us -> 80.4 us (level)
    ppermute x20, waiting for transfers between devices: 35.2 us -> 34.3 us  [swap(): lax.ppermute(array, axis, [(i, i ^ offset) for i in range(lax.axis_size(a...]
    pallas_call x11 -> x12, Pallas kernels: 9.18 us -> 9.79 us  [call(): pl.pallas_call(body, out_shape=outs, in_specs=[SPECS[spec] for spec, _ in...]
  transfers between devices with their start and end apart: 22 -> 22, of which waited for: 13 -> 13; matrix products, arithmetic and copies ran while one was open for 0% -> 0% of each run, Pallas kernels for 4% -> 5%
where the time goes in v7:
time: 80.4 us; the launch traced here: 80 us
  waiting for transfers between devices  35.7 us (44%)
  starting transfers between devices  31.1 us (39%)
  Pallas kernels  9.79 us (12%)
  local copies, waits for them, and re-layouts  2.68 us (3%)
    ppermute x20, waiting for transfers between devices, swap(): lax.ppermute(array, axis, [(i, i ^ offset) for i in range(lax.axis_size(a...  34.3 us
    ppermute x20, starting transfers between devices, swap(): lax.ppermute(array, axis, [(i, i ^ offset) for i in range(lax.axis_size(a...  20 us
    all_to_all x2, starting transfers between devices, exchange(): lax.all_to_all(array.reshape(peers, slots, cols), 'dom', split_axis=0, co...  11.1 us
    pallas_call x12, Pallas kernels, call(): pl.pallas_call(body, out_shape=outs, in_specs=[SPECS[spec] for spec, _ in...  9.79 us
    unnamed x16, local copies, waits for them, and re-layouts  2.68 us
  transfers between devices with their start and end apart: 22, of which 13 were waited for; matrix products, arithmetic and copies ran while one was open for 0% of the time, Pallas kernels for 5%

profile of v7, /device:TPU:0, one launch (start us, length us, event | category | flops | bytes accessed | tf_op | source)
XLA Modules:
  0.0 80.0 jit_solution(16181315145607560767)
XLA Ops:
  0.6 2.1 %shard_map.120 = (bf16[256,512]{1,0:T(8,128)(2,1)}, bf16[512,256]{1,0:T(8,128)(2,1)}) custom-call(s32[8]{0:T(128)} %count_hbm.1, s32[8,64]{1,0:T(8,128)} %list_hbm.1, bf16[256,256]{1,0:T(8,128)(2,1)} %refs_0_.1), custom_call_target="tpu_custom_call" | custom-call | flops 67108864 | bytes 600000 | tf_op jit(solution)/shard_map/pallas_call | solution.py:22
  2.8 7.4 %all-to-all-start = ((bf16[8,64,256]{2,1,0:T(8,128)(2,1)}), bf16[8,64,256]{2,1,0:T(8,128)(2,1)S(1)}, u32[]{:S(2)}, u32[]{:S(2)}) async-start(bf16[8,64,256]{2,1,0:T(8,128)(2,1)} %bitcast.8), calls=%async_computation | async-start | bytes 524288 | tf_op jit(solution)/shard_map/all_to_all | solution.py:304
  10.2 2.0 %collective-permute-start = (bf16[256,256]{1,0:T(8,128)(2,1)S(1)}, bf16[256,256]{1,0:T(8,128)(2,1)S(1)}, u32[]{:S(2)}, u32[]{:S(2)}) collective-permute-start(bf16[256,256]{1,0:T(8,128)(2,1)S(1)} %copy-done.4), channel_id=1, source_target_pairs={{0,4},{4,0},{8,12},{12,8},{16,20},{20,16},{24,28},{28,24},{1,5},{5... | collective-permute-start | bytes 393224 | tf_op jit(solution)/shard_map/ppermute | solution.py:268
  12.9 1.0 %copy-done.1 = bf16[256,1024]{1,0:T(8,128)(2,1)S(1)} copy-done((bf16[256,1024]{1,0:T(8,128)(2,1)S(1)}, bf16[256,1024]{1,0:T(8,128)(2,1)}, u32[]{:S(2)}) %copy-start.1) | copy-done | bytes 524312
  14.0 0.9 %copy-done.3 = bf16[8,128,128]{2,1,0:T(8,128)(2,1)S(1)} copy-done((bf16[8,128,128]{2,1,0:T(8,128)(2,1)S(1)}, bf16[8,128,128]{2,1,0:T(8,128)(2,1)}, u32[]{:S(2)}) %copy-start.3) | copy-done | bytes 262168
  14.9 0.9 %shard_map.121 = (bf16[256,768]{1,0:T(8,128)(2,1)S(1)}, bf16[256,768]{1,0:T(8,128)(2,1)S(1)}, f32[256,128]{1,0:T(8,128)S(1)}, bf16[256,1024]{1,0:T(8,128)(2,1)S(1)}, bf16[256,1024]{1,0:T(8,128)(2,1)S(1)}) custom-call(s32[8]{0:T(128)S(1)} %copy-done.6, s32[8]{0:T(128)S(1)} %copy-done.7, bf16[8,128,128]{2,1,0:T(8,128)(2,1)S(1)} %copy-done.3, ...), custom_call_target="tpu_custom_call" | custom-call | flops 1000000 | bytes 3000000 | tf_op jit(solution)/shard_map/pallas_call | solution.py:22
  15.9 2.0 %collective-permute-done.refs_1_ = bf16[256,256]{1,0:T(8,128)(2,1)S(1)} collective-permute-done((bf16[256,256]{1,0:T(8,128)(2,1)S(1)}, bf16[256,256]{1,0:T(8,128)(2,1)S(1)}, u32[]{:S(2)}, u32[]{:S(2)}) %collective-permute-start) | collective-permute-done | bytes 131104 | tf_op jit(solution)/shard_map/ppermute | solution.py:268
  17.8 1.3 %all-to-all-done = bf16[8,64,256]{2,1,0:T(8,128)(2,1)S(1)} async-done(((bf16[8,64,256]{2,1,0:T(8,128)(2,1)}), bf16[8,64,256]{2,1,0:T(8,128)(2,1)S(1)}, u32[]{:S(2)}, u32[]{:S(2)}) %all-to-all-start) | async-done | bytes 262176 | tf_op jit(solution)/shard_map/all_to_all | solution.py:304
  19.1 1.0 %shard_map.122 = (f32[256,256]{1,0:T(8,128)S(1)}, bf16[256,256]{1,0:T(8,128)(2,1)S(1)}, f32[256,256]{1,0:T(8,128)S(1)}, bf16[2,256,256]{2,1,0:T(8,128)(2,1)S(1)}) custom-call(s32[1]{0:T(128)} %bitcast.1.rep_ref, bf16[256,256]{1,0:T(8,128)(2,1)S(1)} %copy-done.4, bf16[512,256]{1,0:T(8,128)(2,1)S(1)} %bitcast.7, ...), custom_call_target="tpu_custom_call" | custom-call | flops 600000000 | bytes 3000000 | tf_op jit(solution)/shard_map/pallas_call | solution.py:22
  20.2 1.5 %collective-permute-start.1 = (bf16[256,256]{1,0:T(8,128)(2,1)S(1)}, bf16[256,256]{1,0:T(8,128)(2,1)S(1)}, u32[]{:S(2)}, u32[]{:S(2)}) collective-permute-start(bf16[256,256]{1,0:T(8,128)(2,1)S(1)} %get-tuple-element.49.refs_2_), channel_id=1, source_target_pairs={{0,4},{4,0},{8,12},{12,8},{16,20},{20,16},{24,28},{28,24},{1,5},{5... | collective-permute-start | bytes 393224 | tf_op jit(solution)/shard_map/ppermute | solution.py:268
  21.7 1.6 %collective-permute-start.3 = (bf16[256,256]{1,0:T(8,128)(2,1)S(1)}, bf16[256,256]{1,0:T(8,128)(2,1)S(1)}, u32[]{:S(2)}, u32[]{:S(2)}) collective-permute-start(bf16[256,256]{1,0:T(8,128)(2,1)S(1)} %shard_map.123), channel_id=1, source_target_pairs={{0,2},{1,3},{2,0},{3,1},{4,6},{5,7},{6,4},{7,5},{8,10},{9,11},{10,... | collective-permute-start | bytes 393224 | tf_op jit(solution)/shard_map/ppermute | solution.py:268
  23.3 2.8 %collective-permute-done.1.refs_3_ = bf16[256,256]{1,0:T(8,128)(2,1)S(1)} collective-permute-done((bf16[256,256]{1,0:T(8,128)(2,1)S(1)}, bf16[256,256]{1,0:T(8,128)(2,1)S(1)}, u32[]{:S(2)}, u32[]{:S(2)}) %collective-permute-start.1) | collective-permute-done | bytes 131104 | tf_op jit(solution)/shard_map/ppermute | solution.py:268
  26.1 1.2 %collective-permute-done.3.across_ref = bf16[256,256]{1,0:T(8,128)(2,1)S(1)} collective-permute-done((bf16[256,256]{1,0:T(8,128)(2,1)S(1)}, bf16[256,256]{1,0:T(8,128)(2,1)S(1)}, u32[]{:S(2)}, u32[]{:S(2)}) %collective-permute-start.3) | collective-permute-done | bytes 131104 | tf_op jit(solution)/shard_map/ppermute | solution.py:268
  28.1 1.5 %collective-permute-start.5 = (bf16[256,256]{1,0:T(8,128)(2,1)S(1)}, bf16[256,256]{1,0:T(8,128)(2,1)S(1)}, u32[]{:S(2)}, u32[]{:S(2)}) collective-permute-start(bf16[256,256]{1,0:T(8,128)(2,1)S(1)} %get-tuple-element.55.refs_0_.refs_4_), channel_id=1, source_target_pairs={{0,2},{1,3},{2,0},{3,1},{4,6},{5,7},{6,4},{7,5},{8,10},{9,11},{10,... | collective-permute-start | bytes 393224 | tf_op jit(solution)/shard_map/ppermute | solution.py:268
  29.6 1.4 %collective-permute-start.7 = (bf16[256,128]{1,0:T(8,128)(2,1)S(1)}, bf16[256,128]{1,0:T(8,128)(2,1)S(1)}, u32[]{:S(2)}, u32[]{:S(2)}) collective-permute-start(bf16[256,128]{1,0:T(8,128)(2,1)S(1)} %get-tuple-element.60), channel_id=1, source_target_pairs={{0,4},{4,0},{8,12},{12,8},{16,20},{20,16},{24,28},{28,24},{1,5},{5... | collective-permute-start | bytes 196616 | tf_op jit(solution)/shard_map/ppermute | solution.py:268
  31.0 2.9 %collective-permute-done.7.refs_8_ = bf16[256,128]{1,0:T(8,128)(2,1)S(1)} collective-permute-done((bf16[256,128]{1,0:T(8,128)(2,1)S(1)}, bf16[256,128]{1,0:T(8,128)(2,1)S(1)}, u32[]{:S(2)}, u32[]{:S(2)}) %collective-permute-start.7) | collective-permute-done | bytes 65568 | tf_op jit(solution)/shard_map/ppermute | solution.py:268
  34.9 3.2 %collective-permute-done.9.refs_10_ = bf16[256,128]{1,0:T(8,128)(2,1)S(1)} collective-permute-done((bf16[256,128]{1,0:T(8,128)(2,1)S(1)}, bf16[256,128]{1,0:T(8,128)(2,1)S(1)}, u32[]{:S(2)}, u32[]{:S(2)}) %collective-permute-start.9) | collective-permute-done | bytes 65568 | tf_op jit(solution)/shard_map/ppermute | solution.py:268
  38.1 1.2 %collective-permute-done.10.refs_11_ = bf16[256,128]{1,0:T(8,128)(2,1)S(1)} collective-permute-done((bf16[256,128]{1,0:T(8,128)(2,1)S(1)}, bf16[256,128]{1,0:T(8,128)(2,1)S(1)}, u32[]{:S(2)}, u32[]{:S(2)}) %collective-permute-start.10) | collective-permute-done | bytes 65568 | tf_op jit(solution)/shard_map/ppermute | solution.py:268
  40.2 1.1 %collective-permute-start.11 = (bf16[2,2,256,128]{3,2,1,0:T(8,128)(2,1)S(1)}, bf16[2,2,256,128]{3,2,1,0:T(8,128)(2,1)S(1)}, u32[]{:S(2)}, u32[]{:S(2)}) collective-permute-start(bf16[2,2,256,128]{3,2,1,0:T(8,128)(2,1)S(1)} %get-tuple-element.62), channel_id=1, source_target_pairs={{0,8},{4,12},{8,0},{12,4},{16,24},{20,28},{24,16},{28,20},{1,9},{5... | collective-permute-start | bytes 786440 | tf_op jit(solution)/shard_map/ppermute | solution.py:268
  41.3 7.3 %collective-permute-done.11.beside_ref.next_ref = bf16[2,2,256,128]{3,2,1,0:T(8,128)(2,1)S(1)} collective-permute-done((bf16[2,2,256,128]{3,2,1,0:T(8,128)(2,1)S(1)}, bf16[2,2,256,128]{3,2,1,0:T(8,128)(2,1)S(1)}, u32[]{:S(2)}, u32[]{:S(2)}) %collective-permute-start.11) | collective-permute-done | bytes 262176 | tf_op jit(solution)/shard_map/ppermute | solution.py:268
  48.6 1.5 %collective-permute-start.12 = (bf16[2,256,128]{2,1,0:T(8,128)(2,1)S(1)}, bf16[2,256,128]{2,1,0:T(8,128)(2,1)S(1)}, u32[]{:S(2)}, u32[]{:S(2)}) collective-permute-start(bf16[2,256,128]{2,1,0:T(8,128)(2,1)S(1)} %shard_map.128), channel_id=1, source_target_pairs={{0,16},{4,20},{8,24},{12,28},{16,0},{20,4},{24,8},{28,12},{1,17},{... | collective-permute-start | bytes 393224 | tf_op jit(solution)/shard_map/ppermute | solution.py:268
  50.1 1.5 %shard_map.125 = (f32[256,256]{1,0:T(8,128)S(1)}, bf16[512,256]{1,0:T(8,128)(2,1)}) custom-call(s32[1]{0:T(128)} %bitcast.1.rep_ref, bf16[256,768]{1,0:T(8,128)(2,1)S(1)} %get-tuple-element.43.high_ref, bf16[256,768]{1,0:T(8,128)(2,1)S(1)} %get-tuple-element.44.low_ref, f32[256,128]{1,0:T(8,128)S(1)} %get-tuple-element.45.deg_ref, ...), custom_call_target="tpu_custom_call" | custom-call | flops 600000000 | bytes 3000000 | tf_op jit(solution)/shard_map/pallas_call | solution.py:22
  51.6 3.6 %all-to-all-start.1 = ((bf16[8,64,256]{2,1,0:T(8,128)(2,1)}), bf16[8,64,256]{2,1,0:T(8,128)(2,1)S(1)}, u32[]{:S(2)}, u32[]{:S(2)}) async-start(bf16[8,64,256]{2,1,0:T(8,128)(2,1)} %bitcast.4), calls=%async_computation.1 | async-start | bytes 524288 | tf_op jit(solution)/shard_map/all_to_all | solution.py:304
  55.3 1.9 %collective-permute-done.12.far_ref = bf16[2,256,128]{2,1,0:T(8,128)(2,1)S(1)} collective-permute-done((bf16[2,256,128]{2,1,0:T(8,128)(2,1)S(1)}, bf16[2,256,128]{2,1,0:T(8,128)(2,1)S(1)}, u32[]{:S(2)}, u32[]{:S(2)}) %collective-permute-start.12) | collective-permute-done | bytes 131104 | tf_op jit(solution)/shard_map/ppermute | solution.py:268
  57.2 1.1 %collective-permute-start.15 = (bf16[2,256,128]{2,1,0:T(8,128)(2,1)S(1)}, bf16[2,256,128]{2,1,0:T(8,128)(2,1)S(1)}, u32[]{:S(2)}, u32[]{:S(2)}) collective-permute-start(bf16[2,256,128]{2,1,0:T(8,128)(2,1)S(1)} %shard_map.129.refs_0_), channel_id=1, source_target_pairs={{0,16},{4,20},{8,24},{12,28},{16,0},{20,4},{24,8},{28,12},{1,17},{... | collective-permute-start | bytes 393224 | tf_op jit(solution)/shard_map/ppermute | solution.py:268
  58.3 1.5 %collective-permute-start.16 = (bf16[2,256,128]{2,1,0:T(8,128)(2,1)S(1)}, bf16[2,256,128]{2,1,0:T(8,128)(2,1)S(1)}, u32[]{:S(2)}, u32[]{:S(2)}) collective-permute-start(bf16[2,256,128]{2,1,0:T(8,128)(2,1)S(1)} %shard_map.129.refs_0_), channel_id=1, source_target_pairs={{0,4},{4,0},{8,12},{12,8},{16,20},{20,16},{24,28},{28,24},{1,5},{5... | collective-permute-start | bytes 393224 | tf_op jit(solution)/shard_map/ppermute | solution.py:268
  59.8 2.4 %collective-permute-start.13 = (bf16[2,256,128]{2,1,0:T(8,128)(2,1)S(1)}, bf16[2,256,128]{2,1,0:T(8,128)(2,1)S(1)}, u32[]{:S(2)}, u32[]{:S(2)}) collective-permute-start(bf16[2,256,128]{2,1,0:T(8,128)(2,1)S(1)} %shard_map.129.refs_0_), channel_id=1, source_target_pairs={{0,8},{4,12},{8,0},{12,4},{16,24},{20,28},{24,16},{28,20},{1,9},{5... | collective-permute-start | bytes 393224 | tf_op jit(solution)/shard_map/ppermute | solution.py:268
  62.2 7.0 %collective-permute-done.15.refs_3_ = bf16[2,256,128]{2,1,0:T(8,128)(2,1)S(1)} collective-permute-done((bf16[2,256,128]{2,1,0:T(8,128)(2,1)S(1)}, bf16[2,256,128]{2,1,0:T(8,128)(2,1)S(1)}, u32[]{:S(2)}, u32[]{:S(2)}) %collective-permute-start.15) | collective-permute-done | bytes 131104 | tf_op jit(solution)/shard_map/ppermute | solution.py:268
  69.2 1.4 %collective-permute-start.17 = (bf16[2,256,128]{2,1,0:T(8,128)(2,1)S(1)}, bf16[2,256,128]{2,1,0:T(8,128)(2,1)S(1)}, u32[]{:S(2)}, u32[]{:S(2)}) collective-permute-start(bf16[2,256,128]{2,1,0:T(8,128)(2,1)S(1)} %collective-permute-done.15.refs_3_), channel_id=1, source_target_pairs={{0,4},{4,0},{8,12},{12,8},{16,20},{20,16},{24,28},{28,24},{1,5},{5... | collective-permute-start | bytes 393224 | tf_op jit(solution)/shard_map/ppermute | solution.py:268
  71.2 2.9 %collective-permute-done.18.refs_2_ = bf16[2,256,128]{2,1,0:T(8,128)(2,1)S(1)} collective-permute-done((bf16[2,256,128]{2,1,0:T(8,128)(2,1)S(1)}, bf16[2,256,128]{2,1,0:T(8,128)(2,1)S(1)}, u32[]{:S(2)}, u32[]{:S(2)}) %collective-permute-start.18) | collective-permute-done | bytes 131104 | tf_op jit(solution)/shard_map/ppermute | solution.py:268
  74.1 1.4 %collective-permute-start.19 = (bf16[2,256,128]{2,1,0:T(8,128)(2,1)S(1)}, bf16[2,256,128]{2,1,0:T(8,128)(2,1)S(1)}, u32[]{:S(2)}, u32[]{:S(2)}) collective-permute-start(bf16[2,256,128]{2,1,0:T(8,128)(2,1)S(1)} %collective-permute-done.18.refs_2_), channel_id=1, source_target_pairs={{0,4},{4,0},{8,12},{12,8},{16,20},{20,16},{24,28},{28,24},{1,5},{5... | collective-permute-start | bytes 393224 | tf_op jit(solution)/shard_map/ppermute | solution.py:268
  77.5 1.6 %collective-permute-done.19.refs_3_ = bf16[2,256,128]{2,1,0:T(8,128)(2,1)S(1)} collective-permute-done((bf16[2,256,128]{2,1,0:T(8,128)(2,1)S(1)}, bf16[2,256,128]{2,1,0:T(8,128)(2,1)S(1)}, u32[]{:S(2)}, u32[]{:S(2)}) %collective-permute-start.19) | collective-permute-done | bytes 131104 | tf_op jit(solution)/shard_map/ppermute | solution.py:268
  (40 shorter events, 7.0 us)
Async XLA Ops:
  0.6 11.6 %copy-start = (bf16[256,1024]{1,0:T(8,128)(2,1)S(1)}, bf16[256,1024]{1,0:T(8,128)(2,1)}, u32[]{:S(2)}) copy-start(bf16[256,1024]{1,0:T(8,128)(2,1)} %self_hbm) | copy-start | bytes 1572868
  2.8 7.4 %copy-start.4 = (bf16[256,256]{1,0:T(8,128)(2,1)S(1)}, bf16[256,256]{1,0:T(8,128)(2,1)}, u32[]{:S(2)}) copy-start(bf16[256,256]{1,0:T(8,128)(2,1)} %refs_0_.1) | copy-start | bytes 393220
  2.8 16.3 %all-to-all-start = ((bf16[8,64,256]{2,1,0:T(8,128)(2,1)}), bf16[8,64,256]{2,1,0:T(8,128)(2,1)S(1)}, u32[]{:S(2)}, u32[]{:S(2)}) async-start(bf16[8,64,256]{2,1,0:T(8,128)(2,1)} %bitcast.8), calls=%async_computation | async-start | bytes 524288 | tf_op jit(solution)/shard_map/all_to_all | solution.py:304
  10.2 7.6 %collective-permute-start = (bf16[256,256]{1,0:T(8,128)(2,1)S(1)}, bf16[256,256]{1,0:T(8,128)(2,1)S(1)}, u32[]{:S(2)}, u32[]{:S(2)}) collective-permute-start(bf16[256,256]{1,0:T(8,128)(2,1)S(1)} %copy-done.4), channel_id=1, source_target_pairs={{0,4},{4,0},{8,12},{12,8},{16,20},{20,16},{24,28},{28,24},{1,5},{5... | collective-permute-start | bytes 393224 | tf_op jit(solution)/shard_map/ppermute | solution.py:268
  12.2 0.7 copy-start.6
  12.2 0.7 copy-start.7
  12.9 1.0 %copy-start.1 = (bf16[256,1024]{1,0:T(8,128)(2,1)S(1)}, bf16[256,1024]{1,0:T(8,128)(2,1)}, u32[]{:S(2)}) copy-start(bf16[256,1024]{1,0:T(8,128)(2,1)} %neigh_hbm) | copy-start | bytes 1572868
  14.0 0.9 %copy-start.3 = (bf16[8,128,128]{2,1,0:T(8,128)(2,1)S(1)}, bf16[8,128,128]{2,1,0:T(8,128)(2,1)}, u32[]{:S(2)}) copy-start(bf16[8,128,128]{2,1,0:T(8,128)(2,1)} %tiles_ref) | copy-start | bytes 786436
  20.1 1.6 %collective-permute-start.2 = (bf16[2,256,256]{2,1,0:T(8,128)(2,1)S(1)}, bf16[2,256,256]{2,1,0:T(8,128)(2,1)S(1)}, u32[]{:S(2)}, u32[]{:S(2)}) collective-permute-start(bf16[2,256,256]{2,1,0:T(8,128)(2,1)S(1)} %get-tuple-element.51), channel_id=1, source_target_pairs={{0,1},{1,0},{2,3},{3,2},{4,5},{5,4},{6,7},{7,6},{8,9},{9,8},{10,11... | collective-permute-start | bytes 786440 | tf_op jit(solution)/shard_map/ppermute | solution.py:268
  20.2 5.9 %collective-permute-start.1 = (bf16[256,256]{1,0:T(8,128)(2,1)S(1)}, bf16[256,256]{1,0:T(8,128)(2,1)S(1)}, u32[]{:S(2)}, u32[]{:S(2)}) collective-permute-start(bf16[256,256]{1,0:T(8,128)(2,1)S(1)} %get-tuple-element.49.refs_2_), channel_id=1, source_target_pairs={{0,4},{4,0},{8,12},{12,8},{16,20},{20,16},{24,28},{28,24},{1,5},{5... | collective-permute-start | bytes 393224 | tf_op jit(solution)/shard_map/ppermute | solution.py:268
  21.7 5.6 %copy-start.5 = (bf16[256,256]{1,0:T(8,128)(2,1)S(1)}, bf16[256,256]{1,0:T(8,128)(2,1)}, u32[]{:S(2)}) copy-start(bf16[256,256]{1,0:T(8,128)(2,1)} %gout_ref) | copy-start | bytes 393220
  21.7 5.6 %collective-permute-start.3 = (bf16[256,256]{1,0:T(8,128)(2,1)S(1)}, bf16[256,256]{1,0:T(8,128)(2,1)S(1)}, u32[]{:S(2)}, u32[]{:S(2)}) collective-permute-start(bf16[256,256]{1,0:T(8,128)(2,1)S(1)} %shard_map.123), channel_id=1, source_target_pairs={{0,2},{1,3},{2,0},{3,1},{4,6},{5,7},{6,4},{7,5},{8,10},{9,11},{10,... | collective-permute-start | bytes 393224 | tf_op jit(solution)/shard_map/ppermute | solution.py:268
  28.1 6.3 %collective-permute-start.5 = (bf16[256,256]{1,0:T(8,128)(2,1)S(1)}, bf16[256,256]{1,0:T(8,128)(2,1)S(1)}, u32[]{:S(2)}, u32[]{:S(2)}) collective-permute-start(bf16[256,256]{1,0:T(8,128)(2,1)S(1)} %get-tuple-element.55.refs_0_.refs_4_), channel_id=1, source_target_pairs={{0,2},{1,3},{2,0},{3,1},{4,6},{5,7},{6,4},{7,5},{8,10},{9,11},{10,... | collective-permute-start | bytes 393224 | tf_op jit(solution)/shard_map/ppermute | solution.py:268
  29.6 4.3 %collective-permute-start.7 = (bf16[256,128]{1,0:T(8,128)(2,1)S(1)}, bf16[256,128]{1,0:T(8,128)(2,1)S(1)}, u32[]{:S(2)}, u32[]{:S(2)}) collective-permute-start(bf16[256,128]{1,0:T(8,128)(2,1)S(1)} %get-tuple-element.60), channel_id=1, source_target_pairs={{0,4},{4,0},{8,12},{12,8},{16,20},{20,16},{24,28},{28,24},{1,5},{5... | collective-permute-start | bytes 196616 | tf_op jit(solution)/shard_map/ppermute | solution.py:268
  31.0 7.1 %collective-permute-start.4 = (bf16[256,256]{1,0:T(8,128)(2,1)S(1)}, bf16[256,256]{1,0:T(8,128)(2,1)S(1)}, u32[]{:S(2)}, u32[]{:S(2)}) collective-permute-start(bf16[256,256]{1,0:T(8,128)(2,1)S(1)} %get-tuple-element.55.refs_0_.refs_4_), channel_id=1, source_target_pairs={{0,1},{1,0},{2,3},{3,2},{4,5},{5,4},{6,7},{7,6},{8,9},{9,8},{10,11... | collective-permute-start | bytes 393224 | tf_op jit(solution)/shard_map/ppermute | solution.py:268
  33.9 4.3 %collective-permute-start.9 = (bf16[256,128]{1,0:T(8,128)(2,1)S(1)}, bf16[256,128]{1,0:T(8,128)(2,1)S(1)}, u32[]{:S(2)}, u32[]{:S(2)}) collective-permute-start(bf16[256,128]{1,0:T(8,128)(2,1)S(1)} %collective-permute-done.7.refs_8_), channel_id=1, source_target_pairs={{0,2},{1,3},{2,0},{3,1},{4,6},{5,7},{6,4},{7,5},{8,10},{9,11},{10,... | collective-permute-start | bytes 196616 | tf_op jit(solution)/shard_map/ppermute | solution.py:268
  34.4 5.0 %collective-permute-start.6 = (bf16[256,256]{1,0:T(8,128)(2,1)S(1)}, bf16[256,256]{1,0:T(8,128)(2,1)S(1)}, u32[]{:S(2)}, u32[]{:S(2)}) collective-permute-start(bf16[256,256]{1,0:T(8,128)(2,1)S(1)} %collective-permute-done.5.refs_2_.refs_6_), channel_id=1, source_target_pairs={{0,1},{1,0},{2,3},{3,2},{4,5},{5,4},{6,7},{7,6},{8,9},{9,8},{10,11... | collective-permute-start | bytes 393224 | tf_op jit(solution)/shard_map/ppermute | solution.py:268
  34.4 3.7 %collective-permute-start.8 = (bf16[256,128]{1,0:T(8,128)(2,1)S(1)}, bf16[256,128]{1,0:T(8,128)(2,1)S(1)}, u32[]{:S(2)}, u32[]{:S(2)}) collective-permute-start(bf16[256,128]{1,0:T(8,128)(2,1)S(1)} %collective-permute-done.7.refs_8_), channel_id=1, source_target_pairs={{0,1},{1,0},{2,3},{3,2},{4,5},{5,4},{6,7},{7,6},{8,9},{9,8},{10,11... | collective-permute-start | bytes 196616 | tf_op jit(solution)/shard_map/ppermute | solution.py:268
  38.1 1.3 %collective-permute-start.10 = (bf16[256,128]{1,0:T(8,128)(2,1)S(1)}, bf16[256,128]{1,0:T(8,128)(2,1)S(1)}, u32[]{:S(2)}, u32[]{:S(2)}) collective-permute-start(bf16[256,128]{1,0:T(8,128)(2,1)S(1)} %collective-permute-done.9.refs_10_), channel_id=1, source_target_pairs={{0,1},{1,0},{2,3},{3,2},{4,5},{5,4},{6,7},{7,6},{8,9},{9,8},{10,11... | collective-permute-start | bytes 196616 | tf_op jit(solution)/shard_map/ppermute | solution.py:268
  40.2 8.4 %collective-permute-start.11 = (bf16[2,2,256,128]{3,2,1,0:T(8,128)(2,1)S(1)}, bf16[2,2,256,128]{3,2,1,0:T(8,128)(2,1)S(1)}, u32[]{:S(2)}, u32[]{:S(2)}) collective-permute-start(bf16[2,2,256,128]{3,2,1,0:T(8,128)(2,1)S(1)} %get-tuple-element.62), channel_id=1, source_target_pairs={{0,8},{4,12},{8,0},{12,4},{16,24},{20,28},{24,16},{28,20},{1,9},{5... | collective-permute-start | bytes 786440 | tf_op jit(solution)/shard_map/ppermute | solution.py:268
  48.6 8.5 %collective-permute-start.12 = (bf16[2,256,128]{2,1,0:T(8,128)(2,1)S(1)}, bf16[2,256,128]{2,1,0:T(8,128)(2,1)S(1)}, u32[]{:S(2)}, u32[]{:S(2)}) collective-permute-start(bf16[2,256,128]{2,1,0:T(8,128)(2,1)S(1)} %shard_map.128), channel_id=1, source_target_pairs={{0,16},{4,20},{8,24},{12,28},{16,0},{20,4},{24,8},{28,12},{1,17},{... | collective-permute-start | bytes 393224 | tf_op jit(solution)/shard_map/ppermute | solution.py:268
  51.6 23.9 %all-to-all-start.1 = ((bf16[8,64,256]{2,1,0:T(8,128)(2,1)}), bf16[8,64,256]{2,1,0:T(8,128)(2,1)S(1)}, u32[]{:S(2)}, u32[]{:S(2)}) async-start(bf16[8,64,256]{2,1,0:T(8,128)(2,1)} %bitcast.4), calls=%async_computation.1 | async-start | bytes 524288 | tf_op jit(solution)/shard_map/all_to_all | solution.py:304
  57.2 18.4 %copy-start.2 = (bf16[256,512]{1,0:T(8,128)(2,1)S(1)}, bf16[256,512]{1,0:T(8,128)(2,1)}, u32[]{:S(2)}) copy-start(bf16[256,512]{1,0:T(8,128)(2,1)} %get-tuple-element.54.onehot_ref) | copy-start | bytes 786436
  57.2 12.0 %collective-permute-start.15 = (bf16[2,256,128]{2,1,0:T(8,128)(2,1)S(1)}, bf16[2,256,128]{2,1,0:T(8,128)(2,1)S(1)}, u32[]{:S(2)}, u32[]{:S(2)}) collective-permute-start(bf16[2,256,128]{2,1,0:T(8,128)(2,1)S(1)} %shard_map.129.refs_0_), channel_id=1, source_target_pairs={{0,16},{4,20},{8,24},{12,28},{16,0},{20,4},{24,8},{28,12},{1,17},{... | collective-permute-start | bytes 393224 | tf_op jit(solution)/shard_map/ppermute | solution.py:268
  58.3 10.8 %collective-permute-start.16 = (bf16[2,256,128]{2,1,0:T(8,128)(2,1)S(1)}, bf16[2,256,128]{2,1,0:T(8,128)(2,1)S(1)}, u32[]{:S(2)}, u32[]{:S(2)}) collective-permute-start(bf16[2,256,128]{2,1,0:T(8,128)(2,1)S(1)} %shard_map.129.refs_0_), channel_id=1, source_target_pairs={{0,4},{4,0},{8,12},{12,8},{16,20},{20,16},{24,28},{28,24},{1,5},{5... | collective-permute-start | bytes 393224 | tf_op jit(solution)/shard_map/ppermute | solution.py:268
  59.8 10.8 %collective-permute-start.13 = (bf16[2,256,128]{2,1,0:T(8,128)(2,1)S(1)}, bf16[2,256,128]{2,1,0:T(8,128)(2,1)S(1)}, u32[]{:S(2)}, u32[]{:S(2)}) collective-permute-start(bf16[2,256,128]{2,1,0:T(8,128)(2,1)S(1)} %shard_map.129.refs_0_), channel_id=1, source_target_pairs={{0,8},{4,12},{8,0},{12,4},{16,24},{20,28},{24,16},{28,20},{1,9},{5... | collective-permute-start | bytes 393224 | tf_op jit(solution)/shard_map/ppermute | solution.py:268
  69.2 5.0 %collective-permute-start.18 = (bf16[2,256,128]{2,1,0:T(8,128)(2,1)S(1)}, bf16[2,256,128]{2,1,0:T(8,128)(2,1)S(1)}, u32[]{:S(2)}, u32[]{:S(2)}) collective-permute-start(bf16[2,256,128]{2,1,0:T(8,128)(2,1)S(1)} %collective-permute-done.15.refs_3_), channel_id=1, source_target_pairs={{0,8},{4,12},{8,0},{12,4},{16,24},{20,28},{24,16},{28,20},{1,9},{5... | collective-permute-start | bytes 393224 | tf_op jit(solution)/shard_map/ppermute | solution.py:268
  69.2 8.3 %collective-permute-start.17 = (bf16[2,256,128]{2,1,0:T(8,128)(2,1)S(1)}, bf16[2,256,128]{2,1,0:T(8,128)(2,1)S(1)}, u32[]{:S(2)}, u32[]{:S(2)}) collective-permute-start(bf16[2,256,128]{2,1,0:T(8,128)(2,1)S(1)} %collective-permute-done.15.refs_3_), channel_id=1, source_target_pairs={{0,4},{4,0},{8,12},{12,8},{16,20},{20,16},{24,28},{28,24},{1,5},{5... | collective-permute-start | bytes 393224 | tf_op jit(solution)/shard_map/ppermute | solution.py:268
  70.5 7.0 %collective-permute-start.14 = (bf16[2,256,128]{2,1,0:T(8,128)(2,1)S(1)}, bf16[2,256,128]{2,1,0:T(8,128)(2,1)S(1)}, u32[]{:S(2)}, u32[]{:S(2)}) collective-permute-start(bf16[2,256,128]{2,1,0:T(8,128)(2,1)S(1)} %collective-permute-done.13.refs_2_), channel_id=1, source_target_pairs={{0,4},{4,0},{8,12},{12,8},{16,20},{20,16},{24,28},{28,24},{1,5},{5... | collective-permute-start | bytes 393224 | tf_op jit(solution)/shard_map/ppermute | solution.py:268
  74.1 5.0 %collective-permute-start.19 = (bf16[2,256,128]{2,1,0:T(8,128)(2,1)S(1)}, bf16[2,256,128]{2,1,0:T(8,128)(2,1)S(1)}, u32[]{:S(2)}, u32[]{:S(2)}) collective-permute-start(bf16[2,256,128]{2,1,0:T(8,128)(2,1)S(1)} %collective-permute-done.18.refs_2_), channel_id=1, source_target_pairs={{0,4},{4,0},{8,12},{12,8},{16,20},{20,16},{24,28},{28,24},{1,5},{5... | collective-permute-start | bytes 393224 | tf_op jit(solution)/shard_map/ppermute | solution.py:268

commit v8 on v7

--- a/solution.py
+++ b/solution.py
@@ -276,10 +276,12 @@
 def gather_pieces(array, peers):
     out = {0: array, 4: swap(array, "dom", 4), 2: swap(array, "dom", 2)}
     out[1] = swap(array, "dom", 1)
+    out[3] = swap(out[2], "dom", 1)
     out[4], out[1] = lax.optimization_barrier((out[4], out[1]))
     out[6] = swap(out[4], "dom", 2)
-    for offset in range(2, peers, 2):
-        out[offset + 1] = swap(out[offset], "dom", 1)
+    late, out[3] = lax.optimization_barrier((out[4], out[3]))
+    out[5] = swap(late, "dom", 1)
+    out[7] = swap(out[6], "dom", 1)
     return [out[offset] for offset in range(peers)]
 
 
@@ -408,7 +410,7 @@
     )
     if split:
         outs = ()
-        for offsets in ((0, 1, 2, 4), (3, 5, 6, 7)):
+        for offsets in ((0, 1, 2, 3, 4), (5, 6, 7)):
             outs = call(
                 functools.partial(place_body, offsets), (struct((rows, width), BF16),) * 2,
                 [("s", dom)] + [("v", pieces[k]) for k in offsets] + [("h", out) for out in outs],

time: 80.4 us -> 80.3 us (level)
  waiting for transfers between devices: 35.7 us -> 32.4 us
  starting transfers between devices: 31.1 us -> 34.3 us
    ppermute x20, waiting for transfers between devices: 34.3 us -> 31.1 us  [swap(): lax.ppermute(array, axis, [(i, i ^ offset) for i in range(lax.axis_size(a...]
    ppermute x20, starting transfers between devices: 20 us -> 23.2 us  [swap(): lax.ppermute(array, axis, [(i, i ^ offset) for i in range(lax.axis_size(a...]
  transfers between devices with their start and end apart: 22 -> 22, of which waited for: 13 -> 14; matrix products, arithmetic and copies ran while one was open for 0% -> 0% of each run, Pallas kernels for 5% -> 5%
where the time goes in v8:
time: 80.3 us; the launch traced here: 79.9 us
  starting transfers between devices  34.3 us (43%)
  waiting for transfers between devices  32.4 us (40%)
  Pallas kernels  9.79 us (12%)
  local copies, waits for them, and re-layouts  2.68 us (3%)
    ppermute x20, waiting for transfers between devices, swap(): lax.ppermute(array, axis, [(i, i ^ offset) for i in range(lax.axis_size(a...  31.1 us
    ppermute x20, starting transfers between devices, swap(): lax.ppermute(array, axis, [(i, i ^ offset) for i in range(lax.axis_size(a...  23.2 us
    all_to_all x2, starting transfers between devices, exchange(): lax.all_to_all(array.reshape(peers, slots, cols), 'dom', split_axis=0, co...  11.1 us
    pallas_call x12, Pallas kernels, call(): pl.pallas_call(body, out_shape=outs, in_specs=[SPECS[spec] for spec, _ in...  9.79 us
    unnamed x16, local copies, waits for them, and re-layouts  2.68 us
  transfers between devices with their start and end apart: 22, of which 14 were waited for; matrix products, arithmetic and copies ran while one was open for 0% of the time, Pallas kernels for 5%

profile of v8, /device:TPU:0, one launch (start us, length us, event | category | flops | bytes accessed | tf_op | source)
XLA Modules:
  0.0 79.9 jit_solution(15262764256422535316)
XLA Ops:
  0.6 2.1 %shard_map.120 = (bf16[256,512]{1,0:T(8,128)(2,1)}, bf16[512,256]{1,0:T(8,128)(2,1)}) custom-call(s32[8]{0:T(128)} %count_hbm.1, s32[8,64]{1,0:T(8,128)} %list_hbm.1, bf16[256,256]{1,0:T(8,128)(2,1)} %refs_0_.1), custom_call_target="tpu_custom_call" | custom-call | flops 67108864 | bytes 600000 | tf_op jit(solution)/shard_map/pallas_call | solution.py:22
  2.8 7.4 %all-to-all-start = ((bf16[8,64,256]{2,1,0:T(8,128)(2,1)}), bf16[8,64,256]{2,1,0:T(8,128)(2,1)S(1)}, u32[]{:S(2)}, u32[]{:S(2)}) async-start(bf16[8,64,256]{2,1,0:T(8,128)(2,1)} %bitcast.8), calls=%async_computation | async-start | bytes 524288 | tf_op jit(solution)/shard_map/all_to_all | solution.py:306
  10.2 2.0 %collective-permute-start = (bf16[256,256]{1,0:T(8,128)(2,1)S(1)}, bf16[256,256]{1,0:T(8,128)(2,1)S(1)}, u32[]{:S(2)}, u32[]{:S(2)}) collective-permute-start(bf16[256,256]{1,0:T(8,128)(2,1)S(1)} %copy-done.4), channel_id=1, source_target_pairs={{0,4},{4,0},{8,12},{12,8},{16,20},{20,16},{24,28},{28,24},{1,5},{5... | collective-permute-start | bytes 393224 | tf_op jit(solution)/shard_map/ppermute | solution.py:268
  12.9 1.0 %copy-done.1 = bf16[256,1024]{1,0:T(8,128)(2,1)S(1)} copy-done((bf16[256,1024]{1,0:T(8,128)(2,1)S(1)}, bf16[256,1024]{1,0:T(8,128)(2,1)}, u32[]{:S(2)}) %copy-start.1) | copy-done | bytes 524312
  14.0 0.9 %copy-done.3 = bf16[8,128,128]{2,1,0:T(8,128)(2,1)S(1)} copy-done((bf16[8,128,128]{2,1,0:T(8,128)(2,1)S(1)}, bf16[8,128,128]{2,1,0:T(8,128)(2,1)}, u32[]{:S(2)}) %copy-start.3) | copy-done | bytes 262168
  14.9 0.9 %shard_map.121 = (bf16[256,768]{1,0:T(8,128)(2,1)S(1)}, bf16[256,768]{1,0:T(8,128)(2,1)S(1)}, f32[256,128]{1,0:T(8,128)S(1)}, bf16[256,1024]{1,0:T(8,128)(2,1)S(1)}, bf16[256,1024]{1,0:T(8,128)(2,1)S(1)}) custom-call(s32[8]{0:T(128)S(1)} %copy-done.6, s32[8]{0:T(128)S(1)} %copy-done.7, bf16[8,128,128]{2,1,0:T(8,128)(2,1)S(1)} %copy-done.3, ...), custom_call_target="tpu_custom_call" | custom-call | flops 1000000 | bytes 3000000 | tf_op jit(solution)/shard_map/pallas_call | solution.py:22
  15.9 2.0 %collective-permute-done.refs_1_ = bf16[256,256]{1,0:T(8,128)(2,1)S(1)} collective-permute-done((bf16[256,256]{1,0:T(8,128)(2,1)S(1)}, bf16[256,256]{1,0:T(8,128)(2,1)S(1)}, u32[]{:S(2)}, u32[]{:S(2)}) %collective-permute-start) | collective-permute-done | bytes 131104 | tf_op jit(solution)/shard_map/ppermute | solution.py:268
  17.8 1.3 %all-to-all-done = bf16[8,64,256]{2,1,0:T(8,128)(2,1)S(1)} async-done(((bf16[8,64,256]{2,1,0:T(8,128)(2,1)}), bf16[8,64,256]{2,1,0:T(8,128)(2,1)S(1)}, u32[]{:S(2)}, u32[]{:S(2)}) %all-to-all-start) | async-done | bytes 262176 | tf_op jit(solution)/shard_map/all_to_all | solution.py:306
  19.1 1.0 %shard_map.122 = (f32[256,256]{1,0:T(8,128)S(1)}, bf16[256,256]{1,0:T(8,128)(2,1)S(1)}, f32[256,256]{1,0:T(8,128)S(1)}, bf16[2,256,256]{2,1,0:T(8,128)(2,1)S(1)}) custom-call(s32[1]{0:T(128)} %bitcast.1.rep_ref, bf16[256,256]{1,0:T(8,128)(2,1)S(1)} %copy-done.4, bf16[512,256]{1,0:T(8,128)(2,1)S(1)} %bitcast.7, ...), custom_call_target="tpu_custom_call" | custom-call | flops 600000000 | bytes 3000000 | tf_op jit(solution)/shard_map/pallas_call | solution.py:22
  20.2 1.5 %collective-permute-start.1 = (bf16[256,256]{1,0:T(8,128)(2,1)S(1)}, bf16[256,256]{1,0:T(8,128)(2,1)S(1)}, u32[]{:S(2)}, u32[]{:S(2)}) collective-permute-start(bf16[256,256]{1,0:T(8,128)(2,1)S(1)} %get-tuple-element.51.refs_2_), channel_id=1, source_target_pairs={{0,4},{4,0},{8,12},{12,8},{16,20},{20,16},{24,28},{28,24},{1,5},{5... | collective-permute-start | bytes 393224 | tf_op jit(solution)/shard_map/ppermute | solution.py:268
  21.7 1.6 %collective-permute-start.3 = (bf16[256,256]{1,0:T(8,128)(2,1)S(1)}, bf16[256,256]{1,0:T(8,128)(2,1)S(1)}, u32[]{:S(2)}, u32[]{:S(2)}) collective-permute-start(bf16[256,256]{1,0:T(8,128)(2,1)S(1)} %shard_map.123), channel_id=1, source_target_pairs={{0,2},{1,3},{2,0},{3,1},{4,6},{5,7},{6,4},{7,5},{8,10},{9,11},{10,... | collective-permute-start | bytes 393224 | tf_op jit(solution)/shard_map/ppermute | solution.py:268
  23.3 2.8 %collective-permute-done.1.refs_3_ = bf16[256,256]{1,0:T(8,128)(2,1)S(1)} collective-permute-done((bf16[256,256]{1,0:T(8,128)(2,1)S(1)}, bf16[256,256]{1,0:T(8,128)(2,1)S(1)}, u32[]{:S(2)}, u32[]{:S(2)}) %collective-permute-start.1) | collective-permute-done | bytes 131104 | tf_op jit(solution)/shard_map/ppermute | solution.py:268
  26.1 1.2 %collective-permute-done.3.across_ref = bf16[256,256]{1,0:T(8,128)(2,1)S(1)} collective-permute-done((bf16[256,256]{1,0:T(8,128)(2,1)S(1)}, bf16[256,256]{1,0:T(8,128)(2,1)S(1)}, u32[]{:S(2)}, u32[]{:S(2)}) %collective-permute-start.3) | collective-permute-done | bytes 131104 | tf_op jit(solution)/shard_map/ppermute | solution.py:268
  28.1 1.5 %collective-permute-start.5 = (bf16[256,256]{1,0:T(8,128)(2,1)S(1)}, bf16[256,256]{1,0:T(8,128)(2,1)S(1)}, u32[]{:S(2)}, u32[]{:S(2)}) collective-permute-start(bf16[256,256]{1,0:T(8,128)(2,1)S(1)} %get-tuple-element.57.refs_0_.refs_4_), channel_id=1, source_target_pairs={{0,2},{1,3},{2,0},{3,1},{4,6},{5,7},{6,4},{7,5},{8,10},{9,11},{10,... | collective-permute-start | bytes 393224 | tf_op jit(solution)/shard_map/ppermute | solution.py:268
  29.6 1.4 %collective-permute-start.7 = (bf16[256,128]{1,0:T(8,128)(2,1)S(1)}, bf16[256,128]{1,0:T(8,128)(2,1)S(1)}, u32[]{:S(2)}, u32[]{:S(2)}) collective-permute-start(bf16[256,128]{1,0:T(8,128)(2,1)S(1)} %get-tuple-element.62), channel_id=1, source_target_pairs={{0,4},{4,0},{8,12},{12,8},{16,20},{20,16},{24,28},{28,24},{1,5},{5... | collective-permute-start | bytes 196616 | tf_op jit(solution)/shard_map/ppermute | solution.py:268
  31.0 2.9 %collective-permute-done.7.refs_8_ = bf16[256,128]{1,0:T(8,128)(2,1)S(1)} collective-permute-done((bf16[256,128]{1,0:T(8,128)(2,1)S(1)}, bf16[256,128]{1,0:T(8,128)(2,1)S(1)}, u32[]{:S(2)}, u32[]{:S(2)}) %collective-permute-start.7) | collective-permute-done | bytes 65568 | tf_op jit(solution)/shard_map/ppermute | solution.py:268
  34.9 3.2 %collective-permute-done.9.refs_10_ = bf16[256,128]{1,0:T(8,128)(2,1)S(1)} collective-permute-done((bf16[256,128]{1,0:T(8,128)(2,1)S(1)}, bf16[256,128]{1,0:T(8,128)(2,1)S(1)}, u32[]{:S(2)}, u32[]{:S(2)}) %collective-permute-start.9) | collective-permute-done | bytes 65568 | tf_op jit(solution)/shard_map/ppermute | solution.py:268
  38.1 1.2 %collective-permute-done.10.refs_11_ = bf16[256,128]{1,0:T(8,128)(2,1)S(1)} collective-permute-done((bf16[256,128]{1,0:T(8,128)(2,1)S(1)}, bf16[256,128]{1,0:T(8,128)(2,1)S(1)}, u32[]{:S(2)}, u32[]{:S(2)}) %collective-permute-start.10) | collective-permute-done | bytes 65568 | tf_op jit(solution)/shard_map/ppermute | solution.py:268
  40.2 1.1 %collective-permute-start.11 = (bf16[2,2,256,128]{3,2,1,0:T(8,128)(2,1)S(1)}, bf16[2,2,256,128]{3,2,1,0:T(8,128)(2,1)S(1)}, u32[]{:S(2)}, u32[]{:S(2)}) collective-permute-start(bf16[2,2,256,128]{3,2,1,0:T(8,128)(2,1)S(1)} %get-tuple-element.64), channel_id=1, source_target_pairs={{0,8},{4,12},{8,0},{12,4},{16,24},{20,28},{24,16},{28,20},{1,9},{5... | collective-permute-start | bytes 786440 | tf_op jit(solution)/shard_map/ppermute | solution.py:268
  41.3 7.3 %collective-permute-done.11.beside_ref.next_ref = bf16[2,2,256,128]{3,2,1,0:T(8,128)(2,1)S(1)} collective-permute-done((bf16[2,2,256,128]{3,2,1,0:T(8,128)(2,1)S(1)}, bf16[2,2,256,128]{3,2,1,0:T(8,128)(2,1)S(1)}, u32[]{:S(2)}, u32[]{:S(2)}) %collective-permute-start.11) | collective-permute-done | bytes 262176 | tf_op jit(solution)/shard_map/ppermute | solution.py:268
  48.6 1.5 %collective-permute-start.12 = (bf16[2,256,128]{2,1,0:T(8,128)(2,1)S(1)}, bf16[2,256,128]{2,1,0:T(8,128)(2,1)S(1)}, u32[]{:S(2)}, u32[]{:S(2)}) collective-permute-start(bf16[2,256,128]{2,1,0:T(8,128)(2,1)S(1)} %shard_map.128), channel_id=1, source_target_pairs={{0,16},{4,20},{8,24},{12,28},{16,0},{20,4},{24,8},{28,12},{1,17},{... | collective-permute-start | bytes 393224 | tf_op jit(solution)/shard_map/ppermute | solution.py:268
  50.1 1.5 %shard_map.125 = (f32[256,256]{1,0:T(8,128)S(1)}, bf16[512,256]{1,0:T(8,128)(2,1)}) custom-call(s32[1]{0:T(128)} %bitcast.1.rep_ref, bf16[256,768]{1,0:T(8,128)(2,1)S(1)} %get-tuple-element.45.high_ref, bf16[256,768]{1,0:T(8,128)(2,1)S(1)} %get-tuple-element.46.low_ref, f32[256,128]{1,0:T(8,128)S(1)} %get-tuple-element.47.deg_ref, ...), custom_call_target="tpu_custom_call" | custom-call | flops 600000000 | bytes 3000000 | tf_op jit(solution)/shard_map/pallas_call | solution.py:22
  51.6 3.6 %all-to-all-start.1 = ((bf16[8,64,256]{2,1,0:T(8,128)(2,1)}), bf16[8,64,256]{2,1,0:T(8,128)(2,1)S(1)}, u32[]{:S(2)}, u32[]{:S(2)}) async-start(bf16[8,64,256]{2,1,0:T(8,128)(2,1)} %bitcast.4), calls=%async_computation.1 | async-start | bytes 524288 | tf_op jit(solution)/shard_map/all_to_all | solution.py:306
  55.3 1.9 %collective-permute-done.12.far_ref = bf16[2,256,128]{2,1,0:T(8,128)(2,1)S(1)} collective-permute-done((bf16[2,256,128]{2,1,0:T(8,128)(2,1)S(1)}, bf16[2,256,128]{2,1,0:T(8,128)(2,1)S(1)}, u32[]{:S(2)}, u32[]{:S(2)}) %collective-permute-start.12) | collective-permute-done | bytes 131104 | tf_op jit(solution)/shard_map/ppermute | solution.py:268
  57.5 4.6 %collective-permute-start.13 = (bf16[2,256,128]{2,1,0:T(8,128)(2,1)S(1)}, bf16[2,256,128]{2,1,0:T(8,128)(2,1)S(1)}, u32[]{:S(2)}, u32[]{:S(2)}) collective-permute-start(bf16[2,256,128]{2,1,0:T(8,128)(2,1)S(1)} %shard_map.129.refs_0_), channel_id=1, source_target_pairs={{0,16},{4,20},{8,24},{12,28},{16,0},{20,4},{24,8},{28,12},{1,17},{... | collective-permute-start | bytes 393224 | tf_op jit(solution)/shard_map/ppermute | solution.py:268
  62.1 3.7 %collective-permute-done.15.refs_2_ = bf16[2,256,128]{2,1,0:T(8,128)(2,1)S(1)} collective-permute-done((bf16[2,256,128]{2,1,0:T(8,128)(2,1)S(1)}, bf16[2,256,128]{2,1,0:T(8,128)(2,1)S(1)}, u32[]{:S(2)}, u32[]{:S(2)}) %collective-permute-start.15) | collective-permute-done | bytes 131104 | tf_op jit(solution)/shard_map/ppermute | solution.py:268
  65.8 3.0 %collective-permute-start.16 = (bf16[2,256,128]{2,1,0:T(8,128)(2,1)S(1)}, bf16[2,256,128]{2,1,0:T(8,128)(2,1)S(1)}, u32[]{:S(2)}, u32[]{:S(2)}) collective-permute-start(bf16[2,256,128]{2,1,0:T(8,128)(2,1)S(1)} %collective-permute-done.15.refs_2_), channel_id=1, source_target_pairs={{0,4},{4,0},{8,12},{12,8},{16,20},{20,16},{24,28},{28,24},{1,5},{5... | collective-permute-start | bytes 393224 | tf_op jit(solution)/shard_map/ppermute | solution.py:268
  69.2 2.6 %collective-permute-done.16.refs_3_ = bf16[2,256,128]{2,1,0:T(8,128)(2,1)S(1)} collective-permute-done((bf16[2,256,128]{2,1,0:T(8,128)(2,1)S(1)}, bf16[2,256,128]{2,1,0:T(8,128)(2,1)S(1)}, u32[]{:S(2)}, u32[]{:S(2)}) %collective-permute-start.16) | collective-permute-done | bytes 131104 | tf_op jit(solution)/shard_map/ppermute | solution.py:268
  71.8 2.3 %collective-permute-start.17 = (bf16[2,256,128]{2,1,0:T(8,128)(2,1)S(1)}, bf16[2,256,128]{2,1,0:T(8,128)(2,1)S(1)}, u32[]{:S(2)}, u32[]{:S(2)}) collective-permute-start(bf16[2,256,128]{2,1,0:T(8,128)(2,1)S(1)} %collective-permute-done.13.refs_4_), channel_id=1, source_target_pairs={{0,4},{4,0},{8,12},{12,8},{16,20},{20,16},{24,28},{28,24},{1,5},{5... | collective-permute-start | bytes 393224 | tf_op jit(solution)/shard_map/ppermute | solution.py:268
  74.1 1.4 %collective-permute-start.19 = (bf16[2,256,128]{2,1,0:T(8,128)(2,1)S(1)}, bf16[2,256,128]{2,1,0:T(8,128)(2,1)S(1)}, u32[]{:S(2)}, u32[]{:S(2)}) collective-permute-start(bf16[2,256,128]{2,1,0:T(8,128)(2,1)S(1)} %collective-permute-done.18.refs_1_), channel_id=1, source_target_pairs={{0,4},{4,0},{8,12},{12,8},{16,20},{20,16},{24,28},{28,24},{1,5},{5... | collective-permute-start | bytes 393224 | tf_op jit(solution)/shard_map/ppermute | solution.py:268
  76.4 0.9 %shard_map.130 = (bf16[256,1024]{1,0:T(8,128)(2,1)}, bf16[256,1024]{1,0:T(8,128)(2,1)}) custom-call(s32[1]{0:T(128)} %bitcast.dom_ref, bf16[2,256,128]{2,1,0:T(8,128)(2,1)S(1)} %shard_map.129.refs_0_, bf16[2,256,128]{2,1,0:T(8,128)(2,1)S(1)} %collective-permute-done.14.refs_1_, bf16[2,256,128]{2,1,0:T(8,128)(2,1)S(1)} %collective-permute-done.15.refs_2_, ...), custom_call_target="tpu_custom_call" | custom-call | bytes 1000000 | tf_op jit(solution)/shard_map/pallas_call | solution.py:22
  77.3 1.8 %collective-permute-done.19.refs_2_ = bf16[2,256,128]{2,1,0:T(8,128)(2,1)S(1)} collective-permute-done((bf16[2,256,128]{2,1,0:T(8,128)(2,1)S(1)}, bf16[2,256,128]{2,1,0:T(8,128)(2,1)S(1)}, u32[]{:S(2)}, u32[]{:S(2)}) %collective-permute-start.19) | collective-permute-done | bytes 131104 | tf_op jit(solution)/shard_map/ppermute | solution.py:268
  (40 shorter events, 6.0 us)
Async XLA Ops:
  0.6 11.6 %copy-start = (bf16[256,1024]{1,0:T(8,128)(2,1)S(1)}, bf16[256,1024]{1,0:T(8,128)(2,1)}, u32[]{:S(2)}) copy-start(bf16[256,1024]{1,0:T(8,128)(2,1)} %self_hbm) | copy-start | bytes 1572868
  2.8 7.4 %copy-start.4 = (bf16[256,256]{1,0:T(8,128)(2,1)S(1)}, bf16[256,256]{1,0:T(8,128)(2,1)}, u32[]{:S(2)}) copy-start(bf16[256,256]{1,0:T(8,128)(2,1)} %refs_0_.1) | copy-start | bytes 393220
  2.8 16.3 %all-to-all-start = ((bf16[8,64,256]{2,1,0:T(8,128)(2,1)}), bf16[8,64,256]{2,1,0:T(8,128)(2,1)S(1)}, u32[]{:S(2)}, u32[]{:S(2)}) async-start(bf16[8,64,256]{2,1,0:T(8,128)(2,1)} %bitcast.8), calls=%async_computation | async-start | bytes 524288 | tf_op jit(solution)/shard_map/all_to_all | solution.py:306
  10.2 7.6 %collective-permute-start = (bf16[256,256]{1,0:T(8,128)(2,1)S(1)}, bf16[256,256]{1,0:T(8,128)(2,1)S(1)}, u32[]{:S(2)}, u32[]{:S(2)}) collective-permute-start(bf16[256,256]{1,0:T(8,128)(2,1)S(1)} %copy-done.4), channel_id=1, source_target_pairs={{0,4},{4,0},{8,12},{12,8},{16,20},{20,16},{24,28},{28,24},{1,5},{5... | collective-permute-start | bytes 393224 | tf_op jit(solution)/shard_map/ppermute | solution.py:268
  12.2 0.7 copy-start.6
  12.2 0.7 copy-start.7
  12.9 1.0 %copy-start.1 = (bf16[256,1024]{1,0:T(8,128)(2,1)S(1)}, bf16[256,1024]{1,0:T(8,128)(2,1)}, u32[]{:S(2)}) copy-start(bf16[256,1024]{1,0:T(8,128)(2,1)} %neigh_hbm) | copy-start | bytes 1572868
  14.0 0.9 %copy-start.3 = (bf16[8,128,128]{2,1,0:T(8,128)(2,1)S(1)}, bf16[8,128,128]{2,1,0:T(8,128)(2,1)}, u32[]{:S(2)}) copy-start(bf16[8,128,128]{2,1,0:T(8,128)(2,1)} %tiles_ref) | copy-start | bytes 786436
  20.1 1.6 %collective-permute-start.2 = (bf16[2,256,256]{2,1,0:T(8,128)(2,1)S(1)}, bf16[2,256,256]{2,1,0:T(8,128)(2,1)S(1)}, u32[]{:S(2)}, u32[]{:S(2)}) collective-permute-start(bf16[2,256,256]{2,1,0:T(8,128)(2,1)S(1)} %get-tuple-element.53), channel_id=1, source_target_pairs={{0,1},{1,0},{2,3},{3,2},{4,5},{5,4},{6,7},{7,6},{8,9},{9,8},{10,11... | collective-permute-start | bytes 786440 | tf_op jit(solution)/shard_map/ppermute | solution.py:268
  20.2 5.9 %collective-permute-start.1 = (bf16[256,256]{1,0:T(8,128)(2,1)S(1)}, bf16[256,256]{1,0:T(8,128)(2,1)S(1)}, u32[]{:S(2)}, u32[]{:S(2)}) collective-permute-start(bf16[256,256]{1,0:T(8,128)(2,1)S(1)} %get-tuple-element.51.refs_2_), channel_id=1, source_target_pairs={{0,4},{4,0},{8,12},{12,8},{16,20},{20,16},{24,28},{28,24},{1,5},{5... | collective-permute-start | bytes 393224 | tf_op jit(solution)/shard_map/ppermute | solution.py:268
  21.7 5.6 %copy-start.5 = (bf16[256,256]{1,0:T(8,128)(2,1)S(1)}, bf16[256,256]{1,0:T(8,128)(2,1)}, u32[]{:S(2)}) copy-start(bf16[256,256]{1,0:T(8,128)(2,1)} %gout_ref) | copy-start | bytes 393220
  21.7 5.6 %collective-permute-start.3 = (bf16[256,256]{1,0:T(8,128)(2,1)S(1)}, bf16[256,256]{1,0:T(8,128)(2,1)S(1)}, u32[]{:S(2)}, u32[]{:S(2)}) collective-permute-start(bf16[256,256]{1,0:T(8,128)(2,1)S(1)} %shard_map.123), channel_id=1, source_target_pairs={{0,2},{1,3},{2,0},{3,1},{4,6},{5,7},{6,4},{7,5},{8,10},{9,11},{10,... | collective-permute-start | bytes 393224 | tf_op jit(solution)/shard_map/ppermute | solution.py:268
  28.1 6.3 %collective-permute-start.5 = (bf16[256,256]{1,0:T(8,128)(2,1)S(1)}, bf16[256,256]{1,0:T(8,128)(2,1)S(1)}, u32[]{:S(2)}, u32[]{:S(2)}) collective-permute-start(bf16[256,256]{1,0:T(8,128)(2,1)S(1)} %get-tuple-element.57.refs_0_.refs_4_), channel_id=1, source_target_pairs={{0,2},{1,3},{2,0},{3,1},{4,6},{5,7},{6,4},{7,5},{8,10},{9,11},{10,... | collective-permute-start | bytes 393224 | tf_op jit(solution)/shard_map/ppermute | solution.py:268
  29.6 4.3 %collective-permute-start.7 = (bf16[256,128]{1,0:T(8,128)(2,1)S(1)}, bf16[256,128]{1,0:T(8,128)(2,1)S(1)}, u32[]{:S(2)}, u32[]{:S(2)}) collective-permute-start(bf16[256,128]{1,0:T(8,128)(2,1)S(1)} %get-tuple-element.62), channel_id=1, source_target_pairs={{0,4},{4,0},{8,12},{12,8},{16,20},{20,16},{24,28},{28,24},{1,5},{5... | collective-permute-start | bytes 196616 | tf_op jit(solution)/shard_map/ppermute | solution.py:268
  31.0 7.1 %collective-permute-start.4 = (bf16[256,256]{1,0:T(8,128)(2,1)S(1)}, bf16[256,256]{1,0:T(8,128)(2,1)S(1)}, u32[]{:S(2)}, u32[]{:S(2)}) collective-permute-start(bf16[256,256]{1,0:T(8,128)(2,1)S(1)} %get-tuple-element.57.refs_0_.refs_4_), channel_id=1, source_target_pairs={{0,1},{1,0},{2,3},{3,2},{4,5},{5,4},{6,7},{7,6},{8,9},{9,8},{10,11... | collective-permute-start | bytes 393224 | tf_op jit(solution)/shard_map/ppermute | solution.py:268
  33.9 4.3 %collective-permute-start.9 = (bf16[256,128]{1,0:T(8,128)(2,1)S(1)}, bf16[256,128]{1,0:T(8,128)(2,1)S(1)}, u32[]{:S(2)}, u32[]{:S(2)}) collective-permute-start(bf16[256,128]{1,0:T(8,128)(2,1)S(1)} %collective-permute-done.7.refs_8_), channel_id=1, source_target_pairs={{0,2},{1,3},{2,0},{3,1},{4,6},{5,7},{6,4},{7,5},{8,10},{9,11},{10,... | collective-permute-start | bytes 196616 | tf_op jit(solution)/shard_map/ppermute | solution.py:268
  34.4 5.0 %collective-permute-start.6 = (bf16[256,256]{1,0:T(8,128)(2,1)S(1)}, bf16[256,256]{1,0:T(8,128)(2,1)S(1)}, u32[]{:S(2)}, u32[]{:S(2)}) collective-permute-start(bf16[256,256]{1,0:T(8,128)(2,1)S(1)} %collective-permute-done.5.refs_2_.refs_6_), channel_id=1, source_target_pairs={{0,1},{1,0},{2,3},{3,2},{4,5},{5,4},{6,7},{7,6},{8,9},{9,8},{10,11... | collective-permute-start | bytes 393224 | tf_op jit(solution)/shard_map/ppermute | solution.py:268
  34.4 3.7 %collective-permute-start.8 = (bf16[256,128]{1,0:T(8,128)(2,1)S(1)}, bf16[256,128]{1,0:T(8,128)(2,1)S(1)}, u32[]{:S(2)}, u32[]{:S(2)}) collective-permute-start(bf16[256,128]{1,0:T(8,128)(2,1)S(1)} %collective-permute-done.7.refs_8_), channel_id=1, source_target_pairs={{0,1},{1,0},{2,3},{3,2},{4,5},{5,4},{6,7},{7,6},{8,9},{9,8},{10,11... | collective-permute-start | bytes 196616 | tf_op jit(solution)/shard_map/ppermute | solution.py:268
  38.1 1.3 %collective-permute-start.10 = (bf16[256,128]{1,0:T(8,128)(2,1)S(1)}, bf16[256,128]{1,0:T(8,128)(2,1)S(1)}, u32[]{:S(2)}, u32[]{:S(2)}) collective-permute-start(bf16[256,128]{1,0:T(8,128)(2,1)S(1)} %collective-permute-done.9.refs_10_), channel_id=1, source_target_pairs={{0,1},{1,0},{2,3},{3,2},{4,5},{5,4},{6,7},{7,6},{8,9},{9,8},{10,11... | collective-permute-start | bytes 196616 | tf_op jit(solution)/shard_map/ppermute | solution.py:268
  40.2 8.4 %collective-permute-start.11 = (bf16[2,2,256,128]{3,2,1,0:T(8,128)(2,1)S(1)}, bf16[2,2,256,128]{3,2,1,0:T(8,128)(2,1)S(1)}, u32[]{:S(2)}, u32[]{:S(2)}) collective-permute-start(bf16[2,2,256,128]{3,2,1,0:T(8,128)(2,1)S(1)} %get-tuple-element.64), channel_id=1, source_target_pairs={{0,8},{4,12},{8,0},{12,4},{16,24},{20,28},{24,16},{28,20},{1,9},{5... | collective-permute-start | bytes 786440 | tf_op jit(solution)/shard_map/ppermute | solution.py:268
  48.6 8.5 %collective-permute-start.12 = (bf16[2,256,128]{2,1,0:T(8,128)(2,1)S(1)}, bf16[2,256,128]{2,1,0:T(8,128)(2,1)S(1)}, u32[]{:S(2)}, u32[]{:S(2)}) collective-permute-start(bf16[2,256,128]{2,1,0:T(8,128)(2,1)S(1)} %shard_map.128), channel_id=1, source_target_pairs={{0,16},{4,20},{8,24},{12,28},{16,0},{20,4},{24,8},{28,12},{1,17},{... | collective-permute-start | bytes 393224 | tf_op jit(solution)/shard_map/ppermute | solution.py:268
  51.6 23.9 %all-to-all-start.1 = ((bf16[8,64,256]{2,1,0:T(8,128)(2,1)}), bf16[8,64,256]{2,1,0:T(8,128)(2,1)S(1)}, u32[]{:S(2)}, u32[]{:S(2)}) async-start(bf16[8,64,256]{2,1,0:T(8,128)(2,1)} %bitcast.4), calls=%async_computation.1 | async-start | bytes 524288 | tf_op jit(solution)/shard_map/all_to_all | solution.py:306
  57.2 18.4 %copy-start.2 = (bf16[256,512]{1,0:T(8,128)(2,1)S(1)}, bf16[256,512]{1,0:T(8,128)(2,1)}, u32[]{:S(2)}) copy-start(bf16[256,512]{1,0:T(8,128)(2,1)} %get-tuple-element.56.onehot_ref) | copy-start | bytes 786436
  57.2 8.6 %collective-permute-start.15 = (bf16[2,256,128]{2,1,0:T(8,128)(2,1)S(1)}, bf16[2,256,128]{2,1,0:T(8,128)(2,1)S(1)}, u32[]{:S(2)}, u32[]{:S(2)}) collective-permute-start(bf16[2,256,128]{2,1,0:T(8,128)(2,1)S(1)} %shard_map.129.refs_0_), channel_id=1, source_target_pairs={{0,8},{4,12},{8,0},{12,4},{16,24},{20,28},{24,16},{28,20},{1,9},{5... | collective-permute-start | bytes 393224 | tf_op jit(solution)/shard_map/ppermute | solution.py:268
  57.5 11.6 %collective-permute-start.13 = (bf16[2,256,128]{2,1,0:T(8,128)(2,1)S(1)}, bf16[2,256,128]{2,1,0:T(8,128)(2,1)S(1)}, u32[]{:S(2)}, u32[]{:S(2)}) collective-permute-start(bf16[2,256,128]{2,1,0:T(8,128)(2,1)S(1)} %shard_map.129.refs_0_), channel_id=1, source_target_pairs={{0,16},{4,20},{8,24},{12,28},{16,0},{20,4},{24,8},{28,12},{1,17},{... | collective-permute-start | bytes 393224 | tf_op jit(solution)/shard_map/ppermute | solution.py:268
  62.1 7.0 %collective-permute-start.14 = (bf16[2,256,128]{2,1,0:T(8,128)(2,1)S(1)}, bf16[2,256,128]{2,1,0:T(8,128)(2,1)S(1)}, u32[]{:S(2)}, u32[]{:S(2)}) collective-permute-start(bf16[2,256,128]{2,1,0:T(8,128)(2,1)S(1)} %shard_map.129.refs_0_), channel_id=1, source_target_pairs={{0,4},{4,0},{8,12},{12,8},{16,20},{20,16},{24,28},{28,24},{1,5},{5... | collective-permute-start | bytes 393224 | tf_op jit(solution)/shard_map/ppermute | solution.py:268
  65.8 5.9 %collective-permute-start.16 = (bf16[2,256,128]{2,1,0:T(8,128)(2,1)S(1)}, bf16[2,256,128]{2,1,0:T(8,128)(2,1)S(1)}, u32[]{:S(2)}, u32[]{:S(2)}) collective-permute-start(bf16[2,256,128]{2,1,0:T(8,128)(2,1)S(1)} %collective-permute-done.15.refs_2_), channel_id=1, source_target_pairs={{0,4},{4,0},{8,12},{12,8},{16,20},{20,16},{24,28},{28,24},{1,5},{5... | collective-permute-start | bytes 393224 | tf_op jit(solution)/shard_map/ppermute | solution.py:268
  69.2 5.0 %collective-permute-start.18 = (bf16[2,256,128]{2,1,0:T(8,128)(2,1)S(1)}, bf16[2,256,128]{2,1,0:T(8,128)(2,1)S(1)}, u32[]{:S(2)}, u32[]{:S(2)}) collective-permute-start(bf16[2,256,128]{2,1,0:T(8,128)(2,1)S(1)} %collective-permute-done.13.refs_4_), channel_id=1, source_target_pairs={{0,8},{4,12},{8,0},{12,4},{16,24},{20,28},{24,16},{28,20},{1,9},{5... | collective-permute-start | bytes 393224 | tf_op jit(solution)/shard_map/ppermute | solution.py:268
  71.8 5.5 %collective-permute-start.17 = (bf16[2,256,128]{2,1,0:T(8,128)(2,1)S(1)}, bf16[2,256,128]{2,1,0:T(8,128)(2,1)S(1)}, u32[]{:S(2)}, u32[]{:S(2)}) collective-permute-start(bf16[2,256,128]{2,1,0:T(8,128)(2,1)S(1)} %collective-permute-done.13.refs_4_), channel_id=1, source_target_pairs={{0,4},{4,0},{8,12},{12,8},{16,20},{20,16},{24,28},{28,24},{1,5},{5... | collective-permute-start | bytes 393224 | tf_op jit(solution)/shard_map/ppermute | solution.py:268
  74.1 5.0 %collective-permute-start.19 = (bf16[2,256,128]{2,1,0:T(8,128)(2,1)S(1)}, bf16[2,256,128]{2,1,0:T(8,128)(2,1)S(1)}, u32[]{:S(2)}, u32[]{:S(2)}) collective-permute-start(bf16[2,256,128]{2,1,0:T(8,128)(2,1)S(1)} %collective-permute-done.18.refs_1_), channel_id=1, source_target_pairs={{0,4},{4,0},{8,12},{12,8},{16,20},{20,16},{24,28},{28,24},{1,5},{5... | collective-permute-start | bytes 393224 | tf_op jit(solution)/shard_map/ppermute | solution.py:268

commit v9 on v8

--- a/solution.py
+++ b/solution.py
@@ -410,7 +410,7 @@
     )
     if split:
         outs = ()
-        for offsets in ((0, 1, 2, 3, 4), (5, 6, 7)):
+        for offsets in ((0, 1, 2, 3, 4, 5, 6), (7,)):
             outs = call(
                 functools.partial(place_body, offsets), (struct((rows, width), BF16),) * 2,
                 [("s", dom)] + [("v", pieces[k]) for k in offsets] + [("h", out) for out in outs],

time: 80.3 us -> 80.2 us (level)
  transfers between devices with their start and end apart: 22 -> 22, of which waited for: 14 -> 15; matrix products, arithmetic and copies ran while one was open for 0% -> 0% of each run, Pallas kernels for 5% -> 6%
where the time goes in v9:
time: 80.2 us; the launch traced here: 79.8 us
  starting transfers between devices  34.3 us (43%)
  waiting for transfers between devices  32.3 us (40%)
  Pallas kernels  9.79 us (12%)
  local copies, waits for them, and re-layouts  2.68 us (3%)
    ppermute x20, waiting for transfers between devices, swap(): lax.ppermute(array, axis, [(i, i ^ offset) for i in range(lax.axis_size(a...  31 us
    ppermute x20, starting transfers between devices, swap(): lax.ppermute(array, axis, [(i, i ^ offset) for i in range(lax.axis_size(a...  23.2 us
    all_to_all x2, starting transfers between devices, exchange(): lax.all_to_all(array.reshape(peers, slots, cols), 'dom', split_axis=0, co...  11.1 us
    pallas_call x12, Pallas kernels, call(): pl.pallas_call(body, out_shape=outs, in_specs=[SPECS[spec] for spec, _ in...  9.79 us
    unnamed x16, local copies, waits for them, and re-layouts  2.68 us
  transfers between devices with their start and end apart: 22, of which 15 were waited for; matrix products, arithmetic and copies ran while one was open for 0% of the time, Pallas kernels for 6%

profile of v9, /device:TPU:0, one launch (start us, length us, event | category | flops | bytes accessed | tf_op | source)
XLA Modules:
  0.0 79.8 jit_solution(12317560083639652910)
XLA Ops:
  0.6 2.1 %shard_map.120 = (bf16[256,512]{1,0:T(8,128)(2,1)}, bf16[512,256]{1,0:T(8,128)(2,1)}) custom-call(s32[8]{0:T(128)} %count_hbm.1, s32[8,64]{1,0:T(8,128)} %list_hbm.1, bf16[256,256]{1,0:T(8,128)(2,1)} %refs_0_.1), custom_call_target="tpu_custom_call" | custom-call | flops 67108864 | bytes 600000 | tf_op jit(solution)/shard_map/pallas_call | solution.py:22
  2.8 7.4 %all-to-all-start = ((bf16[8,64,256]{2,1,0:T(8,128)(2,1)}), bf16[8,64,256]{2,1,0:T(8,128)(2,1)S(1)}, u32[]{:S(2)}, u32[]{:S(2)}) async-start(bf16[8,64,256]{2,1,0:T(8,128)(2,1)} %bitcast.8), calls=%async_computation | async-start | bytes 524288 | tf_op jit(solution)/shard_map/all_to_all | solution.py:306
  10.2 2.0 %collective-permute-start = (bf16[256,256]{1,0:T(8,128)(2,1)S(1)}, bf16[256,256]{1,0:T(8,128)(2,1)S(1)}, u32[]{:S(2)}, u32[]{:S(2)}) collective-permute-start(bf16[256,256]{1,0:T(8,128)(2,1)S(1)} %copy-done.4), channel_id=1, source_target_pairs={{0,4},{4,0},{8,12},{12,8},{16,20},{20,16},{24,28},{28,24},{1,5},{5... | collective-permute-start | bytes 393224 | tf_op jit(solution)/shard_map/ppermute | solution.py:268
  12.9 1.0 %copy-done.1 = bf16[256,1024]{1,0:T(8,128)(2,1)S(1)} copy-done((bf16[256,1024]{1,0:T(8,128)(2,1)S(1)}, bf16[256,1024]{1,0:T(8,128)(2,1)}, u32[]{:S(2)}) %copy-start.1) | copy-done | bytes 524312
  14.0 0.9 %copy-done.3 = bf16[8,128,128]{2,1,0:T(8,128)(2,1)S(1)} copy-done((bf16[8,128,128]{2,1,0:T(8,128)(2,1)S(1)}, bf16[8,128,128]{2,1,0:T(8,128)(2,1)}, u32[]{:S(2)}) %copy-start.3) | copy-done | bytes 262168
  14.9 0.9 %shard_map.121 = (bf16[256,768]{1,0:T(8,128)(2,1)S(1)}, bf16[256,768]{1,0:T(8,128)(2,1)S(1)}, f32[256,128]{1,0:T(8,128)S(1)}, bf16[256,1024]{1,0:T(8,128)(2,1)S(1)}, bf16[256,1024]{1,0:T(8,128)(2,1)S(1)}) custom-call(s32[8]{0:T(128)S(1)} %copy-done.6, s32[8]{0:T(128)S(1)} %copy-done.7, bf16[8,128,128]{2,1,0:T(8,128)(2,1)S(1)} %copy-done.3, ...), custom_call_target="tpu_custom_call" | custom-call | flops 1000000 | bytes 3000000 | tf_op jit(solution)/shard_map/pallas_call | solution.py:22
  15.9 2.0 %collective-permute-done.refs_1_ = bf16[256,256]{1,0:T(8,128)(2,1)S(1)} collective-permute-done((bf16[256,256]{1,0:T(8,128)(2,1)S(1)}, bf16[256,256]{1,0:T(8,128)(2,1)S(1)}, u32[]{:S(2)}, u32[]{:S(2)}) %collective-permute-start) | collective-permute-done | bytes 131104 | tf_op jit(solution)/shard_map/ppermute | solution.py:268
  17.8 1.3 %all-to-all-done = bf16[8,64,256]{2,1,0:T(8,128)(2,1)S(1)} async-done(((bf16[8,64,256]{2,1,0:T(8,128)(2,1)}), bf16[8,64,256]{2,1,0:T(8,128)(2,1)S(1)}, u32[]{:S(2)}, u32[]{:S(2)}) %all-to-all-start) | async-done | bytes 262176 | tf_op jit(solution)/shard_map/all_to_all | solution.py:306
  19.1 1.0 %shard_map.122 = (f32[256,256]{1,0:T(8,128)S(1)}, bf16[256,256]{1,0:T(8,128)(2,1)S(1)}, f32[256,256]{1,0:T(8,128)S(1)}, bf16[2,256,256]{2,1,0:T(8,128)(2,1)S(1)}) custom-call(s32[1]{0:T(128)} %bitcast.1.rep_ref, bf16[256,256]{1,0:T(8,128)(2,1)S(1)} %copy-done.4, bf16[512,256]{1,0:T(8,128)(2,1)S(1)} %bitcast.7, ...), custom_call_target="tpu_custom_call" | custom-call | flops 600000000 | bytes 3000000 | tf_op jit(solution)/shard_map/pallas_call | solution.py:22
  20.2 1.5 %collective-permute-start.1 = (bf16[256,256]{1,0:T(8,128)(2,1)S(1)}, bf16[256,256]{1,0:T(8,128)(2,1)S(1)}, u32[]{:S(2)}, u32[]{:S(2)}) collective-permute-start(bf16[256,256]{1,0:T(8,128)(2,1)S(1)} %get-tuple-element.51.refs_2_), channel_id=1, source_target_pairs={{0,4},{4,0},{8,12},{12,8},{16,20},{20,16},{24,28},{28,24},{1,5},{5... | collective-permute-start | bytes 393224 | tf_op jit(solution)/shard_map/ppermute | solution.py:268
  21.7 1.6 %collective-permute-start.3 = (bf16[256,256]{1,0:T(8,128)(2,1)S(1)}, bf16[256,256]{1,0:T(8,128)(2,1)S(1)}, u32[]{:S(2)}, u32[]{:S(2)}) collective-permute-start(bf16[256,256]{1,0:T(8,128)(2,1)S(1)} %shard_map.123), channel_id=1, source_target_pairs={{0,2},{1,3},{2,0},{3,1},{4,6},{5,7},{6,4},{7,5},{8,10},{9,11},{10,... | collective-permute-start | bytes 393224 | tf_op jit(solution)/shard_map/ppermute | solution.py:268
  23.3 2.8 %collective-permute-done.1.refs_3_ = bf16[256,256]{1,0:T(8,128)(2,1)S(1)} collective-permute-done((bf16[256,256]{1,0:T(8,128)(2,1)S(1)}, bf16[256,256]{1,0:T(8,128)(2,1)S(1)}, u32[]{:S(2)}, u32[]{:S(2)}) %collective-permute-start.1) | collective-permute-done | bytes 131104 | tf_op jit(solution)/shard_map/ppermute | solution.py:268
  26.1 1.2 %collective-permute-done.3.across_ref = bf16[256,256]{1,0:T(8,128)(2,1)S(1)} collective-permute-done((bf16[256,256]{1,0:T(8,128)(2,1)S(1)}, bf16[256,256]{1,0:T(8,128)(2,1)S(1)}, u32[]{:S(2)}, u32[]{:S(2)}) %collective-permute-start.3) | collective-permute-done | bytes 131104 | tf_op jit(solution)/shard_map/ppermute | solution.py:268
  28.1 1.5 %collective-permute-start.5 = (bf16[256,256]{1,0:T(8,128)(2,1)S(1)}, bf16[256,256]{1,0:T(8,128)(2,1)S(1)}, u32[]{:S(2)}, u32[]{:S(2)}) collective-permute-start(bf16[256,256]{1,0:T(8,128)(2,1)S(1)} %get-tuple-element.57.refs_0_.refs_4_), channel_id=1, source_target_pairs={{0,2},{1,3},{2,0},{3,1},{4,6},{5,7},{6,4},{7,5},{8,10},{9,11},{10,... | collective-permute-start | bytes 393224 | tf_op jit(solution)/shard_map/ppermute | solution.py:268
  29.6 1.4 %collective-permute-start.7 = (bf16[256,128]{1,0:T(8,128)(2,1)S(1)}, bf16[256,128]{1,0:T(8,128)(2,1)S(1)}, u32[]{:S(2)}, u32[]{:S(2)}) collective-permute-start(bf16[256,128]{1,0:T(8,128)(2,1)S(1)} %get-tuple-element.62), channel_id=1, source_target_pairs={{0,4},{4,0},{8,12},{12,8},{16,20},{20,16},{24,28},{28,24},{1,5},{5... | collective-permute-start | bytes 196616 | tf_op jit(solution)/shard_map/ppermute | solution.py:268
  31.0 2.9 %collective-permute-done.7.refs_8_ = bf16[256,128]{1,0:T(8,128)(2,1)S(1)} collective-permute-done((bf16[256,128]{1,0:T(8,128)(2,1)S(1)}, bf16[256,128]{1,0:T(8,128)(2,1)S(1)}, u32[]{:S(2)}, u32[]{:S(2)}) %collective-permute-start.7) | collective-permute-done | bytes 65568 | tf_op jit(solution)/shard_map/ppermute | solution.py:268
  34.9 3.2 %collective-permute-done.9.refs_10_ = bf16[256,128]{1,0:T(8,128)(2,1)S(1)} collective-permute-done((bf16[256,128]{1,0:T(8,128)(2,1)S(1)}, bf16[256,128]{1,0:T(8,128)(2,1)S(1)}, u32[]{:S(2)}, u32[]{:S(2)}) %collective-permute-start.9) | collective-permute-done | bytes 65568 | tf_op jit(solution)/shard_map/ppermute | solution.py:268
  38.1 1.2 %collective-permute-done.10.refs_11_ = bf16[256,128]{1,0:T(8,128)(2,1)S(1)} collective-permute-done((bf16[256,128]{1,0:T(8,128)(2,1)S(1)}, bf16[256,128]{1,0:T(8,128)(2,1)S(1)}, u32[]{:S(2)}, u32[]{:S(2)}) %collective-permute-start.10) | collective-permute-done | bytes 65568 | tf_op jit(solution)/shard_map/ppermute | solution.py:268
  40.2 1.1 %collective-permute-start.11 = (bf16[2,2,256,128]{3,2,1,0:T(8,128)(2,1)S(1)}, bf16[2,2,256,128]{3,2,1,0:T(8,128)(2,1)S(1)}, u32[]{:S(2)}, u32[]{:S(2)}) collective-permute-start(bf16[2,2,256,128]{3,2,1,0:T(8,128)(2,1)S(1)} %get-tuple-element.64), channel_id=1, source_target_pairs={{0,8},{4,12},{8,0},{12,4},{16,24},{20,28},{24,16},{28,20},{1,9},{5... | collective-permute-start | bytes 786440 | tf_op jit(solution)/shard_map/ppermute | solution.py:268
  41.3 7.3 %collective-permute-done.11.beside_ref.next_ref = bf16[2,2,256,128]{3,2,1,0:T(8,128)(2,1)S(1)} collective-permute-done((bf16[2,2,256,128]{3,2,1,0:T(8,128)(2,1)S(1)}, bf16[2,2,256,128]{3,2,1,0:T(8,128)(2,1)S(1)}, u32[]{:S(2)}, u32[]{:S(2)}) %collective-permute-start.11) | collective-permute-done | bytes 262176 | tf_op jit(solution)/shard_map/ppermute | solution.py:268
  48.6 1.5 %collective-permute-start.12 = (bf16[2,256,128]{2,1,0:T(8,128)(2,1)S(1)}, bf16[2,256,128]{2,1,0:T(8,128)(2,1)S(1)}, u32[]{:S(2)}, u32[]{:S(2)}) collective-permute-start(bf16[2,256,128]{2,1,0:T(8,128)(2,1)S(1)} %shard_map.128), channel_id=1, source_target_pairs={{0,16},{4,20},{8,24},{12,28},{16,0},{20,4},{24,8},{28,12},{1,17},{... | collective-permute-start | bytes 393224 | tf_op jit(solution)/shard_map/ppermute | solution.py:268
  50.1 1.5 %shard_map.125 = (f32[256,256]{1,0:T(8,128)S(1)}, bf16[512,256]{1,0:T(8,128)(2,1)}) custom-call(s32[1]{0:T(128)} %bitcast.1.rep_ref, bf16[256,768]{1,0:T(8,128)(2,1)S(1)} %get-tuple-element.45.high_ref, bf16[256,768]{1,0:T(8,128)(2,1)S(1)} %get-tuple-element.46.low_ref, f32[256,128]{1,0:T(8,128)S(1)} %get-tuple-element.47.deg_ref, ...), custom_call_target="tpu_custom_call" | custom-call | flops 600000000 | bytes 3000000 | tf_op jit(solution)/shard_map/pallas_call | solution.py:22
  51.6 3.6 %all-to-all-start.1 = ((bf16[8,64,256]{2,1,0:T(8,128)(2,1)}), bf16[8,64,256]{2,1,0:T(8,128)(2,1)S(1)}, u32[]{:S(2)}, u32[]{:S(2)}) async-start(bf16[8,64,256]{2,1,0:T(8,128)(2,1)} %bitcast.4), calls=%async_computation.1 | async-start | bytes 524288 | tf_op jit(solution)/shard_map/all_to_all | solution.py:306
  55.3 1.9 %collective-permute-done.12.far_ref = bf16[2,256,128]{2,1,0:T(8,128)(2,1)S(1)} collective-permute-done((bf16[2,256,128]{2,1,0:T(8,128)(2,1)S(1)}, bf16[2,256,128]{2,1,0:T(8,128)(2,1)S(1)}, u32[]{:S(2)}, u32[]{:S(2)}) %collective-permute-start.12) | collective-permute-done | bytes 131104 | tf_op jit(solution)/shard_map/ppermute | solution.py:268
  57.5 4.6 %collective-permute-start.13 = (bf16[2,256,128]{2,1,0:T(8,128)(2,1)S(1)}, bf16[2,256,128]{2,1,0:T(8,128)(2,1)S(1)}, u32[]{:S(2)}, u32[]{:S(2)}) collective-permute-start(bf16[2,256,128]{2,1,0:T(8,128)(2,1)S(1)} %shard_map.129.refs_0_), channel_id=1, source_target_pairs={{0,16},{4,20},{8,24},{12,28},{16,0},{20,4},{24,8},{28,12},{1,17},{... | collective-permute-start | bytes 393224 | tf_op jit(solution)/shard_map/ppermute | solution.py:268
  62.1 3.7 %collective-permute-done.17.refs_2_ = bf16[2,256,128]{2,1,0:T(8,128)(2,1)S(1)} collective-permute-done((bf16[2,256,128]{2,1,0:T(8,128)(2,1)S(1)}, bf16[2,256,128]{2,1,0:T(8,128)(2,1)S(1)}, u32[]{:S(2)}, u32[]{:S(2)}) %collective-permute-start.17) | collective-permute-done | bytes 131104 | tf_op jit(solution)/shard_map/ppermute | solution.py:268
  65.8 3.0 %collective-permute-start.18 = (bf16[2,256,128]{2,1,0:T(8,128)(2,1)S(1)}, bf16[2,256,128]{2,1,0:T(8,128)(2,1)S(1)}, u32[]{:S(2)}, u32[]{:S(2)}) collective-permute-start(bf16[2,256,128]{2,1,0:T(8,128)(2,1)S(1)} %collective-permute-done.17.refs_2_), channel_id=1, source_target_pairs={{0,4},{4,0},{8,12},{12,8},{16,20},{20,16},{24,28},{28,24},{1,5},{5... | collective-permute-start | bytes 393224 | tf_op jit(solution)/shard_map/ppermute | solution.py:268
  69.2 2.6 %collective-permute-done.18.refs_3_ = bf16[2,256,128]{2,1,0:T(8,128)(2,1)S(1)} collective-permute-done((bf16[2,256,128]{2,1,0:T(8,128)(2,1)S(1)}, bf16[2,256,128]{2,1,0:T(8,128)(2,1)S(1)}, u32[]{:S(2)}, u32[]{:S(2)}) %collective-permute-start.18) | collective-permute-done | bytes 131104 | tf_op jit(solution)/shard_map/ppermute | solution.py:268
  71.8 2.3 %collective-permute-start.19 = (bf16[2,256,128]{2,1,0:T(8,128)(2,1)S(1)}, bf16[2,256,128]{2,1,0:T(8,128)(2,1)S(1)}, u32[]{:S(2)}, u32[]{:S(2)}) collective-permute-start(bf16[2,256,128]{2,1,0:T(8,128)(2,1)S(1)} %collective-permute-done.13.refs_4_), channel_id=1, source_target_pairs={{0,4},{4,0},{8,12},{12,8},{16,20},{20,16},{24,28},{28,24},{1,5},{5... | collective-permute-start | bytes 393224 | tf_op jit(solution)/shard_map/ppermute | solution.py:268
  74.1 1.4 %collective-permute-start.16 = (bf16[2,256,128]{2,1,0:T(8,128)(2,1)S(1)}, bf16[2,256,128]{2,1,0:T(8,128)(2,1)S(1)}, u32[]{:S(2)}, u32[]{:S(2)}) collective-permute-start(bf16[2,256,128]{2,1,0:T(8,128)(2,1)S(1)} %collective-permute-done.15.refs_6_), channel_id=1, source_target_pairs={{0,4},{4,0},{8,12},{12,8},{16,20},{20,16},{24,28},{28,24},{1,5},{5... | collective-permute-start | bytes 393224 | tf_op jit(solution)/shard_map/ppermute | solution.py:268
  77.0 1.0 %shard_map.130 = (bf16[256,1024]{1,0:T(8,128)(2,1)}, bf16[256,1024]{1,0:T(8,128)(2,1)}) custom-call(s32[1]{0:T(128)} %bitcast.dom_ref, bf16[2,256,128]{2,1,0:T(8,128)(2,1)S(1)} %shard_map.129.refs_0_, bf16[2,256,128]{2,1,0:T(8,128)(2,1)S(1)} %collective-permute-done.14.refs_1_, bf16[2,256,128]{2,1,0:T(8,128)(2,1)S(1)} %collective-permute-done.17.refs_2_, ...), custom_call_target="tpu_custom_call" | custom-call | bytes 1000000 | tf_op jit(solution)/shard_map/pallas_call | solution.py:22
  78.0 1.1 %collective-permute-done.16.refs_0_ = bf16[2,256,128]{2,1,0:T(8,128)(2,1)S(1)} collective-permute-done((bf16[2,256,128]{2,1,0:T(8,128)(2,1)S(1)}, bf16[2,256,128]{2,1,0:T(8,128)(2,1)S(1)}, u32[]{:S(2)}, u32[]{:S(2)}) %collective-permute-start.16) | collective-permute-done | bytes 131104 | tf_op jit(solution)/shard_map/ppermute | solution.py:268
  (40 shorter events, 6.4 us)
Async XLA Ops:
  0.6 11.6 %copy-start = (bf16[256,1024]{1,0:T(8,128)(2,1)S(1)}, bf16[256,1024]{1,0:T(8,128)(2,1)}, u32[]{:S(2)}) copy-start(bf16[256,1024]{1,0:T(8,128)(2,1)} %self_hbm) | copy-start | bytes 1572868
  2.8 7.4 %copy-start.4 = (bf16[256,256]{1,0:T(8,128)(2,1)S(1)}, bf16[256,256]{1,0:T(8,128)(2,1)}, u32[]{:S(2)}) copy-start(bf16[256,256]{1,0:T(8,128)(2,1)} %refs_0_.1) | copy-start | bytes 393220
  2.8 16.3 %all-to-all-start = ((bf16[8,64,256]{2,1,0:T(8,128)(2,1)}), bf16[8,64,256]{2,1,0:T(8,128)(2,1)S(1)}, u32[]{:S(2)}, u32[]{:S(2)}) async-start(bf16[8,64,256]{2,1,0:T(8,128)(2,1)} %bitcast.8), calls=%async_computation | async-start | bytes 524288 | tf_op jit(solution)/shard_map/all_to_all | solution.py:306
  10.2 7.6 %collective-permute-start = (bf16[256,256]{1,0:T(8,128)(2,1)S(1)}, bf16[256,256]{1,0:T(8,128)(2,1)S(1)}, u32[]{:S(2)}, u32[]{:S(2)}) collective-permute-start(bf16[256,256]{1,0:T(8,128)(2,1)S(1)} %copy-done.4), channel_id=1, source_target_pairs={{0,4},{4,0},{8,12},{12,8},{16,20},{20,16},{24,28},{28,24},{1,5},{5... | collective-permute-start | bytes 393224 | tf_op jit(solution)/shard_map/ppermute | solution.py:268
  12.2 0.7 copy-start.6
  12.2 0.7 copy-start.7
  12.9 1.0 %copy-start.1 = (bf16[256,1024]{1,0:T(8,128)(2,1)S(1)}, bf16[256,1024]{1,0:T(8,128)(2,1)}, u32[]{:S(2)}) copy-start(bf16[256,1024]{1,0:T(8,128)(2,1)} %neigh_hbm) | copy-start | bytes 1572868
  14.0 0.9 %copy-start.3 = (bf16[8,128,128]{2,1,0:T(8,128)(2,1)S(1)}, bf16[8,128,128]{2,1,0:T(8,128)(2,1)}, u32[]{:S(2)}) copy-start(bf16[8,128,128]{2,1,0:T(8,128)(2,1)} %tiles_ref) | copy-start | bytes 786436
  20.1 1.6 %collective-permute-start.2 = (bf16[2,256,256]{2,1,0:T(8,128)(2,1)S(1)}, bf16[2,256,256]{2,1,0:T(8,128)(2,1)S(1)}, u32[]{:S(2)}, u32[]{:S(2)}) collective-permute-start(bf16[2,256,256]{2,1,0:T(8,128)(2,1)S(1)} %get-tuple-element.53), channel_id=1, source_target_pairs={{0,1},{1,0},{2,3},{3,2},{4,5},{5,4},{6,7},{7,6},{8,9},{9,8},{10,11... | collective-permute-start | bytes 786440 | tf_op jit(solution)/shard_map/ppermute | solution.py:268
  20.2 5.9 %collective-permute-start.1 = (bf16[256,256]{1,0:T(8,128)(2,1)S(1)}, bf16[256,256]{1,0:T(8,128)(2,1)S(1)}, u32[]{:S(2)}, u32[]{:S(2)}) collective-permute-start(bf16[256,256]{1,0:T(8,128)(2,1)S(1)} %get-tuple-element.51.refs_2_), channel_id=1, source_target_pairs={{0,4},{4,0},{8,12},{12,8},{16,20},{20,16},{24,28},{28,24},{1,5},{5... | collective-permute-start | bytes 393224 | tf_op jit(solution)/shard_map/ppermute | solution.py:268
  21.7 5.6 %copy-start.5 = (bf16[256,256]{1,0:T(8,128)(2,1)S(1)}, bf16[256,256]{1,0:T(8,128)(2,1)}, u32[]{:S(2)}) copy-start(bf16[256,256]{1,0:T(8,128)(2,1)} %gout_ref) | copy-start | bytes 393220
  21.7 5.6 %collective-permute-start.3 = (bf16[256,256]{1,0:T(8,128)(2,1)S(1)}, bf16[256,256]{1,0:T(8,128)(2,1)S(1)}, u32[]{:S(2)}, u32[]{:S(2)}) collective-permute-start(bf16[256,256]{1,0:T(8,128)(2,1)S(1)} %shard_map.123), channel_id=1, source_target_pairs={{0,2},{1,3},{2,0},{3,1},{4,6},{5,7},{6,4},{7,5},{8,10},{9,11},{10,... | collective-permute-start | bytes 393224 | tf_op jit(solution)/shard_map/ppermute | solution.py:268
  28.1 6.3 %collective-permute-start.5 = (bf16[256,256]{1,0:T(8,128)(2,1)S(1)}, bf16[256,256]{1,0:T(8,128)(2,1)S(1)}, u32[]{:S(2)}, u32[]{:S(2)}) collective-permute-start(bf16[256,256]{1,0:T(8,128)(2,1)S(1)} %get-tuple-element.57.refs_0_.refs_4_), channel_id=1, source_target_pairs={{0,2},{1,3},{2,0},{3,1},{4,6},{5,7},{6,4},{7,5},{8,10},{9,11},{10,... | collective-permute-start | bytes 393224 | tf_op jit(solution)/shard_map/ppermute | solution.py:268
  29.6 4.3 %collective-permute-start.7 = (bf16[256,128]{1,0:T(8,128)(2,1)S(1)}, bf16[256,128]{1,0:T(8,128)(2,1)S(1)}, u32[]{:S(2)}, u32[]{:S(2)}) collective-permute-start(bf16[256,128]{1,0:T(8,128)(2,1)S(1)} %get-tuple-element.62), channel_id=1, source_target_pairs={{0,4},{4,0},{8,12},{12,8},{16,20},{20,16},{24,28},{28,24},{1,5},{5... | collective-permute-start | bytes 196616 | tf_op jit(solution)/shard_map/ppermute | solution.py:268
  31.0 7.1 %collective-permute-start.4 = (bf16[256,256]{1,0:T(8,128)(2,1)S(1)}, bf16[256,256]{1,0:T(8,128)(2,1)S(1)}, u32[]{:S(2)}, u32[]{:S(2)}) collective-permute-start(bf16[256,256]{1,0:T(8,128)(2,1)S(1)} %get-tuple-element.57.refs_0_.refs_4_), channel_id=1, source_target_pairs={{0,1},{1,0},{2,3},{3,2},{4,5},{5,4},{6,7},{7,6},{8,9},{9,8},{10,11... | collective-permute-start | bytes 393224 | tf_op jit(solution)/shard_map/ppermute | solution.py:268
  33.9 4.3 %collective-permute-start.9 = (bf16[256,128]{1,0:T(8,128)(2,1)S(1)}, bf16[256,128]{1,0:T(8,128)(2,1)S(1)}, u32[]{:S(2)}, u32[]{:S(2)}) collective-permute-start(bf16[256,128]{1,0:T(8,128)(2,1)S(1)} %collective-permute-done.7.refs_8_), channel_id=1, source_target_pairs={{0,2},{1,3},{2,0},{3,1},{4,6},{5,7},{6,4},{7,5},{8,10},{9,11},{10,... | collective-permute-start | bytes 196616 | tf_op jit(solution)/shard_map/ppermute | solution.py:268
  34.4 5.0 %collective-permute-start.6 = (bf16[256,256]{1,0:T(8,128)(2,1)S(1)}, bf16[256,256]{1,0:T(8,128)(2,1)S(1)}, u32[]{:S(2)}, u32[]{:S(2)}) collective-permute-start(bf16[256,256]{1,0:T(8,128)(2,1)S(1)} %collective-permute-done.5.refs_2_.refs_6_), channel_id=1, source_target_pairs={{0,1},{1,0},{2,3},{3,2},{4,5},{5,4},{6,7},{7,6},{8,9},{9,8},{10,11... | collective-permute-start | bytes 393224 | tf_op jit(solution)/shard_map/ppermute | solution.py:268
  34.4 3.7 %collective-permute-start.8 = (bf16[256,128]{1,0:T(8,128)(2,1)S(1)}, bf16[256,128]{1,0:T(8,128)(2,1)S(1)}, u32[]{:S(2)}, u32[]{:S(2)}) collective-permute-start(bf16[256,128]{1,0:T(8,128)(2,1)S(1)} %collective-permute-done.7.refs_8_), channel_id=1, source_target_pairs={{0,1},{1,0},{2,3},{3,2},{4,5},{5,4},{6,7},{7,6},{8,9},{9,8},{10,11... | collective-permute-start | bytes 196616 | tf_op jit(solution)/shard_map/ppermute | solution.py:268
  38.1 1.3 %collective-permute-start.10 = (bf16[256,128]{1,0:T(8,128)(2,1)S(1)}, bf16[256,128]{1,0:T(8,128)(2,1)S(1)}, u32[]{:S(2)}, u32[]{:S(2)}) collective-permute-start(bf16[256,128]{1,0:T(8,128)(2,1)S(1)} %collective-permute-done.9.refs_10_), channel_id=1, source_target_pairs={{0,1},{1,0},{2,3},{3,2},{4,5},{5,4},{6,7},{7,6},{8,9},{9,8},{10,11... | collective-permute-start | bytes 196616 | tf_op jit(solution)/shard_map/ppermute | solution.py:268
  40.2 8.4 %collective-permute-start.11 = (bf16[2,2,256,128]{3,2,1,0:T(8,128)(2,1)S(1)}, bf16[2,2,256,128]{3,2,1,0:T(8,128)(2,1)S(1)}, u32[]{:S(2)}, u32[]{:S(2)}) collective-permute-start(bf16[2,2,256,128]{3,2,1,0:T(8,128)(2,1)S(1)} %get-tuple-element.64), channel_id=1, source_target_pairs={{0,8},{4,12},{8,0},{12,4},{16,24},{20,28},{24,16},{28,20},{1,9},{5... | collective-permute-start | bytes 786440 | tf_op jit(solution)/shard_map/ppermute | solution.py:268
  48.6 8.5 %collective-permute-start.12 = (bf16[2,256,128]{2,1,0:T(8,128)(2,1)S(1)}, bf16[2,256,128]{2,1,0:T(8,128)(2,1)S(1)}, u32[]{:S(2)}, u32[]{:S(2)}) collective-permute-start(bf16[2,256,128]{2,1,0:T(8,128)(2,1)S(1)} %shard_map.128), channel_id=1, source_target_pairs={{0,16},{4,20},{8,24},{12,28},{16,0},{20,4},{24,8},{28,12},{1,17},{... | collective-permute-start | bytes 393224 | tf_op jit(solution)/shard_map/ppermute | solution.py:268
  51.6 23.9 %all-to-all-start.1 = ((bf16[8,64,256]{2,1,0:T(8,128)(2,1)}), bf16[8,64,256]{2,1,0:T(8,128)(2,1)S(1)}, u32[]{:S(2)}, u32[]{:S(2)}) async-start(bf16[8,64,256]{2,1,0:T(8,128)(2,1)} %bitcast.4), calls=%async_computation.1 | async-start | bytes 524288 | tf_op jit(solution)/shard_map/all_to_all | solution.py:306
  57.2 18.4 %copy-start.2 = (bf16[256,512]{1,0:T(8,128)(2,1)S(1)}, bf16[256,512]{1,0:T(8,128)(2,1)}, u32[]{:S(2)}) copy-start(bf16[256,512]{1,0:T(8,128)(2,1)} %get-tuple-element.56.onehot_ref) | copy-start | bytes 786436
  57.2 8.6 %collective-permute-start.17 = (bf16[2,256,128]{2,1,0:T(8,128)(2,1)S(1)}, bf16[2,256,128]{2,1,0:T(8,128)(2,1)S(1)}, u32[]{:S(2)}, u32[]{:S(2)}) collective-permute-start(bf16[2,256,128]{2,1,0:T(8,128)(2,1)S(1)} %shard_map.129.refs_0_), channel_id=1, source_target_pairs={{0,8},{4,12},{8,0},{12,4},{16,24},{20,28},{24,16},{28,20},{1,9},{5... | collective-permute-start | bytes 393224 | tf_op jit(solution)/shard_map/ppermute | solution.py:268
  57.5 11.6 %collective-permute-start.13 = (bf16[2,256,128]{2,1,0:T(8,128)(2,1)S(1)}, bf16[2,256,128]{2,1,0:T(8,128)(2,1)S(1)}, u32[]{:S(2)}, u32[]{:S(2)}) collective-permute-start(bf16[2,256,128]{2,1,0:T(8,128)(2,1)S(1)} %shard_map.129.refs_0_), channel_id=1, source_target_pairs={{0,16},{4,20},{8,24},{12,28},{16,0},{20,4},{24,8},{28,12},{1,17},{... | collective-permute-start | bytes 393224 | tf_op jit(solution)/shard_map/ppermute | solution.py:268
  62.1 7.0 %collective-permute-start.14 = (bf16[2,256,128]{2,1,0:T(8,128)(2,1)S(1)}, bf16[2,256,128]{2,1,0:T(8,128)(2,1)S(1)}, u32[]{:S(2)}, u32[]{:S(2)}) collective-permute-start(bf16[2,256,128]{2,1,0:T(8,128)(2,1)S(1)} %shard_map.129.refs_0_), channel_id=1, source_target_pairs={{0,4},{4,0},{8,12},{12,8},{16,20},{20,16},{24,28},{28,24},{1,5},{5... | collective-permute-start | bytes 393224 | tf_op jit(solution)/shard_map/ppermute | solution.py:268
  65.8 5.9 %collective-permute-start.18 = (bf16[2,256,128]{2,1,0:T(8,128)(2,1)S(1)}, bf16[2,256,128]{2,1,0:T(8,128)(2,1)S(1)}, u32[]{:S(2)}, u32[]{:S(2)}) collective-permute-start(bf16[2,256,128]{2,1,0:T(8,128)(2,1)S(1)} %collective-permute-done.17.refs_2_), channel_id=1, source_target_pairs={{0,4},{4,0},{8,12},{12,8},{16,20},{20,16},{24,28},{28,24},{1,5},{5... | collective-permute-start | bytes 393224 | tf_op jit(solution)/shard_map/ppermute | solution.py:268
  69.2 5.0 %collective-permute-start.15 = (bf16[2,256,128]{2,1,0:T(8,128)(2,1)S(1)}, bf16[2,256,128]{2,1,0:T(8,128)(2,1)S(1)}, u32[]{:S(2)}, u32[]{:S(2)}) collective-permute-start(bf16[2,256,128]{2,1,0:T(8,128)(2,1)S(1)} %collective-permute-done.13.refs_4_), channel_id=1, source_target_pairs={{0,8},{4,12},{8,0},{12,4},{16,24},{20,28},{24,16},{28,20},{1,9},{5... | collective-permute-start | bytes 393224 | tf_op jit(solution)/shard_map/ppermute | solution.py:268
  71.8 5.2 %collective-permute-start.19 = (bf16[2,256,128]{2,1,0:T(8,128)(2,1)S(1)}, bf16[2,256,128]{2,1,0:T(8,128)(2,1)S(1)}, u32[]{:S(2)}, u32[]{:S(2)}) collective-permute-start(bf16[2,256,128]{2,1,0:T(8,128)(2,1)S(1)} %collective-permute-done.13.refs_4_), channel_id=1, source_target_pairs={{0,4},{4,0},{8,12},{12,8},{16,20},{20,16},{24,28},{28,24},{1,5},{5... | collective-permute-start | bytes 393224 | tf_op jit(solution)/shard_map/ppermute | solution.py:268
  74.1 5.0 %collective-permute-start.16 = (bf16[2,256,128]{2,1,0:T(8,128)(2,1)S(1)}, bf16[2,256,128]{2,1,0:T(8,128)(2,1)S(1)}, u32[]{:S(2)}, u32[]{:S(2)}) collective-permute-start(bf16[2,256,128]{2,1,0:T(8,128)(2,1)S(1)} %collective-permute-done.15.refs_6_), channel_id=1, source_target_pairs={{0,4},{4,0},{8,12},{12,8},{16,20},{20,16},{24,28},{28,24},{1,5},{5... | collective-permute-start | bytes 393224 | tf_op jit(solution)/shard_map/ppermute | solution.py:268
